TPU v7x, 32 devices: a whole 2x2x4 slice. The times are simulated.
32 devices in a mesh: row: 4 (over z), col: 4 (over x, core), layer: 2 (over y).
Axes of the slice: x: 2, y: 2, z: 4, core: 2. Of those that a mesh axis runs over, the one named last changes fastest.
Arguments:
- density: bfloat16 [64, 11, 128, 128], P(('row', 'layer'), None, 'col'), may hold values from -1.5 to 1.5, as said below
- pattern: int32 [64, 11], replicated, may hold values from -1 to 63, as said below
- square_filter: int32 [64, 12], replicated, may hold values from 0 to 63, as said below
- cube_filter: int32 [64, 16], replicated, may hold values from 0 to 63, as said below
Outputs:
- purified: float32 [64, 16, 128, 128], P(('row', 'layer'), 'col')
Inputs may be any that keep to these rules, and one draw needn't show every extreme that they name: `density`: slot s of block row i holds the block of P at (i, pattern[i, s]), and zeros where pattern[i, s] is -1; the matrix so described is exactly symmetric. Row i lists distinct block columns, each within 5 of i modulo 64, i itself among them; unused slots hold -1; the block pattern is symmetric; some block row uses all 11 slots. `square_filter`: row i lists 12 distinct block columns, each within 10 of i modulo 64. `cube_filter`: row i lists 16 distinct block columns, each within 15 of i modulo 64.
All inputs are finite; a program needn't handle non-finite values.
Results may differ from a plain program's by a relative error of at most 0.0023.
Values may be sent and summed in bfloat16 or wider, within the bound.
No kernel may reach another device: no remote copies, remote signals or barrier semaphores. Data moves between devices by JAX's collectives and lax.ppermute only.
A program may use at most 64 MiB of HBM per device.

v0:
```python
import jax
import jax.numpy as jnp
from jax import lax
from jax.sharding import PartitionSpec as P

RADIUS = 5


def extended_2(x, sides, width):
    for axis, dim in sides:
        size, length = (lax.axis_size(axis), x.shape[dim])
        up = [(i, (i + 1) % size) for i in range(size)]
        down = [(j, i) for i, j in up]
        last = lax.slice_in_dim(x, length - width, length, axis=dim)
        leading = lax.slice_in_dim(x, 0, width, axis=dim)
        before = lax.ppermute(last, axis, up)
        after = lax.ppermute(leading, axis, down)
        x = jnp.concatenate([before, x, after], axis=dim)
    return x


def matched_slots(listed, targets):
    match = listed[:, None, :] == targets[None, :, None]
    slot_ids = jnp.arange(listed.shape[1], dtype=jnp.int32)
    picked_slot = jnp.sum(jnp.where(match, slot_ids[None, None, :], 0), axis=2)
    return (picked_slot, jnp.any(match, axis=2))


def per_device(density, pattern, square_filter, cube_filter):
    layer_count = lax.axis_size("layer")
    stack_count = lax.axis_size("row") * layer_count
    col_count = lax.axis_size("col")
    col_index = lax.axis_index("col")
    local_rows = density.shape[0]
    total_rows = local_rows * stack_count
    first_row = (lax.axis_index("row") * layer_count + lax.axis_index("layer")) * local_rows
    rows_iota = jnp.arange(local_rows, dtype=jnp.int32)
    whole_rows = lax.all_gather(density, "col", axis=2, tiled=True)
    extended = extended_2(whole_rows, ((("row", "layer"), 0),), RADIUS)

    def product_row(local_row, right_blocks, right_lists, targets):
        global_row = first_row + local_row
        listed = lax.dynamic_index_in_dim(pattern, global_row, 0, keepdims=False)
        source = jnp.where(listed >= 0, listed, global_row)
        offset = (source - global_row + RADIUS + total_rows) % total_rows - RADIUS
        position = local_row + RADIUS + offset
        right_listed = jnp.take(right_lists, source, axis=0)
        picked_slot, found = matched_slots(right_listed, targets)
        picked = right_blocks[position[:, None], picked_slot]
        picked = jnp.where(found[:, :, None, None], picked, jnp.zeros((), picked.dtype))
        left = extended[local_row + RADIUS]
        return jnp.einsum("axy,ajyz->jxz", left, picked, preferred_element_type=jnp.float32)

    def square_whole(local_row):
        targets = lax.dynamic_index_in_dim(square_filter, first_row + local_row, 0, keepdims=False)
        return product_row(local_row, extended, pattern, targets).astype(jnp.bfloat16)

    square_full = lax.map(square_whole, rows_iota)
    square_ext = extended_2(square_full, ((("row", "layer"), 0),), RADIUS)
    cube_share = cube_filter.shape[1] // col_count

    def purified_row(local_row):
        global_row = first_row + local_row
        row_cube = lax.dynamic_index_in_dim(cube_filter, global_row, 0, keepdims=False)
        targets = lax.dynamic_slice_in_dim(row_cube, col_index * cube_share, cube_share, 0)
        cube = product_row(local_row, square_ext, square_filter, targets)
        own_filter = lax.dynamic_index_in_dim(square_filter, global_row, 0, keepdims=False)
        chooser = (targets[:, None] == own_filter[None, :]).astype(jnp.bfloat16)
        own_square = jnp.einsum(
            "tj,jxz->txz",
            chooser,
            square_ext[local_row + RADIUS],
            preferred_element_type=jnp.float32,
        )
        return 3.0 * own_square - 2.0 * cube

    return lax.map(purified_row, rows_iota)


def solution(mesh):
    in_specs = (P(("row", "layer"), None, "col", None), P(), P(), P())
    out_specs = P(("row", "layer"), "col", None, None)
    return jax.shard_map(
        per_device, mesh=mesh, in_specs=in_specs, out_specs=out_specs, check_vma=False
    )
```

profile of v0, /device:TPU:0, one launch (start us, length us, event | category | flops | bytes accessed | tf_op | source)
XLA Modules:
  0.0 649.2 jit_solution(404499562796002998)
XLA Ops:
  7.3 31.4 %all-gather.2.cloned.1.call-done = bf16[8,11,128,128]{3,2,1,0:T(8,128)(2,1)} async-done(((bf16[8,11,32,128]{3,2,1,0:T(8,128)(2,1)}), bf16[8,11,128,128]{3,2,1,0:T(8,128)(2,1)}) %all-gather.2.cloned.1.call-update) | async-done | bytes 2883600 | tf_op jit(solution)/shard_map/all_gather | solution.py:38
  38.7 4.4 fusion.70
  43.1 1.5 collective-permute-start
  44.5 3.2 collective-permute-start.1
  49.2 73.3 %collective-permute-done = bf16[5,11,128,128]{3,2,1,0:T(8,128)(2,1)} collective-permute-done((bf16[5,11,128,128]{3,2,1,0:T(8,128)(2,1)}, bf16[5,11,128,128]{3,2,1,0:T(8,128)(2,1)}, u32[]{:S(2)}, u32[]{:S(2)}) %collective-permute-start) | collective-permute-done | bytes 1802272 | tf_op jit(solution)/shard_map/ppermute | solution.py:16
  122.5 1.6 constant_dynamic-update-slice_fusion.4
  124.7 1.8 constant_dynamic-update-slice_fusion.2
  126.5 2.7 copy-done
  129.2 279.3 %while.25 = (s32[]{:T(128)}, bf16[8,12,128,128]{3,2,1,0:T(8,128)(2,1)S(1)}, s32[8]{0:T(128)S(1)}, s32[]{:T(128)}, s32[64,11]{1,0:T(8,128)}, /*index=5*/s32[64,12...) while((s32[]{:T(128)}, ...), condition=%wide.region_3.4_spmd, body=%wide.region_0.3_spmd.sunk | while | flops 556016768 | bytes 23965456 | solution.py:58
  135.8 15.0 %gather_fusion.1 = bf16[132,128,128]{2,1,0:T(8,128)(2,1)} fusion(bf16[18,11,128,128]{3,2,1,0:T(8,128)(2,1)} %get-tuple-element.525, s32[132]{0:T(256)S(1)} %reshape.262), kind=kCustom, calls=%fused_computation.1.clone.1 | custom fusion | bytes 8651808 | tf_op jit(solution)/shard_map/while/body/eval_jaxpr/gather | solution.py:49
  150.8 6.5 %copy.83 = bf16[11,12,128,128]{2,3,0,1:T(8,128)(2,1)} copy(bf16[11,12,128,128]{3,2,1,0:T(8,128)(2,1)} %bitcast.135) | data formatting | bytes 8650752 | tf_op jit(solution)/shard_map/while/body/eval_jaxpr/gather | solution.py:49
  158.4 4.4 fusion.97
  170.7 15.0 %gather_fusion.1 = bf16[132,128,128]{2,1,0:T(8,128)(2,1)} fusion(bf16[18,11,128,128]{3,2,1,0:T(8,128)(2,1)} %get-tuple-element.525, s32[132]{0:T(256)S(1)} %reshape.262), kind=kCustom, calls=%fused_computation.1.clone.1 | custom fusion | bytes 8651808 | tf_op jit(solution)/shard_map/while/body/eval_jaxpr/gather | solution.py:49
  185.7 6.5 %copy.83 = bf16[11,12,128,128]{2,3,0,1:T(8,128)(2,1)} copy(bf16[11,12,128,128]{3,2,1,0:T(8,128)(2,1)} %bitcast.135) | data formatting | bytes 8650752 | tf_op jit(solution)/shard_map/while/body/eval_jaxpr/gather | solution.py:49
  193.3 4.4 fusion.97
  201.0 1.3 gather_fusion
  205.6 15.0 %gather_fusion.1 = bf16[132,128,128]{2,1,0:T(8,128)(2,1)} fusion(bf16[18,11,128,128]{3,2,1,0:T(8,128)(2,1)} %get-tuple-element.525, s32[132]{0:T(256)S(1)} %reshape.262), kind=kCustom, calls=%fused_computation.1.clone.1 | custom fusion | bytes 8651808 | tf_op jit(solution)/shard_map/while/body/eval_jaxpr/gather | solution.py:49
  220.6 6.5 %copy.83 = bf16[11,12,128,128]{2,3,0,1:T(8,128)(2,1)} copy(bf16[11,12,128,128]{3,2,1,0:T(8,128)(2,1)} %bitcast.135) | data formatting | bytes 8650752 | tf_op jit(solution)/shard_map/while/body/eval_jaxpr/gather | solution.py:49
  228.3 4.4 fusion.97
  240.5 15.0 %gather_fusion.1 = bf16[132,128,128]{2,1,0:T(8,128)(2,1)} fusion(bf16[18,11,128,128]{3,2,1,0:T(8,128)(2,1)} %get-tuple-element.525, s32[132]{0:T(256)S(1)} %reshape.262), kind=kCustom, calls=%fused_computation.1.clone.1 | custom fusion | bytes 8651808 | tf_op jit(solution)/shard_map/while/body/eval_jaxpr/gather | solution.py:49
  255.5 6.5 %copy.83 = bf16[11,12,128,128]{2,3,0,1:T(8,128)(2,1)} copy(bf16[11,12,128,128]{3,2,1,0:T(8,128)(2,1)} %bitcast.135) | data formatting | bytes 8650752 | tf_op jit(solution)/shard_map/while/body/eval_jaxpr/gather | solution.py:49
  263.2 4.4 fusion.97
  270.8 1.3 gather_fusion
  275.4 15.0 %gather_fusion.1 = bf16[132,128,128]{2,1,0:T(8,128)(2,1)} fusion(bf16[18,11,128,128]{3,2,1,0:T(8,128)(2,1)} %get-tuple-element.525, s32[132]{0:T(256)S(1)} %reshape.262), kind=kCustom, calls=%fused_computation.1.clone.1 | custom fusion | bytes 8651808 | tf_op jit(solution)/shard_map/while/body/eval_jaxpr/gather | solution.py:49
  290.4 6.5 %copy.83 = bf16[11,12,128,128]{2,3,0,1:T(8,128)(2,1)} copy(bf16[11,12,128,128]{3,2,1,0:T(8,128)(2,1)} %bitcast.135) | data formatting | bytes 8650752 | tf_op jit(solution)/shard_map/while/body/eval_jaxpr/gather | solution.py:49
  298.1 4.4 fusion.97
  305.7 1.3 gather_fusion
  310.3 15.0 %gather_fusion.1 = bf16[132,128,128]{2,1,0:T(8,128)(2,1)} fusion(bf16[18,11,128,128]{3,2,1,0:T(8,128)(2,1)} %get-tuple-element.525, s32[132]{0:T(256)S(1)} %reshape.262), kind=kCustom, calls=%fused_computation.1.clone.1 | custom fusion | bytes 8651808 | tf_op jit(solution)/shard_map/while/body/eval_jaxpr/gather | solution.py:49
  325.4 6.5 %copy.83 = bf16[11,12,128,128]{2,3,0,1:T(8,128)(2,1)} copy(bf16[11,12,128,128]{3,2,1,0:T(8,128)(2,1)} %bitcast.135) | data formatting | bytes 8650752 | tf_op jit(solution)/shard_map/while/body/eval_jaxpr/gather | solution.py:49
  333.0 4.4 fusion.97
  345.3 15.0 %gather_fusion.1 = bf16[132,128,128]{2,1,0:T(8,128)(2,1)} fusion(bf16[18,11,128,128]{3,2,1,0:T(8,128)(2,1)} %get-tuple-element.525, s32[132]{0:T(256)S(1)} %reshape.262), kind=kCustom, calls=%fused_computation.1.clone.1 | custom fusion | bytes 8651808 | tf_op jit(solution)/shard_map/while/body/eval_jaxpr/gather | solution.py:49
  360.3 6.5 %copy.83 = bf16[11,12,128,128]{2,3,0,1:T(8,128)(2,1)} copy(bf16[11,12,128,128]{3,2,1,0:T(8,128)(2,1)} %bitcast.135) | data formatting | bytes 8650752 | tf_op jit(solution)/shard_map/while/body/eval_jaxpr/gather | solution.py:49
  367.9 4.4 fusion.97
  380.2 15.0 %gather_fusion.1 = bf16[132,128,128]{2,1,0:T(8,128)(2,1)} fusion(bf16[18,11,128,128]{3,2,1,0:T(8,128)(2,1)} %get-tuple-element.525, s32[132]{0:T(256)S(1)} %reshape.262), kind=kCustom, calls=%fused_computation.1.clone.1 | custom fusion | bytes 8651808 | tf_op jit(solution)/shard_map/while/body/eval_jaxpr/gather | solution.py:49
  395.2 6.5 %copy.83 = bf16[11,12,128,128]{2,3,0,1:T(8,128)(2,1)} copy(bf16[11,12,128,128]{3,2,1,0:T(8,128)(2,1)} %bitcast.135) | data formatting | bytes 8650752 | tf_op jit(solution)/shard_map/while/body/eval_jaxpr/gather | solution.py:49
  402.8 4.4 fusion.97
  408.5 2.6 fusion.69
  411.1 2.4 collective-permute-start.2
  413.4 2.7 collective-permute-start.3
  416.8 80.7 %collective-permute-done.2 = bf16[5,12,128,128]{3,2,1,0:T(8,128)(2,1)} collective-permute-done((bf16[5,12,128,128]{3,2,1,0:T(8,128)(2,1)}, bf16[5,12,128,128]{3,2,1,0:T(8,128)(2,1)}, u32[]{:S(2)}, u32[]{:S(2)}) %collective-permute-start.2) | collective-permute-done | bytes 1966112 | tf_op jit(solution)/shard_map/ppermute | solution.py:16
  497.5 2.2 collective-permute-done.3
  499.7 5.7 pad_maximum_fusion
  505.4 137.0 %while.26 = (s32[]{:T(128)}, f32[8,4,128,128]{3,2,1,0:T(8,128)}, s32[8]{0:T(128)S(1)}, s32[]{:T(128)}, s32[64,16]{1,0:T(8,128)}, /*index=5*/s32[]{:T(128)}, s32[...) while((s32[]{:T(128)}, f32[8,4,128,128]{3,2,1,0:T(8,128)}, ...), condition=%wide.region_7.8_spmd, body=%wide.region_4.7_spmd.sunk | while | flops 187044160 | bytes 8235483 | solution.py:77
  512.4 4.0 gather_fusion.3
  519.7 2.0 fusion.108
  529.5 4.0 gather_fusion.3
  536.8 2.0 fusion.108
  546.6 4.0 gather_fusion.3
  553.9 2.0 fusion.108
  558.9 1.3 gather_fusion.2
  563.8 4.0 gather_fusion.3
  571.0 2.0 fusion.108
  576.0 1.3 gather_fusion.2
  580.9 4.0 gather_fusion.3
  588.1 2.0 fusion.108
  593.1 1.3 gather_fusion.2
  598.0 4.0 gather_fusion.3
  605.3 2.0 fusion.108
  610.2 1.3 gather_fusion.2
  615.1 4.0 gather_fusion.3
  622.4 2.0 fusion.108
  627.3 1.3 gather_fusion.2
  632.2 4.0 gather_fusion.3
  639.5 2.0 fusion.108
  (292 shorter events, 120.5 us)
Async XLA Ops:
  6.5 32.2 %all-gather.2.cloned.1.call-start = ((), (), s32[]{:S(2)}) async-start(), calls=%async_computation | async-start | bytes 3604480 | tf_op jit(solution)/shard_map/all_gather | solution.py:38
  7.3 40.5 %copy-start.2 = (s32[64,11]{0,1:T(8,128)S(1)}, s32[64,11]{0,1:T(8,128)}, u32[]{:S(2)}) copy-start(s32[64,11]{0,1:T(8,128)} %param.9) | copy-start | bytes 8452
  7.3 41.2 %copy-start.3 = (s32[64,12]{0,1:T(8,128)S(1)}, s32[64,12]{0,1:T(8,128)}, u32[]{:S(2)}) copy-start(s32[64,12]{0,1:T(8,128)} %param.10) | copy-start | bytes 9220
  43.1 79.4 %collective-permute-start = (bf16[5,11,128,128]{3,2,1,0:T(8,128)(2,1)}, bf16[5,11,128,128]{3,2,1,0:T(8,128)(2,1)}, u32[]{:S(2)}, u32[]{:S(2)}) collective-permute-start(bf16[5,11,128,128]{3,2,1,0:T(8,128)(2,1)} %get-tuple-element.390), channel_id=1, source_target_pairs={{0,1},{1,8},{8,9},{9,16},{16,17},{17,24},{24,25},{25,0},{2,3},{3,1... | collective-permute-start | bytes 5406728 | tf_op jit(solution)/shard_map/ppermute | solution.py:16
  44.5 80.1 %collective-permute-start.1 = (bf16[5,11,128,128]{3,2,1,0:T(8,128)(2,1)}, bf16[5,11,128,128]{3,2,1,0:T(8,128)(2,1)}, u32[]{:S(2)}, u32[]{:S(2)}) collective-permute-start(bf16[5,11,128,128]{3,2,1,0:T(8,128)(2,1)} %get-tuple-element.389), channel_id=1, source_target_pairs={{1,0},{8,1},{9,8},{16,9},{17,16},{24,17},{25,24},{0,25},{3,2},{10,... | collective-permute-start | bytes 5406728 | tf_op jit(solution)/shard_map/ppermute | solution.py:17
  49.2 74.9 %copy-start.1 = (bf16[8,11,128,128]{3,2,1,0:T(8,128)(2,1)S(1)}, bf16[8,11,128,128]{3,2,1,0:T(8,128)(2,1)}, u32[]{:S(2)}) copy-start(bf16[8,11,128,128]{3,2,1,0:T(8,128)(2,1)} %all-gather.2.cloned.1.call-done) | copy-start | bytes 8650756
  126.5 2.7 copy-start
  408.5 7.6 %copy-start.4 = (s32[64,16]{0,1:T(8,128)S(1)}, s32[64,16]{0,1:T(8,128)}, u32[]{:S(2)}) copy-start(s32[64,16]{0,1:T(8,128)} %param.11) | copy-start | bytes 12292
  411.1 86.5 %collective-permute-start.2 = (bf16[5,12,128,128]{3,2,1,0:T(8,128)(2,1)}, bf16[5,12,128,128]{3,2,1,0:T(8,128)(2,1)}, u32[]{:S(2)}, u32[]{:S(2)}) collective-permute-start(bf16[5,12,128,128]{3,2,1,0:T(8,128)(2,1)} %get-tuple-element.387), channel_id=1, source_target_pairs={{0,1},{1,8},{8,9},{9,16},{16,17},{17,24},{24,25},{25,0},{2,3},{3,1... | collective-permute-start | bytes 5898248 | tf_op jit(solution)/shard_map/ppermute | solution.py:16
  413.4 86.3 %collective-permute-start.3 = (bf16[5,12,128,128]{3,2,1,0:T(8,128)(2,1)}, bf16[5,12,128,128]{3,2,1,0:T(8,128)(2,1)}, u32[]{:S(2)}, u32[]{:S(2)}) collective-permute-start(bf16[5,12,128,128]{3,2,1,0:T(8,128)(2,1)} %get-tuple-element.388), channel_id=1, source_target_pairs={{1,0},{8,1},{9,8},{16,9},{17,16},{24,17},{25,24},{0,25},{3,2},{10,... | collective-permute-start | bytes 5898248 | tf_op jit(solution)/shard_map/ppermute | solution.py:17
Sparse Core Ops, SparseCore 0:
  8.9 29.7 all-gather.1
where the time goes:
time: 656 us; the launch traced here: 649 us
  local copies, waits for them, and re-layouts  298 us (45%)
  waiting for transfers between devices  189 us (29%)
  matrix products  53.8 us (8%)
  other arithmetic  52.5 us (8%)
  loops' own time  33.4 us (5%)
  between operations  13.5 us (2%)
  starting transfers between devices  9.77 us (1%)
    gather x24, local copies, waits for them, and re-layouts, product_row(): picked = right_blocks[position[:, None], picked_slot]  204 us
    ppermute x2, waiting for transfers between devices, extended_2(): before = lax.ppermute(last, axis, up)  154 us
    dot_general x16, matrix products, product_row(): jnp.einsum('axy,ajyz->jxz', left, picked, preferred_element_type=jnp.floa...  51.1 us
    all_gather x1, waiting for transfers between devices, per_device(): whole_rows = lax.all_gather(density, 'col', axis=2, tiled=True)  31.4 us
    gather x16, local copies, waits for them, and re-layouts, product_row(): right_listed = jnp.take(right_lists, source, axis=0)  21 us
    another operation x1, loops' own time, per_device(): return lax.map(purified_row, rows_iota)  17.2 us
    another operation x1, loops' own time, per_device(): square_full = lax.map(square_whole, rows_iota)  16.2 us
  transfers between devices with their start and end apart: 5, of which 5 were waited for; matrix products, arithmetic and copies ran while one was open for 1% of the time, Pallas kernels for 0%

commit v1 on v0

v1 whole, which is shorter than its diff:
```python
import functools

import jax
import jax.numpy as jnp
from jax import lax
from jax.experimental import pallas as pl
from jax.experimental.pallas import tpu as pltpu
from jax.sharding import PartitionSpec as P

RADIUS = 5
BAND = 2 * RADIUS + 1
ROWS = 8
NEAR = ROWS + 2 * RADIUS
STRIPS = ROWS + 4 * RADIUS
REACH = ROWS + 6 * RADIUS
NT = (((1,), (1,)), ((), ()))
VMEM = pl.BlockSpec(memory_space=pltpu.VMEM)
SMEM = pl.BlockSpec(memory_space=pltpu.SMEM)


def forward_count(j):
    return min(BAND, j + 2 * RADIUS - ROWS + 1)


def forward_list():
    return [(j, o) for j in range(ROWS) for o in range(BAND) if j + o >= ROWS]


def backward_list():
    return [(j, o) for j in range(ROWS) for o in range(BAND) if j + o < BAND - 1]


def forward2_list():
    return [(j, o) for j in range(ROWS) for o in range(BAND) if j + o >= 2 * ROWS]


def backward2_list():
    return [(j, o) for j in range(ROWS) for o in range(BAND) if j + o < BAND - 1 - ROWS]


LISTS = (forward_list(), backward_list(), forward2_list(), backward2_list())
SHIFTS = (1, -1, 2, -2)


def reorder_kernel(off, density, *refs):
    outs, band = refs[:4], refs[4]
    band[...] = jnp.zeros_like(band)
    for i in range(ROWS):
        for s in range(density.shape[1]):
            band[i, off[i, s]] = density[i, s]
    for out, entries in zip(outs, LISTS):
        for e, (j, o) in enumerate(entries):
            out[e] = band[j, o]


def square_kernel(meta, off, sq, l0, l1, l2, l3, h0, h1, h2, h3, square, left, strips):
    col = meta[0]
    strips[...] = jnp.zeros_like(strips)
    left[...] = jnp.zeros_like(left)
    for halo, entries, shift in zip((h0, h1, h2, h3), LISTS, SHIFTS):
        for e, (j, o) in enumerate(entries):
            row = j - shift * ROWS
            strips[row + 2 * RADIUS, row + o] = halo[e]
    for i in range(ROWS):
        for s in range(l0.shape[1]):
            o = off[i, s]
            for b, l in enumerate((l0, l1, l2, l3)):
                start = pl.multiple_of((col ^ b) * 32, 32)
                left[i, o, pl.ds(start, 32), :] = l[i, s]
            used = o < BAND
            strips[jnp.where(used, i + 2 * RADIUS, STRIPS), jnp.where(used, i + o, 0)] = l0[i, s]

    @pl.loop(0, ROWS)
    def _(i):
        w = jnp.concatenate([left[i, o] for o in range(BAND)], axis=1)
        rows = []
        for s in range(square.shape[1]):
            t = sq[i + RADIUS, s] - RADIUS
            rows.append(jnp.concatenate([strips[t, i + o] for o in range(BAND)], axis=1))
        x = jnp.concatenate(rows, axis=0)
        acc = lax.dot_general(x, w, NT, preferred_element_type=jnp.float32)
        square[i] = acc.reshape(square.shape[1:]).astype(square.dtype)


def cube_kernel(meta, sq, cube, before, own, after, left, o0, o1, o2, o3, strips):
    col = meta[0]
    strips[...] = jnp.zeros_like(strips)
    for ref, first in ((before, 0), (own, RADIUS), (after, RADIUS + ROWS)):
        for k in range(ref.shape[0]):
            for s in range(ref.shape[1]):
                strips[sq[first + k, s], first + k] = ref[k, s]
    outs = (o0, o1, o2, o3)
    share = o0.shape[1]

    @pl.loop(0, ROWS)
    def _(i):
        w = jnp.concatenate([left[i, o] for o in range(BAND)], axis=1)
        targets = [cube[i, (col ^ b) * share + q] for b in range(4) for q in range(share)]
        rows = [jnp.concatenate([strips[t, i + o] for o in range(BAND)], axis=1) for t in targets]
        x = jnp.concatenate(rows, axis=0)
        acc = lax.dot_general(x, w, NT, preferred_element_type=jnp.float32)
        for e, t in enumerate(targets):
            mine = strips[t, i + RADIUS].astype(jnp.float32)
            piece = 3.0 * mine - 2.0 * acc[e * 32 : (e + 1) * 32]
            outs[e // share][i, e % share] = piece.astype(o0.dtype)


def final_kernel(meta, p0, p1, p2, p3, out, whole):
    col = meta[0]
    rows = lax.broadcasted_iota(jnp.int32, (128, 128), 0)
    cols = lax.broadcasted_iota(jnp.int32, (128, 128), 1)
    eye = (rows == cols).astype(p0.dtype)
    for b, p in enumerate((p0, p1, p2, p3)):
        start = pl.multiple_of((col ^ b) * 32, 32)
        whole[:, :, pl.ds(start, 32), :] = p[...]

    @pl.loop(0, ROWS)
    def _(i):
        for q in range(out.shape[1]):
            out[i, q] = lax.dot_general(eye, whole[i, q], NT, preferred_element_type=jnp.float32)


def call(kernel, n_smem, outs, scratch, args, flops, limit=40):
    size = sum(a.size * a.dtype.itemsize for a in args[n_smem:])
    size += sum(o.size * o.dtype.itemsize for o in outs)
    return pl.pallas_call(
        kernel,
        out_shape=outs,
        in_specs=[SMEM] * n_smem + [VMEM] * (len(args) - n_smem),
        out_specs=[VMEM] * len(outs),
        scratch_shapes=scratch,
        compiler_params=pltpu.CompilerParams(vmem_limit_bytes=limit << 20),
        cost_estimate=pl.CostEstimate(flops=flops, bytes_accessed=size, transcendentals=0),
    )(*args)


def shape(*dims, dtype=jnp.bfloat16):
    return jax.ShapeDtypeStruct(dims, dtype)


def per_device(density, pattern, square_filter, cube_filter):
    layers = lax.axis_size("layer")
    groups = lax.axis_size("row") * layers
    total = groups * ROWS
    assert density.shape[0] == ROWS and lax.axis_size("col") == 4
    piece = density.shape[2:]
    col = lax.axis_index("col")
    first = (lax.axis_index("row") * layers + lax.axis_index("layer")) * ROWS

    def shifted(x, d):
        return lax.ppermute(x, ("row", "layer"), [(g, (g + d) % groups) for g in range(groups)])

    def across(x, bits):
        return lax.ppermute(x, "col", [(c, c ^ bits) for c in range(4)])

    meta = jnp.reshape(col, (1,)).astype(jnp.int32)
    own_rows = first + jnp.arange(ROWS, dtype=jnp.int32)[:, None]
    listed = lax.dynamic_slice_in_dim(pattern, first, ROWS, 0)
    off = jnp.where(listed >= 0, (listed - own_rows + RADIUS + total) % total, BAND)
    near = (first - RADIUS + jnp.arange(NEAR, dtype=jnp.int32) + total) % total
    low = first - 3 * RADIUS
    sq = (jnp.take(square_filter, near, axis=0) - low + total) % total
    cube = (lax.dynamic_slice_in_dim(cube_filter, first, ROWS, 0) - low + total) % total

    l2 = across(density, 2)
    l1 = across(density, 1)
    payload = call(
        reorder_kernel, 1, [shape(len(e), *piece) for e in LISTS],
        [pltpu.VMEM((ROWS, BAND + 1, *piece), density.dtype)], (off, density), 0,
    )
    halos = [shifted(p, d) for p, d in zip(payload, SHIFTS)]
    l3 = across(l2, 1)

    kept = square_filter.shape[1]
    square, left = call(
        square_kernel, 3,
        [shape(ROWS, kept, *piece), shape(ROWS, BAND + 1, 128, 128)],
        [pltpu.VMEM((STRIPS + 1, NEAR, *piece), density.dtype)],
        (meta, off, sq, density, l1, l2, l3, *halos), 2 * ROWS * kept * BAND * 128 * 128 * 32,
    )
    before = shifted(square[ROWS - RADIUS :], 1)
    after = shifted(square[:RADIUS], -1)
    slots = cube_filter.shape[1]
    share = slots // 4
    pieces = call(
        cube_kernel, 3, [shape(ROWS, share, *piece)] * 4,
        [pltpu.VMEM((REACH, NEAR, *piece), density.dtype)],
        (meta, sq, cube, before, square, after, left), 2 * ROWS * slots * BAND * 128 * 128 * 32,
    )
    got = [pieces[0]] + [across(pieces[b], b) for b in (1, 2, 3)]
    return call(
        final_kernel, 1, [shape(ROWS, share, 128, 128, dtype=jnp.float32)],
        [pltpu.VMEM((ROWS, share, 128, 128), density.dtype)], (meta, *got), 2 * ROWS * share * 128**3,
    )[0]


def solution(mesh):
    in_specs = (P(("row", "layer"), None, "col", None), P(), P(), P())
    out_specs = P(("row", "layer"), "col", None, None)
    return jax.shard_map(
        per_device, mesh=mesh, in_specs=in_specs, out_specs=out_specs, check_vma=False
    )
```

time: 656 us -> 104 us (0.16)
  local copies, waits for them, and re-layouts: 298 us -> 9.98 us
  waiting for transfers between devices: 189 us -> 60.1 us
  matrix products: 53.8 us -> 0 us
  other arithmetic: 52.5 us -> 0.22 us
  loops' own time: 33.4 us -> 0 us
  Pallas kernels: 0 us -> 16.9 us
  between operations: 13.5 us -> 0.07 us
    gather x40 -> x1, local copies, waits for them, and re-layouts: 225 us -> 0.56 us  [per_device(): sq = (jnp.take(square_filter, near, axis=0) - low + total) % total]
    ppermute x4 -> x12, waiting for transfers between devices: 156 us -> 60.1 us  [the longest x6 34.7 us: shifted(): lax.ppermute(x, ('row', 'layer'), [(g, (g + d) % groups) for g in range(g...]
    dot_general x24 -> x0, matrix products: 53.8 us -> none  [the longest x16 51.1 us: product_row(): jnp.einsum('axy,ajyz->jxz', left, picked, preferred_element_type=jnp.floa...]
    another operation x2 -> x0, loops' own time: 33.4 us -> none  [the longest x1 17.2 us: per_device(): return lax.map(purified_row, rows_iota)]
    all_gather x1 -> x0, waiting for transfers between devices: 31.4 us -> none  [per_device(): whole_rows = lax.all_gather(density, 'col', axis=2, tiled=True)]
    concatenate x33 -> x0, other arithmetic: 17.7 us -> none  [the longest x32 12 us: product_row(): picked = right_blocks[position[:, None], picked_slot]]
    dynamic_slice x24 -> x2, local copies, waits for them, and re-layouts: 18.2 us -> 0.84 us  [the longest x1 0.77 us: per_device(): listed = lax.dynamic_slice_in_dim(pattern, first, ROWS, 0)]
    dynamic_update_slice x32 -> x0, local copies, waits for them, and re-layouts: 17 us -> none  [the longest x16 10.2 us: per_device(): square_full = lax.map(square_whole, rows_iota)]
  transfers between devices with their start and end apart: 5 -> 12, of which waited for: 5 -> 8; matrix products, arithmetic and copies ran while one was open for 1% -> 2% of each run, Pallas kernels for 0% -> 2%
where the time goes in v1:
time: 104 us
  waiting for transfers between devices  60.1 us (58%)
  Pallas kernels  16.9 us (16%)
  starting transfers between devices  16.3 us (16%)
  local copies, waits for them, and re-layouts  9.98 us (10%)
    ppermute x6, waiting for transfers between devices, shifted(): lax.ppermute(x, ('row', 'layer'), [(g, (g + d) % groups) for g in range(g...  34.7 us
    ppermute x6, waiting for transfers between devices, across(): return lax.ppermute(x, 'col', [(c, c ^ bits) for c in range(4)])  25.4 us
    pallas_call x4, Pallas kernels, call(): pl.pallas_call(kernel, out_shape=outs, in_specs=[SMEM] * n_smem + [VMEM]...  16.9 us
    ppermute x6, starting transfers between devices, shifted(): lax.ppermute(x, ('row', 'layer'), [(g, (g + d) % groups) for g in range(g...  11.1 us
    unnamed x17, local copies, waits for them, and re-layouts  8.45 us
    ppermute x6, starting transfers between devices, across(): return lax.ppermute(x, 'col', [(c, c ^ bits) for c in range(4)])  5.15 us
  transfers between devices with their start and end apart: 12, of which 8 were waited for; matrix products, arithmetic and copies ran while one was open for 2% of the time, Pallas kernels for 2%

profile of v1, /device:TPU:0, one launch (start us, length us, event | category | flops | bytes accessed | tf_op | source)
XLA Modules:
  0.0 103.6 jit_solution(18114635748440460532)
XLA Ops:
  0.0 0.0 copy-start
  0.0 2.9 %collective-permute-start.1 = (bf16[8,11,32,128]{3,2,1,0:T(8,128)(2,1)}, bf16[8,11,32,128]{3,2,1,0:T(8,128)(2,1)S(1)}, u32[]{:S(2)}, u32[]{:S(2)}) collective-permute-start(bf16[8,11,32,128]{3,2,1,0:T(8,128)(2,1)} %l0.1), channel_id=1, source_target_pairs={{0,4},{2,6},{4,0},{6,2},{1,5},{3,7},{5,1},{7,3},{8,12},{10,14},{12... | collective-permute-start | bytes 2162696 | tf_op jit(solution)/shard_map/ppermute | solution.py:154
  2.9 0.0 collective-permute-start
  2.9 0.8 constant_dynamic-slice_fusion
  3.7 0.1 copy.9
  3.8 15.5 %collective-permute-done.1.l2 = bf16[8,11,32,128]{3,2,1,0:T(8,128)(2,1)S(1)} collective-permute-done((bf16[8,11,32,128]{3,2,1,0:T(8,128)(2,1)}, bf16[8,11,32,128]{3,2,1,0:T(8,128)(2,1)S(1)}, u32[]{:S(2)}, u32[]{:S(2)}) %collective-permute-start.1) | collective-permute-done | bytes 720928 | tf_op jit(solution)/shard_map/ppermute | solution.py:154
  19.3 0.0 collective-permute-start.2
  19.3 0.1 fusion.3.off
  19.4 0.0 copy-start.1
  19.4 1.1 %copy-done.1 = bf16[8,11,32,128]{3,2,1,0:T(8,128)(2,1)S(1)} copy-done((bf16[8,11,32,128]{3,2,1,0:T(8,128)(2,1)S(1)}, bf16[8,11,32,128]{3,2,1,0:T(8,128)(2,1)}, u32[]{:S(2)}) %copy-start.1) | copy-done | bytes 720920
  20.5 1.7 %shard_map.46 = (bf16[52,32,128]{2,1,0:T(8,128)(2,1)}, bf16[52,32,128]{2,1,0:T(8,128)(2,1)}, bf16[3,32,128]{2,1,0:T(8,128)(2,1)S(1)}, bf16[3,32,128]{2,1,0:T(8,128)(2,1)S(1)}) custom-call(s32[8,11]{1,0:T(8,128)S(1)} %fusion.3.off, bf16[8,11,32,128]{3,2,1,0:T(8,128)(2,1)S(1)} %copy-done.1), custom_call_target="tpu_custom_call" | custom-call | bytes 1622016 | tf_op jit(solution)/shard_map/pallas_call | solution.py:126
  22.2 1.8 %collective-permute-start.3 = (bf16[52,32,128]{2,1,0:T(8,128)(2,1)}, bf16[52,32,128]{2,1,0:T(8,128)(2,1)S(1)}, u32[]{:S(2)}, u32[]{:S(2)}) collective-permute-start(bf16[52,32,128]{2,1,0:T(8,128)(2,1)} %get-tuple-element.15), channel_id=1, source_target_pairs={{0,1},{1,8},{8,9},{9,16},{16,17},{17,24},{24,25},{25,0},{2,3},{3,1... | collective-permute-start | bytes 1277960 | tf_op jit(solution)/shard_map/ppermute | solution.py:151
  23.9 3.0 %collective-permute-start.4 = (bf16[52,32,128]{2,1,0:T(8,128)(2,1)}, bf16[52,32,128]{2,1,0:T(8,128)(2,1)S(1)}, u32[]{:S(2)}, u32[]{:S(2)}) collective-permute-start(bf16[52,32,128]{2,1,0:T(8,128)(2,1)} %get-tuple-element.16), channel_id=1, source_target_pairs={{0,25},{1,0},{8,1},{9,8},{16,9},{17,16},{24,17},{25,24},{2,27},{3,... | collective-permute-start | bytes 1277960 | tf_op jit(solution)/shard_map/ppermute | solution.py:151
  27.0 0.0 collective-permute-start.5
  27.0 0.8 copy.5
  27.8 0.6 gather_fusion
  28.4 11.4 %collective-permute-done.5.h2 = bf16[3,32,128]{2,1,0:T(8,128)(2,1)S(1)} collective-permute-done((bf16[3,32,128]{2,1,0:T(8,128)(2,1)S(1)}, bf16[3,32,128]{2,1,0:T(8,128)(2,1)S(1)}, u32[]{:S(2)}, u32[]{:S(2)}) %collective-permute-start.5) | collective-permute-done | bytes 24608 | tf_op jit(solution)/shard_map/ppermute | solution.py:151
  39.8 1.5 %collective-permute-start.6 = (bf16[3,32,128]{2,1,0:T(8,128)(2,1)S(1)}, bf16[3,32,128]{2,1,0:T(8,128)(2,1)S(1)}, u32[]{:S(2)}, u32[]{:S(2)}) collective-permute-start(bf16[3,32,128]{2,1,0:T(8,128)(2,1)S(1)} %get-tuple-element.18), channel_id=1, source_target_pairs={{0,24},{1,25},{8,0},{9,1},{16,8},{17,9},{24,16},{25,17},{2,26},{3,... | collective-permute-start | bytes 73736 | tf_op jit(solution)/shard_map/ppermute | solution.py:151
  41.3 0.1 add_select_fusion.sq
  41.4 2.2 %collective-permute-done.6.h3 = bf16[3,32,128]{2,1,0:T(8,128)(2,1)S(1)} collective-permute-done((bf16[3,32,128]{2,1,0:T(8,128)(2,1)S(1)}, bf16[3,32,128]{2,1,0:T(8,128)(2,1)S(1)}, u32[]{:S(2)}, u32[]{:S(2)}) %collective-permute-start.6) | collective-permute-done | bytes 24608 | tf_op jit(solution)/shard_map/ppermute | solution.py:151
  43.6 0.0 collective-permute-done.3.h0
  43.6 1.6 %collective-permute-done.4.h1 = bf16[52,32,128]{2,1,0:T(8,128)(2,1)S(1)} collective-permute-done((bf16[52,32,128]{2,1,0:T(8,128)(2,1)}, bf16[52,32,128]{2,1,0:T(8,128)(2,1)S(1)}, u32[]{:S(2)}, u32[]{:S(2)}) %collective-permute-start.4) | collective-permute-done | bytes 426016 | tf_op jit(solution)/shard_map/ppermute | solution.py:151
  45.2 0.0 copy-start.3
  45.2 0.8 copy-done.3
  46.0 0.0 collective-permute-done.l1
  46.0 0.0 collective-permute-done.2.l3
  46.0 0.0 copy-start.2
  46.0 1.1 %copy-done.2 = bf16[8,11,32,128]{3,2,1,0:T(8,128)(2,1)S(1)} copy-done((bf16[8,11,32,128]{3,2,1,0:T(8,128)(2,1)S(1)}, bf16[8,11,32,128]{3,2,1,0:T(8,128)(2,1)}, u32[]{:S(2)}) %copy-start.2) | copy-done | bytes 720920
  47.1 0.0 copy-start.4
  47.1 1.0 copy-done.4
  48.1 6.2 %shard_map.47 = (bf16[8,12,32,128]{3,2,1,0:T(8,128)(2,1)S(1)}, bf16[8,12,128,128]{3,2,1,0:T(8,128)(2,1)S(1)}) custom-call(s32[1]{0:T(128)} %bitcast.meta, s32[8,11]{1,0:T(8,128)S(1)} %fusion.3.off, s32[18,12]{1,0:T(8,128)S(1)} %add_select_fusion.sq, bf16[8,11,32,128]{3,2,1,0:T(8,128)(2,1)S(1)} %copy-done.2, ...), custom_call_target="tpu_custom_call" | custom-call | flops 1107296256 | bytes 7716864 | tf_op jit(solution)/shard_map/pallas_call | solution.py:126
  54.3 0.0 copy-start.5
  54.3 1.6 %copy-done.5 = bf16[8,12,128,128]{3,2,1,0:T(8,128)(2,1)} copy-done((bf16[8,12,128,128]{3,2,1,0:T(8,128)(2,1)}, bf16[8,12,128,128]{3,2,1,0:T(8,128)(2,1)S(1)}, u32[]{:S(2)}) %copy-start.5) | copy-done | bytes 3145752
  55.9 0.1 fusion.7
  56.1 0.3 collective-permute-start.7
  56.4 4.4 %collective-permute-start.8 = (bf16[5,12,32,128]{3,2,1,0:T(8,128)(2,1)S(1)}, bf16[5,12,32,128]{3,2,1,0:T(8,128)(2,1)S(1)}, u32[]{:S(2)}, u32[]{:S(2)}) collective-permute-start(bf16[5,12,32,128]{3,2,1,0:T(8,128)(2,1)S(1)} %get-tuple-element.25), channel_id=1, source_target_pairs={{0,25},{1,0},{8,1},{9,8},{16,9},{17,16},{24,17},{25,24},{2,27},{3,... | collective-permute-start | bytes 1474568 | tf_op jit(solution)/shard_map/ppermute | solution.py:151
  60.8 0.0 copy-done
  60.8 0.1 constant_dynamic-slice_fusion.1
  60.9 0.1 copy.8
  61.0 16.3 %collective-permute-done.7.before = bf16[5,12,32,128]{3,2,1,0:T(8,128)(2,1)S(1)} collective-permute-done((bf16[5,12,32,128]{3,2,1,0:T(8,128)(2,1)S(1)}, bf16[5,12,32,128]{3,2,1,0:T(8,128)(2,1)S(1)}, u32[]{:S(2)}, u32[]{:S(2)}) %collective-permute-start.7) | collective-permute-done | bytes 491552 | tf_op jit(solution)/shard_map/ppermute | solution.py:151
  77.3 3.2 %collective-permute-done.8.after = bf16[5,12,32,128]{3,2,1,0:T(8,128)(2,1)S(1)} collective-permute-done((bf16[5,12,32,128]{3,2,1,0:T(8,128)(2,1)S(1)}, bf16[5,12,32,128]{3,2,1,0:T(8,128)(2,1)S(1)}, u32[]{:S(2)}, u32[]{:S(2)}) %collective-permute-start.8) | collective-permute-done | bytes 491552 | tf_op jit(solution)/shard_map/ppermute | solution.py:151
  80.5 0.0 copy-start.6
  80.5 1.9 %copy-done.6 = bf16[8,12,128,128]{3,2,1,0:T(8,128)(2,1)S(1)} copy-done((bf16[8,12,128,128]{3,2,1,0:T(8,128)(2,1)S(1)}, bf16[8,12,128,128]{3,2,1,0:T(8,128)(2,1)}, u32[]{:S(2)}) %copy-start.6) | copy-done | bytes 3145752
  82.4 6.0 %shard_map.48 = (bf16[8,4,32,128]{3,2,1,0:T(8,128)(2,1)S(1)}, bf16[8,4,32,128]{3,2,1,0:T(8,128)(2,1)S(1)}, bf16[8,4,32,128]{3,2,1,0:T(8,128)(2,1)S(1)}, bf16[8,4,32,128]{3,2,1,0:T(8,128)(2,1)S(1)}) custom-call(s32[1]{0:T(128)} %bitcast.meta, s32[18,12]{1,0:T(8,128)S(1)} %add_select_fusion.sq, s32[8,16]{1,0:T(8,128)S(1)} %add_select_fusion.2.cube, ...), custom_call_target="tpu_custom_call" | custom-call | flops 1476395008 | bytes 5963776 | tf_op jit(solution)/shard_map/pallas_call | solution.py:126
  88.4 1.6 %collective-permute-start.10 = (bf16[8,4,32,128]{3,2,1,0:T(8,128)(2,1)S(1)}, bf16[8,4,32,128]{3,2,1,0:T(8,128)(2,1)S(1)}, u32[]{:S(2)}, u32[]{:S(2)}) collective-permute-start(bf16[8,4,32,128]{3,2,1,0:T(8,128)(2,1)S(1)} %get-tuple-element.23), channel_id=1, source_target_pairs={{0,4},{2,6},{4,0},{6,2},{1,5},{3,7},{5,1},{7,3},{8,12},{10,14},{12... | collective-permute-start | bytes 786440 | tf_op jit(solution)/shard_map/ppermute | solution.py:154
  90.0 0.0 collective-permute-start.11
  90.0 0.6 collective-permute-start.9
  90.6 7.1 %collective-permute-done.10.p2 = bf16[8,4,32,128]{3,2,1,0:T(8,128)(2,1)S(1)} collective-permute-done((bf16[8,4,32,128]{3,2,1,0:T(8,128)(2,1)S(1)}, bf16[8,4,32,128]{3,2,1,0:T(8,128)(2,1)S(1)}, u32[]{:S(2)}, u32[]{:S(2)}) %collective-permute-start.10) | collective-permute-done | bytes 262176 | tf_op jit(solution)/shard_map/ppermute | solution.py:154
  97.7 2.8 %collective-permute-done.11.p3 = bf16[8,4,32,128]{3,2,1,0:T(8,128)(2,1)S(1)} collective-permute-done((bf16[8,4,32,128]{3,2,1,0:T(8,128)(2,1)S(1)}, bf16[8,4,32,128]{3,2,1,0:T(8,128)(2,1)S(1)}, u32[]{:S(2)}, u32[]{:S(2)}) %collective-permute-start.11) | collective-permute-done | bytes 262176 | tf_op jit(solution)/shard_map/ppermute | solution.py:154
  100.5 0.0 collective-permute-done.9.p1
  100.5 3.1 %shard_map.49 = f32[8,4,128,128]{3,2,1,0:T(8,128)} custom-call(s32[1]{0:T(128)} %bitcast.meta, bf16[8,4,32,128]{3,2,1,0:T(8,128)(2,1)S(1)} %get-tuple-element.21.p0, bf16[8,4,32,128]{3,2,1,0:T(8,128)(2,1)S(1)} %collective-permute-done.9.p1, bf16[8,4,32,128]{3,2,1,0:T(8,128)(2,1)S(1)} %collective-permute-done.10.p2, ...), custom_call_target="tpu_custom_call" | custom-call | flops 134217728 | bytes 3145728 | tf_op jit(solution)/shard_map/pallas_call | solution.py:126
  (5 shorter events, 0.1 us)
Async XLA Ops:
  0.0 60.8 %copy-start = (s32[64,16]{0,1:T(8,128)S(1)}, s32[64,16]{0,1:T(8,128)}, u32[]{:S(2)}) copy-start(s32[64,16]{0,1:T(8,128)} %param.7) | copy-start | bytes 12292
  0.0 19.3 %collective-permute-start.1 = (bf16[8,11,32,128]{3,2,1,0:T(8,128)(2,1)}, bf16[8,11,32,128]{3,2,1,0:T(8,128)(2,1)S(1)}, u32[]{:S(2)}, u32[]{:S(2)}) collective-permute-start(bf16[8,11,32,128]{3,2,1,0:T(8,128)(2,1)} %l0.1), channel_id=1, source_target_pairs={{0,4},{2,6},{4,0},{6,2},{1,5},{3,7},{5,1},{7,3},{8,12},{10,14},{12... | collective-permute-start | bytes 2162696 | tf_op jit(solution)/shard_map/ppermute | solution.py:154
  2.9 43.0 %collective-permute-start = (bf16[8,11,32,128]{3,2,1,0:T(8,128)(2,1)}, bf16[8,11,32,128]{3,2,1,0:T(8,128)(2,1)S(1)}, u32[]{:S(2)}, u32[]{:S(2)}) collective-permute-start(bf16[8,11,32,128]{3,2,1,0:T(8,128)(2,1)} %l0.1), channel_id=1, source_target_pairs={{0,2},{2,0},{4,6},{6,4},{1,3},{3,1},{5,7},{7,5},{8,10},{10,8},{12,... | collective-permute-start | bytes 2162696 | tf_op jit(solution)/shard_map/ppermute | solution.py:154
  19.3 26.7 %collective-permute-start.2 = (bf16[8,11,32,128]{3,2,1,0:T(8,128)(2,1)S(1)}, bf16[8,11,32,128]{3,2,1,0:T(8,128)(2,1)S(1)}, u32[]{:S(2)}, u32[]{:S(2)}) collective-permute-start(bf16[8,11,32,128]{3,2,1,0:T(8,128)(2,1)S(1)} %collective-permute-done.1.l2), channel_id=1, source_target_pairs={{0,2},{2,0},{4,6},{6,4},{1,3},{3,1},{5,7},{7,5},{8,10},{10,8},{12,... | collective-permute-start | bytes 2162696 | tf_op jit(solution)/shard_map/ppermute | solution.py:154
  19.4 1.1 %copy-start.1 = (bf16[8,11,32,128]{3,2,1,0:T(8,128)(2,1)S(1)}, bf16[8,11,32,128]{3,2,1,0:T(8,128)(2,1)}, u32[]{:S(2)}) copy-start(bf16[8,11,32,128]{3,2,1,0:T(8,128)(2,1)} %l0.1) | copy-start | bytes 2162692
  22.2 21.4 %collective-permute-start.3 = (bf16[52,32,128]{2,1,0:T(8,128)(2,1)}, bf16[52,32,128]{2,1,0:T(8,128)(2,1)S(1)}, u32[]{:S(2)}, u32[]{:S(2)}) collective-permute-start(bf16[52,32,128]{2,1,0:T(8,128)(2,1)} %get-tuple-element.15), channel_id=1, source_target_pairs={{0,1},{1,8},{8,9},{9,16},{16,17},{17,24},{24,25},{25,0},{2,3},{3,1... | collective-permute-start | bytes 1277960 | tf_op jit(solution)/shard_map/ppermute | solution.py:151
  23.9 21.3 %collective-permute-start.4 = (bf16[52,32,128]{2,1,0:T(8,128)(2,1)}, bf16[52,32,128]{2,1,0:T(8,128)(2,1)S(1)}, u32[]{:S(2)}, u32[]{:S(2)}) collective-permute-start(bf16[52,32,128]{2,1,0:T(8,128)(2,1)} %get-tuple-element.16), channel_id=1, source_target_pairs={{0,25},{1,0},{8,1},{9,8},{16,9},{17,16},{24,17},{25,24},{2,27},{3,... | collective-permute-start | bytes 1277960 | tf_op jit(solution)/shard_map/ppermute | solution.py:151
  27.0 12.8 %collective-permute-start.5 = (bf16[3,32,128]{2,1,0:T(8,128)(2,1)S(1)}, bf16[3,32,128]{2,1,0:T(8,128)(2,1)S(1)}, u32[]{:S(2)}, u32[]{:S(2)}) collective-permute-start(bf16[3,32,128]{2,1,0:T(8,128)(2,1)S(1)} %get-tuple-element.17), channel_id=1, source_target_pairs={{0,8},{1,9},{8,16},{9,17},{16,24},{17,25},{24,0},{25,1},{2,10},{3,... | collective-permute-start | bytes 73736 | tf_op jit(solution)/shard_map/ppermute | solution.py:151
  39.8 3.8 %collective-permute-start.6 = (bf16[3,32,128]{2,1,0:T(8,128)(2,1)S(1)}, bf16[3,32,128]{2,1,0:T(8,128)(2,1)S(1)}, u32[]{:S(2)}, u32[]{:S(2)}) collective-permute-start(bf16[3,32,128]{2,1,0:T(8,128)(2,1)S(1)} %get-tuple-element.18), channel_id=1, source_target_pairs={{0,24},{1,25},{8,0},{9,1},{16,8},{17,9},{24,16},{25,17},{2,26},{3,... | collective-permute-start | bytes 73736 | tf_op jit(solution)/shard_map/ppermute | solution.py:151
  45.2 0.8 copy-start.3
  46.0 1.1 %copy-start.2 = (bf16[8,11,32,128]{3,2,1,0:T(8,128)(2,1)S(1)}, bf16[8,11,32,128]{3,2,1,0:T(8,128)(2,1)}, u32[]{:S(2)}) copy-start(bf16[8,11,32,128]{3,2,1,0:T(8,128)(2,1)} %l0.1) | copy-start | bytes 2162692
  47.1 1.0 copy-start.4
  54.3 1.6 %copy-start.5 = (bf16[8,12,128,128]{3,2,1,0:T(8,128)(2,1)}, bf16[8,12,128,128]{3,2,1,0:T(8,128)(2,1)S(1)}, u32[]{:S(2)}) copy-start(bf16[8,12,128,128]{3,2,1,0:T(8,128)(2,1)S(1)} %get-tuple-element.20.left) | copy-start | bytes 9437188
  56.1 21.2 %collective-permute-start.7 = (bf16[5,12,32,128]{3,2,1,0:T(8,128)(2,1)S(1)}, bf16[5,12,32,128]{3,2,1,0:T(8,128)(2,1)S(1)}, u32[]{:S(2)}, u32[]{:S(2)}) collective-permute-start(bf16[5,12,32,128]{3,2,1,0:T(8,128)(2,1)S(1)} %get-tuple-element.26), channel_id=1, source_target_pairs={{0,1},{1,8},{8,9},{9,16},{16,17},{17,24},{24,25},{25,0},{2,3},{3,1... | collective-permute-start | bytes 1474568 | tf_op jit(solution)/shard_map/ppermute | solution.py:151
  56.4 24.1 %collective-permute-start.8 = (bf16[5,12,32,128]{3,2,1,0:T(8,128)(2,1)S(1)}, bf16[5,12,32,128]{3,2,1,0:T(8,128)(2,1)S(1)}, u32[]{:S(2)}, u32[]{:S(2)}) collective-permute-start(bf16[5,12,32,128]{3,2,1,0:T(8,128)(2,1)S(1)} %get-tuple-element.25), channel_id=1, source_target_pairs={{0,25},{1,0},{8,1},{9,8},{16,9},{17,16},{24,17},{25,24},{2,27},{3,... | collective-permute-start | bytes 1474568 | tf_op jit(solution)/shard_map/ppermute | solution.py:151
  80.5 1.9 %copy-start.6 = (bf16[8,12,128,128]{3,2,1,0:T(8,128)(2,1)S(1)}, bf16[8,12,128,128]{3,2,1,0:T(8,128)(2,1)}, u32[]{:S(2)}) copy-start(bf16[8,12,128,128]{3,2,1,0:T(8,128)(2,1)} %copy-done.5) | copy-start | bytes 9437188
  88.4 9.3 %collective-permute-start.10 = (bf16[8,4,32,128]{3,2,1,0:T(8,128)(2,1)S(1)}, bf16[8,4,32,128]{3,2,1,0:T(8,128)(2,1)S(1)}, u32[]{:S(2)}, u32[]{:S(2)}) collective-permute-start(bf16[8,4,32,128]{3,2,1,0:T(8,128)(2,1)S(1)} %get-tuple-element.23), channel_id=1, source_target_pairs={{0,4},{2,6},{4,0},{6,2},{1,5},{3,7},{5,1},{7,3},{8,12},{10,14},{12... | collective-permute-start | bytes 786440 | tf_op jit(solution)/shard_map/ppermute | solution.py:154
  90.0 10.5 %collective-permute-start.11 = (bf16[8,4,32,128]{3,2,1,0:T(8,128)(2,1)S(1)}, bf16[8,4,32,128]{3,2,1,0:T(8,128)(2,1)S(1)}, u32[]{:S(2)}, u32[]{:S(2)}) collective-permute-start(bf16[8,4,32,128]{3,2,1,0:T(8,128)(2,1)S(1)} %get-tuple-element.24), channel_id=1, source_target_pairs={{0,6},{2,4},{4,2},{6,0},{1,7},{3,5},{5,3},{7,1},{8,14},{10,12},{12... | collective-permute-start | bytes 786440 | tf_op jit(solution)/shard_map/ppermute | solution.py:154
  90.0 10.5 %collective-permute-start.9 = (bf16[8,4,32,128]{3,2,1,0:T(8,128)(2,1)S(1)}, bf16[8,4,32,128]{3,2,1,0:T(8,128)(2,1)S(1)}, u32[]{:S(2)}, u32[]{:S(2)}) collective-permute-start(bf16[8,4,32,128]{3,2,1,0:T(8,128)(2,1)S(1)} %get-tuple-element.22), channel_id=1, source_target_pairs={{0,2},{2,0},{4,6},{6,4},{1,3},{3,1},{5,7},{7,5},{8,10},{10,8},{12,... | collective-permute-start | bytes 786440 | tf_op jit(solution)/shard_map/ppermute | solution.py:154

commit v2 on v1

--- a/solution.py
+++ b/solution.py
@@ -42,12 +42,16 @@
 SHIFTS = (1, -1, 2, -2)
 
 
-def reorder_kernel(off, density, *refs):
+def reorder_kernel(meta, pattern, density, *refs):
     outs, band = refs[:4], refs[4]
+    first, total = meta[1], pattern.shape[0]
     band[...] = jnp.zeros_like(band)
     for i in range(ROWS):
         for s in range(density.shape[1]):
-            band[i, off[i, s]] = density[i, s]
+            listed = pattern[first + i, s]
+            o = listed - (first + i) + RADIUS
+            o = jnp.where(o < 0, o + total, jnp.where(o >= total, o - total, o))
+            band[i, jnp.where(listed >= 0, o, BAND)] = density[i, s]
     for out, entries in zip(outs, LISTS):
         for e, (j, o) in enumerate(entries):
             out[e] = band[j, o]
@@ -120,7 +124,7 @@
             out[i, q] = lax.dot_general(eye, whole[i, q], NT, preferred_element_type=jnp.float32)
 
 
-def call(kernel, n_smem, outs, scratch, args, flops, limit=40):
+def call(kernel, n_smem, outs, scratch, args, flops, limit=16):
     size = sum(a.size * a.dtype.itemsize for a in args[n_smem:])
     size += sum(o.size * o.dtype.itemsize for o in outs)
     return pl.pallas_call(
@@ -153,7 +157,7 @@
     def across(x, bits):
         return lax.ppermute(x, "col", [(c, c ^ bits) for c in range(4)])
 
-    meta = jnp.reshape(col, (1,)).astype(jnp.int32)
+    meta = jnp.stack([col, first]).astype(jnp.int32)
     own_rows = first + jnp.arange(ROWS, dtype=jnp.int32)[:, None]
     listed = lax.dynamic_slice_in_dim(pattern, first, ROWS, 0)
     off = jnp.where(listed >= 0, (listed - own_rows + RADIUS + total) % total, BAND)
@@ -165,10 +169,12 @@
     l2 = across(density, 2)
     l1 = across(density, 1)
     payload = call(
-        reorder_kernel, 1, [shape(len(e), *piece) for e in LISTS],
-        [pltpu.VMEM((ROWS, BAND + 1, *piece), density.dtype)], (off, density), 0,
-    )
+        reorder_kernel, 2, [shape(len(e), *piece) for e in LISTS],
+        [pltpu.VMEM((ROWS, BAND + 1, *piece), density.dtype)], (meta, pattern, density), 0,
+    )
+    payload, l1 = lax.optimization_barrier((payload, l1))
     halos = [shifted(p, d) for p, d in zip(payload, SHIFTS)]
+    l2, halos = lax.optimization_barrier((l2, halos))
     l3 = across(l2, 1)
 
     kept = square_filter.shape[1]

time: 104 us -> 91.7 us (0.88)
  waiting for transfers between devices: 60.1 us -> 43.4 us
  starting transfers between devices: 16.3 us -> 18.5 us
  Pallas kernels: 16.9 us -> 18.1 us
    ppermute x6, waiting for transfers between devices: 25.4 us -> 14 us  [across(): return lax.ppermute(x, 'col', [(c, c ^ bits) for c in range(4)])]
    ppermute x6, waiting for transfers between devices: 34.7 us -> 29.4 us  [shifted(): lax.ppermute(x, ('row', 'layer'), [(g, (g + d) % groups) for g in range(g...]
    ppermute x6, starting transfers between devices: 11.1 us -> 13.3 us  [shifted(): lax.ppermute(x, ('row', 'layer'), [(g, (g + d) % groups) for g in range(g...]
    pallas_call x4, Pallas kernels: 16.9 us -> 18.1 us  [call(): pl.pallas_call(kernel, out_shape=outs, in_specs=[SMEM] * n_smem + [VMEM]...]
  transfers between devices with their start and end apart: 12 -> 12, of which waited for: 8 -> 9; matrix products, arithmetic and copies ran while one was open for 2% -> 3% of each run, Pallas kernels for 2% -> 3%
where the time goes in v2:
time: 91.7 us; the launch traced here: 90.3 us
  waiting for transfers between devices  43.4 us (47%)
  starting transfers between devices  18.5 us (20%)
  Pallas kernels  18.1 us (20%)
  local copies, waits for them, and re-layouts  9.91 us (11%)
    ppermute x6, waiting for transfers between devices, shifted(): lax.ppermute(x, ('row', 'layer'), [(g, (g + d) % groups) for g in range(g...  29.4 us
    pallas_call x4, Pallas kernels, call(): pl.pallas_call(kernel, out_shape=outs, in_specs=[SMEM] * n_smem + [VMEM]...  18.1 us
    ppermute x6, waiting for transfers between devices, across(): return lax.ppermute(x, 'col', [(c, c ^ bits) for c in range(4)])  14 us
    ppermute x6, starting transfers between devices, shifted(): lax.ppermute(x, ('row', 'layer'), [(g, (g + d) % groups) for g in range(g...  13.3 us
    unnamed x17, local copies, waits for them, and re-layouts  9.15 us
    ppermute x6, starting transfers between devices, across(): return lax.ppermute(x, 'col', [(c, c ^ bits) for c in range(4)])  5.22 us
  transfers between devices with their start and end apart: 12, of which 9 were waited for; matrix products, arithmetic and copies ran while one was open for 3% of the time, Pallas kernels for 3%

profile of v2, /device:TPU:0, one launch (start us, length us, event | category | flops | bytes accessed | tf_op | source)
XLA Modules:
  0.0 90.3 jit_solution(9861569803368530070)
XLA Ops:
  0.0 0.0 copy-start
  0.0 0.5 collective-permute-start
  0.5 2.6 %collective-permute-start.1 = (bf16[8,11,32,128]{3,2,1,0:T(8,128)(2,1)}, bf16[8,11,32,128]{3,2,1,0:T(8,128)(2,1)S(1)}, u32[]{:S(2)}, u32[]{:S(2)}) collective-permute-start(bf16[8,11,32,128]{3,2,1,0:T(8,128)(2,1)} %l0.1), channel_id=1, source_target_pairs={{0,4},{2,6},{4,0},{6,2},{1,5},{3,7},{5,1},{7,3},{8,12},{10,14},{12... | collective-permute-start | bytes 2162696 | tf_op jit(solution)/shard_map/ppermute | solution.py:158
  3.0 0.8 copy.7.pattern
  3.8 0.1 pad_add_fusion.meta
  3.9 0.0 copy-start.1
  3.9 1.1 %copy-done.1 = bf16[8,11,32,128]{3,2,1,0:T(8,128)(2,1)S(1)} copy-done((bf16[8,11,32,128]{3,2,1,0:T(8,128)(2,1)S(1)}, bf16[8,11,32,128]{3,2,1,0:T(8,128)(2,1)}, u32[]{:S(2)}) %copy-start.1) | copy-done | bytes 720920
  5.0 2.3 %shard_map.46 = (bf16[52,32,128]{2,1,0:T(8,128)(2,1)}, bf16[52,32,128]{2,1,0:T(8,128)(2,1)S(1)}, bf16[3,32,128]{2,1,0:T(8,128)(2,1)S(1)}, bf16[3,32,128]{2,1,0:T(8,128)(2,1)S(1)}) custom-call(s32[2]{0:T(128)S(1)} %pad_add_fusion.meta, s32[64,11]{1,0:T(8,128)S(1)} %copy.7.pattern, bf16[8,11,32,128]{3,2,1,0:T(8,128)(2,1)S(1)} %copy-done.1), custom_call_target="tpu_custom_call" | custom-call | bytes 1622016 | tf_op jit(solution)/shard_map/pallas_call | solution.py:130
  7.3 0.0 collective-permute-done.l1
  7.3 1.5 %collective-permute-start.2 = (bf16[52,32,128]{2,1,0:T(8,128)(2,1)}, bf16[52,32,128]{2,1,0:T(8,128)(2,1)S(1)}, u32[]{:S(2)}, u32[]{:S(2)}) collective-permute-start(bf16[52,32,128]{2,1,0:T(8,128)(2,1)} %get-tuple-element.30), channel_id=1, source_target_pairs={{0,1},{1,8},{8,9},{9,16},{16,17},{17,24},{24,25},{25,0},{2,3},{3,1... | collective-permute-start | bytes 1277960 | tf_op jit(solution)/shard_map/ppermute | solution.py:155
  8.8 3.2 %collective-permute-start.3 = (bf16[52,32,128]{2,1,0:T(8,128)(2,1)S(1)}, bf16[52,32,128]{2,1,0:T(8,128)(2,1)S(1)}, u32[]{:S(2)}, u32[]{:S(2)}) collective-permute-start(bf16[52,32,128]{2,1,0:T(8,128)(2,1)S(1)} %get-tuple-element.31), channel_id=1, source_target_pairs={{0,25},{1,0},{8,1},{9,8},{16,9},{17,16},{24,17},{25,24},{2,27},{3,... | collective-permute-start | bytes 1277960 | tf_op jit(solution)/shard_map/ppermute | solution.py:155
  12.0 0.0 collective-permute-start.4
  12.0 3.8 %collective-permute-start.5 = (bf16[3,32,128]{2,1,0:T(8,128)(2,1)S(1)}, bf16[3,32,128]{2,1,0:T(8,128)(2,1)S(1)}, u32[]{:S(2)}, u32[]{:S(2)}) collective-permute-start(bf16[3,32,128]{2,1,0:T(8,128)(2,1)S(1)} %get-tuple-element.33), channel_id=1, source_target_pairs={{0,24},{1,25},{8,0},{9,1},{16,8},{17,9},{24,16},{25,17},{2,26},{3,... | collective-permute-start | bytes 73736 | tf_op jit(solution)/shard_map/ppermute | solution.py:155
  15.8 4.1 %collective-permute-done.1.l2 = bf16[8,11,32,128]{3,2,1,0:T(8,128)(2,1)S(1)} collective-permute-done((bf16[8,11,32,128]{3,2,1,0:T(8,128)(2,1)}, bf16[8,11,32,128]{3,2,1,0:T(8,128)(2,1)S(1)}, u32[]{:S(2)}, u32[]{:S(2)}) %collective-permute-start.1) | collective-permute-done | bytes 720928 | tf_op jit(solution)/shard_map/ppermute | solution.py:158
  20.0 4.2 %collective-permute-done.4.h2 = bf16[3,32,128]{2,1,0:T(8,128)(2,1)S(1)} collective-permute-done((bf16[3,32,128]{2,1,0:T(8,128)(2,1)S(1)}, bf16[3,32,128]{2,1,0:T(8,128)(2,1)S(1)}, u32[]{:S(2)}, u32[]{:S(2)}) %collective-permute-start.4) | collective-permute-done | bytes 24608 | tf_op jit(solution)/shard_map/ppermute | solution.py:155
  24.2 0.0 collective-permute-done.5.h3
  24.2 3.4 %collective-permute-done.2.h0 = bf16[52,32,128]{2,1,0:T(8,128)(2,1)S(1)} collective-permute-done((bf16[52,32,128]{2,1,0:T(8,128)(2,1)}, bf16[52,32,128]{2,1,0:T(8,128)(2,1)S(1)}, u32[]{:S(2)}, u32[]{:S(2)}) %collective-permute-start.2) | collective-permute-done | bytes 426016 | tf_op jit(solution)/shard_map/ppermute | solution.py:155
  27.6 1.9 %collective-permute-done.3.h1 = bf16[52,32,128]{2,1,0:T(8,128)(2,1)S(1)} collective-permute-done((bf16[52,32,128]{2,1,0:T(8,128)(2,1)S(1)}, bf16[52,32,128]{2,1,0:T(8,128)(2,1)S(1)}, u32[]{:S(2)}, u32[]{:S(2)}) %collective-permute-start.3) | collective-permute-done | bytes 426016 | tf_op jit(solution)/shard_map/ppermute | solution.py:155
  29.5 0.0 copy-start.3
  29.5 0.8 copy-done.3
  30.3 0.0 collective-permute-start.6
  30.3 0.8 copy.5
  31.1 0.6 gather_fusion
  31.7 0.1 fusion.3.off
  31.8 0.1 add_select_fusion.sq
  31.8 0.6 collective-permute-done.6.l3
  32.5 0.0 copy-start.2
  32.5 1.1 %copy-done.2 = bf16[8,11,32,128]{3,2,1,0:T(8,128)(2,1)S(1)} copy-done((bf16[8,11,32,128]{3,2,1,0:T(8,128)(2,1)S(1)}, bf16[8,11,32,128]{3,2,1,0:T(8,128)(2,1)}, u32[]{:S(2)}) %copy-start.2) | copy-done | bytes 720920
  33.6 0.0 copy-start.4
  33.6 1.0 %copy-done.4 = bf16[52,32,128]{2,1,0:T(8,128)(2,1)S(1)} copy-done((bf16[52,32,128]{2,1,0:T(8,128)(2,1)S(1)}, bf16[52,32,128]{2,1,0:T(8,128)(2,1)}, u32[]{:S(2)}) %copy-start.4) | copy-done | bytes 426008
  34.6 6.2 %shard_map.47 = (bf16[8,12,32,128]{3,2,1,0:T(8,128)(2,1)S(1)}, bf16[8,12,128,128]{3,2,1,0:T(8,128)(2,1)S(1)}) custom-call(s32[2]{0:T(128)S(1)} %pad_add_fusion.meta, s32[8,11]{1,0:T(8,128)S(1)} %fusion.3.off, s32[18,12]{1,0:T(8,128)S(1)} %add_select_fusion.sq, bf16[8,11,32,128]{3,2,1,0:T(8,128)(2,1)S(1)} %copy-done.2, ...), custom_call_target="tpu_custom_call" | custom-call | flops 1107296256 | bytes 7716864 | tf_op jit(solution)/shard_map/pallas_call | solution.py:130
  40.8 0.0 copy-start.5
  40.8 1.6 %copy-done.5 = bf16[8,12,128,128]{3,2,1,0:T(8,128)(2,1)} copy-done((bf16[8,12,128,128]{3,2,1,0:T(8,128)(2,1)}, bf16[8,12,128,128]{3,2,1,0:T(8,128)(2,1)S(1)}, u32[]{:S(2)}) %copy-start.5) | copy-done | bytes 3145752
  42.4 0.1 fusion.7
  42.5 0.5 collective-permute-start.7
  43.1 4.2 %collective-permute-start.8 = (bf16[5,12,32,128]{3,2,1,0:T(8,128)(2,1)S(1)}, bf16[5,12,32,128]{3,2,1,0:T(8,128)(2,1)S(1)}, u32[]{:S(2)}, u32[]{:S(2)}) collective-permute-start(bf16[5,12,32,128]{3,2,1,0:T(8,128)(2,1)S(1)} %get-tuple-element.45), channel_id=1, source_target_pairs={{0,25},{1,0},{8,1},{9,8},{16,9},{17,16},{24,17},{25,24},{2,27},{3,... | collective-permute-start | bytes 1474568 | tf_op jit(solution)/shard_map/ppermute | solution.py:155
  47.3 0.0 copy-done
  47.3 0.1 constant_dynamic-slice_fusion
  47.4 0.1 copy.9
  47.5 16.9 %collective-permute-done.7.before = bf16[5,12,32,128]{3,2,1,0:T(8,128)(2,1)S(1)} collective-permute-done((bf16[5,12,32,128]{3,2,1,0:T(8,128)(2,1)S(1)}, bf16[5,12,32,128]{3,2,1,0:T(8,128)(2,1)S(1)}, u32[]{:S(2)}, u32[]{:S(2)}) %collective-permute-start.7) | collective-permute-done | bytes 491552 | tf_op jit(solution)/shard_map/ppermute | solution.py:155
  64.4 2.9 %collective-permute-done.8.after = bf16[5,12,32,128]{3,2,1,0:T(8,128)(2,1)S(1)} collective-permute-done((bf16[5,12,32,128]{3,2,1,0:T(8,128)(2,1)S(1)}, bf16[5,12,32,128]{3,2,1,0:T(8,128)(2,1)S(1)}, u32[]{:S(2)}, u32[]{:S(2)}) %collective-permute-start.8) | collective-permute-done | bytes 491552 | tf_op jit(solution)/shard_map/ppermute | solution.py:155
  67.3 0.0 copy-start.6
  67.3 1.9 %copy-done.6 = bf16[8,12,128,128]{3,2,1,0:T(8,128)(2,1)S(1)} copy-done((bf16[8,12,128,128]{3,2,1,0:T(8,128)(2,1)S(1)}, bf16[8,12,128,128]{3,2,1,0:T(8,128)(2,1)}, u32[]{:S(2)}) %copy-start.6) | copy-done | bytes 3145752
  69.2 6.0 %shard_map.48 = (bf16[8,4,32,128]{3,2,1,0:T(8,128)(2,1)S(1)}, bf16[8,4,32,128]{3,2,1,0:T(8,128)(2,1)S(1)}, bf16[8,4,32,128]{3,2,1,0:T(8,128)(2,1)S(1)}, bf16[8,4,32,128]{3,2,1,0:T(8,128)(2,1)S(1)}) custom-call(s32[2]{0:T(128)S(1)} %pad_add_fusion.meta, s32[18,12]{1,0:T(8,128)S(1)} %add_select_fusion.sq, s32[8,16]{1,0:T(8,128)S(1)} %add_select_fusion.2.cube, ...), custom_call_target="tpu_custom_call" | custom-call | flops 1476395008 | bytes 5963776 | tf_op jit(solution)/shard_map/pallas_call | solution.py:130
  75.2 0.6 collective-permute-start.10
  75.8 0.1 collective-permute-start.11
  75.9 1.5 %collective-permute-start.9 = (bf16[8,4,32,128]{3,2,1,0:T(8,128)(2,1)S(1)}, bf16[8,4,32,128]{3,2,1,0:T(8,128)(2,1)S(1)}, u32[]{:S(2)}, u32[]{:S(2)}) collective-permute-start(bf16[8,4,32,128]{3,2,1,0:T(8,128)(2,1)S(1)} %get-tuple-element.42), channel_id=1, source_target_pairs={{0,2},{2,0},{4,6},{6,4},{1,3},{3,1},{5,7},{7,5},{8,10},{10,8},{12,... | collective-permute-start | bytes 786440 | tf_op jit(solution)/shard_map/ppermute | solution.py:158
  77.4 7.1 %collective-permute-done.10.p2 = bf16[8,4,32,128]{3,2,1,0:T(8,128)(2,1)S(1)} collective-permute-done((bf16[8,4,32,128]{3,2,1,0:T(8,128)(2,1)S(1)}, bf16[8,4,32,128]{3,2,1,0:T(8,128)(2,1)S(1)}, u32[]{:S(2)}, u32[]{:S(2)}) %collective-permute-start.10) | collective-permute-done | bytes 262176 | tf_op jit(solution)/shard_map/ppermute | solution.py:158
  84.5 2.2 %collective-permute-done.11.p3 = bf16[8,4,32,128]{3,2,1,0:T(8,128)(2,1)S(1)} collective-permute-done((bf16[8,4,32,128]{3,2,1,0:T(8,128)(2,1)S(1)}, bf16[8,4,32,128]{3,2,1,0:T(8,128)(2,1)S(1)}, u32[]{:S(2)}, u32[]{:S(2)}) %collective-permute-start.11) | collective-permute-done | bytes 262176 | tf_op jit(solution)/shard_map/ppermute | solution.py:158
  86.7 0.0 collective-permute-done.9.p1
  86.7 3.6 %shard_map.49 = f32[8,4,128,128]{3,2,1,0:T(8,128)} custom-call(s32[2]{0:T(128)S(1)} %pad_add_fusion.meta, bf16[8,4,32,128]{3,2,1,0:T(8,128)(2,1)S(1)} %get-tuple-element.41.p0, bf16[8,4,32,128]{3,2,1,0:T(8,128)(2,1)S(1)} %collective-permute-done.9.p1, bf16[8,4,32,128]{3,2,1,0:T(8,128)(2,1)S(1)} %collective-permute-done.10.p2, ...), custom_call_target="tpu_custom_call" | custom-call | flops 134217728 | bytes 3145728 | tf_op jit(solution)/shard_map/pallas_call | solution.py:130
  (5 shorter events, 0.1 us)
Async XLA Ops:
  0.0 47.3 %copy-start = (s32[64,16]{0,1:T(8,128)S(1)}, s32[64,16]{0,1:T(8,128)}, u32[]{:S(2)}) copy-start(s32[64,16]{0,1:T(8,128)} %param.7) | copy-start | bytes 12292
  0.0 7.3 %collective-permute-start = (bf16[8,11,32,128]{3,2,1,0:T(8,128)(2,1)}, bf16[8,11,32,128]{3,2,1,0:T(8,128)(2,1)S(1)}, u32[]{:S(2)}, u32[]{:S(2)}) collective-permute-start(bf16[8,11,32,128]{3,2,1,0:T(8,128)(2,1)} %l0.1), channel_id=1, source_target_pairs={{0,2},{2,0},{4,6},{6,4},{1,3},{3,1},{5,7},{7,5},{8,10},{10,8},{12,... | collective-permute-start | bytes 2162696 | tf_op jit(solution)/shard_map/ppermute | solution.py:158
  0.5 19.5 %collective-permute-start.1 = (bf16[8,11,32,128]{3,2,1,0:T(8,128)(2,1)}, bf16[8,11,32,128]{3,2,1,0:T(8,128)(2,1)S(1)}, u32[]{:S(2)}, u32[]{:S(2)}) collective-permute-start(bf16[8,11,32,128]{3,2,1,0:T(8,128)(2,1)} %l0.1), channel_id=1, source_target_pairs={{0,4},{2,6},{4,0},{6,2},{1,5},{3,7},{5,1},{7,3},{8,12},{10,14},{12... | collective-permute-start | bytes 2162696 | tf_op jit(solution)/shard_map/ppermute | solution.py:158
  3.9 1.1 %copy-start.1 = (bf16[8,11,32,128]{3,2,1,0:T(8,128)(2,1)S(1)}, bf16[8,11,32,128]{3,2,1,0:T(8,128)(2,1)}, u32[]{:S(2)}) copy-start(bf16[8,11,32,128]{3,2,1,0:T(8,128)(2,1)} %l0.1) | copy-start | bytes 2162692
  7.3 20.4 %collective-permute-start.2 = (bf16[52,32,128]{2,1,0:T(8,128)(2,1)}, bf16[52,32,128]{2,1,0:T(8,128)(2,1)S(1)}, u32[]{:S(2)}, u32[]{:S(2)}) collective-permute-start(bf16[52,32,128]{2,1,0:T(8,128)(2,1)} %get-tuple-element.30), channel_id=1, source_target_pairs={{0,1},{1,8},{8,9},{9,16},{16,17},{17,24},{24,25},{25,0},{2,3},{3,1... | collective-permute-start | bytes 1277960 | tf_op jit(solution)/shard_map/ppermute | solution.py:155
  8.8 20.7 %collective-permute-start.3 = (bf16[52,32,128]{2,1,0:T(8,128)(2,1)S(1)}, bf16[52,32,128]{2,1,0:T(8,128)(2,1)S(1)}, u32[]{:S(2)}, u32[]{:S(2)}) collective-permute-start(bf16[52,32,128]{2,1,0:T(8,128)(2,1)S(1)} %get-tuple-element.31), channel_id=1, source_target_pairs={{0,25},{1,0},{8,1},{9,8},{16,9},{17,16},{24,17},{25,24},{2,27},{3,... | collective-permute-start | bytes 1277960 | tf_op jit(solution)/shard_map/ppermute | solution.py:155
  12.0 12.2 %collective-permute-start.4 = (bf16[3,32,128]{2,1,0:T(8,128)(2,1)S(1)}, bf16[3,32,128]{2,1,0:T(8,128)(2,1)S(1)}, u32[]{:S(2)}, u32[]{:S(2)}) collective-permute-start(bf16[3,32,128]{2,1,0:T(8,128)(2,1)S(1)} %get-tuple-element.32), channel_id=1, source_target_pairs={{0,8},{1,9},{8,16},{9,17},{16,24},{17,25},{24,0},{25,1},{2,10},{3,... | collective-permute-start | bytes 73736 | tf_op jit(solution)/shard_map/ppermute | solution.py:155
  12.0 12.2 %collective-permute-start.5 = (bf16[3,32,128]{2,1,0:T(8,128)(2,1)S(1)}, bf16[3,32,128]{2,1,0:T(8,128)(2,1)S(1)}, u32[]{:S(2)}, u32[]{:S(2)}) collective-permute-start(bf16[3,32,128]{2,1,0:T(8,128)(2,1)S(1)} %get-tuple-element.33), channel_id=1, source_target_pairs={{0,24},{1,25},{8,0},{9,1},{16,8},{17,9},{24,16},{25,17},{2,26},{3,... | collective-permute-start | bytes 73736 | tf_op jit(solution)/shard_map/ppermute | solution.py:155
  29.5 0.8 copy-start.3
  30.3 2.2 %collective-permute-start.6 = (bf16[8,11,32,128]{3,2,1,0:T(8,128)(2,1)S(1)}, bf16[8,11,32,128]{3,2,1,0:T(8,128)(2,1)S(1)}, u32[]{:S(2)}, u32[]{:S(2)}) collective-permute-start(bf16[8,11,32,128]{3,2,1,0:T(8,128)(2,1)S(1)} %collective-permute-done.1.l2), channel_id=1, source_target_pairs={{0,2},{2,0},{4,6},{6,4},{1,3},{3,1},{5,7},{7,5},{8,10},{10,8},{12,... | collective-permute-start | bytes 2162696 | tf_op jit(solution)/shard_map/ppermute | solution.py:158
  32.5 1.1 %copy-start.2 = (bf16[8,11,32,128]{3,2,1,0:T(8,128)(2,1)S(1)}, bf16[8,11,32,128]{3,2,1,0:T(8,128)(2,1)}, u32[]{:S(2)}) copy-start(bf16[8,11,32,128]{3,2,1,0:T(8,128)(2,1)} %l0.1) | copy-start | bytes 2162692
  33.6 1.0 %copy-start.4 = (bf16[52,32,128]{2,1,0:T(8,128)(2,1)S(1)}, bf16[52,32,128]{2,1,0:T(8,128)(2,1)}, u32[]{:S(2)}) copy-start(bf16[52,32,128]{2,1,0:T(8,128)(2,1)} %copy-done.3) | copy-start | bytes 1277956
  40.8 1.6 %copy-start.5 = (bf16[8,12,128,128]{3,2,1,0:T(8,128)(2,1)}, bf16[8,12,128,128]{3,2,1,0:T(8,128)(2,1)S(1)}, u32[]{:S(2)}) copy-start(bf16[8,12,128,128]{3,2,1,0:T(8,128)(2,1)S(1)} %get-tuple-element.40.left) | copy-start | bytes 9437188
  42.5 21.9 %collective-permute-start.7 = (bf16[5,12,32,128]{3,2,1,0:T(8,128)(2,1)S(1)}, bf16[5,12,32,128]{3,2,1,0:T(8,128)(2,1)S(1)}, u32[]{:S(2)}, u32[]{:S(2)}) collective-permute-start(bf16[5,12,32,128]{3,2,1,0:T(8,128)(2,1)S(1)} %get-tuple-element.46), channel_id=1, source_target_pairs={{0,1},{1,8},{8,9},{9,16},{16,17},{17,24},{24,25},{25,0},{2,3},{3,1... | collective-permute-start | bytes 1474568 | tf_op jit(solution)/shard_map/ppermute | solution.py:155
  43.1 24.2 %collective-permute-start.8 = (bf16[5,12,32,128]{3,2,1,0:T(8,128)(2,1)S(1)}, bf16[5,12,32,128]{3,2,1,0:T(8,128)(2,1)S(1)}, u32[]{:S(2)}, u32[]{:S(2)}) collective-permute-start(bf16[5,12,32,128]{3,2,1,0:T(8,128)(2,1)S(1)} %get-tuple-element.45), channel_id=1, source_target_pairs={{0,25},{1,0},{8,1},{9,8},{16,9},{17,16},{24,17},{25,24},{2,27},{3,... | collective-permute-start | bytes 1474568 | tf_op jit(solution)/shard_map/ppermute | solution.py:155
  67.3 1.9 %copy-start.6 = (bf16[8,12,128,128]{3,2,1,0:T(8,128)(2,1)S(1)}, bf16[8,12,128,128]{3,2,1,0:T(8,128)(2,1)}, u32[]{:S(2)}) copy-start(bf16[8,12,128,128]{3,2,1,0:T(8,128)(2,1)} %copy-done.5) | copy-start | bytes 9437188
  75.2 9.3 %collective-permute-start.10 = (bf16[8,4,32,128]{3,2,1,0:T(8,128)(2,1)S(1)}, bf16[8,4,32,128]{3,2,1,0:T(8,128)(2,1)S(1)}, u32[]{:S(2)}, u32[]{:S(2)}) collective-permute-start(bf16[8,4,32,128]{3,2,1,0:T(8,128)(2,1)S(1)} %get-tuple-element.43), channel_id=1, source_target_pairs={{0,4},{2,6},{4,0},{6,2},{1,5},{3,7},{5,1},{7,3},{8,12},{10,14},{12... | collective-permute-start | bytes 786440 | tf_op jit(solution)/shard_map/ppermute | solution.py:158
  75.8 10.9 %collective-permute-start.11 = (bf16[8,4,32,128]{3,2,1,0:T(8,128)(2,1)S(1)}, bf16[8,4,32,128]{3,2,1,0:T(8,128)(2,1)S(1)}, u32[]{:S(2)}, u32[]{:S(2)}) collective-permute-start(bf16[8,4,32,128]{3,2,1,0:T(8,128)(2,1)S(1)} %get-tuple-element.44), channel_id=1, source_target_pairs={{0,6},{2,4},{4,2},{6,0},{1,7},{3,5},{5,3},{7,1},{8,14},{10,12},{12... | collective-permute-start | bytes 786440 | tf_op jit(solution)/shard_map/ppermute | solution.py:158
  75.9 10.8 %collective-permute-start.9 = (bf16[8,4,32,128]{3,2,1,0:T(8,128)(2,1)S(1)}, bf16[8,4,32,128]{3,2,1,0:T(8,128)(2,1)S(1)}, u32[]{:S(2)}, u32[]{:S(2)}) collective-permute-start(bf16[8,4,32,128]{3,2,1,0:T(8,128)(2,1)S(1)} %get-tuple-element.42), channel_id=1, source_target_pairs={{0,2},{2,0},{4,6},{6,4},{1,3},{3,1},{5,7},{7,5},{8,10},{10,8},{12,... | collective-permute-start | bytes 786440 | tf_op jit(solution)/shard_map/ppermute | solution.py:158

commit v3 on v1

v3 whole, which is shorter than its diff:
```python
import jax
import jax.numpy as jnp
from jax import lax
from jax.experimental import pallas as pl
from jax.experimental.pallas import tpu as pltpu
from jax.sharding import PartitionSpec as P

RADIUS = 5
BAND = 2 * RADIUS + 1
ROWS = 8
NEAR = ROWS + 2 * RADIUS
STRIPS = ROWS + 4 * RADIUS
REACH = ROWS + 6 * RADIUS
NT = (((1,), (1,)), ((), ()))
VMEM = pl.BlockSpec(memory_space=pltpu.VMEM)
SMEM = pl.BlockSpec(memory_space=pltpu.SMEM)

SHIFTS = (1, -1, 2, -2)
OWN = [(j, o) for j in range(ROWS) for o in range(BAND)]
LISTS = (
    [(j, o) for j, o in OWN if ROWS <= j + o <= ROWS + RADIUS - 1],
    [(j, o) for j, o in OWN if RADIUS <= j + o <= 2 * RADIUS - 1],
    [(j, o) for j, o in OWN if j + o >= 2 * ROWS],
    [(j, o) for j, o in OWN if j + o < BAND - 1 - ROWS],
)
EDGE = [(m, o) for m, o in OWN if not RADIUS <= m + o < RADIUS + ROWS]


def wrapped(value, total):
    return jnp.where(value < 0, value + total, jnp.where(value >= total, value - total, value))


def offset_slot(pattern, i, s, first):
    listed = pattern[s, first + i]
    o = wrapped(listed - (first + i) + RADIUS, pattern.shape[1])
    return jnp.where(listed >= 0, o, BAND)


def reorder_kernel(meta, pattern, density, *refs):
    outs, band = refs[:4], refs[4]
    first = meta[1]
    band[...] = jnp.zeros_like(band)
    for i in range(ROWS):
        for s in range(density.shape[1]):
            band[i, offset_slot(pattern, i, s, first)] = density[i, s]
    for out, entries in zip(outs, LISTS):
        for e, (j, o) in enumerate(entries):
            out[e] = band[j, o]


def place(left, piece, i, o, s, col, b):
    left[i, o, pl.ds(pl.multiple_of((col ^ b) * 32, 32), 32), :] = piece[i, s]


def prepare_kernel(meta, pattern, l0, l1, strips, left):
    col, first = meta[0], meta[1]
    strips[...] = jnp.zeros_like(strips)
    left[...] = jnp.zeros_like(left)
    for i in range(ROWS):
        for s in range(l0.shape[1]):
            o = offset_slot(pattern, i, s, first)
            place(left, l0, i, o, s, col, 0)
            place(left, l1, i, o, s, col, 1)
            used = o < BAND
            strips[jnp.where(used, i + 2 * RADIUS, STRIPS), jnp.where(used, i + o, 0)] = l0[i, s]


def square_kernel(meta, pattern, kept, l2, l3, h0, h1, h2, h3, strips_in, left_in,
                  square, low, high, strips, left):
    del strips_in, left_in
    col, first = meta[0], meta[1]
    for halo, entries, shift in zip((h0, h1, h2, h3), LISTS, SHIFTS):
        for e, (j, o) in enumerate(entries):
            row = j - shift * ROWS
            strips[row + 2 * RADIUS, row + o] = halo[e]
    for i in range(ROWS):
        for s in range(l2.shape[1]):
            o = offset_slot(pattern, i, s, first)
            place(left, l2, i, o, s, col, 2)
            place(left, l3, i, o, s, col, 3)
    shape = (32, 128)
    pick = lax.broadcasted_iota(jnp.int32, shape, 1) == lax.broadcasted_iota(jnp.int32, shape, 0) + col * 32
    pick = pick.astype(left.dtype)
    for m, o in EDGE:
        turned = lax.dot_general(pick, left[m, o], NT, preferred_element_type=jnp.float32)
        strips[m + o + RADIUS, m + RADIUS] = turned.astype(strips.dtype)

    @pl.loop(0, ROWS)
    def _(i):
        w = jnp.concatenate([left[i, o] for o in range(BAND)], axis=1)
        rows = []
        for s in range(square.shape[1]):
            t = wrapped(kept[s, first + i] - first + 2 * RADIUS, kept.shape[1])
            rows.append(jnp.concatenate([strips[t, i + o] for o in range(BAND)], axis=1))
        x = jnp.concatenate(rows, axis=0)
        acc = lax.dot_general(x, w, NT, preferred_element_type=jnp.float32)
        square[i] = acc.reshape(square.shape[1:]).astype(square.dtype)

    low[...] = square[:RADIUS]
    high[...] = square[ROWS - RADIUS :]


def gather_dot(strips, left, targets, i, offsets):
    w = jnp.concatenate([left[i, o] for o in offsets], axis=1)
    rows = [jnp.concatenate([strips[t, i + o] for o in offsets], axis=1) for t in targets]
    x = jnp.concatenate(rows, axis=0)
    return lax.dot_general(x, w, NT, preferred_element_type=jnp.float32)


def strip_of(table, s, row, first):
    total = table.shape[1]
    return wrapped(table[s, wrapped(row, total)] - first + 3 * RADIUS, total)


def cube_targets(cube, i, col, first, share):
    return [strip_of(cube, (col ^ b) * share + q, first + i, first) for b in range(4) for q in range(share)]


def inner_kernel(meta, kept, cube, own, left, strips, partial):
    col, first = meta[0], meta[1]
    strips[...] = jnp.zeros_like(strips)
    for k in range(ROWS):
        for s in range(own.shape[1]):
            strips[strip_of(kept, s, first + k, first), RADIUS + k] = own[k, s]
    share = cube.shape[0] // 4
    for i in range(ROWS):
        targets = cube_targets(cube, i, col, first, share)
        offsets = [o for o in range(BAND) if RADIUS <= i + o < RADIUS + ROWS]
        acc = gather_dot(strips, left, targets, i, offsets)
        for e, t in enumerate(targets):
            mine = strips[t, i + RADIUS].astype(jnp.float32)
            partial[i, e] = 3.0 * mine - 2.0 * acc[e * 32 : (e + 1) * 32]


def cube_kernel(meta, kept, cube, before, after, left, partial, strips_in, o0, o1, o2, o3, strips):
    del strips_in
    col, first = meta[0], meta[1]
    for k in range(RADIUS):
        for s in range(before.shape[1]):
            strips[strip_of(kept, s, first - RADIUS + k, first), k] = before[k, s]
            strips[strip_of(kept, s, first + ROWS + k, first), RADIUS + ROWS + k] = after[k, s]
    outs = (o0, o1, o2, o3)
    share = o0.shape[1]
    for i in range(ROWS):
        targets = cube_targets(cube, i, col, first, share)
        offsets = [o for o in range(BAND) if not RADIUS <= i + o < RADIUS + ROWS]
        acc = gather_dot(strips, left, targets, i, offsets)
        for e in range(len(targets)):
            piece = partial[i, e] - 2.0 * acc[e * 32 : (e + 1) * 32]
            outs[e // share][i, e % share] = piece.astype(o0.dtype)


def final_kernel(meta, p0, p1, p2, p3, out, whole):
    col = meta[0]
    rows = lax.broadcasted_iota(jnp.int32, (128, 128), 0)
    cols = lax.broadcasted_iota(jnp.int32, (128, 128), 1)
    eye = (rows == cols).astype(p0.dtype)
    for b, p in enumerate((p0, p1, p2, p3)):
        start = pl.multiple_of((col ^ b) * 32, 32)
        whole[:, pl.ds(start, 32), :] = p[0]
    for q in range(out.shape[1]):
        out[0, q] = lax.dot_general(eye, whole[q], NT, preferred_element_type=jnp.float32)


def call(kernel, specs, outs, scratch, args, flops=0, limit=16, aliases=None):
    size = sum(a.size * a.dtype.itemsize for a in args) + sum(o.size * o.dtype.itemsize for o in outs)
    return pl.pallas_call(
        kernel,
        out_shape=outs,
        in_specs=specs,
        out_specs=[VMEM] * len(outs),
        scratch_shapes=scratch,
        input_output_aliases=aliases or {},
        compiler_params=pltpu.CompilerParams(vmem_limit_bytes=limit << 20),
        cost_estimate=pl.CostEstimate(flops=flops, bytes_accessed=size, transcendentals=0),
    )(*args)


def shape(*dims, dtype=jnp.bfloat16):
    return jax.ShapeDtypeStruct(dims, dtype)


def per_device(density, pattern, square_filter, cube_filter):
    layers = lax.axis_size("layer")
    groups = lax.axis_size("row") * layers
    assert density.shape[0] == ROWS and lax.axis_size("col") == 4
    piece = density.shape[2:]
    col = lax.axis_index("col")
    first = (lax.axis_index("row") * layers + lax.axis_index("layer")) * ROWS
    meta = jnp.stack([col, first]).astype(jnp.int32)
    pattern, kept, cube = pattern.T, square_filter.T, cube_filter.T

    def shifted(x, d):
        return lax.ppermute(x, ("row", "layer"), [(g, (g + d) % groups) for g in range(groups)])

    def across(x, bits):
        return lax.ppermute(x, "col", [(c, c ^ bits) for c in range(4)])

    l2 = across(density, 2)
    l1 = across(density, 1)
    payload = call(
        reorder_kernel, [SMEM, SMEM, VMEM], [shape(len(e), *piece) for e in LISTS],
        [pltpu.VMEM((ROWS, BAND + 1, *piece), density.dtype)],
        (meta, pattern, density),
    )
    payload, l1 = lax.optimization_barrier((payload, l1))
    halos = [shifted(p, d) for p, d in zip(payload, SHIFTS)]
    strips, left = call(
        prepare_kernel, [SMEM, SMEM, VMEM, VMEM],
        [shape(STRIPS + 1, NEAR, *piece), shape(ROWS, BAND + 1, 128, 128)],
        [], (meta, pattern, density, l1),
    )
    l2, halos, strips, left = lax.optimization_barrier((l2, halos, strips, left))
    l3 = across(l2, 1)

    width = kept.shape[0]
    square, low, high, _, left = call(
        square_kernel, [SMEM] * 3 + [VMEM] * 8,
        [shape(ROWS, width, *piece), shape(RADIUS, width, *piece), shape(RADIUS, width, *piece),
         shape(*strips.shape), shape(*left.shape)],
        [], (meta, pattern, kept, l2, l3, *halos, strips, left),
        2 * ROWS * width * BAND * 128 * 128 * 32, aliases={9: 3, 10: 4},
    )
    after = shifted(low, -1)
    before = shifted(high, 1)
    slots = cube.shape[0]
    share = slots // 4
    work = 2 * ROWS * slots * BAND * 128 * 128 * 32
    strips, partial = call(
        inner_kernel, [SMEM] * 3 + [VMEM] * 2,
        [shape(REACH, NEAR, *piece), shape(ROWS, slots, *piece, dtype=jnp.float32)],
        [], (meta, kept, cube, square, left), work * 2 // 3,
    )
    pieces = call(
        cube_kernel, [SMEM] * 3 + [VMEM] * 5,
        [shape(ROWS, share, *piece)] * 4 + [shape(*strips.shape)],
        [], (meta, kept, cube, before, after, left, partial, strips), work // 3,
        aliases={7: 4},
    )
    got = [pieces[0]] + [across(pieces[b], b) for b in (1, 2, 3)]
    return pl.pallas_call(
        final_kernel,
        grid=(ROWS,),
        out_shape=shape(ROWS, share, 128, 128, dtype=jnp.float32),
        in_specs=[SMEM] + [pl.BlockSpec((1, share, *piece), lambda i: (i, 0, 0, 0))] * 4,
        out_specs=pl.BlockSpec((1, share, 128, 128), lambda i: (i, 0, 0, 0)),
        scratch_shapes=[pltpu.VMEM((share, 128, 128), density.dtype)],
        compiler_params=pltpu.CompilerParams(vmem_limit_bytes=16 << 20),
    )(meta, *got)


def solution(mesh):
    in_specs = (P(("row", "layer"), None, "col", None), P(), P(), P())
    out_specs = P(("row", "layer"), "col", None, None)
    return jax.shard_map(
        per_device, mesh=mesh, in_specs=in_specs, out_specs=out_specs, check_vma=False
    )
```

time: 104 us -> 77.4 us (0.74)
  waiting for transfers between devices: 60.1 us -> 36.4 us
  local copies, waits for them, and re-layouts: 9.98 us -> 2.51 us
  Pallas kernels: 16.9 us -> 19.8 us
  starting transfers between devices: 16.3 us -> 18.3 us
    ppermute x6, waiting for transfers between devices: 34.7 us -> 18.8 us  [shifted(): lax.ppermute(x, ('row', 'layer'), [(g, (g + d) % groups) for g in range(g...]
    ppermute x6, waiting for transfers between devices: 25.4 us -> 17.6 us  [across(): return lax.ppermute(x, 'col', [(c, c ^ bits) for c in range(4)])]
    unnamed x17 -> x10, local copies, waits for them, and re-layouts: 8.45 us -> 2.51 us
    pallas_call x4 -> x6, Pallas kernels: 16.9 us -> 19.8 us  [the longest x5 15.3 us: call(): pl.pallas_call(kernel, out_shape=outs, in_specs=specs, out_specs=[VMEM] *...]
    ppermute x6, starting transfers between devices: 11.1 us -> 13.4 us  [shifted(): lax.ppermute(x, ('row', 'layer'), [(g, (g + d) % groups) for g in range(g...]
  transfers between devices with their start and end apart: 12 -> 12, of which waited for: 8 -> 9; matrix products, arithmetic and copies ran while one was open for 2% -> 0% of each run, Pallas kernels for 2% -> 9%
where the time goes in v3:
time: 77.4 us; the launch traced here: 77.2 us
  waiting for transfers between devices  36.4 us (47%)
  Pallas kernels  19.8 us (26%)
  starting transfers between devices  18.3 us (24%)
  local copies, waits for them, and re-layouts  2.51 us (3%)
    ppermute x6, waiting for transfers between devices, shifted(): lax.ppermute(x, ('row', 'layer'), [(g, (g + d) % groups) for g in range(g...  18.8 us
    ppermute x6, waiting for transfers between devices, across(): return lax.ppermute(x, 'col', [(c, c ^ bits) for c in range(4)])  17.6 us
    pallas_call x5, Pallas kernels, call(): pl.pallas_call(kernel, out_shape=outs, in_specs=specs, out_specs=[VMEM] *...  15.3 us
    ppermute x6, starting transfers between devices, shifted(): lax.ppermute(x, ('row', 'layer'), [(g, (g + d) % groups) for g in range(g...  13.4 us
    ppermute x6, starting transfers between devices, across(): return lax.ppermute(x, 'col', [(c, c ^ bits) for c in range(4)])  4.88 us
    pallas_call x1, Pallas kernels, per_device(): pl.pallas_call(final_kernel, grid=(ROWS,), out_shape=shape(ROWS, share, 1...  4.51 us
    unnamed x10, local copies, waits for them, and re-layouts  2.51 us
  transfers between devices with their start and end apart: 12, of which 9 were waited for; matrix products, arithmetic and copies ran while one was open for 0% of the time, Pallas kernels for 9%

profile of v3, /device:TPU:0, one launch (start us, length us, event | category | flops | bytes accessed | tf_op | source)
XLA Modules:
  0.0 77.2 jit_solution(13583166839911531998)
XLA Ops:
  0.0 0.5 collective-permute-start.1
  0.5 2.5 %collective-permute-start = (bf16[8,11,32,128]{3,2,1,0:T(8,128)(2,1)}, bf16[8,11,32,128]{3,2,1,0:T(8,128)(2,1)S(1)}, u32[]{:S(2)}, u32[]{:S(2)}) collective-permute-start(bf16[8,11,32,128]{3,2,1,0:T(8,128)(2,1)} %l0.1), channel_id=1, source_target_pairs={{0,4},{2,6},{4,0},{6,2},{1,5},{3,7},{5,1},{7,3},{8,12},{10,14},{12... | collective-permute-start | bytes 2162696 | tf_op jit(solution)/shard_map/ppermute | solution.py:197
  2.9 0.1 pad_add_fusion.meta
  3.0 0.0 copy-start
  3.0 1.1 %copy-done = bf16[8,11,32,128]{3,2,1,0:T(8,128)(2,1)S(1)} copy-done((bf16[8,11,32,128]{3,2,1,0:T(8,128)(2,1)S(1)}, bf16[8,11,32,128]{3,2,1,0:T(8,128)(2,1)}, u32[]{:S(2)}) %copy-start) | copy-done | bytes 720920
  4.1 0.0 copy-start.1
  4.1 0.7 copy-done.1
  4.8 1.1 %shard_map.46 = (bf16[37,32,128]{2,1,0:T(8,128)(2,1)S(1)}, bf16[37,32,128]{2,1,0:T(8,128)(2,1)S(1)}, bf16[3,32,128]{2,1,0:T(8,128)(2,1)S(1)}, bf16[3,32,128]{2,1,0:T(8,128)(2,1)S(1)}) custom-call(s32[2]{0:T(128)S(1)} %pad_add_fusion.meta, s32[11,64]{1,0:T(8,128)S(1)} %bitcast.5, bf16[8,11,32,128]{3,2,1,0:T(8,128)(2,1)S(1)} %copy-done), custom_call_target="tpu_custom_call" | custom-call | bytes 1379080 | tf_op jit(solution)/shard_map/pallas_call | solution.py:167
  6.0 0.0 collective-permute-done.1.l1
  6.0 1.6 %collective-permute-start.2 = (bf16[37,32,128]{2,1,0:T(8,128)(2,1)S(1)}, bf16[37,32,128]{2,1,0:T(8,128)(2,1)S(1)}, u32[]{:S(2)}, u32[]{:S(2)}) collective-permute-start(bf16[37,32,128]{2,1,0:T(8,128)(2,1)S(1)} %get-tuple-element.37), channel_id=1, source_target_pairs={{0,1},{1,8},{8,9},{9,16},{16,17},{17,24},{24,25},{25,0},{2,3},{3,1... | collective-permute-start | bytes 909320 | tf_op jit(solution)/shard_map/ppermute | solution.py:194
  7.5 3.2 %collective-permute-start.3 = (bf16[37,32,128]{2,1,0:T(8,128)(2,1)S(1)}, bf16[37,32,128]{2,1,0:T(8,128)(2,1)S(1)}, u32[]{:S(2)}, u32[]{:S(2)}) collective-permute-start(bf16[37,32,128]{2,1,0:T(8,128)(2,1)S(1)} %get-tuple-element.38), channel_id=1, source_target_pairs={{0,25},{1,0},{8,1},{9,8},{16,9},{17,16},{24,17},{25,24},{2,27},{3,... | collective-permute-start | bytes 909320 | tf_op jit(solution)/shard_map/ppermute | solution.py:194
  10.7 0.0 collective-permute-start.4
  10.8 3.8 %collective-permute-start.5 = (bf16[3,32,128]{2,1,0:T(8,128)(2,1)S(1)}, bf16[3,32,128]{2,1,0:T(8,128)(2,1)S(1)}, u32[]{:S(2)}, u32[]{:S(2)}) collective-permute-start(bf16[3,32,128]{2,1,0:T(8,128)(2,1)S(1)} %get-tuple-element.40), channel_id=1, source_target_pairs={{0,24},{1,25},{8,0},{9,1},{16,8},{17,9},{24,16},{25,17},{2,26},{3,... | collective-permute-start | bytes 73736 | tf_op jit(solution)/shard_map/ppermute | solution.py:194
  14.6 2.0 %shard_map.47 = (bf16[29,18,32,128]{3,2,1,0:T(8,128)(2,1)S(1)}, bf16[8,12,128,128]{3,2,1,0:T(8,128)(2,1)S(1)}) custom-call(s32[2]{0:T(128)S(1)} %pad_add_fusion.meta, s32[11,64]{1,0:T(8,128)S(1)} %bitcast.6, bf16[8,11,32,128]{3,2,1,0:T(8,128)(2,1)S(1)} %copy-done, bf16[8,11,32,128]{3,2,1,0:T(8,128)(2,1)S(1)} %collective-permute-done.1.l1), custom_call_target="tpu_custom_call" | custom-call | bytes 8866568 | tf_op jit(solution)/shard_map/pallas_call | solution.py:167
  16.6 3.4 %collective-permute-done.l2 = bf16[8,11,32,128]{3,2,1,0:T(8,128)(2,1)S(1)} collective-permute-done((bf16[8,11,32,128]{3,2,1,0:T(8,128)(2,1)}, bf16[8,11,32,128]{3,2,1,0:T(8,128)(2,1)S(1)}, u32[]{:S(2)}, u32[]{:S(2)}) %collective-permute-start) | collective-permute-done | bytes 720928 | tf_op jit(solution)/shard_map/ppermute | solution.py:197
  20.0 0.4 collective-permute-done.4.h2
  20.4 0.0 collective-permute-done.5.h3
  20.4 0.5 collective-permute-done.2.h0
  20.9 2.2 %collective-permute-done.3.h1 = bf16[37,32,128]{2,1,0:T(8,128)(2,1)S(1)} collective-permute-done((bf16[37,32,128]{2,1,0:T(8,128)(2,1)S(1)}, bf16[37,32,128]{2,1,0:T(8,128)(2,1)S(1)}, u32[]{:S(2)}, u32[]{:S(2)}) %collective-permute-start.3) | collective-permute-done | bytes 303136 | tf_op jit(solution)/shard_map/ppermute | solution.py:194
  23.1 0.0 collective-permute-start.6
  23.1 2.2 %collective-permute-done.6.l3 = bf16[8,11,32,128]{3,2,1,0:T(8,128)(2,1)S(1)} collective-permute-done((bf16[8,11,32,128]{3,2,1,0:T(8,128)(2,1)S(1)}, bf16[8,11,32,128]{3,2,1,0:T(8,128)(2,1)S(1)}, u32[]{:S(2)}, u32[]{:S(2)}) %collective-permute-start.6) | collective-permute-done | bytes 720928 | tf_op jit(solution)/shard_map/ppermute | solution.py:197
  25.3 0.0 copy-start.2
  25.3 0.7 copy-done.2
  26.0 0.0 copy-start.3
  26.0 0.0 copy-start.4
  26.0 5.8 %shard_map.48 = (bf16[8,12,32,128]{3,2,1,0:T(8,128)(2,1)S(1)}, bf16[5,12,32,128]{3,2,1,0:T(8,128)(2,1)S(1)}, bf16[5,12,32,128]{3,2,1,0:T(8,128)(2,1)S(1)}, bf16[...) custom-call(s32[2]{0:T(128)S(1)} %pad_add_fusion.meta, ...), custom_call_target="tpu_custom_call", output_to_operand_aliasing={{3}: (9, {}), {4}: (10, {})} | custom-call | flops 1107296256 | bytes 18716424 | tf_op jit(solution)/shard_map/pallas_call | solution.py:167
  31.7 0.3 collective-permute-start.7
  32.1 4.4 %collective-permute-start.8 = (bf16[5,12,32,128]{3,2,1,0:T(8,128)(2,1)S(1)}, bf16[5,12,32,128]{3,2,1,0:T(8,128)(2,1)S(1)}, u32[]{:S(2)}, u32[]{:S(2)}) collective-permute-start(bf16[5,12,32,128]{3,2,1,0:T(8,128)(2,1)S(1)} %get-tuple-element.52), channel_id=1, source_target_pairs={{0,25},{1,0},{8,1},{9,8},{16,9},{17,16},{24,17},{25,24},{2,27},{3,... | collective-permute-start | bytes 1474568 | tf_op jit(solution)/shard_map/ppermute | solution.py:194
  36.5 0.0 copy-done.3
  36.5 0.0 copy-done.4
  36.5 4.0 %shard_map.49 = (bf16[38,18,32,128]{3,2,1,0:T(8,128)(2,1)S(1)}, f32[8,16,32,128]{3,2,1,0:T(8,128)S(1)}) custom-call(s32[2]{0:T(128)S(1)} %pad_add_fusion.meta, s32[12,64]{1,0:T(8,128)S(1)} %bitcast.9, s32[16,64]{1,0:T(8,128)S(1)} %bitcast.11, bf16[8,12,32,128]{3,2,1,0:T(8,128)(2,1)S(1)} %get-tuple-element.54.own, ...), custom_call_target="tpu_custom_call" | custom-call | flops 984263360 | bytes 11639816 | tf_op jit(solution)/shard_map/pallas_call | solution.py:167
  40.5 12.9 %collective-permute-done.7.before = bf16[5,12,32,128]{3,2,1,0:T(8,128)(2,1)S(1)} collective-permute-done((bf16[5,12,32,128]{3,2,1,0:T(8,128)(2,1)S(1)}, bf16[5,12,32,128]{3,2,1,0:T(8,128)(2,1)S(1)}, u32[]{:S(2)}, u32[]{:S(2)}) %collective-permute-start.7) | collective-permute-done | bytes 491552 | tf_op jit(solution)/shard_map/ppermute | solution.py:194
  53.4 2.9 %collective-permute-done.8.after = bf16[5,12,32,128]{3,2,1,0:T(8,128)(2,1)S(1)} collective-permute-done((bf16[5,12,32,128]{3,2,1,0:T(8,128)(2,1)S(1)}, bf16[5,12,32,128]{3,2,1,0:T(8,128)(2,1)S(1)}, u32[]{:S(2)}, u32[]{:S(2)}) %collective-permute-start.8) | collective-permute-done | bytes 491552 | tf_op jit(solution)/shard_map/ppermute | solution.py:194
  56.3 2.4 %shard_map.50 = (bf16[8,4,32,128]{3,2,1,0:T(8,128)(2,1)S(1)}, bf16[8,4,32,128]{3,2,1,0:T(8,128)(2,1)S(1)}, bf16[8,4,32,128]{3,2,1,0:T(8,128)(2,1)S(1)}, bf16[8,4...) custom-call(s32[2]{0:T(128)S(1)} %pad_add_fusion.meta, ...), custom_call_target="tpu_custom_call", output_to_operand_aliasing={{4}: (7, {})} | custom-call | flops 492131680 | bytes 18488328 | tf_op jit(solution)/shard_map/pallas_call | solution.py:167
  58.7 0.1 collective-permute-start.9
  58.8 0.6 collective-permute-start.10
  59.4 1.3 %collective-permute-start.11 = (bf16[8,4,32,128]{3,2,1,0:T(8,128)(2,1)S(1)}, bf16[8,4,32,128]{3,2,1,0:T(8,128)(2,1)S(1)}, u32[]{:S(2)}, u32[]{:S(2)}) collective-permute-start(bf16[8,4,32,128]{3,2,1,0:T(8,128)(2,1)S(1)} %get-tuple-element.60), channel_id=1, source_target_pairs={{0,6},{2,4},{4,2},{6,0},{1,7},{3,5},{5,3},{7,1},{8,14},{10,12},{12... | collective-permute-start | bytes 786440 | tf_op jit(solution)/shard_map/ppermute | solution.py:197
  60.6 0.0 collective-permute-done.9.p1
  60.6 7.3 %collective-permute-done.10.p2 = bf16[8,4,32,128]{3,2,1,0:T(8,128)(2,1)S(1)} collective-permute-done((bf16[8,4,32,128]{3,2,1,0:T(8,128)(2,1)S(1)}, bf16[8,4,32,128]{3,2,1,0:T(8,128)(2,1)S(1)}, u32[]{:S(2)}, u32[]{:S(2)}) %collective-permute-start.10) | collective-permute-done | bytes 262176 | tf_op jit(solution)/shard_map/ppermute | solution.py:197
  67.9 4.7 %collective-permute-done.11.p3 = bf16[8,4,32,128]{3,2,1,0:T(8,128)(2,1)S(1)} collective-permute-done((bf16[8,4,32,128]{3,2,1,0:T(8,128)(2,1)S(1)}, bf16[8,4,32,128]{3,2,1,0:T(8,128)(2,1)S(1)}, u32[]{:S(2)}, u32[]{:S(2)}) %collective-permute-start.11) | collective-permute-done | bytes 262176 | tf_op jit(solution)/shard_map/ppermute | solution.py:197
  72.6 4.5 %shard_map.51 = f32[8,4,128,128]{3,2,1,0:T(8,128)} custom-call(s32[2]{0:T(128)S(1)} %pad_add_fusion.meta, bf16[8,4,32,128]{3,2,1,0:T(8,128)(2,1)S(1)} %get-tuple-element.57.p0, bf16[8,4,32,128]{3,2,1,0:T(8,128)(2,1)S(1)} %collective-permute-done.9.p1, bf16[8,4,32,128]{3,2,1,0:T(8,128)(2,1)S(1)} %collective-permute-done.10.p2, ...), custom_call_target="tpu_custom_call" | custom-call | tf_op jit(solution)/shard_map/pallas_call | solution.py:241
Async XLA Ops:
  0.0 6.0 %collective-permute-start.1 = (bf16[8,11,32,128]{3,2,1,0:T(8,128)(2,1)}, bf16[8,11,32,128]{3,2,1,0:T(8,128)(2,1)S(1)}, u32[]{:S(2)}, u32[]{:S(2)}) collective-permute-start(bf16[8,11,32,128]{3,2,1,0:T(8,128)(2,1)} %l0.1), channel_id=1, source_target_pairs={{0,2},{2,0},{4,6},{6,4},{1,3},{3,1},{5,7},{7,5},{8,10},{10,8},{12,... | collective-permute-start | bytes 2162696 | tf_op jit(solution)/shard_map/ppermute | solution.py:197
  0.5 19.5 %collective-permute-start = (bf16[8,11,32,128]{3,2,1,0:T(8,128)(2,1)}, bf16[8,11,32,128]{3,2,1,0:T(8,128)(2,1)S(1)}, u32[]{:S(2)}, u32[]{:S(2)}) collective-permute-start(bf16[8,11,32,128]{3,2,1,0:T(8,128)(2,1)} %l0.1), channel_id=1, source_target_pairs={{0,4},{2,6},{4,0},{6,2},{1,5},{3,7},{5,1},{7,3},{8,12},{10,14},{12... | collective-permute-start | bytes 2162696 | tf_op jit(solution)/shard_map/ppermute | solution.py:197
  3.0 1.1 %copy-start = (bf16[8,11,32,128]{3,2,1,0:T(8,128)(2,1)S(1)}, bf16[8,11,32,128]{3,2,1,0:T(8,128)(2,1)}, u32[]{:S(2)}) copy-start(bf16[8,11,32,128]{3,2,1,0:T(8,128)(2,1)} %l0.1) | copy-start | bytes 2162692
  4.1 0.7 copy-start.1
  6.0 14.9 %collective-permute-start.2 = (bf16[37,32,128]{2,1,0:T(8,128)(2,1)S(1)}, bf16[37,32,128]{2,1,0:T(8,128)(2,1)S(1)}, u32[]{:S(2)}, u32[]{:S(2)}) collective-permute-start(bf16[37,32,128]{2,1,0:T(8,128)(2,1)S(1)} %get-tuple-element.37), channel_id=1, source_target_pairs={{0,1},{1,8},{8,9},{9,16},{16,17},{17,24},{24,25},{25,0},{2,3},{3,1... | collective-permute-start | bytes 909320 | tf_op jit(solution)/shard_map/ppermute | solution.py:194
  7.5 15.5 %collective-permute-start.3 = (bf16[37,32,128]{2,1,0:T(8,128)(2,1)S(1)}, bf16[37,32,128]{2,1,0:T(8,128)(2,1)S(1)}, u32[]{:S(2)}, u32[]{:S(2)}) collective-permute-start(bf16[37,32,128]{2,1,0:T(8,128)(2,1)S(1)} %get-tuple-element.38), channel_id=1, source_target_pairs={{0,25},{1,0},{8,1},{9,8},{16,9},{17,16},{24,17},{25,24},{2,27},{3,... | collective-permute-start | bytes 909320 | tf_op jit(solution)/shard_map/ppermute | solution.py:194
  10.7 9.6 %collective-permute-start.4 = (bf16[3,32,128]{2,1,0:T(8,128)(2,1)S(1)}, bf16[3,32,128]{2,1,0:T(8,128)(2,1)S(1)}, u32[]{:S(2)}, u32[]{:S(2)}) collective-permute-start(bf16[3,32,128]{2,1,0:T(8,128)(2,1)S(1)} %get-tuple-element.39), channel_id=1, source_target_pairs={{0,8},{1,9},{8,16},{9,17},{16,24},{17,25},{24,0},{25,1},{2,10},{3,... | collective-permute-start | bytes 73736 | tf_op jit(solution)/shard_map/ppermute | solution.py:194
  10.8 9.6 %collective-permute-start.5 = (bf16[3,32,128]{2,1,0:T(8,128)(2,1)S(1)}, bf16[3,32,128]{2,1,0:T(8,128)(2,1)S(1)}, u32[]{:S(2)}, u32[]{:S(2)}) collective-permute-start(bf16[3,32,128]{2,1,0:T(8,128)(2,1)S(1)} %get-tuple-element.40), channel_id=1, source_target_pairs={{0,24},{1,25},{8,0},{9,1},{16,8},{17,9},{24,16},{25,17},{2,26},{3,... | collective-permute-start | bytes 73736 | tf_op jit(solution)/shard_map/ppermute | solution.py:194
  23.1 2.2 %collective-permute-start.6 = (bf16[8,11,32,128]{3,2,1,0:T(8,128)(2,1)S(1)}, bf16[8,11,32,128]{3,2,1,0:T(8,128)(2,1)S(1)}, u32[]{:S(2)}, u32[]{:S(2)}) collective-permute-start(bf16[8,11,32,128]{3,2,1,0:T(8,128)(2,1)S(1)} %collective-permute-done.l2), channel_id=1, source_target_pairs={{0,2},{2,0},{4,6},{6,4},{1,3},{3,1},{5,7},{7,5},{8,10},{10,8},{12,... | collective-permute-start | bytes 2162696 | tf_op jit(solution)/shard_map/ppermute | solution.py:197
  25.3 0.7 copy-start.2
  26.0 10.6 %copy-start.3 = (s32[64,12]{0,1:T(8,128)S(1)}, s32[64,12]{0,1:T(8,128)}, u32[]{:S(2)}) copy-start(s32[64,12]{0,1:T(8,128)} %param.6) | copy-start | bytes 9220
  26.0 10.6 %copy-start.4 = (s32[64,16]{0,1:T(8,128)S(1)}, s32[64,16]{0,1:T(8,128)}, u32[]{:S(2)}) copy-start(s32[64,16]{0,1:T(8,128)} %param.7) | copy-start | bytes 12292
  31.7 21.7 %collective-permute-start.7 = (bf16[5,12,32,128]{3,2,1,0:T(8,128)(2,1)S(1)}, bf16[5,12,32,128]{3,2,1,0:T(8,128)(2,1)S(1)}, u32[]{:S(2)}, u32[]{:S(2)}) collective-permute-start(bf16[5,12,32,128]{3,2,1,0:T(8,128)(2,1)S(1)} %get-tuple-element.51), channel_id=1, source_target_pairs={{0,1},{1,8},{8,9},{9,16},{16,17},{17,24},{24,25},{25,0},{2,3},{3,1... | collective-permute-start | bytes 1474568 | tf_op jit(solution)/shard_map/ppermute | solution.py:194
  32.1 24.2 %collective-permute-start.8 = (bf16[5,12,32,128]{3,2,1,0:T(8,128)(2,1)S(1)}, bf16[5,12,32,128]{3,2,1,0:T(8,128)(2,1)S(1)}, u32[]{:S(2)}, u32[]{:S(2)}) collective-permute-start(bf16[5,12,32,128]{3,2,1,0:T(8,128)(2,1)S(1)} %get-tuple-element.52), channel_id=1, source_target_pairs={{0,25},{1,0},{8,1},{9,8},{16,9},{17,16},{24,17},{25,24},{2,27},{3,... | collective-permute-start | bytes 1474568 | tf_op jit(solution)/shard_map/ppermute | solution.py:194
  58.7 1.9 %collective-permute-start.9 = (bf16[8,4,32,128]{3,2,1,0:T(8,128)(2,1)S(1)}, bf16[8,4,32,128]{3,2,1,0:T(8,128)(2,1)S(1)}, u32[]{:S(2)}, u32[]{:S(2)}) collective-permute-start(bf16[8,4,32,128]{3,2,1,0:T(8,128)(2,1)S(1)} %get-tuple-element.58), channel_id=1, source_target_pairs={{0,2},{2,0},{4,6},{6,4},{1,3},{3,1},{5,7},{7,5},{8,10},{10,8},{12,... | collective-permute-start | bytes 786440 | tf_op jit(solution)/shard_map/ppermute | solution.py:197
  58.8 9.2 %collective-permute-start.10 = (bf16[8,4,32,128]{3,2,1,0:T(8,128)(2,1)S(1)}, bf16[8,4,32,128]{3,2,1,0:T(8,128)(2,1)S(1)}, u32[]{:S(2)}, u32[]{:S(2)}) collective-permute-start(bf16[8,4,32,128]{3,2,1,0:T(8,128)(2,1)S(1)} %get-tuple-element.59), channel_id=1, source_target_pairs={{0,4},{2,6},{4,0},{6,2},{1,5},{3,7},{5,1},{7,3},{8,12},{10,14},{12... | collective-permute-start | bytes 786440 | tf_op jit(solution)/shard_map/ppermute | solution.py:197
  59.4 13.3 %collective-permute-start.11 = (bf16[8,4,32,128]{3,2,1,0:T(8,128)(2,1)S(1)}, bf16[8,4,32,128]{3,2,1,0:T(8,128)(2,1)S(1)}, u32[]{:S(2)}, u32[]{:S(2)}) collective-permute-start(bf16[8,4,32,128]{3,2,1,0:T(8,128)(2,1)S(1)} %get-tuple-element.60), channel_id=1, source_target_pairs={{0,6},{2,4},{4,2},{6,0},{1,7},{3,5},{5,3},{7,1},{8,14},{10,12},{12... | collective-permute-start | bytes 786440 | tf_op jit(solution)/shard_map/ppermute | solution.py:197

commit v4 on v3

v4 whole, which is shorter than its diff:
```python
import jax
import jax.numpy as jnp
from jax import lax
from jax.experimental import pallas as pl
from jax.experimental.pallas import tpu as pltpu
from jax.sharding import PartitionSpec as P

RADIUS = 5
BAND = 2 * RADIUS + 1
ROWS = 8
NEAR = ROWS + 2 * RADIUS
STRIPS = ROWS + 4 * RADIUS
REACH = ROWS + 6 * RADIUS
NT = (((1,), (1,)), ((), ()))
VMEM = pl.BlockSpec(memory_space=pltpu.VMEM)
SMEM = pl.BlockSpec(memory_space=pltpu.SMEM)
ANY = pl.BlockSpec(memory_space=pl.ANY)

SHIFTS = (1, -1, 2, -2)
OWN = [(j, o) for j in range(ROWS) for o in range(BAND)]
LISTS = (
    [(j, o) for j, o in OWN if ROWS <= j + o <= ROWS + RADIUS - 1],
    [(j, o) for j, o in OWN if RADIUS <= j + o <= 2 * RADIUS - 1],
    [(j, o) for j, o in OWN if j + o >= 2 * ROWS],
    [(j, o) for j, o in OWN if j + o < BAND - 1 - ROWS],
)
EDGES = (
    [(m, o) for m, o in OWN if m + o < RADIUS],
    [(m, o) for m, o in OWN if m + o >= RADIUS + ROWS],
)
LATE = range(RADIUS, ROWS)
MIDDLE = range(ROWS - RADIUS, RADIUS)
EARLY = range(0, ROWS - RADIUS)
AFTER = range(RADIUS + ROWS, NEAR)
CLOSE = range(ROWS - RADIUS, RADIUS)
FAR = range(0, ROWS - RADIUS)


def wrapped(value, total):
    return jnp.where(value < 0, value + total, jnp.where(value >= total, value - total, value))


def offset_slot(pattern, i, s, first):
    listed = pattern[s, first + i]
    o = wrapped(listed - (first + i) + RADIUS, pattern.shape[1])
    return jnp.where(listed >= 0, o, BAND)


def position(pattern, i, s, first):
    o = offset_slot(pattern, i, s, first)
    return jnp.where(o < BAND, i + o, (i + BAND) % NEAR)


def reorder_kernel(meta, pattern, density, h0, h1, h2, h3, band, blocks, table, sems):
    first = meta[1]
    copies = (
        pltpu.make_async_copy(density, blocks, sems.at[0]),
        pltpu.make_async_copy(pattern, table, sems.at[1]),
    )
    for copy in copies:
        copy.start()
    band[...] = jnp.zeros_like(band)
    for copy in copies:
        copy.wait()
    for i in range(ROWS):
        for s in range(blocks.shape[1]):
            band[i, offset_slot(table, i, s, first)] = blocks[i, s]
    for out, entries in zip((h0, h1, h2, h3), LISTS):
        for e, (j, o) in enumerate(entries):
            out[e] = band[j, o]


def place(left, piece, i, p, s, col, b):
    left[i, p, pl.ds(pl.multiple_of((col ^ b) * 32, 32), 32), :] = piece[i, s]


def prepare_kernel(meta, pattern, l0, l1, strips, left):
    col, first = meta[0], meta[1]
    strips[...] = jnp.zeros_like(strips)
    left[...] = jnp.zeros_like(left)
    for i in range(ROWS):
        for s in range(l0.shape[1]):
            p = position(pattern, i, s, first)
            place(left, l0, i, p, s, col, 0)
            place(left, l1, i, p, s, col, 1)
            strips[i + 2 * RADIUS, p] = l0[i, s]


def insert_kernel(meta, pattern, l2, h0, h1, h2, h3, strips_in, left_in, strips, left):
    del strips_in, left_in
    col, first = meta[0], meta[1]
    for halo, entries, shift in zip((h0, h1, h2, h3), LISTS, SHIFTS):
        for e, (j, o) in enumerate(entries):
            row = j - shift * ROWS
            strips[row + 2 * RADIUS, row + o] = halo[e]
    for i in range(ROWS):
        for s in range(l2.shape[1]):
            place(left, l2, i, position(pattern, i, s, first), s, col, 2)


def gather_dot(strips, left, targets, i, places):
    w = jnp.concatenate([left[i, p] for p in places], axis=1)
    rows = [jnp.concatenate([strips[t, p] for p in places], axis=1) for t in targets]
    x = jnp.concatenate(rows, axis=0)
    return lax.dot_general(x, w, NT, preferred_element_type=jnp.float32)


def square_row(kept, strips, left, i, first):
    total = kept.shape[1]
    targets = [wrapped(kept[s, first + i] - first + 2 * RADIUS, total) for s in range(kept.shape[0])]
    acc = gather_dot(strips, left, targets, i, range(i, i + BAND))
    return acc.reshape(len(targets), 32, 128).astype(strips.dtype)


def low_kernel(meta, pattern, kept, l3, strips_in, left_in, low, strips, left):
    del strips_in, left_in
    col, first = meta[0], meta[1]
    for i in range(ROWS):
        for s in range(l3.shape[1]):
            place(left, l3, i, position(pattern, i, s, first), s, col, 3)
    shape = (32, 128)
    pick = lax.broadcasted_iota(jnp.int32, shape, 1) == lax.broadcasted_iota(jnp.int32, shape, 0) + col * 32
    pick = pick.astype(left.dtype)
    for edge in EDGES:
        blocks = jnp.concatenate([left[m, m + o] for m, o in edge], axis=0)
        turned = lax.dot_general(pick, blocks, NT, preferred_element_type=jnp.float32)
        for e, (m, o) in enumerate(edge):
            strips[m + o + RADIUS, m + RADIUS] = turned[:, e * 128 : (e + 1) * 128].astype(strips.dtype)
    for i in range(RADIUS):
        low[i] = square_row(kept, strips, left, i, first)


def high_kernel(meta, kept, low, strips, left, far, close):
    first = meta[1]
    for i in range(RADIUS, ROWS):
        row = square_row(kept, strips, left, i, first)
        if i < ROWS - len(CLOSE):
            far[i - ROWS + RADIUS] = row
        else:
            close[i - ROWS + len(CLOSE)] = row
    for i in range(ROWS - RADIUS, RADIUS):
        far[i - ROWS + RADIUS] = low[i]


def strip_of(table, s, row, first):
    total = table.shape[1]
    return wrapped(table[s, wrapped(row, total)] - first + 3 * RADIUS, total)


def cube_targets(cube, i, col, first, share):
    return [strip_of(cube, (col ^ b) * share + q, first + i, first) for b in range(4) for q in range(share)]


def insert_rows(strips, kept, rows, places, first):
    for k, p in enumerate(places):
        for s in range(rows.shape[1]):
            strips[strip_of(kept, s, first - RADIUS + p, first), p] = rows[k, s]


def inner_kernel(meta, kept, cube, low, far, close, left, strips, partial):
    col, first = meta[0], meta[1]
    strips[...] = jnp.zeros_like(strips)
    insert_rows(strips, kept, low, range(RADIUS, 2 * RADIUS), first)
    insert_rows(strips, kept, far, range(ROWS, ROWS + len(FAR)), first)
    insert_rows(strips, kept, close, range(RADIUS + ROWS - len(CLOSE), RADIUS + ROWS), first)
    share = cube.shape[0] // 4

    @pl.loop(0, ROWS)
    def _(i):
        targets = cube_targets(cube, i, col, first, share)
        acc = gather_dot(strips, left, targets, i, range(RADIUS, RADIUS + ROWS))
        for e, t in enumerate(targets):
            mine = strips[t, i + RADIUS].astype(jnp.float32)
            partial[i, e] = 3.0 * mine - 2.0 * acc[e * 32 : (e + 1) * 32]


def outer_kernel(rows, places, arrived):
    def kernel(meta, kept, cube, halo, left, partial, strips_in, o0, o1, o2, o3, strips):
        del strips_in
        col, first = meta[0], meta[1]
        insert_rows(strips, kept, halo, arrived, first)
        share = cube.shape[0] // 4
        for n, i in enumerate(rows):
            targets = cube_targets(cube, i, col, first, share)
            acc = gather_dot(strips, left, targets, i, [p for p in places if i <= p < i + BAND])
            for e in range(len(targets)):
                piece = partial[i, e] - 2.0 * acc[e * 32 : (e + 1) * 32]
                (o0, o1, o2, o3)[e // share][n, e % share] = piece.astype(o0.dtype)

    return kernel


def final_kernel(parts, aliased):
    def kernel(meta, *refs):
        col = meta[0]
        out, whole, turned, sems = refs[-4:]
        copies = []
        for n, rows in enumerate(parts):
            for b, p in enumerate(refs[4 * n : 4 * n + 4]):
                start = pl.multiple_of((col ^ b) * 32, 32)
                whole[pl.ds(rows[0], len(rows)), :, pl.ds(start, 32), :] = p[...]
            for i in rows:
                for q in range(out.shape[1]):
                    turned[i, q] = whole[i, q].T.astype(turned.dtype)
                copies.append(pltpu.make_async_copy(turned.at[i], out.at[i], sems.at[i]))
                copies[-1].start()
        for copy in copies:
            copy.wait()

    return kernel


def shape(*dims, dtype=jnp.bfloat16):
    return jax.ShapeDtypeStruct(dims, dtype)


def call(kernel, specs, outs, args, scratch=(), flops=0, aliases=None, out_specs=None, limit=16):
    size = sum(a.size * a.dtype.itemsize for a in args) + sum(o.size * o.dtype.itemsize for o in outs)
    return pl.pallas_call(
        kernel,
        out_shape=outs,
        in_specs=specs,
        out_specs=out_specs or [VMEM] * len(outs),
        scratch_shapes=scratch,
        input_output_aliases=aliases or {},
        compiler_params=pltpu.CompilerParams(vmem_limit_bytes=limit << 20),
        cost_estimate=pl.CostEstimate(flops=flops, bytes_accessed=size, transcendentals=0),
    )(*args)


def per_device(density, pattern, square_filter, cube_filter):
    layers = lax.axis_size("layer")
    groups = lax.axis_size("row") * layers
    assert density.shape[0] == ROWS and lax.axis_size("col") == 4
    piece = density.shape[2:]
    col = lax.axis_index("col")
    first = (lax.axis_index("row") * layers + lax.axis_index("layer")) * ROWS
    meta = jnp.stack([col, first]).astype(jnp.int32)
    pattern, kept, cube = pattern.T, square_filter.T, cube_filter.T
    width, slots = kept.shape[0], cube.shape[0]
    share = slots // 4

    def shifted(x, d):
        return lax.ppermute(x, ("row", "layer"), [(g, (g + d) % groups) for g in range(groups)])

    def across(x, bits):
        return lax.ppermute(x, "col", [(c, c ^ bits) for c in range(4)])

    l2 = across(density, 2)
    l1 = across(density, 1)
    payload = call(
        reorder_kernel, [SMEM, ANY, ANY], [shape(len(e), *piece) for e in LISTS], (meta, pattern, density),
        [pltpu.VMEM((ROWS, BAND + 1, *piece), density.dtype), pltpu.VMEM(density.shape, density.dtype),
         pltpu.SMEM(pattern.shape, pattern.dtype), pltpu.SemaphoreType.DMA((2,))],
    )
    payload, l1 = lax.optimization_barrier((payload, l1))
    halos = [shifted(p, d) for p, d in zip(payload, SHIFTS)]
    strips, left = call(
        prepare_kernel, [SMEM] * 2 + [VMEM] * 2,
        [shape(STRIPS, NEAR, *piece), shape(ROWS, NEAR, 128, 128)], (meta, pattern, density, l1),
    )
    l2, halos, strips, left = lax.optimization_barrier((l2, halos, strips, left))
    l3 = across(l2, 1)
    both = [shape(*strips.shape), shape(*left.shape)]
    strips, left = call(
        insert_kernel, [SMEM] * 2 + [VMEM] * 7, both, (meta, pattern, l2, *halos, strips, left),
        aliases={7: 0, 8: 1},
    )
    work = 2 * width * BAND * 128 * 128 * 32
    low, strips, left = call(
        low_kernel, [SMEM] * 3 + [VMEM] * 3, [shape(RADIUS, width, *piece), *both],
        (meta, pattern, kept, l3, strips, left), flops=work * RADIUS, aliases={4: 1, 5: 2},
    )
    after = shifted(low, -1)
    far, close = call(
        high_kernel, [SMEM] * 2 + [VMEM] * 3,
        [shape(len(FAR), width, *piece), shape(len(CLOSE), width, *piece)],
        (meta, kept, low, strips, left), flops=work * (ROWS - RADIUS),
    )
    close_in = shifted(close, 1)
    far_in = shifted(far, 1)

    tables = (meta, kept, cube)
    strips, partial = call(
        inner_kernel, [SMEM] * 3 + [VMEM] * 4,
        [shape(REACH, NEAR, *piece), shape(ROWS, slots, *piece, dtype=jnp.float32)],
        (*tables, low, far, close, left), flops=2 * slots * ROWS * ROWS * 128 * 128 * 32,
    )
    parts = []
    for rows, places, arrived, halo in (
        (LATE, AFTER, AFTER, after),
        (MIDDLE, [*CLOSE, *AFTER], CLOSE, close_in),
        (EARLY, [*FAR, *CLOSE], FAR, far_in),
    ):
        *own, strips = call(
            outer_kernel(rows, places, arrived), [SMEM] * 3 + [VMEM] * 4,
            [shape(len(rows), share, *piece)] * 4 + [shape(*strips.shape)],
            (*tables, halo, left, partial, strips), flops=work * len(rows) // 2, aliases={6: 4},
        )
        parts.append([own[0], *(across(own[b], b) for b in (1, 2, 3))])

    result = shape(ROWS, share, 128, 128, dtype=jnp.float32)
    scratch = [
        pltpu.VMEM((ROWS, share, 128, 128), density.dtype),
        pltpu.VMEM((ROWS, share, 128, 128), jnp.float32),
        pltpu.SemaphoreType.DMA((ROWS,)),
    ]
    out = call(
        final_kernel((LATE, MIDDLE), False), [SMEM] + [VMEM] * 8, [result], (meta, *parts[0], *parts[1]),
        scratch, out_specs=[ANY],
    )[0]
    return call(
        final_kernel((EARLY,), True), [SMEM] + [VMEM] * 4 + [ANY], [result], (meta, *parts[2], out),
        scratch, out_specs=[ANY], aliases={5: 0},
    )[0]


def solution(mesh):
    in_specs = (P(("row", "layer"), None, "col", None), P(), P(), P())
    out_specs = P(("row", "layer"), "col", None, None)
    return jax.shard_map(
        per_device, mesh=mesh, in_specs=in_specs, out_specs=out_specs, check_vma=False
    )
```

time: 77.4 us -> 72.7 us (0.939)
  waiting for transfers between devices: 36.4 us -> 26.4 us
  Pallas kernels: 19.8 us -> 23.4 us
  starting transfers between devices: 18.3 us -> 20.7 us
    ppermute x6 -> x12, waiting for transfers between devices: 17.6 us -> 9.28 us  [across(): return lax.ppermute(x, 'col', [(c, c ^ bits) for c in range(4)])]
    ppermute x6 -> x12, starting transfers between devices: 4.88 us -> 8.6 us  [across(): return lax.ppermute(x, 'col', [(c, c ^ bits) for c in range(4)])]
    pallas_call x6 -> x11, Pallas kernels: 19.8 us -> 23.4 us  [call(): pl.pallas_call(kernel, out_shape=outs, in_specs=specs, out_specs=out_spec...]
    ppermute x6 -> x7, waiting for transfers between devices: 18.8 us -> 17.1 us  [shifted(): lax.ppermute(x, ('row', 'layer'), [(g, (g + d) % groups) for g in range(g...]
    ppermute x6 -> x7, starting transfers between devices: 13.4 us -> 12.1 us  [shifted(): lax.ppermute(x, ('row', 'layer'), [(g, (g + d) % groups) for g in range(g...]
    unnamed x10 -> x8, local copies, waits for them, and re-layouts: 2.51 us -> 1.82 us
  transfers between devices with their start and end apart: 12 -> 19, of which waited for: 9 -> 11; matrix products, arithmetic and copies ran while one was open for 0% -> 0% of each run, Pallas kernels for 9% -> 25%
where the time goes in v4:
time: 72.7 us; the launch traced here: 72.5 us
  waiting for transfers between devices  26.4 us (36%)
  Pallas kernels  23.4 us (32%)
  starting transfers between devices  20.7 us (28%)
  local copies, waits for them, and re-layouts  1.82 us (3%)
    pallas_call x11, Pallas kernels, call(): pl.pallas_call(kernel, out_shape=outs, in_specs=specs, out_specs=out_spec...  23.4 us
    ppermute x7, waiting for transfers between devices, shifted(): lax.ppermute(x, ('row', 'layer'), [(g, (g + d) % groups) for g in range(g...  17.1 us
    ppermute x7, starting transfers between devices, shifted(): lax.ppermute(x, ('row', 'layer'), [(g, (g + d) % groups) for g in range(g...  12.1 us
    ppermute x12, waiting for transfers between devices, across(): return lax.ppermute(x, 'col', [(c, c ^ bits) for c in range(4)])  9.28 us
    ppermute x12, starting transfers between devices, across(): return lax.ppermute(x, 'col', [(c, c ^ bits) for c in range(4)])  8.6 us
    unnamed x8, local copies, waits for them, and re-layouts  1.82 us
  transfers between devices with their start and end apart: 19, of which 11 were waited for; matrix products, arithmetic and copies ran while one was open for 0% of the time, Pallas kernels for 25%

profile of v4, /device:TPU:0, one launch (start us, length us, event | category | flops | bytes accessed | tf_op | source)
XLA Modules:
  0.0 72.5 jit_solution(14777139310128429519)
XLA Ops:
  0.0 0.5 collective-permute-start.1
  0.5 2.5 %collective-permute-start = (bf16[8,11,32,128]{3,2,1,0:T(8,128)(2,1)}, bf16[8,11,32,128]{3,2,1,0:T(8,128)(2,1)S(1)}, u32[]{:S(2)}, u32[]{:S(2)}) collective-permute-start(bf16[8,11,32,128]{3,2,1,0:T(8,128)(2,1)} %l0.1), channel_id=1, source_target_pairs={{0,4},{2,6},{4,0},{6,2},{1,5},{3,7},{5,1},{7,3},{8,12},{10,14},{12... | collective-permute-start | bytes 2162696 | tf_op jit(solution)/shard_map/ppermute | solution.py:247
  2.9 0.1 pad_add_fusion.meta
  3.0 0.0 copy-start
  3.0 1.1 %copy-done = bf16[8,11,32,128]{3,2,1,0:T(8,128)(2,1)S(1)} copy-done((bf16[8,11,32,128]{3,2,1,0:T(8,128)(2,1)S(1)}, bf16[8,11,32,128]{3,2,1,0:T(8,128)(2,1)}, u32[]{:S(2)}) %copy-start) | copy-done | bytes 720920
  4.1 0.0 copy-start.3
  4.1 0.7 copy-done.3
  4.8 1.9 %shard_map.46 = (bf16[37,32,128]{2,1,0:T(8,128)(2,1)S(1)}, bf16[37,32,128]{2,1,0:T(8,128)(2,1)S(1)}, bf16[3,32,128]{2,1,0:T(8,128)(2,1)S(1)}, bf16[3,32,128]{2,1,0:T(8,128)(2,1)S(1)}) custom-call(s32[2]{0:T(128)S(1)} %pad_add_fusion.meta, s32[11,64]{1,0:T(8,128)S(1)} %bitcast.15, bf16[8,11,32,128]{3,2,1,0:T(8,128)(2,1)S(1)} %copy-done), custom_call_target="tpu_custom_call" | custom-call | bytes 1379080 | tf_op jit(solution)/shard_map/pallas_call | solution.py:219
  6.7 0.0 collective-permute-done.1.l1
  6.7 1.6 %collective-permute-start.2 = (bf16[37,32,128]{2,1,0:T(8,128)(2,1)S(1)}, bf16[37,32,128]{2,1,0:T(8,128)(2,1)S(1)}, u32[]{:S(2)}, u32[]{:S(2)}) collective-permute-start(bf16[37,32,128]{2,1,0:T(8,128)(2,1)S(1)} %get-tuple-element.50), channel_id=1, source_target_pairs={{0,1},{1,8},{8,9},{9,16},{16,17},{17,24},{24,25},{25,0},{2,3},{3,1... | collective-permute-start | bytes 909320 | tf_op jit(solution)/shard_map/ppermute | solution.py:244
  8.3 3.2 %collective-permute-start.3 = (bf16[37,32,128]{2,1,0:T(8,128)(2,1)S(1)}, bf16[37,32,128]{2,1,0:T(8,128)(2,1)S(1)}, u32[]{:S(2)}, u32[]{:S(2)}) collective-permute-start(bf16[37,32,128]{2,1,0:T(8,128)(2,1)S(1)} %get-tuple-element.51), channel_id=1, source_target_pairs={{0,25},{1,0},{8,1},{9,8},{16,9},{17,16},{24,17},{25,24},{2,27},{3,... | collective-permute-start | bytes 909320 | tf_op jit(solution)/shard_map/ppermute | solution.py:244
  11.5 0.0 collective-permute-start.4
  11.5 3.8 %collective-permute-start.5 = (bf16[3,32,128]{2,1,0:T(8,128)(2,1)S(1)}, bf16[3,32,128]{2,1,0:T(8,128)(2,1)S(1)}, u32[]{:S(2)}, u32[]{:S(2)}) collective-permute-start(bf16[3,32,128]{2,1,0:T(8,128)(2,1)S(1)} %get-tuple-element.53), channel_id=1, source_target_pairs={{0,24},{1,25},{8,0},{9,1},{16,8},{17,9},{24,16},{25,17},{2,26},{3,... | collective-permute-start | bytes 73736 | tf_op jit(solution)/shard_map/ppermute | solution.py:244
  15.3 2.2 %shard_map.47 = (bf16[28,18,32,128]{3,2,1,0:T(8,128)(2,1)S(1)}, bf16[8,18,128,128]{3,2,1,0:T(8,128)(2,1)S(1)}) custom-call(s32[2]{0:T(128)S(1)} %pad_add_fusion.meta, s32[11,64]{1,0:T(8,128)S(1)} %bitcast.16, bf16[8,11,32,128]{3,2,1,0:T(8,128)(2,1)S(1)} %copy-done, bf16[8,11,32,128]{3,2,1,0:T(8,128)(2,1)S(1)} %collective-permute-done.1.l1), custom_call_target="tpu_custom_call" | custom-call | bytes 10291976 | tf_op jit(solution)/shard_map/pallas_call | solution.py:219
  17.5 2.5 %collective-permute-done.l2 = bf16[8,11,32,128]{3,2,1,0:T(8,128)(2,1)S(1)} collective-permute-done((bf16[8,11,32,128]{3,2,1,0:T(8,128)(2,1)}, bf16[8,11,32,128]{3,2,1,0:T(8,128)(2,1)S(1)}, u32[]{:S(2)}, u32[]{:S(2)}) %collective-permute-start) | collective-permute-done | bytes 720928 | tf_op jit(solution)/shard_map/ppermute | solution.py:247
  20.0 1.2 %collective-permute-done.4.h2 = bf16[3,32,128]{2,1,0:T(8,128)(2,1)S(1)} collective-permute-done((bf16[3,32,128]{2,1,0:T(8,128)(2,1)S(1)}, bf16[3,32,128]{2,1,0:T(8,128)(2,1)S(1)}, u32[]{:S(2)}, u32[]{:S(2)}) %collective-permute-start.4) | collective-permute-done | bytes 24608 | tf_op jit(solution)/shard_map/ppermute | solution.py:244
  21.2 0.0 collective-permute-done.5.h3
  21.2 0.5 collective-permute-done.2.h0
  21.6 2.2 %collective-permute-done.3.h1 = bf16[37,32,128]{2,1,0:T(8,128)(2,1)S(1)} collective-permute-done((bf16[37,32,128]{2,1,0:T(8,128)(2,1)S(1)}, bf16[37,32,128]{2,1,0:T(8,128)(2,1)S(1)}, u32[]{:S(2)}, u32[]{:S(2)}) %collective-permute-start.3) | collective-permute-done | bytes 303136 | tf_op jit(solution)/shard_map/ppermute | solution.py:244
  23.8 0.0 copy-start.1
  23.8 0.0 collective-permute-start.6
  23.8 1.2 %shard_map.48 = (bf16[28,18,32,128]{3,2,1,0:T(8,128)(2,1)S(1)}, bf16[8,18,128,128]{3,2,1,0:T(8,128)(2,1)S(1)}) custom-call(s32[2]{0:T(128)S(1)} %pad_add_fusion.meta, s32[11,64]{1,0:T(8,128)S(1)} %bitcast.17, bf16[8,11,32,128]{3,2,1,0:T(8,128)(2,1)S(1)} %collective-permute-done.l2, ...), custom_call_target="tpu_custom_call", output_to_operand_aliasing={{0}: (7, {}), {1}: (8, {})} | custom-call | bytes 19073800 | tf_op jit(solution)/shard_map/pallas_call | solution.py:219
  25.1 1.0 %collective-permute-done.6.l3 = bf16[8,11,32,128]{3,2,1,0:T(8,128)(2,1)S(1)} collective-permute-done((bf16[8,11,32,128]{3,2,1,0:T(8,128)(2,1)S(1)}, bf16[8,11,32,128]{3,2,1,0:T(8,128)(2,1)S(1)}, u32[]{:S(2)}, u32[]{:S(2)}) %collective-permute-start.6) | collective-permute-done | bytes 720928 | tf_op jit(solution)/shard_map/ppermute | solution.py:247
  26.0 0.0 copy-done.1
  26.0 3.3 %shard_map.49 = (bf16[5,12,32,128]{3,2,1,0:T(8,128)(2,1)S(1)}, bf16[28,18,32,128]{3,2,1,0:T(8,128)(2,1)S(1)}, bf16[8,18,128,128]{3,2,1,0:T(8,128)(2,1)S(1)}) custom-call(s32[2]{0:T(128)S(1)} %pad_add_fusion.meta, s32[11,64]{1,0:T(8,128)S(1)} %bitcast.18, s32[12,64]{1,0:T(8,128)S(1)} %bitcast.5, ...), custom_call_target="tpu_custom_call", output_to_operand_aliasing={{1}: (4, {}), {2}: (5, {})} | custom-call | flops 692060160 | bytes 18913032 | tf_op jit(solution)/shard_map/pallas_call | solution.py:219
  29.4 0.0 copy-start.2
  29.4 3.4 %collective-permute-start.9 = (bf16[5,12,32,128]{3,2,1,0:T(8,128)(2,1)S(1)}, bf16[5,12,32,128]{3,2,1,0:T(8,128)(2,1)S(1)}, u32[]{:S(2)}, u32[]{:S(2)}) collective-permute-start(bf16[5,12,32,128]{3,2,1,0:T(8,128)(2,1)S(1)} %get-tuple-element.66.low), channel_id=1, source_target_pairs={{0,25},{1,0},{8,1},{9,8},{16,9},{17,16},{24,17},{25,24},{2,27},{3,... | collective-permute-start | bytes 1474568 | tf_op jit(solution)/shard_map/ppermute | solution.py:244
  32.8 1.7 %shard_map.50 = (bf16[3,12,32,128]{3,2,1,0:T(8,128)(2,1)S(1)}, bf16[2,12,32,128]{3,2,1,0:T(8,128)(2,1)S(1)}) custom-call(s32[2]{0:T(128)S(1)} %pad_add_fusion.meta, s32[12,64]{1,0:T(8,128)S(1)} %bitcast.6, bf16[5,12,32,128]{3,2,1,0:T(8,128)(2,1)S(1)} %get-tuple-element.66.low, bf16[28,18,32,128]{3,2,1,0:T(8,128)(2,1)S(1)} %get-tuple-element.67.strips, ...), custom_call_target="tpu_custom_call" | custom-call | flops 415236096 | bytes 9833480 | tf_op jit(solution)/shard_map/pallas_call | solution.py:219
  34.4 0.1 collective-permute-start.7
  34.5 0.1 collective-permute-start.8
  34.6 0.0 copy-done.2
  34.6 5.4 %shard_map.51 = (bf16[38,18,32,128]{3,2,1,0:T(8,128)(2,1)S(1)}, f32[8,16,32,128]{3,2,1,0:T(8,128)S(1)}) custom-call(s32[2]{0:T(128)S(1)} %pad_add_fusion.meta, s32[12,64]{1,0:T(8,128)S(1)} %bitcast.7, s32[16,64]{1,0:T(8,128)S(1)} %bitcast.11, bf16[5,12,32,128]{3,2,1,0:T(8,128)(2,1)S(1)} %get-tuple-element.66.low, ...), custom_call_target="tpu_custom_call" | custom-call | flops 1073741824 | bytes 13409288 | tf_op jit(solution)/shard_map/pallas_call | solution.py:219
  40.0 13.2 %collective-permute-done.9.halo = bf16[5,12,32,128]{3,2,1,0:T(8,128)(2,1)S(1)} collective-permute-done((bf16[5,12,32,128]{3,2,1,0:T(8,128)(2,1)S(1)}, bf16[5,12,32,128]{3,2,1,0:T(8,128)(2,1)S(1)}, u32[]{:S(2)}, u32[]{:S(2)}) %collective-permute-start.9) | collective-permute-done | bytes 491552 | tf_op jit(solution)/shard_map/ppermute | solution.py:244
  53.2 1.6 %shard_map.52 = (bf16[3,4,32,128]{3,2,1,0:T(8,128)(2,1)S(1)}, bf16[3,4,32,128]{3,2,1,0:T(8,128)(2,1)S(1)}, bf16[3,4,32,128]{3,2,1,0:T(8,128)(2,1)S(1)}, bf16[3,4...) custom-call(s32[2]{0:T(128)S(1)} %pad_add_fusion.meta, ...), custom_call_target="tpu_custom_call", output_to_operand_aliasing={{4}: (6, {})} | custom-call | flops 207618048 | bytes 18914312 | tf_op jit(solution)/shard_map/pallas_call | solution.py:219
  54.8 0.1 collective-permute-start.13
  54.9 0.0 collective-permute-done.8.halo
  54.9 1.3 %shard_map.53 = (bf16[2,4,32,128]{3,2,1,0:T(8,128)(2,1)S(1)}, bf16[2,4,32,128]{3,2,1,0:T(8,128)(2,1)S(1)}, bf16[2,4,32,128]{3,2,1,0:T(8,128)(2,1)S(1)}, bf16[2,4...) custom-call(s32[2]{0:T(128)S(1)} %pad_add_fusion.meta, ...), custom_call_target="tpu_custom_call", output_to_operand_aliasing={{4}: (6, {})} | custom-call | flops 138412032 | bytes 18488328 | tf_op jit(solution)/shard_map/pallas_call | solution.py:219
  56.2 0.5 collective-permute-start.16
  56.7 0.5 collective-permute-start.17
  57.2 0.9 %collective-permute-start.18 = (bf16[2,4,32,128]{3,2,1,0:T(8,128)(2,1)S(1)}, bf16[2,4,32,128]{3,2,1,0:T(8,128)(2,1)S(1)}, u32[]{:S(2)}, u32[]{:S(2)}) collective-permute-start(bf16[2,4,32,128]{3,2,1,0:T(8,128)(2,1)S(1)} %get-tuple-element.86), channel_id=1, source_target_pairs={{0,6},{2,4},{4,2},{6,0},{1,7},{3,5},{5,3},{7,1},{8,14},{10,12},{12... | collective-permute-start | bytes 196616 | tf_op jit(solution)/shard_map/ppermute | solution.py:247
  58.1 0.0 collective-permute-done.7.halo
  58.1 1.5 %shard_map.54 = (bf16[3,4,32,128]{3,2,1,0:T(8,128)(2,1)S(1)}, bf16[3,4,32,128]{3,2,1,0:T(8,128)(2,1)S(1)}, bf16[3,4,32,128]{3,2,1,0:T(8,128)(2,1)S(1)}, bf16[3,4...) custom-call(s32[2]{0:T(128)S(1)} %pad_add_fusion.meta, ...), custom_call_target="tpu_custom_call", output_to_operand_aliasing={{4}: (6, {})} | custom-call | flops 207618048 | bytes 18717704 | tf_op jit(solution)/shard_map/pallas_call | solution.py:219
  59.7 0.8 %collective-permute-start.10 = (bf16[3,4,32,128]{3,2,1,0:T(8,128)(2,1)S(1)}, bf16[3,4,32,128]{3,2,1,0:T(8,128)(2,1)S(1)}, u32[]{:S(2)}, u32[]{:S(2)}) collective-permute-start(bf16[3,4,32,128]{3,2,1,0:T(8,128)(2,1)S(1)} %get-tuple-element.76), channel_id=1, source_target_pairs={{0,2},{2,0},{4,6},{6,4},{1,3},{3,1},{5,7},{7,5},{8,10},{10,8},{12,... | collective-permute-start | bytes 294920 | tf_op jit(solution)/shard_map/ppermute | solution.py:247
  60.4 0.0 collective-permute-done.16.refs_5_
  60.4 0.5 collective-permute-start.14
  61.0 0.7 collective-permute-done.17.refs_6_
  61.6 0.2 collective-permute-start.15
  61.9 0.0 collective-permute-done.18.refs_7_
  61.9 1.2 %collective-permute-start.11 = (bf16[3,4,32,128]{3,2,1,0:T(8,128)(2,1)S(1)}, bf16[3,4,32,128]{3,2,1,0:T(8,128)(2,1)S(1)}, u32[]{:S(2)}, u32[]{:S(2)}) collective-permute-start(bf16[3,4,32,128]{3,2,1,0:T(8,128)(2,1)S(1)} %get-tuple-element.77), channel_id=1, source_target_pairs={{0,4},{2,6},{4,0},{6,2},{1,5},{3,7},{5,1},{7,3},{8,12},{10,14},{12... | collective-permute-start | bytes 294920 | tf_op jit(solution)/shard_map/ppermute | solution.py:247
  63.1 0.0 collective-permute-done.13.refs_1_
  63.1 0.8 %collective-permute-start.12 = (bf16[3,4,32,128]{3,2,1,0:T(8,128)(2,1)S(1)}, bf16[3,4,32,128]{3,2,1,0:T(8,128)(2,1)S(1)}, u32[]{:S(2)}, u32[]{:S(2)}) collective-permute-start(bf16[3,4,32,128]{3,2,1,0:T(8,128)(2,1)S(1)} %get-tuple-element.78), channel_id=1, source_target_pairs={{0,6},{2,4},{4,2},{6,0},{1,7},{3,5},{5,3},{7,1},{8,14},{10,12},{12... | collective-permute-start | bytes 294920 | tf_op jit(solution)/shard_map/ppermute | solution.py:247
  64.0 1.9 %collective-permute-done.14.refs_2_ = bf16[3,4,32,128]{3,2,1,0:T(8,128)(2,1)S(1)} collective-permute-done((bf16[3,4,32,128]{3,2,1,0:T(8,128)(2,1)S(1)}, bf16[3,4,32,128]{3,2,1,0:T(8,128)(2,1)S(1)}, u32[]{:S(2)}, u32[]{:S(2)}) %collective-permute-start.14) | collective-permute-done | bytes 98336 | tf_op jit(solution)/shard_map/ppermute | solution.py:247
  65.9 0.8 %collective-permute-done.15.refs_3_ = bf16[3,4,32,128]{3,2,1,0:T(8,128)(2,1)S(1)} collective-permute-done((bf16[3,4,32,128]{3,2,1,0:T(8,128)(2,1)S(1)}, bf16[3,4,32,128]{3,2,1,0:T(8,128)(2,1)S(1)}, u32[]{:S(2)}, u32[]{:S(2)}) %collective-permute-start.15) | collective-permute-done | bytes 98336 | tf_op jit(solution)/shard_map/ppermute | solution.py:247
  66.7 1.8 %shard_map.55.refs_4_ = f32[8,4,128,128]{3,2,1,0:T(8,128)} custom-call(s32[2]{0:T(128)S(1)} %pad_add_fusion.meta, bf16[3,4,32,128]{3,2,1,0:T(8,128)(2,1)S(1)} %get-tuple-element.79.refs_0_, bf16[3,4,32,128]{3,2,1,0:T(8,128)(2,1)S(1)} %collective-permute-done.13.refs_1_, bf16[3,4,32,128]{3,2,1,0:T(8,128)(2,1)S(1)} %collective-permute-done.14.refs_2_, ...), custom_call_target="tpu_custom_call" | custom-call | bytes 2752520 | tf_op jit(solution)/shard_map/pallas_call | solution.py:219
  68.5 0.0 collective-permute-done.10.refs_1_
  68.5 1.6 %collective-permute-done.11.refs_2_ = bf16[3,4,32,128]{3,2,1,0:T(8,128)(2,1)S(1)} collective-permute-done((bf16[3,4,32,128]{3,2,1,0:T(8,128)(2,1)S(1)}, bf16[3,4,32,128]{3,2,1,0:T(8,128)(2,1)S(1)}, u32[]{:S(2)}, u32[]{:S(2)}) %collective-permute-start.11) | collective-permute-done | bytes 98336 | tf_op jit(solution)/shard_map/ppermute | solution.py:247
  70.1 0.8 %collective-permute-done.12.refs_3_ = bf16[3,4,32,128]{3,2,1,0:T(8,128)(2,1)S(1)} collective-permute-done((bf16[3,4,32,128]{3,2,1,0:T(8,128)(2,1)S(1)}, bf16[3,4,32,128]{3,2,1,0:T(8,128)(2,1)S(1)}, u32[]{:S(2)}, u32[]{:S(2)}) %collective-permute-start.12) | collective-permute-done | bytes 98336 | tf_op jit(solution)/shard_map/ppermute | solution.py:247
  70.9 1.6 %shard_map.56 = f32[8,4,128,128]{3,2,1,0:T(8,128)} custom-call(s32[2]{0:T(128)S(1)} %pad_add_fusion.meta, bf16[3,4,32,128]{3,2,1,0:T(8,128)(2,1)S(1)} %get-tuple-element.75.refs_0_, bf16[3,4,32,128]{3,2,1,0:T(8,128)(2,1)S(1)} %collective-permute-done.10.refs_1_, ...), custom_call_target="tpu_custom_call", output_to_operand_aliasing={{}: (5, {})} | custom-call | bytes 4587528 | tf_op jit(solution)/shard_map/pallas_call | solution.py:219
Async XLA Ops:
  0.0 6.7 %collective-permute-start.1 = (bf16[8,11,32,128]{3,2,1,0:T(8,128)(2,1)}, bf16[8,11,32,128]{3,2,1,0:T(8,128)(2,1)S(1)}, u32[]{:S(2)}, u32[]{:S(2)}) collective-permute-start(bf16[8,11,32,128]{3,2,1,0:T(8,128)(2,1)} %l0.1), channel_id=1, source_target_pairs={{0,2},{2,0},{4,6},{6,4},{1,3},{3,1},{5,7},{7,5},{8,10},{10,8},{12,... | collective-permute-start | bytes 2162696 | tf_op jit(solution)/shard_map/ppermute | solution.py:247
  0.5 19.5 %collective-permute-start = (bf16[8,11,32,128]{3,2,1,0:T(8,128)(2,1)}, bf16[8,11,32,128]{3,2,1,0:T(8,128)(2,1)S(1)}, u32[]{:S(2)}, u32[]{:S(2)}) collective-permute-start(bf16[8,11,32,128]{3,2,1,0:T(8,128)(2,1)} %l0.1), channel_id=1, source_target_pairs={{0,4},{2,6},{4,0},{6,2},{1,5},{3,7},{5,1},{7,3},{8,12},{10,14},{12... | collective-permute-start | bytes 2162696 | tf_op jit(solution)/shard_map/ppermute | solution.py:247
  3.0 1.1 %copy-start = (bf16[8,11,32,128]{3,2,1,0:T(8,128)(2,1)S(1)}, bf16[8,11,32,128]{3,2,1,0:T(8,128)(2,1)}, u32[]{:S(2)}) copy-start(bf16[8,11,32,128]{3,2,1,0:T(8,128)(2,1)} %l0.1) | copy-start | bytes 2162692
  4.1 0.7 copy-start.3
  6.7 14.9 %collective-permute-start.2 = (bf16[37,32,128]{2,1,0:T(8,128)(2,1)S(1)}, bf16[37,32,128]{2,1,0:T(8,128)(2,1)S(1)}, u32[]{:S(2)}, u32[]{:S(2)}) collective-permute-start(bf16[37,32,128]{2,1,0:T(8,128)(2,1)S(1)} %get-tuple-element.50), channel_id=1, source_target_pairs={{0,1},{1,8},{8,9},{9,16},{16,17},{17,24},{24,25},{25,0},{2,3},{3,1... | collective-permute-start | bytes 909320 | tf_op jit(solution)/shard_map/ppermute | solution.py:244
  8.3 15.5 %collective-permute-start.3 = (bf16[37,32,128]{2,1,0:T(8,128)(2,1)S(1)}, bf16[37,32,128]{2,1,0:T(8,128)(2,1)S(1)}, u32[]{:S(2)}, u32[]{:S(2)}) collective-permute-start(bf16[37,32,128]{2,1,0:T(8,128)(2,1)S(1)} %get-tuple-element.51), channel_id=1, source_target_pairs={{0,25},{1,0},{8,1},{9,8},{16,9},{17,16},{24,17},{25,24},{2,27},{3,... | collective-permute-start | bytes 909320 | tf_op jit(solution)/shard_map/ppermute | solution.py:244
  11.5 9.6 %collective-permute-start.4 = (bf16[3,32,128]{2,1,0:T(8,128)(2,1)S(1)}, bf16[3,32,128]{2,1,0:T(8,128)(2,1)S(1)}, u32[]{:S(2)}, u32[]{:S(2)}) collective-permute-start(bf16[3,32,128]{2,1,0:T(8,128)(2,1)S(1)} %get-tuple-element.52), channel_id=1, source_target_pairs={{0,8},{1,9},{8,16},{9,17},{16,24},{17,25},{24,0},{25,1},{2,10},{3,... | collective-permute-start | bytes 73736 | tf_op jit(solution)/shard_map/ppermute | solution.py:244
  11.5 9.6 %collective-permute-start.5 = (bf16[3,32,128]{2,1,0:T(8,128)(2,1)S(1)}, bf16[3,32,128]{2,1,0:T(8,128)(2,1)S(1)}, u32[]{:S(2)}, u32[]{:S(2)}) collective-permute-start(bf16[3,32,128]{2,1,0:T(8,128)(2,1)S(1)} %get-tuple-element.53), channel_id=1, source_target_pairs={{0,24},{1,25},{8,0},{9,1},{16,8},{17,9},{24,16},{25,17},{2,26},{3,... | collective-permute-start | bytes 73736 | tf_op jit(solution)/shard_map/ppermute | solution.py:244
  23.8 2.2 %copy-start.1 = (s32[64,12]{0,1:T(8,128)S(1)}, s32[64,12]{0,1:T(8,128)}, u32[]{:S(2)}) copy-start(s32[64,12]{0,1:T(8,128)} %param.6) | copy-start | bytes 9220
  23.8 2.2 %collective-permute-start.6 = (bf16[8,11,32,128]{3,2,1,0:T(8,128)(2,1)S(1)}, bf16[8,11,32,128]{3,2,1,0:T(8,128)(2,1)S(1)}, u32[]{:S(2)}, u32[]{:S(2)}) collective-permute-start(bf16[8,11,32,128]{3,2,1,0:T(8,128)(2,1)S(1)} %collective-permute-done.l2), channel_id=1, source_target_pairs={{0,2},{2,0},{4,6},{6,4},{1,3},{3,1},{5,7},{7,5},{8,10},{10,8},{12,... | collective-permute-start | bytes 2162696 | tf_op jit(solution)/shard_map/ppermute | solution.py:247
  29.4 5.2 %copy-start.2 = (s32[64,16]{0,1:T(8,128)S(1)}, s32[64,16]{0,1:T(8,128)}, u32[]{:S(2)}) copy-start(s32[64,16]{0,1:T(8,128)} %param.7) | copy-start | bytes 12292
  29.4 23.8 %collective-permute-start.9 = (bf16[5,12,32,128]{3,2,1,0:T(8,128)(2,1)S(1)}, bf16[5,12,32,128]{3,2,1,0:T(8,128)(2,1)S(1)}, u32[]{:S(2)}, u32[]{:S(2)}) collective-permute-start(bf16[5,12,32,128]{3,2,1,0:T(8,128)(2,1)S(1)} %get-tuple-element.66.low), channel_id=1, source_target_pairs={{0,25},{1,0},{8,1},{9,8},{16,9},{17,16},{24,17},{25,24},{2,27},{3,... | collective-permute-start | bytes 1474568 | tf_op jit(solution)/shard_map/ppermute | solution.py:244
  34.4 23.7 %collective-permute-start.7 = (bf16[3,12,32,128]{3,2,1,0:T(8,128)(2,1)S(1)}, bf16[3,12,32,128]{3,2,1,0:T(8,128)(2,1)S(1)}, u32[]{:S(2)}, u32[]{:S(2)}) collective-permute-start(bf16[3,12,32,128]{3,2,1,0:T(8,128)(2,1)S(1)} %get-tuple-element.69.far), channel_id=1, source_target_pairs={{0,1},{1,8},{8,9},{9,16},{16,17},{17,24},{24,25},{25,0},{2,3},{3,1... | collective-permute-start | bytes 884744 | tf_op jit(solution)/shard_map/ppermute | solution.py:244
  34.5 20.4 %collective-permute-start.8 = (bf16[2,12,32,128]{3,2,1,0:T(8,128)(2,1)S(1)}, bf16[2,12,32,128]{3,2,1,0:T(8,128)(2,1)S(1)}, u32[]{:S(2)}, u32[]{:S(2)}) collective-permute-start(bf16[2,12,32,128]{3,2,1,0:T(8,128)(2,1)S(1)} %get-tuple-element.70.close), channel_id=1, source_target_pairs={{0,1},{1,8},{8,9},{9,16},{16,17},{17,24},{24,25},{25,0},{2,3},{3,1... | collective-permute-start | bytes 589832 | tf_op jit(solution)/shard_map/ppermute | solution.py:244
  54.8 8.3 %collective-permute-start.13 = (bf16[3,4,32,128]{3,2,1,0:T(8,128)(2,1)S(1)}, bf16[3,4,32,128]{3,2,1,0:T(8,128)(2,1)S(1)}, u32[]{:S(2)}, u32[]{:S(2)}) collective-permute-start(bf16[3,4,32,128]{3,2,1,0:T(8,128)(2,1)S(1)} %get-tuple-element.80), channel_id=1, source_target_pairs={{0,2},{2,0},{4,6},{6,4},{1,3},{3,1},{5,7},{7,5},{8,10},{10,8},{12,... | collective-permute-start | bytes 294920 | tf_op jit(solution)/shard_map/ppermute | solution.py:247
  56.2 4.3 %collective-permute-start.16 = (bf16[2,4,32,128]{3,2,1,0:T(8,128)(2,1)S(1)}, bf16[2,4,32,128]{3,2,1,0:T(8,128)(2,1)S(1)}, u32[]{:S(2)}, u32[]{:S(2)}) collective-permute-start(bf16[2,4,32,128]{3,2,1,0:T(8,128)(2,1)S(1)} %get-tuple-element.84), channel_id=1, source_target_pairs={{0,2},{2,0},{4,6},{6,4},{1,3},{3,1},{5,7},{7,5},{8,10},{10,8},{12,... | collective-permute-start | bytes 196616 | tf_op jit(solution)/shard_map/ppermute | solution.py:247
  56.7 4.9 %collective-permute-start.17 = (bf16[2,4,32,128]{3,2,1,0:T(8,128)(2,1)S(1)}, bf16[2,4,32,128]{3,2,1,0:T(8,128)(2,1)S(1)}, u32[]{:S(2)}, u32[]{:S(2)}) collective-permute-start(bf16[2,4,32,128]{3,2,1,0:T(8,128)(2,1)S(1)} %get-tuple-element.85), channel_id=1, source_target_pairs={{0,4},{2,6},{4,0},{6,2},{1,5},{3,7},{5,1},{7,3},{8,12},{10,14},{12... | collective-permute-start | bytes 196616 | tf_op jit(solution)/shard_map/ppermute | solution.py:247
  57.2 4.6 %collective-permute-start.18 = (bf16[2,4,32,128]{3,2,1,0:T(8,128)(2,1)S(1)}, bf16[2,4,32,128]{3,2,1,0:T(8,128)(2,1)S(1)}, u32[]{:S(2)}, u32[]{:S(2)}) collective-permute-start(bf16[2,4,32,128]{3,2,1,0:T(8,128)(2,1)S(1)} %get-tuple-element.86), channel_id=1, source_target_pairs={{0,6},{2,4},{4,2},{6,0},{1,7},{3,5},{5,3},{7,1},{8,14},{10,12},{12... | collective-permute-start | bytes 196616 | tf_op jit(solution)/shard_map/ppermute | solution.py:247
  59.7 8.8 %collective-permute-start.10 = (bf16[3,4,32,128]{3,2,1,0:T(8,128)(2,1)S(1)}, bf16[3,4,32,128]{3,2,1,0:T(8,128)(2,1)S(1)}, u32[]{:S(2)}, u32[]{:S(2)}) collective-permute-start(bf16[3,4,32,128]{3,2,1,0:T(8,128)(2,1)S(1)} %get-tuple-element.76), channel_id=1, source_target_pairs={{0,2},{2,0},{4,6},{6,4},{1,3},{3,1},{5,7},{7,5},{8,10},{10,8},{12,... | collective-permute-start | bytes 294920 | tf_op jit(solution)/shard_map/ppermute | solution.py:247
  60.4 5.4 %collective-permute-start.14 = (bf16[3,4,32,128]{3,2,1,0:T(8,128)(2,1)S(1)}, bf16[3,4,32,128]{3,2,1,0:T(8,128)(2,1)S(1)}, u32[]{:S(2)}, u32[]{:S(2)}) collective-permute-start(bf16[3,4,32,128]{3,2,1,0:T(8,128)(2,1)S(1)} %get-tuple-element.81), channel_id=1, source_target_pairs={{0,4},{2,6},{4,0},{6,2},{1,5},{3,7},{5,1},{7,3},{8,12},{10,14},{12... | collective-permute-start | bytes 294920 | tf_op jit(solution)/shard_map/ppermute | solution.py:247
  61.6 5.0 %collective-permute-start.15 = (bf16[3,4,32,128]{3,2,1,0:T(8,128)(2,1)S(1)}, bf16[3,4,32,128]{3,2,1,0:T(8,128)(2,1)S(1)}, u32[]{:S(2)}, u32[]{:S(2)}) collective-permute-start(bf16[3,4,32,128]{3,2,1,0:T(8,128)(2,1)S(1)} %get-tuple-element.82), channel_id=1, source_target_pairs={{0,6},{2,4},{4,2},{6,0},{1,7},{3,5},{5,3},{7,1},{8,14},{10,12},{12... | collective-permute-start | bytes 294920 | tf_op jit(solution)/shard_map/ppermute | solution.py:247
  61.9 8.2 %collective-permute-start.11 = (bf16[3,4,32,128]{3,2,1,0:T(8,128)(2,1)S(1)}, bf16[3,4,32,128]{3,2,1,0:T(8,128)(2,1)S(1)}, u32[]{:S(2)}, u32[]{:S(2)}) collective-permute-start(bf16[3,4,32,128]{3,2,1,0:T(8,128)(2,1)S(1)} %get-tuple-element.77), channel_id=1, source_target_pairs={{0,4},{2,6},{4,0},{6,2},{1,5},{3,7},{5,1},{7,3},{8,12},{10,14},{12... | collective-permute-start | bytes 294920 | tf_op jit(solution)/shard_map/ppermute | solution.py:247
  63.1 7.8 %collective-permute-start.12 = (bf16[3,4,32,128]{3,2,1,0:T(8,128)(2,1)S(1)}, bf16[3,4,32,128]{3,2,1,0:T(8,128)(2,1)S(1)}, u32[]{:S(2)}, u32[]{:S(2)}) collective-permute-start(bf16[3,4,32,128]{3,2,1,0:T(8,128)(2,1)S(1)} %get-tuple-element.78), channel_id=1, source_target_pairs={{0,6},{2,4},{4,2},{6,0},{1,7},{3,5},{5,3},{7,1},{8,14},{10,12},{12... | collective-permute-start | bytes 294920 | tf_op jit(solution)/shard_map/ppermute | solution.py:247

commit v5 on v4

--- a/solution.py
+++ b/solution.py
@@ -15,6 +15,7 @@
 VMEM = pl.BlockSpec(memory_space=pltpu.VMEM)
 SMEM = pl.BlockSpec(memory_space=pltpu.SMEM)
 ANY = pl.BlockSpec(memory_space=pl.ANY)
+HBM = pl.BlockSpec(memory_space=pltpu.HBM)
 
 SHIFTS = (1, -1, 2, -2)
 OWN = [(j, o) for j in range(ROWS) for o in range(BAND)]
@@ -28,12 +29,12 @@
     [(m, o) for m, o in OWN if m + o < RADIUS],
     [(m, o) for m, o in OWN if m + o >= RADIUS + ROWS],
 )
-LATE = range(RADIUS, ROWS)
-MIDDLE = range(ROWS - RADIUS, RADIUS)
+LATE = range(ROWS - RADIUS, ROWS)
 EARLY = range(0, ROWS - RADIUS)
 AFTER = range(RADIUS + ROWS, NEAR)
 CLOSE = range(ROWS - RADIUS, RADIUS)
 FAR = range(0, ROWS - RADIUS)
+RELAY = 3
 
 
 def wrapped(value, total):
@@ -70,8 +71,8 @@
             out[e] = band[j, o]
 
 
-def place(left, piece, i, p, s, col, b):
-    left[i, p, pl.ds(pl.multiple_of((col ^ b) * 32, 32), 32), :] = piece[i, s]
+def place(left, piece, n, p, s, col, b, i=None):
+    left[n if i is None else i, p, pl.ds(pl.multiple_of((col ^ b) * 32, 32), 32), :] = piece[n, s]
 
 
 def prepare_kernel(meta, pattern, l0, l1, strips, left):
@@ -86,38 +87,23 @@
             strips[i + 2 * RADIUS, p] = l0[i, s]
 
 
-def insert_kernel(meta, pattern, l2, h0, h1, h2, h3, strips_in, left_in, strips, left):
-    del strips_in, left_in
+def relay_kernel(meta, pattern, l2, left_in, left, *pieces):
+    del left_in
     col, first = meta[0], meta[1]
-    for halo, entries, shift in zip((h0, h1, h2, h3), LISTS, SHIFTS):
-        for e, (j, o) in enumerate(entries):
-            row = j - shift * ROWS
-            strips[row + 2 * RADIUS, row + o] = halo[e]
     for i in range(ROWS):
+        piece, n = pieces[i // RELAY], i % RELAY
         for s in range(l2.shape[1]):
             place(left, l2, i, position(pattern, i, s, first), s, col, 2)
-
-
-def gather_dot(strips, left, targets, i, places):
-    w = jnp.concatenate([left[i, p] for p in places], axis=1)
-    rows = [jnp.concatenate([strips[t, p] for p in places], axis=1) for t in targets]
-    x = jnp.concatenate(rows, axis=0)
-    return lax.dot_general(x, w, NT, preferred_element_type=jnp.float32)
-
-
-def square_row(kept, strips, left, i, first):
-    total = kept.shape[1]
-    targets = [wrapped(kept[s, first + i] - first + 2 * RADIUS, total) for s in range(kept.shape[0])]
-    acc = gather_dot(strips, left, targets, i, range(i, i + BAND))
-    return acc.reshape(len(targets), 32, 128).astype(strips.dtype)
-
-
-def low_kernel(meta, pattern, kept, l3, strips_in, left_in, low, strips, left):
-    del strips_in, left_in
+        piece[n] = l2[i]
+
+
+def complete_kernel(meta, pattern, *refs):
+    pieces, (strips, left) = refs[:-4], refs[-2:]
     col, first = meta[0], meta[1]
     for i in range(ROWS):
-        for s in range(l3.shape[1]):
-            place(left, l3, i, position(pattern, i, s, first), s, col, 3)
+        piece, n = pieces[i // RELAY], i % RELAY
+        for s in range(piece.shape[1]):
+            place(left, piece, n, position(pattern, i, s, first), s, col, 3, i)
     shape = (32, 128)
     pick = lax.broadcasted_iota(jnp.int32, shape, 1) == lax.broadcasted_iota(jnp.int32, shape, 0) + col * 32
     pick = pick.astype(left.dtype)
@@ -126,6 +112,29 @@
         turned = lax.dot_general(pick, blocks, NT, preferred_element_type=jnp.float32)
         for e, (m, o) in enumerate(edge):
             strips[m + o + RADIUS, m + RADIUS] = turned[:, e * 128 : (e + 1) * 128].astype(strips.dtype)
+
+
+def gather_dot(strips, left, targets, i, places):
+    w = jnp.concatenate([left[i, p] for p in places], axis=1)
+    rows = [jnp.concatenate([strips[t, p] for p in places], axis=1) for t in targets]
+    x = jnp.concatenate(rows, axis=0)
+    return lax.dot_general(x, w, NT, preferred_element_type=jnp.float32)
+
+
+def square_row(kept, strips, left, i, first):
+    total = kept.shape[1]
+    targets = [wrapped(kept[s, first + i] - first + 2 * RADIUS, total) for s in range(kept.shape[0])]
+    acc = gather_dot(strips, left, targets, i, range(i, i + BAND))
+    return acc.reshape(len(targets), 32, 128).astype(strips.dtype)
+
+
+def low_kernel(meta, kept, h0, h1, h2, h3, left, strips_in, low, strips):
+    del strips_in
+    first = meta[1]
+    for halo, entries, shift in zip((h0, h1, h2, h3), LISTS, SHIFTS):
+        for e, (j, o) in enumerate(entries):
+            row = j - shift * ROWS
+            strips[row + 2 * RADIUS, row + o] = halo[e]
     for i in range(RADIUS):
         low[i] = square_row(kept, strips, left, i, first)
 
@@ -175,10 +184,11 @@
 
 
 def outer_kernel(rows, places, arrived):
-    def kernel(meta, kept, cube, halo, left, partial, strips_in, o0, o1, o2, o3, strips):
-        del strips_in
+    def kernel(meta, kept, cube, *refs):
+        halos, (left, partial, _, o0, o1, o2, o3, strips) = refs[:-8], refs[-8:]
         col, first = meta[0], meta[1]
-        insert_rows(strips, kept, halo, arrived, first)
+        for halo, span in zip(halos, arrived):
+            insert_rows(strips, kept, halo, span, first)
         share = cube.shape[0] // 4
         for n, i in enumerate(rows):
             targets = cube_targets(cube, i, col, first, share)
@@ -190,20 +200,18 @@
     return kernel
 
 
-def final_kernel(parts, aliased):
+def final_kernel(rows):
     def kernel(meta, *refs):
         col = meta[0]
         out, whole, turned, sems = refs[-4:]
+        for b, p in enumerate(refs[:4]):
+            whole[:, :, pl.ds(pl.multiple_of((col ^ b) * 32, 32), 32), :] = p[...]
         copies = []
-        for n, rows in enumerate(parts):
-            for b, p in enumerate(refs[4 * n : 4 * n + 4]):
-                start = pl.multiple_of((col ^ b) * 32, 32)
-                whole[pl.ds(rows[0], len(rows)), :, pl.ds(start, 32), :] = p[...]
-            for i in rows:
-                for q in range(out.shape[1]):
-                    turned[i, q] = whole[i, q].T.astype(turned.dtype)
-                copies.append(pltpu.make_async_copy(turned.at[i], out.at[i], sems.at[i]))
-                copies[-1].start()
+        for n, i in enumerate(rows):
+            for q in range(out.shape[1]):
+                turned[n, q] = whole[n, q].T.astype(turned.dtype)
+            copies.append(pltpu.make_async_copy(turned.at[n], out.at[i], sems.at[n]))
+            copies[-1].start()
         for copy in copies:
             copy.wait()
 
@@ -249,7 +257,7 @@
     l2 = across(density, 2)
     l1 = across(density, 1)
     payload = call(
-        reorder_kernel, [SMEM, ANY, ANY], [shape(len(e), *piece) for e in LISTS], (meta, pattern, density),
+        reorder_kernel, [SMEM, HBM, HBM], [shape(len(e), *piece) for e in LISTS], (meta, pattern, density),
         [pltpu.VMEM((ROWS, BAND + 1, *piece), density.dtype), pltpu.VMEM(density.shape, density.dtype),
          pltpu.SMEM(pattern.shape, pattern.dtype), pltpu.SemaphoreType.DMA((2,))],
     )
@@ -259,17 +267,23 @@
         prepare_kernel, [SMEM] * 2 + [VMEM] * 2,
         [shape(STRIPS, NEAR, *piece), shape(ROWS, NEAR, 128, 128)], (meta, pattern, density, l1),
     )
-    l2, halos, strips, left = lax.optimization_barrier((l2, halos, strips, left))
-    l3 = across(l2, 1)
+    l2, left, halos[2:] = lax.optimization_barrier((l2, left, halos[2:]))
+    sizes = [min(RELAY, ROWS - i) for i in range(0, ROWS, RELAY)]
+    left, *pieces = call(
+        relay_kernel, [SMEM] * 2 + [VMEM] * 2,
+        [shape(*left.shape), *(shape(n, *density.shape[1:]) for n in sizes)], (meta, pattern, l2, left),
+        aliases={3: 0},
+    )
+    pieces = [across(p, 1) for p in pieces]
     both = [shape(*strips.shape), shape(*left.shape)]
     strips, left = call(
-        insert_kernel, [SMEM] * 2 + [VMEM] * 7, both, (meta, pattern, l2, *halos, strips, left),
-        aliases={7: 0, 8: 1},
+        complete_kernel, [SMEM] * 2 + [VMEM] * (len(pieces) + 2), both, (meta, pattern, *pieces, strips, left),
+        aliases={2 + len(pieces): 0, 3 + len(pieces): 1},
     )
     work = 2 * width * BAND * 128 * 128 * 32
-    low, strips, left = call(
-        low_kernel, [SMEM] * 3 + [VMEM] * 3, [shape(RADIUS, width, *piece), *both],
-        (meta, pattern, kept, l3, strips, left), flops=work * RADIUS, aliases={4: 1, 5: 2},
+    low, strips = call(
+        low_kernel, [SMEM] * 2 + [VMEM] * 6, [shape(RADIUS, width, *piece), both[0]],
+        (meta, kept, *halos, left, strips), flops=work * RADIUS, aliases={7: 1},
     )
     after = shifted(low, -1)
     far, close = call(
@@ -277,41 +291,43 @@
         [shape(len(FAR), width, *piece), shape(len(CLOSE), width, *piece)],
         (meta, kept, low, strips, left), flops=work * (ROWS - RADIUS),
     )
-    close_in = shifted(close, 1)
-    far_in = shifted(far, 1)
-
     tables = (meta, kept, cube)
     strips, partial = call(
         inner_kernel, [SMEM] * 3 + [VMEM] * 4,
         [shape(REACH, NEAR, *piece), shape(ROWS, slots, *piece, dtype=jnp.float32)],
         (*tables, low, far, close, left), flops=2 * slots * ROWS * ROWS * 128 * 128 * 32,
     )
-    parts = []
-    for rows, places, arrived, halo in (
-        (LATE, AFTER, AFTER, after),
-        (MIDDLE, [*CLOSE, *AFTER], CLOSE, close_in),
-        (EARLY, [*FAR, *CLOSE], FAR, far_in),
-    ):
+    close_in = shifted(close, 1)
+    far, after, close_in, partial = lax.optimization_barrier((far, after, close_in, partial))
+    far_in = shifted(far, 1)
+
+    def rest(rows, places, halos, partial, strips):
         *own, strips = call(
-            outer_kernel(rows, places, arrived), [SMEM] * 3 + [VMEM] * 4,
+            outer_kernel(rows, places, [p for p, _ in halos]), [SMEM] * 3 + [VMEM] * (3 + len(halos)),
             [shape(len(rows), share, *piece)] * 4 + [shape(*strips.shape)],
-            (*tables, halo, left, partial, strips), flops=work * len(rows) // 2, aliases={6: 4},
+            (*tables, *(h for _, h in halos), left, partial, strips), flops=work * len(rows) // 2,
+            aliases={5 + len(halos): 4},
         )
-        parts.append([own[0], *(across(own[b], b) for b in (1, 2, 3))])
+        return [own[0], *(across(own[b], b) for b in (1, 2, 3))], strips
+
+    late, strips = rest(LATE, [*CLOSE, *AFTER], ((AFTER, after), (CLOSE, close_in)), partial, strips)
+    late, partial = lax.optimization_barrier((late, partial))
+    early, _ = rest(EARLY, [*FAR, *CLOSE], ((FAR, far_in),), partial, strips)
 
     result = shape(ROWS, share, 128, 128, dtype=jnp.float32)
-    scratch = [
-        pltpu.VMEM((ROWS, share, 128, 128), density.dtype),
-        pltpu.VMEM((ROWS, share, 128, 128), jnp.float32),
-        pltpu.SemaphoreType.DMA((ROWS,)),
-    ]
+
+    def scratch(rows):
+        block = (len(rows), share, 128, 128)
+        return [pltpu.VMEM(block, density.dtype), pltpu.VMEM(block, jnp.float32),
+                pltpu.SemaphoreType.DMA((len(rows),))]
+
     out = call(
-        final_kernel((LATE, MIDDLE), False), [SMEM] + [VMEM] * 8, [result], (meta, *parts[0], *parts[1]),
-        scratch, out_specs=[ANY],
+        final_kernel(LATE), [SMEM] + [VMEM] * 4, [result], (meta, *late),
+        scratch(LATE), out_specs=[ANY],
     )[0]
     return call(
-        final_kernel((EARLY,), True), [SMEM] + [VMEM] * 4 + [ANY], [result], (meta, *parts[2], out),
-        scratch, out_specs=[ANY], aliases={5: 0},
+        final_kernel(EARLY), [SMEM] + [VMEM] * 4 + [ANY], [result], (meta, *early, out),
+        scratch(EARLY), out_specs=[ANY], aliases={5: 0},
     )[0]
 
 

time: 72.7 us -> 69.4 us (0.955)
  waiting for transfers between devices: 26.4 us -> 22.9 us
    ppermute x7, waiting for transfers between devices: 17.1 us -> 7.86 us  [shifted(): lax.ppermute(x, ('row', 'layer'), [(g, (g + d) % groups) for g in range(g...]
    ppermute x12 -> x11, waiting for transfers between devices: 9.28 us -> 15.1 us  [across(): return lax.ppermute(x, 'col', [(c, c ^ bits) for c in range(4)])]
    ppermute x7, starting transfers between devices: 12.1 us -> 13.8 us  [shifted(): lax.ppermute(x, ('row', 'layer'), [(g, (g + d) % groups) for g in range(g...]
    ppermute x12 -> x11, starting transfers between devices: 8.6 us -> 7.45 us  [across(): return lax.ppermute(x, 'col', [(c, c ^ bits) for c in range(4)])]
  transfers between devices with their start and end apart: 19 -> 18, of which waited for: 11 -> 9; matrix products, arithmetic and copies ran while one was open for 0% -> 0% of each run, Pallas kernels for 25% -> 25%
where the time goes in v5:
time: 69.4 us; the launch traced here: 69.2 us
  Pallas kernels  22.9 us (33%)
  waiting for transfers between devices  22.9 us (33%)
  starting transfers between devices  21.3 us (31%)
  local copies, waits for them, and re-layouts  1.82 us (3%)
    pallas_call x11, Pallas kernels, call(): pl.pallas_call(kernel, out_shape=outs, in_specs=specs, out_specs=out_spec...  22.9 us
    ppermute x11, waiting for transfers between devices, across(): return lax.ppermute(x, 'col', [(c, c ^ bits) for c in range(4)])  15.1 us
    ppermute x7, starting transfers between devices, shifted(): lax.ppermute(x, ('row', 'layer'), [(g, (g + d) % groups) for g in range(g...  13.8 us
    ppermute x7, waiting for transfers between devices, shifted(): lax.ppermute(x, ('row', 'layer'), [(g, (g + d) % groups) for g in range(g...  7.86 us
    ppermute x11, starting transfers between devices, across(): return lax.ppermute(x, 'col', [(c, c ^ bits) for c in range(4)])  7.45 us
    unnamed x8, local copies, waits for them, and re-layouts  1.82 us
  transfers between devices with their start and end apart: 18, of which 9 were waited for; matrix products, arithmetic and copies ran while one was open for 0% of the time, Pallas kernels for 25%

profile of v5, /device:TPU:0, one launch (start us, length us, event | category | flops | bytes accessed | tf_op | source)
XLA Modules:
  0.0 69.2 jit_solution(7290857432318378908)
XLA Ops:
  0.0 0.5 collective-permute-start
  0.5 2.5 %collective-permute-start.3 = (bf16[8,11,32,128]{3,2,1,0:T(8,128)(2,1)}, bf16[8,11,32,128]{3,2,1,0:T(8,128)(2,1)S(1)}, u32[]{:S(2)}, u32[]{:S(2)}) collective-permute-start(bf16[8,11,32,128]{3,2,1,0:T(8,128)(2,1)} %l0.1), channel_id=1, source_target_pairs={{0,4},{2,6},{4,0},{6,2},{1,5},{3,7},{5,1},{7,3},{8,12},{10,14},{12... | collective-permute-start | bytes 2162696 | tf_op jit(solution)/shard_map/ppermute | solution.py:255
  2.9 0.1 pad_add_fusion.meta
  3.0 0.0 copy-start
  3.0 1.1 %copy-done = bf16[8,11,32,128]{3,2,1,0:T(8,128)(2,1)S(1)} copy-done((bf16[8,11,32,128]{3,2,1,0:T(8,128)(2,1)S(1)}, bf16[8,11,32,128]{3,2,1,0:T(8,128)(2,1)}, u32[]{:S(2)}) %copy-start) | copy-done | bytes 720920
  4.1 0.0 copy-start.2
  4.1 0.7 %copy-done.2 = s32[64,11]{0,1:T(8,128)S(1)} copy-done((s32[64,11]{0,1:T(8,128)S(1)}, s32[64,11]{0,1:T(8,128)}, u32[]{:S(2)}) %copy-start.2) | copy-done | bytes 2840
  4.8 1.9 %shard_map.46 = (bf16[37,32,128]{2,1,0:T(8,128)(2,1)S(1)}, bf16[37,32,128]{2,1,0:T(8,128)(2,1)S(1)}, bf16[3,32,128]{2,1,0:T(8,128)(2,1)S(1)}, bf16[3,32,128]{2,1,0:T(8,128)(2,1)S(1)}) custom-call(s32[2]{0:T(128)S(1)} %pad_add_fusion.meta, s32[11,64]{1,0:T(8,128)S(1)} %bitcast.10, bf16[8,11,32,128]{3,2,1,0:T(8,128)(2,1)S(1)} %copy-done), custom_call_target="tpu_custom_call" | custom-call | bytes 1379080 | tf_op jit(solution)/shard_map/pallas_call | solution.py:227
  6.7 0.0 collective-permute-done.l1
  6.7 1.6 %collective-permute-start.1 = (bf16[37,32,128]{2,1,0:T(8,128)(2,1)S(1)}, bf16[37,32,128]{2,1,0:T(8,128)(2,1)S(1)}, u32[]{:S(2)}, u32[]{:S(2)}) collective-permute-start(bf16[37,32,128]{2,1,0:T(8,128)(2,1)S(1)} %get-tuple-element.54), channel_id=1, source_target_pairs={{0,1},{1,8},{8,9},{9,16},{16,17},{17,24},{24,25},{25,0},{2,3},{3,1... | collective-permute-start | bytes 909320 | tf_op jit(solution)/shard_map/ppermute | solution.py:252
  8.3 3.2 %collective-permute-start.2 = (bf16[37,32,128]{2,1,0:T(8,128)(2,1)S(1)}, bf16[37,32,128]{2,1,0:T(8,128)(2,1)S(1)}, u32[]{:S(2)}, u32[]{:S(2)}) collective-permute-start(bf16[37,32,128]{2,1,0:T(8,128)(2,1)S(1)} %get-tuple-element.55), channel_id=1, source_target_pairs={{0,25},{1,0},{8,1},{9,8},{16,9},{17,16},{24,17},{25,24},{2,27},{3,... | collective-permute-start | bytes 909320 | tf_op jit(solution)/shard_map/ppermute | solution.py:252
  11.5 0.0 collective-permute-start.4
  11.5 3.8 %collective-permute-start.5 = (bf16[3,32,128]{2,1,0:T(8,128)(2,1)S(1)}, bf16[3,32,128]{2,1,0:T(8,128)(2,1)S(1)}, u32[]{:S(2)}, u32[]{:S(2)}) collective-permute-start(bf16[3,32,128]{2,1,0:T(8,128)(2,1)S(1)} %get-tuple-element.59), channel_id=1, source_target_pairs={{0,24},{1,25},{8,0},{9,1},{16,8},{17,9},{24,16},{25,17},{2,26},{3,... | collective-permute-start | bytes 73736 | tf_op jit(solution)/shard_map/ppermute | solution.py:252
  15.3 2.2 %shard_map.47 = (bf16[28,18,32,128]{3,2,1,0:T(8,128)(2,1)S(1)}, bf16[8,18,128,128]{3,2,1,0:T(8,128)(2,1)S(1)}) custom-call(s32[2]{0:T(128)S(1)} %pad_add_fusion.meta, s32[11,64]{1,0:T(8,128)S(1)} %bitcast.11, bf16[8,11,32,128]{3,2,1,0:T(8,128)(2,1)S(1)} %copy-done, bf16[8,11,32,128]{3,2,1,0:T(8,128)(2,1)S(1)} %collective-permute-done.l1), custom_call_target="tpu_custom_call" | custom-call | bytes 10291976 | tf_op jit(solution)/shard_map/pallas_call | solution.py:227
  17.5 2.5 %collective-permute-done.3.l2 = bf16[8,11,32,128]{3,2,1,0:T(8,128)(2,1)S(1)} collective-permute-done((bf16[8,11,32,128]{3,2,1,0:T(8,128)(2,1)}, bf16[8,11,32,128]{3,2,1,0:T(8,128)(2,1)S(1)}, u32[]{:S(2)}, u32[]{:S(2)}) %collective-permute-start.3) | collective-permute-done | bytes 720928 | tf_op jit(solution)/shard_map/ppermute | solution.py:255
  20.0 1.2 %collective-permute-done.4.h2 = bf16[3,32,128]{2,1,0:T(8,128)(2,1)S(1)} collective-permute-done((bf16[3,32,128]{2,1,0:T(8,128)(2,1)S(1)}, bf16[3,32,128]{2,1,0:T(8,128)(2,1)S(1)}, u32[]{:S(2)}, u32[]{:S(2)}) %collective-permute-start.4) | collective-permute-done | bytes 24608 | tf_op jit(solution)/shard_map/ppermute | solution.py:252
  21.2 0.0 collective-permute-done.5.h3
  21.2 1.2 %shard_map.48 = (bf16[8,18,128,128]{3,2,1,0:T(8,128)(2,1)S(1)}, bf16[3,11,32,128]{3,2,1,0:T(8,128)(2,1)S(1)}, bf16[3,11,32,128]{3,2,1,0:T(8,128)(2,1)S(1)}, bf16[2,11,32,128]{3,2,1,0:T(8,128)(2,1)S(1)}) custom-call(s32[2]{0:T(128)S(1)} %pad_add_fusion.meta, s32[11,64]{1,0:T(8,128)S(1)} %bitcast.12, ...), custom_call_target="tpu_custom_call", output_to_operand_aliasing={{0}: (3, {})} | custom-call | bytes 10881800 | tf_op jit(solution)/shard_map/pallas_call | solution.py:227
  22.4 0.1 collective-permute-start.6
  22.5 0.5 collective-permute-start.7
  22.9 0.1 collective-permute-start.8
  23.0 1.6 %collective-permute-done.8.refs_2_ = bf16[2,11,32,128]{3,2,1,0:T(8,128)(2,1)S(1)} collective-permute-done((bf16[2,11,32,128]{3,2,1,0:T(8,128)(2,1)S(1)}, bf16[2,11,32,128]{3,2,1,0:T(8,128)(2,1)S(1)}, u32[]{:S(2)}, u32[]{:S(2)}) %collective-permute-start.8) | collective-permute-done | bytes 180256 | tf_op jit(solution)/shard_map/ppermute | solution.py:255
  24.6 0.0 collective-permute-done.6.refs_0_
  24.6 0.0 collective-permute-done.7.refs_1_
  24.6 0.0 copy-start.1
  24.6 1.6 %shard_map.49 = (bf16[28,18,32,128]{3,2,1,0:T(8,128)(2,1)S(1)}, bf16[8,18,128,128]{3,2,1,0:T(8,128)(2,1)S(1)}) custom-call(s32[2]{0:T(128)S(1)} %pad_add_fusion.meta, s32[11,64]{1,0:T(8,128)S(1)} %bitcast.13, bf16[3,11,32,128]{3,2,1,0:T(8,128)(2,1)S(1)} %collective-permute-done.6.refs_0_, ...), custom_call_target="tpu_custom_call", output_to_operand_aliasing={{0}: (5, {}), {1}: (6, {})} | custom-call | bytes 18418440 | tf_op jit(solution)/shard_map/pallas_call | solution.py:227
  26.2 0.0 collective-permute-done.1.h0
  26.2 0.0 collective-permute-done.2.h1
  26.3 0.0 copy-done.1
  26.3 2.3 %shard_map.50 = (bf16[5,12,32,128]{3,2,1,0:T(8,128)(2,1)S(1)}, bf16[28,18,32,128]{3,2,1,0:T(8,128)(2,1)S(1)}) custom-call(s32[2]{0:T(128)S(1)} %pad_add_fusion.meta, s32[12,64]{1,0:T(8,128)S(1)} %bitcast.5, bf16[37,32,128]{2,1,0:T(8,128)(2,1)S(1)} %collective-permute-done.1.h0, ...), custom_call_target="tpu_custom_call", output_to_operand_aliasing={{1}: (7, {})} | custom-call | flops 692060160 | bytes 14126088 | tf_op jit(solution)/shard_map/pallas_call | solution.py:227
  28.5 0.0 copy-start.3
  28.5 3.7 %collective-permute-start.9 = (bf16[5,12,32,128]{3,2,1,0:T(8,128)(2,1)S(1)}, bf16[5,12,32,128]{3,2,1,0:T(8,128)(2,1)S(1)}, u32[]{:S(2)}, u32[]{:S(2)}) collective-permute-start(bf16[5,12,32,128]{3,2,1,0:T(8,128)(2,1)S(1)} %get-tuple-element.71.low), channel_id=1, source_target_pairs={{0,25},{1,0},{8,1},{9,8},{16,9},{17,16},{24,17},{25,24},{2,27},{3,... | collective-permute-start | bytes 1474568 | tf_op jit(solution)/shard_map/ppermute | solution.py:252
  32.2 1.7 %shard_map.51 = (bf16[3,12,32,128]{3,2,1,0:T(8,128)(2,1)S(1)}, bf16[2,12,32,128]{3,2,1,0:T(8,128)(2,1)S(1)}) custom-call(s32[2]{0:T(128)S(1)} %pad_add_fusion.meta, s32[12,64]{1,0:T(8,128)S(1)} %bitcast.6, bf16[5,12,32,128]{3,2,1,0:T(8,128)(2,1)S(1)} %get-tuple-element.71.low, bf16[28,18,32,128]{3,2,1,0:T(8,128)(2,1)S(1)} %get-tuple-element.72.strips, ...), custom_call_target="tpu_custom_call" | custom-call | flops 415236096 | bytes 9833480 | tf_op jit(solution)/shard_map/pallas_call | solution.py:227
  33.9 0.1 collective-permute-start.10
  34.0 0.0 copy-done.3
  34.0 5.4 %shard_map.52 = (bf16[38,18,32,128]{3,2,1,0:T(8,128)(2,1)S(1)}, f32[8,16,32,128]{3,2,1,0:T(8,128)S(1)}) custom-call(s32[2]{0:T(128)S(1)} %pad_add_fusion.meta, s32[12,64]{1,0:T(8,128)S(1)} %bitcast.7, s32[16,64]{1,0:T(8,128)S(1)} %bitcast.14, bf16[5,12,32,128]{3,2,1,0:T(8,128)(2,1)S(1)} %get-tuple-element.71.low, ...), custom_call_target="tpu_custom_call" | custom-call | flops 1073741824 | bytes 13409288 | tf_op jit(solution)/shard_map/pallas_call | solution.py:227
  39.4 5.6 %collective-permute-done.10.refs_1_ = bf16[2,12,32,128]{3,2,1,0:T(8,128)(2,1)S(1)} collective-permute-done((bf16[2,12,32,128]{3,2,1,0:T(8,128)(2,1)S(1)}, bf16[2,12,32,128]{3,2,1,0:T(8,128)(2,1)S(1)}, u32[]{:S(2)}, u32[]{:S(2)}) %collective-permute-start.10) | collective-permute-done | bytes 196640 | tf_op jit(solution)/shard_map/ppermute | solution.py:252
  45.1 1.0 %collective-permute-done.9.refs_0_ = bf16[5,12,32,128]{3,2,1,0:T(8,128)(2,1)S(1)} collective-permute-done((bf16[5,12,32,128]{3,2,1,0:T(8,128)(2,1)S(1)}, bf16[5,12,32,128]{3,2,1,0:T(8,128)(2,1)S(1)}, u32[]{:S(2)}, u32[]{:S(2)}) %collective-permute-start.9) | collective-permute-done | bytes 491552 | tf_op jit(solution)/shard_map/ppermute | solution.py:252
  46.1 1.5 %collective-permute-start.11 = (bf16[3,12,32,128]{3,2,1,0:T(8,128)(2,1)S(1)}, bf16[3,12,32,128]{3,2,1,0:T(8,128)(2,1)S(1)}, u32[]{:S(2)}, u32[]{:S(2)}) collective-permute-start(bf16[3,12,32,128]{3,2,1,0:T(8,128)(2,1)S(1)} %get-tuple-element.76.far), channel_id=1, source_target_pairs={{0,1},{1,8},{8,9},{9,16},{16,17},{17,24},{24,25},{25,0},{2,3},{3,1... | collective-permute-start | bytes 884744 | tf_op jit(solution)/shard_map/ppermute | solution.py:252
  47.5 1.9 %shard_map.53 = (bf16[5,4,32,128]{3,2,1,0:T(8,128)(2,1)S(1)}, bf16[5,4,32,128]{3,2,1,0:T(8,128)(2,1)S(1)}, bf16[5,4,32,128]{3,2,1,0:T(8,128)(2,1)S(1)}, bf16[5,4...) custom-call(s32[2]{0:T(128)S(1)} %pad_add_fusion.meta, ...), custom_call_target="tpu_custom_call", output_to_operand_aliasing={{4}: (7, {})} | custom-call | flops 346030080 | bytes 19373064 | tf_op jit(solution)/shard_map/pallas_call | solution.py:227
  49.4 0.1 collective-permute-start.12
  49.5 1.6 %collective-permute-start.13 = (bf16[5,4,32,128]{3,2,1,0:T(8,128)(2,1)S(1)}, bf16[5,4,32,128]{3,2,1,0:T(8,128)(2,1)S(1)}, u32[]{:S(2)}, u32[]{:S(2)}) collective-permute-start(bf16[5,4,32,128]{3,2,1,0:T(8,128)(2,1)S(1)} %get-tuple-element.83), channel_id=1, source_target_pairs={{0,4},{2,6},{4,0},{6,2},{1,5},{3,7},{5,1},{7,3},{8,12},{10,14},{12... | collective-permute-start | bytes 491528 | tf_op jit(solution)/shard_map/ppermute | solution.py:255
  51.1 0.3 collective-permute-start.14
  51.4 0.0 collective-permute-done.12.refs_1_
  51.4 5.2 %collective-permute-done.13.refs_2_ = bf16[5,4,32,128]{3,2,1,0:T(8,128)(2,1)S(1)} collective-permute-done((bf16[5,4,32,128]{3,2,1,0:T(8,128)(2,1)S(1)}, bf16[5,4,32,128]{3,2,1,0:T(8,128)(2,1)S(1)}, u32[]{:S(2)}, u32[]{:S(2)}) %collective-permute-start.13) | collective-permute-done | bytes 163872 | tf_op jit(solution)/shard_map/ppermute | solution.py:255
  56.6 2.6 %collective-permute-done.14.refs_3_ = bf16[5,4,32,128]{3,2,1,0:T(8,128)(2,1)S(1)} collective-permute-done((bf16[5,4,32,128]{3,2,1,0:T(8,128)(2,1)S(1)}, bf16[5,4,32,128]{3,2,1,0:T(8,128)(2,1)S(1)}, u32[]{:S(2)}, u32[]{:S(2)}) %collective-permute-start.14) | collective-permute-done | bytes 163872 | tf_op jit(solution)/shard_map/ppermute | solution.py:255
  59.2 0.0 collective-permute-done.11.refs_0_
  59.2 1.5 %shard_map.54 = (bf16[3,4,32,128]{3,2,1,0:T(8,128)(2,1)S(1)}, bf16[3,4,32,128]{3,2,1,0:T(8,128)(2,1)S(1)}, bf16[3,4,32,128]{3,2,1,0:T(8,128)(2,1)S(1)}, bf16[3,4...) custom-call(s32[2]{0:T(128)S(1)} %pad_add_fusion.meta, ...), custom_call_target="tpu_custom_call", output_to_operand_aliasing={{4}: (6, {})} | custom-call | flops 207618048 | bytes 18717704 | tf_op jit(solution)/shard_map/pallas_call | solution.py:227
  60.7 0.3 collective-permute-start.15
  61.0 1.5 %collective-permute-start.16 = (bf16[3,4,32,128]{3,2,1,0:T(8,128)(2,1)S(1)}, bf16[3,4,32,128]{3,2,1,0:T(8,128)(2,1)S(1)}, u32[]{:S(2)}, u32[]{:S(2)}) collective-permute-start(bf16[3,4,32,128]{3,2,1,0:T(8,128)(2,1)S(1)} %get-tuple-element.89), channel_id=1, source_target_pairs={{0,4},{2,6},{4,0},{6,2},{1,5},{3,7},{5,1},{7,3},{8,12},{10,14},{12... | collective-permute-start | bytes 294920 | tf_op jit(solution)/shard_map/ppermute | solution.py:255
  62.5 0.1 collective-permute-start.17
  62.6 1.8 %shard_map.55.refs_4_ = f32[8,4,128,128]{3,2,1,0:T(8,128)} custom-call(s32[2]{0:T(128)S(1)} %pad_add_fusion.meta, bf16[5,4,32,128]{3,2,1,0:T(8,128)(2,1)S(1)} %get-tuple-element.91.refs_0_, bf16[5,4,32,128]{3,2,1,0:T(8,128)(2,1)S(1)} %collective-permute-done.12.refs_1_, bf16[5,4,32,128]{3,2,1,0:T(8,128)(2,1)S(1)} %collective-permute-done.13.refs_2_, ...), custom_call_target="tpu_custom_call" | custom-call | bytes 2752520 | tf_op jit(solution)/shard_map/pallas_call | solution.py:227
  64.4 0.0 collective-permute-done.15.refs_1_
  64.4 2.0 %collective-permute-done.16.refs_2_ = bf16[3,4,32,128]{3,2,1,0:T(8,128)(2,1)S(1)} collective-permute-done((bf16[3,4,32,128]{3,2,1,0:T(8,128)(2,1)S(1)}, bf16[3,4,32,128]{3,2,1,0:T(8,128)(2,1)S(1)}, u32[]{:S(2)}, u32[]{:S(2)}) %collective-permute-start.16) | collective-permute-done | bytes 98336 | tf_op jit(solution)/shard_map/ppermute | solution.py:255
  66.4 1.2 %collective-permute-done.17.refs_3_ = bf16[3,4,32,128]{3,2,1,0:T(8,128)(2,1)S(1)} collective-permute-done((bf16[3,4,32,128]{3,2,1,0:T(8,128)(2,1)S(1)}, bf16[3,4,32,128]{3,2,1,0:T(8,128)(2,1)S(1)}, u32[]{:S(2)}, u32[]{:S(2)}) %collective-permute-start.17) | collective-permute-done | bytes 98336 | tf_op jit(solution)/shard_map/ppermute | solution.py:255
  67.6 1.6 %shard_map.56 = f32[8,4,128,128]{3,2,1,0:T(8,128)} custom-call(s32[2]{0:T(128)S(1)} %pad_add_fusion.meta, bf16[3,4,32,128]{3,2,1,0:T(8,128)(2,1)S(1)} %get-tuple-element.87.refs_0_, bf16[3,4,32,128]{3,2,1,0:T(8,128)(2,1)S(1)} %collective-permute-done.15.refs_1_, ...), custom_call_target="tpu_custom_call", output_to_operand_aliasing={{}: (5, {})} | custom-call | bytes 4587528 | tf_op jit(solution)/shard_map/pallas_call | solution.py:227
Async XLA Ops:
  0.0 6.7 %collective-permute-start = (bf16[8,11,32,128]{3,2,1,0:T(8,128)(2,1)}, bf16[8,11,32,128]{3,2,1,0:T(8,128)(2,1)S(1)}, u32[]{:S(2)}, u32[]{:S(2)}) collective-permute-start(bf16[8,11,32,128]{3,2,1,0:T(8,128)(2,1)} %l0.1), channel_id=1, source_target_pairs={{0,2},{2,0},{4,6},{6,4},{1,3},{3,1},{5,7},{7,5},{8,10},{10,8},{12,... | collective-permute-start | bytes 2162696 | tf_op jit(solution)/shard_map/ppermute | solution.py:255
  0.5 19.5 %collective-permute-start.3 = (bf16[8,11,32,128]{3,2,1,0:T(8,128)(2,1)}, bf16[8,11,32,128]{3,2,1,0:T(8,128)(2,1)S(1)}, u32[]{:S(2)}, u32[]{:S(2)}) collective-permute-start(bf16[8,11,32,128]{3,2,1,0:T(8,128)(2,1)} %l0.1), channel_id=1, source_target_pairs={{0,4},{2,6},{4,0},{6,2},{1,5},{3,7},{5,1},{7,3},{8,12},{10,14},{12... | collective-permute-start | bytes 2162696 | tf_op jit(solution)/shard_map/ppermute | solution.py:255
  3.0 1.1 %copy-start = (bf16[8,11,32,128]{3,2,1,0:T(8,128)(2,1)S(1)}, bf16[8,11,32,128]{3,2,1,0:T(8,128)(2,1)}, u32[]{:S(2)}) copy-start(bf16[8,11,32,128]{3,2,1,0:T(8,128)(2,1)} %l0.1) | copy-start | bytes 2162692
  4.1 0.7 %copy-start.2 = (s32[64,11]{0,1:T(8,128)S(1)}, s32[64,11]{0,1:T(8,128)}, u32[]{:S(2)}) copy-start(s32[64,11]{0,1:T(8,128)} %param.5) | copy-start | bytes 8452
  6.7 19.5 %collective-permute-start.1 = (bf16[37,32,128]{2,1,0:T(8,128)(2,1)S(1)}, bf16[37,32,128]{2,1,0:T(8,128)(2,1)S(1)}, u32[]{:S(2)}, u32[]{:S(2)}) collective-permute-start(bf16[37,32,128]{2,1,0:T(8,128)(2,1)S(1)} %get-tuple-element.54), channel_id=1, source_target_pairs={{0,1},{1,8},{8,9},{9,16},{16,17},{17,24},{24,25},{25,0},{2,3},{3,1... | collective-permute-start | bytes 909320 | tf_op jit(solution)/shard_map/ppermute | solution.py:252
  8.3 17.9 %collective-permute-start.2 = (bf16[37,32,128]{2,1,0:T(8,128)(2,1)S(1)}, bf16[37,32,128]{2,1,0:T(8,128)(2,1)S(1)}, u32[]{:S(2)}, u32[]{:S(2)}) collective-permute-start(bf16[37,32,128]{2,1,0:T(8,128)(2,1)S(1)} %get-tuple-element.55), channel_id=1, source_target_pairs={{0,25},{1,0},{8,1},{9,8},{16,9},{17,16},{24,17},{25,24},{2,27},{3,... | collective-permute-start | bytes 909320 | tf_op jit(solution)/shard_map/ppermute | solution.py:252
  11.5 9.6 %collective-permute-start.4 = (bf16[3,32,128]{2,1,0:T(8,128)(2,1)S(1)}, bf16[3,32,128]{2,1,0:T(8,128)(2,1)S(1)}, u32[]{:S(2)}, u32[]{:S(2)}) collective-permute-start(bf16[3,32,128]{2,1,0:T(8,128)(2,1)S(1)} %get-tuple-element.58), channel_id=1, source_target_pairs={{0,8},{1,9},{8,16},{9,17},{16,24},{17,25},{24,0},{25,1},{2,10},{3,... | collective-permute-start | bytes 73736 | tf_op jit(solution)/shard_map/ppermute | solution.py:252
  11.5 9.6 %collective-permute-start.5 = (bf16[3,32,128]{2,1,0:T(8,128)(2,1)S(1)}, bf16[3,32,128]{2,1,0:T(8,128)(2,1)S(1)}, u32[]{:S(2)}, u32[]{:S(2)}) collective-permute-start(bf16[3,32,128]{2,1,0:T(8,128)(2,1)S(1)} %get-tuple-element.59), channel_id=1, source_target_pairs={{0,24},{1,25},{8,0},{9,1},{16,8},{17,9},{24,16},{25,17},{2,26},{3,... | collective-permute-start | bytes 73736 | tf_op jit(solution)/shard_map/ppermute | solution.py:252
  22.4 2.3 %collective-permute-start.6 = (bf16[3,11,32,128]{3,2,1,0:T(8,128)(2,1)S(1)}, bf16[3,11,32,128]{3,2,1,0:T(8,128)(2,1)S(1)}, u32[]{:S(2)}, u32[]{:S(2)}) collective-permute-start(bf16[3,11,32,128]{3,2,1,0:T(8,128)(2,1)S(1)} %get-tuple-element.64), channel_id=1, source_target_pairs={{0,2},{2,0},{4,6},{6,4},{1,3},{3,1},{5,7},{7,5},{8,10},{10,8},{12,... | collective-permute-start | bytes 811016 | tf_op jit(solution)/shard_map/ppermute | solution.py:255
  22.5 2.2 %collective-permute-start.7 = (bf16[3,11,32,128]{3,2,1,0:T(8,128)(2,1)S(1)}, bf16[3,11,32,128]{3,2,1,0:T(8,128)(2,1)S(1)}, u32[]{:S(2)}, u32[]{:S(2)}) collective-permute-start(bf16[3,11,32,128]{3,2,1,0:T(8,128)(2,1)S(1)} %get-tuple-element.65), channel_id=1, source_target_pairs={{0,2},{2,0},{4,6},{6,4},{1,3},{3,1},{5,7},{7,5},{8,10},{10,8},{12,... | collective-permute-start | bytes 811016 | tf_op jit(solution)/shard_map/ppermute | solution.py:255
  22.9 1.7 %collective-permute-start.8 = (bf16[2,11,32,128]{3,2,1,0:T(8,128)(2,1)S(1)}, bf16[2,11,32,128]{3,2,1,0:T(8,128)(2,1)S(1)}, u32[]{:S(2)}, u32[]{:S(2)}) collective-permute-start(bf16[2,11,32,128]{3,2,1,0:T(8,128)(2,1)S(1)} %get-tuple-element.66), channel_id=1, source_target_pairs={{0,2},{2,0},{4,6},{6,4},{1,3},{3,1},{5,7},{7,5},{8,10},{10,8},{12,... | collective-permute-start | bytes 540680 | tf_op jit(solution)/shard_map/ppermute | solution.py:255
  24.6 1.6 %copy-start.1 = (s32[64,12]{0,1:T(8,128)S(1)}, s32[64,12]{0,1:T(8,128)}, u32[]{:S(2)}) copy-start(s32[64,12]{0,1:T(8,128)} %param.6) | copy-start | bytes 9220
  28.5 5.4 %copy-start.3 = (s32[64,16]{0,1:T(8,128)S(1)}, s32[64,16]{0,1:T(8,128)}, u32[]{:S(2)}) copy-start(s32[64,16]{0,1:T(8,128)} %param.7) | copy-start | bytes 12292
  28.5 17.5 %collective-permute-start.9 = (bf16[5,12,32,128]{3,2,1,0:T(8,128)(2,1)S(1)}, bf16[5,12,32,128]{3,2,1,0:T(8,128)(2,1)S(1)}, u32[]{:S(2)}, u32[]{:S(2)}) collective-permute-start(bf16[5,12,32,128]{3,2,1,0:T(8,128)(2,1)S(1)} %get-tuple-element.71.low), channel_id=1, source_target_pairs={{0,25},{1,0},{8,1},{9,8},{16,9},{17,16},{24,17},{25,24},{2,27},{3,... | collective-permute-start | bytes 1474568 | tf_op jit(solution)/shard_map/ppermute | solution.py:252
  33.9 11.2 %collective-permute-start.10 = (bf16[2,12,32,128]{3,2,1,0:T(8,128)(2,1)S(1)}, bf16[2,12,32,128]{3,2,1,0:T(8,128)(2,1)S(1)}, u32[]{:S(2)}, u32[]{:S(2)}) collective-permute-start(bf16[2,12,32,128]{3,2,1,0:T(8,128)(2,1)S(1)} %get-tuple-element.74.close), channel_id=1, source_target_pairs={{0,1},{1,8},{8,9},{9,16},{16,17},{17,24},{24,25},{25,0},{2,3},{3,1... | collective-permute-start | bytes 589832 | tf_op jit(solution)/shard_map/ppermute | solution.py:252
  46.1 13.1 %collective-permute-start.11 = (bf16[3,12,32,128]{3,2,1,0:T(8,128)(2,1)S(1)}, bf16[3,12,32,128]{3,2,1,0:T(8,128)(2,1)S(1)}, u32[]{:S(2)}, u32[]{:S(2)}) collective-permute-start(bf16[3,12,32,128]{3,2,1,0:T(8,128)(2,1)S(1)} %get-tuple-element.76.far), channel_id=1, source_target_pairs={{0,1},{1,8},{8,9},{9,16},{16,17},{17,24},{24,25},{25,0},{2,3},{3,1... | collective-permute-start | bytes 884744 | tf_op jit(solution)/shard_map/ppermute | solution.py:252
  49.4 1.9 %collective-permute-start.12 = (bf16[5,4,32,128]{3,2,1,0:T(8,128)(2,1)S(1)}, bf16[5,4,32,128]{3,2,1,0:T(8,128)(2,1)S(1)}, u32[]{:S(2)}, u32[]{:S(2)}) collective-permute-start(bf16[5,4,32,128]{3,2,1,0:T(8,128)(2,1)S(1)} %get-tuple-element.82), channel_id=1, source_target_pairs={{0,2},{2,0},{4,6},{6,4},{1,3},{3,1},{5,7},{7,5},{8,10},{10,8},{12,... | collective-permute-start | bytes 491528 | tf_op jit(solution)/shard_map/ppermute | solution.py:255
  49.5 7.1 %collective-permute-start.13 = (bf16[5,4,32,128]{3,2,1,0:T(8,128)(2,1)S(1)}, bf16[5,4,32,128]{3,2,1,0:T(8,128)(2,1)S(1)}, u32[]{:S(2)}, u32[]{:S(2)}) collective-permute-start(bf16[5,4,32,128]{3,2,1,0:T(8,128)(2,1)S(1)} %get-tuple-element.83), channel_id=1, source_target_pairs={{0,4},{2,6},{4,0},{6,2},{1,5},{3,7},{5,1},{7,3},{8,12},{10,14},{12... | collective-permute-start | bytes 491528 | tf_op jit(solution)/shard_map/ppermute | solution.py:255
  51.1 8.1 %collective-permute-start.14 = (bf16[5,4,32,128]{3,2,1,0:T(8,128)(2,1)S(1)}, bf16[5,4,32,128]{3,2,1,0:T(8,128)(2,1)S(1)}, u32[]{:S(2)}, u32[]{:S(2)}) collective-permute-start(bf16[5,4,32,128]{3,2,1,0:T(8,128)(2,1)S(1)} %get-tuple-element.84), channel_id=1, source_target_pairs={{0,6},{2,4},{4,2},{6,0},{1,7},{3,5},{5,3},{7,1},{8,14},{10,12},{12... | collective-permute-start | bytes 491528 | tf_op jit(solution)/shard_map/ppermute | solution.py:255
  60.7 3.7 %collective-permute-start.15 = (bf16[3,4,32,128]{3,2,1,0:T(8,128)(2,1)S(1)}, bf16[3,4,32,128]{3,2,1,0:T(8,128)(2,1)S(1)}, u32[]{:S(2)}, u32[]{:S(2)}) collective-permute-start(bf16[3,4,32,128]{3,2,1,0:T(8,128)(2,1)S(1)} %get-tuple-element.88), channel_id=1, source_target_pairs={{0,2},{2,0},{4,6},{6,4},{1,3},{3,1},{5,7},{7,5},{8,10},{10,8},{12,... | collective-permute-start | bytes 294920 | tf_op jit(solution)/shard_map/ppermute | solution.py:255
  61.0 5.4 %collective-permute-start.16 = (bf16[3,4,32,128]{3,2,1,0:T(8,128)(2,1)S(1)}, bf16[3,4,32,128]{3,2,1,0:T(8,128)(2,1)S(1)}, u32[]{:S(2)}, u32[]{:S(2)}) collective-permute-start(bf16[3,4,32,128]{3,2,1,0:T(8,128)(2,1)S(1)} %get-tuple-element.89), channel_id=1, source_target_pairs={{0,4},{2,6},{4,0},{6,2},{1,5},{3,7},{5,1},{7,3},{8,12},{10,14},{12... | collective-permute-start | bytes 294920 | tf_op jit(solution)/shard_map/ppermute | solution.py:255
  62.5 5.1 %collective-permute-start.17 = (bf16[3,4,32,128]{3,2,1,0:T(8,128)(2,1)S(1)}, bf16[3,4,32,128]{3,2,1,0:T(8,128)(2,1)S(1)}, u32[]{:S(2)}, u32[]{:S(2)}) collective-permute-start(bf16[3,4,32,128]{3,2,1,0:T(8,128)(2,1)S(1)} %get-tuple-element.90), channel_id=1, source_target_pairs={{0,6},{2,4},{4,2},{6,0},{1,7},{3,5},{5,3},{7,1},{8,14},{10,12},{12... | collective-permute-start | bytes 294920 | tf_op jit(solution)/shard_map/ppermute | solution.py:255

commit v6 on v5

--- a/solution.py
+++ b/solution.py
@@ -15,7 +15,6 @@
 VMEM = pl.BlockSpec(memory_space=pltpu.VMEM)
 SMEM = pl.BlockSpec(memory_space=pltpu.SMEM)
 ANY = pl.BlockSpec(memory_space=pl.ANY)
-HBM = pl.BlockSpec(memory_space=pltpu.HBM)
 
 SHIFTS = (1, -1, 2, -2)
 OWN = [(j, o) for j in range(ROWS) for o in range(BAND)]
@@ -29,81 +28,63 @@
     [(m, o) for m, o in OWN if m + o < RADIUS],
     [(m, o) for m, o in OWN if m + o >= RADIUS + ROWS],
 )
+UPPER = [(j, o) for j, o in OWN if o >= RADIUS or j + o < RADIUS]
+LOWER = [(m, j) for m in range(ROWS) for j in range(m + 1, min(ROWS, m + RADIUS + 1))]
 LATE = range(ROWS - RADIUS, ROWS)
 EARLY = range(0, ROWS - RADIUS)
 AFTER = range(RADIUS + ROWS, NEAR)
 CLOSE = range(ROWS - RADIUS, RADIUS)
 FAR = range(0, ROWS - RADIUS)
-RELAY = 3
+RELAY = 21
 
 
 def wrapped(value, total):
     return jnp.where(value < 0, value + total, jnp.where(value >= total, value - total, value))
 
 
-def offset_slot(pattern, i, s, first):
-    listed = pattern[s, first + i]
-    o = wrapped(listed - (first + i) + RADIUS, pattern.shape[1])
-    return jnp.where(listed >= 0, o, BAND)
-
-
-def position(pattern, i, s, first):
-    o = offset_slot(pattern, i, s, first)
-    return jnp.where(o < BAND, i + o, (i + BAND) % NEAR)
-
-
-def reorder_kernel(meta, pattern, density, h0, h1, h2, h3, band, blocks, table, sems):
-    first = meta[1]
-    copies = (
-        pltpu.make_async_copy(density, blocks, sems.at[0]),
-        pltpu.make_async_copy(pattern, table, sems.at[1]),
-    )
-    for copy in copies:
-        copy.start()
+def reorder_kernel(meta, pattern, density, h0, h1, h2, h3, upper, band):
+    first, total = meta[1], pattern.shape[1]
     band[...] = jnp.zeros_like(band)
-    for copy in copies:
-        copy.wait()
     for i in range(ROWS):
-        for s in range(blocks.shape[1]):
-            band[i, offset_slot(table, i, s, first)] = blocks[i, s]
-    for out, entries in zip((h0, h1, h2, h3), LISTS):
+        for s in range(density.shape[1]):
+            listed = pattern[s, first + i]
+            o = wrapped(listed - (first + i) + RADIUS, total)
+            band[i, jnp.where(listed >= 0, o, BAND)] = density[i, s]
+    for out, entries in zip((h0, h1, h2, h3, upper), (*LISTS, UPPER)):
         for e, (j, o) in enumerate(entries):
             out[e] = band[j, o]
 
 
-def place(left, piece, n, p, s, col, b, i=None):
-    left[n if i is None else i, p, pl.ds(pl.multiple_of((col ^ b) * 32, 32), 32), :] = piece[n, s]
-
-
-def prepare_kernel(meta, pattern, l0, l1, strips, left):
-    col, first = meta[0], meta[1]
+def place(left, piece, entries, col, b):
+    start = pl.multiple_of((col ^ b) * 32, 32)
+    for e, (i, o) in enumerate(entries):
+        left[i, i + o, pl.ds(start, 32), :] = piece[e]
+
+
+def prepare_kernel(meta, band, upper, u1, strips, left):
     strips[...] = jnp.zeros_like(strips)
     left[...] = jnp.zeros_like(left)
     for i in range(ROWS):
-        for s in range(l0.shape[1]):
-            p = position(pattern, i, s, first)
-            place(left, l0, i, p, s, col, 0)
-            place(left, l1, i, p, s, col, 1)
-            strips[i + 2 * RADIUS, p] = l0[i, s]
-
-
-def relay_kernel(meta, pattern, l2, left_in, left, *pieces):
+        strips[i + 2 * RADIUS, i : i + BAND] = band[i, :BAND]
+    place(left, upper, UPPER, meta[0], 0)
+    place(left, u1, UPPER, meta[0], 1)
+
+
+def relay_kernel(u2, *pieces):
+    for n, piece in enumerate(pieces):
+        piece[...] = u2[n * RELAY : n * RELAY + piece.shape[0]]
+
+
+def place_kernel(meta, u2, left_in, left):
     del left_in
-    col, first = meta[0], meta[1]
-    for i in range(ROWS):
-        piece, n = pieces[i // RELAY], i % RELAY
-        for s in range(l2.shape[1]):
-            place(left, l2, i, position(pattern, i, s, first), s, col, 2)
-        piece[n] = l2[i]
-
-
-def complete_kernel(meta, pattern, *refs):
+    place(left, u2, UPPER, meta[0], 2)
+
+
+def complete_kernel(meta, *refs):
     pieces, (strips, left) = refs[:-4], refs[-2:]
-    col, first = meta[0], meta[1]
-    for i in range(ROWS):
-        piece, n = pieces[i // RELAY], i % RELAY
-        for s in range(piece.shape[1]):
-            place(left, piece, n, position(pattern, i, s, first), s, col, 3, i)
+    col = meta[0]
+    for n, piece in enumerate(pieces):
+        place(left, piece, UPPER[n * RELAY : n * RELAY + piece.shape[0]], col, 3)
     shape = (32, 128)
     pick = lax.broadcasted_iota(jnp.int32, shape, 1) == lax.broadcasted_iota(jnp.int32, shape, 0) + col * 32
     pick = pick.astype(left.dtype)
@@ -112,6 +93,8 @@
         turned = lax.dot_general(pick, blocks, NT, preferred_element_type=jnp.float32)
         for e, (m, o) in enumerate(edge):
             strips[m + o + RADIUS, m + RADIUS] = turned[:, e * 128 : (e + 1) * 128].astype(strips.dtype)
+    for m, j in LOWER:
+        left[j, m + RADIUS] = left[m, j + RADIUS].T
 
 
 def gather_dot(strips, left, targets, i, places):
@@ -222,8 +205,9 @@
     return jax.ShapeDtypeStruct(dims, dtype)
 
 
-def call(kernel, specs, outs, args, scratch=(), flops=0, aliases=None, out_specs=None, limit=16):
+def call(kernel, specs, outs, args, scratch=(), flops=0, aliases=None, out_specs=None, limit=16, free=False):
     size = sum(a.size * a.dtype.itemsize for a in args) + sum(o.size * o.dtype.itemsize for o in outs)
+    size = 0 if free else size
     return pl.pallas_call(
         kernel,
         out_shape=outs,
@@ -254,31 +238,27 @@
     def across(x, bits):
         return lax.ppermute(x, "col", [(c, c ^ bits) for c in range(4)])
 
-    l2 = across(density, 2)
-    l1 = across(density, 1)
-    payload = call(
-        reorder_kernel, [SMEM, HBM, HBM], [shape(len(e), *piece) for e in LISTS], (meta, pattern, density),
-        [pltpu.VMEM((ROWS, BAND + 1, *piece), density.dtype), pltpu.VMEM(density.shape, density.dtype),
-         pltpu.SMEM(pattern.shape, pattern.dtype), pltpu.SemaphoreType.DMA((2,))],
-    )
-    payload, l1 = lax.optimization_barrier((payload, l1))
-    halos = [shifted(p, d) for p, d in zip(payload, SHIFTS)]
+    *halos, upper, band = call(
+        reorder_kernel, [SMEM, SMEM, VMEM],
+        [*(shape(len(e), *piece) for e in (*LISTS, UPPER)), shape(ROWS, BAND + 1, *piece)],
+        (meta, pattern, density),
+    )
+    u2 = across(upper, 2)
+    u1 = across(upper, 1)
+    halos = [shifted(p, d) for p, d in zip(halos, SHIFTS)]
     strips, left = call(
-        prepare_kernel, [SMEM] * 2 + [VMEM] * 2,
-        [shape(STRIPS, NEAR, *piece), shape(ROWS, NEAR, 128, 128)], (meta, pattern, density, l1),
-    )
-    l2, left, halos[2:] = lax.optimization_barrier((l2, left, halos[2:]))
-    sizes = [min(RELAY, ROWS - i) for i in range(0, ROWS, RELAY)]
-    left, *pieces = call(
-        relay_kernel, [SMEM] * 2 + [VMEM] * 2,
-        [shape(*left.shape), *(shape(n, *density.shape[1:]) for n in sizes)], (meta, pattern, l2, left),
-        aliases={3: 0},
-    )
+        prepare_kernel, [SMEM] + [VMEM] * 3,
+        [shape(STRIPS, NEAR, *piece), shape(ROWS, NEAR, 128, 128)], (meta, band, upper, u1),
+    )
+    u2, left, halos[2:] = lax.optimization_barrier((u2, left, halos[2:]))
+    sizes = [min(RELAY, len(UPPER) - e) for e in range(0, len(UPPER), RELAY)]
+    pieces = call(relay_kernel, [VMEM], [shape(n, *piece) for n in sizes], (u2,))
     pieces = [across(p, 1) for p in pieces]
+    left = call(place_kernel, [SMEM] + [VMEM] * 2, [shape(*left.shape)], (meta, u2, left), aliases={2: 0})[0]
     both = [shape(*strips.shape), shape(*left.shape)]
     strips, left = call(
-        complete_kernel, [SMEM] * 2 + [VMEM] * (len(pieces) + 2), both, (meta, pattern, *pieces, strips, left),
-        aliases={2 + len(pieces): 0, 3 + len(pieces): 1},
+        complete_kernel, [SMEM] + [VMEM] * (len(pieces) + 2), both, (meta, *pieces, strips, left),
+        aliases={1 + len(pieces): 0, 2 + len(pieces): 1},
     )
     work = 2 * width * BAND * 128 * 128 * 32
     low, strips = call(
@@ -298,20 +278,18 @@
         (*tables, low, far, close, left), flops=2 * slots * ROWS * ROWS * 128 * 128 * 32,
     )
     close_in = shifted(close, 1)
-    far, after, close_in, partial = lax.optimization_barrier((far, after, close_in, partial))
+    far, after, partial = lax.optimization_barrier((far, after, partial))
     far_in = shifted(far, 1)
 
     def rest(rows, places, halos, partial, strips):
         *own, strips = call(
             outer_kernel(rows, places, [p for p, _ in halos]), [SMEM] * 3 + [VMEM] * (3 + len(halos)),
             [shape(len(rows), share, *piece)] * 4 + [shape(*strips.shape)],
-            (*tables, *(h for _, h in halos), left, partial, strips), flops=work * len(rows) // 2,
-            aliases={5 + len(halos): 4},
+            (*tables, *(h for _, h in halos), left, partial, strips), aliases={5 + len(halos): 4}, free=True,
         )
         return [own[0], *(across(own[b], b) for b in (1, 2, 3))], strips
 
     late, strips = rest(LATE, [*CLOSE, *AFTER], ((AFTER, after), (CLOSE, close_in)), partial, strips)
-    late, partial = lax.optimization_barrier((late, partial))
     early, _ = rest(EARLY, [*FAR, *CLOSE], ((FAR, far_in),), partial, strips)
 
     result = shape(ROWS, share, 128, 128, dtype=jnp.float32)

time: 69.4 us -> 64.8 us (0.934)
  Pallas kernels: 22.9 us -> 20.7 us
  starting transfers between devices: 21.3 us -> 19.2 us
    ppermute x11, waiting for transfers between devices: 15.1 us -> 3.95 us  [across(): return lax.ppermute(x, 'col', [(c, c ^ bits) for c in range(4)])]
    ppermute x7, waiting for transfers between devices: 7.86 us -> 18.7 us  [shifted(): lax.ppermute(x, ('row', 'layer'), [(g, (g + d) % groups) for g in range(g...]
    ppermute x7, starting transfers between devices: 13.8 us -> 11.6 us  [shifted(): lax.ppermute(x, ('row', 'layer'), [(g, (g + d) % groups) for g in range(g...]
    pallas_call x11 -> x12, Pallas kernels: 22.9 us -> 20.7 us  [call(): pl.pallas_call(kernel, out_shape=outs, in_specs=specs, out_specs=out_spec...]
  transfers between devices with their start and end apart: 18 -> 18, of which waited for: 9 -> 8; matrix products, arithmetic and copies ran while one was open for 0% -> 0% of each run, Pallas kernels for 25% -> 24%
where the time goes in v6:
time: 64.8 us; the launch traced here: 64.6 us
  waiting for transfers between devices  22.6 us (35%)
  Pallas kernels  20.7 us (32%)
  starting transfers between devices  19.2 us (30%)
  local copies, waits for them, and re-layouts  1.82 us (3%)
    pallas_call x12, Pallas kernels, call(): pl.pallas_call(kernel, out_shape=outs, in_specs=specs, out_specs=out_spec...  20.7 us
    ppermute x7, waiting for transfers between devices, shifted(): lax.ppermute(x, ('row', 'layer'), [(g, (g + d) % groups) for g in range(g...  18.7 us
    ppermute x7, starting transfers between devices, shifted(): lax.ppermute(x, ('row', 'layer'), [(g, (g + d) % groups) for g in range(g...  11.6 us
    ppermute x11, starting transfers between devices, across(): return lax.ppermute(x, 'col', [(c, c ^ bits) for c in range(4)])  7.59 us
    ppermute x11, waiting for transfers between devices, across(): return lax.ppermute(x, 'col', [(c, c ^ bits) for c in range(4)])  3.95 us
    unnamed x8, local copies, waits for them, and re-layouts  1.82 us
  transfers between devices with their start and end apart: 18, of which 8 were waited for; matrix products, arithmetic and copies ran while one was open for 0% of the time, Pallas kernels for 24%

profile of v6, /device:TPU:0, one launch (start us, length us, event | category | flops | bytes accessed | tf_op | source)
XLA Modules:
  0.0 64.6 jit_solution(3673109967474524553)
XLA Ops:
  0.0 0.1 pad_add_fusion.meta
  0.1 0.0 copy-start
  0.1 1.1 %copy-done = bf16[8,11,32,128]{3,2,1,0:T(8,128)(2,1)S(1)} copy-done((bf16[8,11,32,128]{3,2,1,0:T(8,128)(2,1)S(1)}, bf16[8,11,32,128]{3,2,1,0:T(8,128)(2,1)}, u32[]{:S(2)}) %copy-start) | copy-done | bytes 720920
  1.2 0.0 copy-start.3
  1.2 0.7 %copy-done.3 = s32[64,11]{0,1:T(8,128)S(1)} copy-done((s32[64,11]{0,1:T(8,128)S(1)}, s32[64,11]{0,1:T(8,128)}, u32[]{:S(2)}) %copy-start.3) | copy-done | bytes 2840
  1.9 1.2 %shard_map.46 = (bf16[37,32,128]{2,1,0:T(8,128)(2,1)S(1)}, bf16[37,32,128]{2,1,0:T(8,128)(2,1)S(1)}, bf16[3,32,128]{2,1,0:T(8,128)(2,1)S(1)}, bf16[3,32,128]{2,1...) custom-call(s32[2]{0:T(128)S(1)} %pad_add_fusion.meta, ...), custom_call_target="tpu_custom_call" | custom-call | bytes 2681608 | tf_op jit(solution)/shard_map/pallas_call | solution.py:211
  3.1 0.5 collective-permute-start.3
  3.6 2.6 %collective-permute-start.2 = (bf16[63,32,128]{2,1,0:T(8,128)(2,1)S(1)}, bf16[63,32,128]{2,1,0:T(8,128)(2,1)S(1)}, u32[]{:S(2)}, u32[]{:S(2)}) collective-permute-start(bf16[63,32,128]{2,1,0:T(8,128)(2,1)S(1)} %get-tuple-element.42.upper), channel_id=1, source_target_pairs={{0,4},{2,6},{4,0},{6,2},{1,5},{3,7},{5,1},{7,3},{8,12},{10,14},{12... | collective-permute-start | bytes 1548296 | tf_op jit(solution)/shard_map/ppermute | solution.py:239
  6.2 1.5 %collective-permute-start = (bf16[37,32,128]{2,1,0:T(8,128)(2,1)S(1)}, bf16[37,32,128]{2,1,0:T(8,128)(2,1)S(1)}, u32[]{:S(2)}, u32[]{:S(2)}) collective-permute-start(bf16[37,32,128]{2,1,0:T(8,128)(2,1)S(1)} %get-tuple-element.40), channel_id=1, source_target_pairs={{0,1},{1,8},{8,9},{9,16},{16,17},{17,24},{24,25},{25,0},{2,3},{3,1... | collective-permute-start | bytes 909320 | tf_op jit(solution)/shard_map/ppermute | solution.py:236
  7.7 3.2 %collective-permute-start.1 = (bf16[37,32,128]{2,1,0:T(8,128)(2,1)S(1)}, bf16[37,32,128]{2,1,0:T(8,128)(2,1)S(1)}, u32[]{:S(2)}, u32[]{:S(2)}) collective-permute-start(bf16[37,32,128]{2,1,0:T(8,128)(2,1)S(1)} %get-tuple-element.41), channel_id=1, source_target_pairs={{0,25},{1,0},{8,1},{9,8},{16,9},{17,16},{24,17},{25,24},{2,27},{3,... | collective-permute-start | bytes 909320 | tf_op jit(solution)/shard_map/ppermute | solution.py:236
  10.9 0.0 collective-permute-start.4
  10.9 0.0 collective-permute-done.3.u1
  10.9 3.8 %collective-permute-start.5 = (bf16[3,32,128]{2,1,0:T(8,128)(2,1)S(1)}, bf16[3,32,128]{2,1,0:T(8,128)(2,1)S(1)}, u32[]{:S(2)}, u32[]{:S(2)}) collective-permute-start(bf16[3,32,128]{2,1,0:T(8,128)(2,1)S(1)} %get-tuple-element.46), channel_id=1, source_target_pairs={{0,24},{1,25},{8,0},{9,1},{16,8},{17,9},{24,16},{25,17},{2,26},{3,... | collective-permute-start | bytes 73736 | tf_op jit(solution)/shard_map/ppermute | solution.py:236
  14.7 1.8 %shard_map.47 = (bf16[28,18,32,128]{3,2,1,0:T(8,128)(2,1)S(1)}, bf16[8,18,128,128]{3,2,1,0:T(8,128)(2,1)S(1)}) custom-call(s32[2]{0:T(128)S(1)} %pad_add_fusion.meta, bf16[8,12,32,128]{3,2,1,0:T(8,128)(2,1)S(1)} %get-tuple-element.43.band, bf16[63,32,128]{2,1,0:T(8,128)(2,1)S(1)} %get-tuple-element.42.upper, bf16[63,32,128]{2,1,0:T(8,128)(2,1)S(1)} %collective-permute-done.3.u1), custom_call_target="tpu_custom_call" | custom-call | bytes 10665992 | tf_op jit(solution)/shard_map/pallas_call | solution.py:211
  16.5 4.0 %collective-permute-done.4.h2 = bf16[3,32,128]{2,1,0:T(8,128)(2,1)S(1)} collective-permute-done((bf16[3,32,128]{2,1,0:T(8,128)(2,1)S(1)}, bf16[3,32,128]{2,1,0:T(8,128)(2,1)S(1)}, u32[]{:S(2)}, u32[]{:S(2)}) %collective-permute-start.4) | collective-permute-done | bytes 24608 | tf_op jit(solution)/shard_map/ppermute | solution.py:236
  20.5 0.0 collective-permute-done.5.h3
  20.5 0.0 collective-permute-done.2.u2
  20.5 0.1 collective-permute-start.6
  20.6 0.5 collective-permute-start.7
  21.1 0.1 collective-permute-start.8
  21.2 0.6 shard_map.49.refs_4_
  21.8 0.0 copy-start.1
  21.8 0.2 collective-permute-done.6.refs_0_
  22.0 0.2 collective-permute-done.7.refs_1_
  22.3 0.3 collective-permute-done.8.refs_2_
  22.5 1.0 %shard_map.50 = (bf16[28,18,32,128]{3,2,1,0:T(8,128)(2,1)S(1)}, bf16[8,18,128,128]{3,2,1,0:T(8,128)(2,1)S(1)}) custom-call(s32[2]{0:T(128)S(1)} %pad_add_fusion.meta, bf16[21,32,128]{2,1,0:T(8,128)(2,1)S(1)} %collective-permute-done.6.refs_0_, bf16[21,32,128]{2,1,0:T(8,128)(2,1)S(1)} %collective-permute-done.7.refs_1_, ...), custom_call_target="tpu_custom_call", output_to_operand_aliasing={{0}: (4, {}), {1}: (5, {})} | custom-call | bytes 18210824 | tf_op jit(solution)/shard_map/pallas_call | solution.py:211
  23.5 0.0 collective-permute-done.h0
  23.6 0.0 collective-permute-done.1.h1
  23.6 0.0 copy-done.1
  23.6 2.3 %shard_map.51 = (bf16[5,12,32,128]{3,2,1,0:T(8,128)(2,1)S(1)}, bf16[28,18,32,128]{3,2,1,0:T(8,128)(2,1)S(1)}) custom-call(s32[2]{0:T(128)S(1)} %pad_add_fusion.meta, s32[12,64]{1,0:T(8,128)S(1)} %bitcast.5, bf16[37,32,128]{2,1,0:T(8,128)(2,1)S(1)} %collective-permute-done.h0, ...), custom_call_target="tpu_custom_call", output_to_operand_aliasing={{1}: (7, {})} | custom-call | flops 692060160 | bytes 14126088 | tf_op jit(solution)/shard_map/pallas_call | solution.py:211
  25.9 0.0 copy-start.2
  25.9 3.0 %collective-permute-start.9 = (bf16[5,12,32,128]{3,2,1,0:T(8,128)(2,1)S(1)}, bf16[5,12,32,128]{3,2,1,0:T(8,128)(2,1)S(1)}, u32[]{:S(2)}, u32[]{:S(2)}) collective-permute-start(bf16[5,12,32,128]{3,2,1,0:T(8,128)(2,1)S(1)} %get-tuple-element.57.low), channel_id=1, source_target_pairs={{0,25},{1,0},{8,1},{9,8},{16,9},{17,16},{24,17},{25,24},{2,27},{3,... | collective-permute-start | bytes 1474568 | tf_op jit(solution)/shard_map/ppermute | solution.py:236
  28.8 1.7 %shard_map.52 = (bf16[3,12,32,128]{3,2,1,0:T(8,128)(2,1)S(1)}, bf16[2,12,32,128]{3,2,1,0:T(8,128)(2,1)S(1)}) custom-call(s32[2]{0:T(128)S(1)} %pad_add_fusion.meta, s32[12,64]{1,0:T(8,128)S(1)} %bitcast.6, bf16[5,12,32,128]{3,2,1,0:T(8,128)(2,1)S(1)} %get-tuple-element.57.low, bf16[28,18,32,128]{3,2,1,0:T(8,128)(2,1)S(1)} %get-tuple-element.58.strips, ...), custom_call_target="tpu_custom_call" | custom-call | flops 415236096 | bytes 9833480 | tf_op jit(solution)/shard_map/pallas_call | solution.py:211
  30.5 0.1 collective-permute-start.11
  30.6 0.0 copy-done.2
  30.6 5.4 %shard_map.53 = (bf16[38,18,32,128]{3,2,1,0:T(8,128)(2,1)S(1)}, f32[8,16,32,128]{3,2,1,0:T(8,128)S(1)}) custom-call(s32[2]{0:T(128)S(1)} %pad_add_fusion.meta, s32[12,64]{1,0:T(8,128)S(1)} %bitcast.7, s32[16,64]{1,0:T(8,128)S(1)} %bitcast.10, bf16[5,12,32,128]{3,2,1,0:T(8,128)(2,1)S(1)} %get-tuple-element.57.low, ...), custom_call_target="tpu_custom_call" | custom-call | flops 1073741824 | bytes 13409288 | tf_op jit(solution)/shard_map/pallas_call | solution.py:211
  36.0 7.5 %collective-permute-done.9.refs_0_ = bf16[5,12,32,128]{3,2,1,0:T(8,128)(2,1)S(1)} collective-permute-done((bf16[5,12,32,128]{3,2,1,0:T(8,128)(2,1)S(1)}, bf16[5,12,32,128]{3,2,1,0:T(8,128)(2,1)S(1)}, u32[]{:S(2)}, u32[]{:S(2)}) %collective-permute-start.9) | collective-permute-done | bytes 491552 | tf_op jit(solution)/shard_map/ppermute | solution.py:236
  43.5 0.0 collective-permute-start.10
  43.5 0.0 collective-permute-done.11.refs_1_
  43.5 1.9 %shard_map.54 = (bf16[5,4,32,128]{3,2,1,0:T(8,128)(2,1)S(1)}, bf16[5,4,32,128]{3,2,1,0:T(8,128)(2,1)S(1)}, bf16[5,4,32,128]{3,2,1,0:T(8,128)(2,1)S(1)}, bf16[5,4...) custom-call(s32[2]{0:T(128)S(1)} %pad_add_fusion.meta, ...), custom_call_target="tpu_custom_call", output_to_operand_aliasing={{4}: (7, {})} | custom-call | tf_op jit(solution)/shard_map/pallas_call | solution.py:211
  45.4 0.1 collective-permute-start.15
  45.5 0.6 collective-permute-start.16
  46.1 1.3 %collective-permute-start.17 = (bf16[5,4,32,128]{3,2,1,0:T(8,128)(2,1)S(1)}, bf16[5,4,32,128]{3,2,1,0:T(8,128)(2,1)S(1)}, u32[]{:S(2)}, u32[]{:S(2)}) collective-permute-start(bf16[5,4,32,128]{3,2,1,0:T(8,128)(2,1)S(1)} %get-tuple-element.74), channel_id=1, source_target_pairs={{0,6},{2,4},{4,2},{6,0},{1,7},{3,5},{5,3},{7,1},{8,14},{10,12},{12... | collective-permute-start | bytes 491528 | tf_op jit(solution)/shard_map/ppermute | solution.py:239
  47.3 7.2 %collective-permute-done.10.refs_0_ = bf16[3,12,32,128]{3,2,1,0:T(8,128)(2,1)S(1)} collective-permute-done((bf16[3,12,32,128]{3,2,1,0:T(8,128)(2,1)S(1)}, bf16[3,12,32,128]{3,2,1,0:T(8,128)(2,1)S(1)}, u32[]{:S(2)}, u32[]{:S(2)}) %collective-permute-start.10) | collective-permute-done | bytes 294944 | tf_op jit(solution)/shard_map/ppermute | solution.py:236
  54.5 1.5 %shard_map.55 = (bf16[3,4,32,128]{3,2,1,0:T(8,128)(2,1)S(1)}, bf16[3,4,32,128]{3,2,1,0:T(8,128)(2,1)S(1)}, bf16[3,4,32,128]{3,2,1,0:T(8,128)(2,1)S(1)}, bf16[3,4...) custom-call(s32[2]{0:T(128)S(1)} %pad_add_fusion.meta, ...), custom_call_target="tpu_custom_call", output_to_operand_aliasing={{4}: (6, {})} | custom-call | tf_op jit(solution)/shard_map/pallas_call | solution.py:211
  56.0 0.1 collective-permute-start.12
  56.1 0.6 collective-permute-start.13
  56.7 0.0 collective-permute-done.15.refs_1_
  56.7 1.3 %collective-permute-start.14 = (bf16[3,4,32,128]{3,2,1,0:T(8,128)(2,1)S(1)}, bf16[3,4,32,128]{3,2,1,0:T(8,128)(2,1)S(1)}, u32[]{:S(2)}, u32[]{:S(2)}) collective-permute-start(bf16[3,4,32,128]{3,2,1,0:T(8,128)(2,1)S(1)} %get-tuple-element.70), channel_id=1, source_target_pairs={{0,6},{2,4},{4,2},{6,0},{1,7},{3,5},{5,3},{7,1},{8,14},{10,12},{12... | collective-permute-start | bytes 294920 | tf_op jit(solution)/shard_map/ppermute | solution.py:239
  58.0 0.0 collective-permute-done.16.refs_2_
  58.0 0.0 collective-permute-done.17.refs_3_
  58.0 1.8 %shard_map.56.refs_4_ = f32[8,4,128,128]{3,2,1,0:T(8,128)} custom-call(s32[2]{0:T(128)S(1)} %pad_add_fusion.meta, bf16[5,4,32,128]{3,2,1,0:T(8,128)(2,1)S(1)} %get-tuple-element.71.refs_0_, bf16[5,4,32,128]{3,2,1,0:T(8,128)(2,1)S(1)} %collective-permute-done.15.refs_1_, bf16[5,4,32,128]{3,2,1,0:T(8,128)(2,1)S(1)} %collective-permute-done.16.refs_2_, ...), custom_call_target="tpu_custom_call" | custom-call | bytes 2752520 | tf_op jit(solution)/shard_map/pallas_call | solution.py:211
  59.8 0.0 collective-permute-done.12.refs_1_
  59.8 2.0 %collective-permute-done.13.refs_2_ = bf16[3,4,32,128]{3,2,1,0:T(8,128)(2,1)S(1)} collective-permute-done((bf16[3,4,32,128]{3,2,1,0:T(8,128)(2,1)S(1)}, bf16[3,4,32,128]{3,2,1,0:T(8,128)(2,1)S(1)}, u32[]{:S(2)}, u32[]{:S(2)}) %collective-permute-start.13) | collective-permute-done | bytes 98336 | tf_op jit(solution)/shard_map/ppermute | solution.py:239
  61.8 1.2 %collective-permute-done.14.refs_3_ = bf16[3,4,32,128]{3,2,1,0:T(8,128)(2,1)S(1)} collective-permute-done((bf16[3,4,32,128]{3,2,1,0:T(8,128)(2,1)S(1)}, bf16[3,4,32,128]{3,2,1,0:T(8,128)(2,1)S(1)}, u32[]{:S(2)}, u32[]{:S(2)}) %collective-permute-start.14) | collective-permute-done | bytes 98336 | tf_op jit(solution)/shard_map/ppermute | solution.py:239
  63.0 1.6 %shard_map.57 = f32[8,4,128,128]{3,2,1,0:T(8,128)} custom-call(s32[2]{0:T(128)S(1)} %pad_add_fusion.meta, bf16[3,4,32,128]{3,2,1,0:T(8,128)(2,1)S(1)} %get-tuple-element.67.refs_0_, bf16[3,4,32,128]{3,2,1,0:T(8,128)(2,1)S(1)} %collective-permute-done.12.refs_1_, ...), custom_call_target="tpu_custom_call", output_to_operand_aliasing={{}: (5, {})} | custom-call | bytes 4587528 | tf_op jit(solution)/shard_map/pallas_call | solution.py:211
  (1 shorter events, 0.0 us)
Async XLA Ops:
  0.1 1.1 %copy-start = (bf16[8,11,32,128]{3,2,1,0:T(8,128)(2,1)S(1)}, bf16[8,11,32,128]{3,2,1,0:T(8,128)(2,1)}, u32[]{:S(2)}) copy-start(bf16[8,11,32,128]{3,2,1,0:T(8,128)(2,1)} %density.1) | copy-start | bytes 2162692
  1.2 0.7 %copy-start.3 = (s32[64,11]{0,1:T(8,128)S(1)}, s32[64,11]{0,1:T(8,128)}, u32[]{:S(2)}) copy-start(s32[64,11]{0,1:T(8,128)} %param.5) | copy-start | bytes 8452
  3.1 7.8 %collective-permute-start.3 = (bf16[63,32,128]{2,1,0:T(8,128)(2,1)S(1)}, bf16[63,32,128]{2,1,0:T(8,128)(2,1)S(1)}, u32[]{:S(2)}, u32[]{:S(2)}) collective-permute-start(bf16[63,32,128]{2,1,0:T(8,128)(2,1)S(1)} %get-tuple-element.42.upper), channel_id=1, source_target_pairs={{0,2},{2,0},{4,6},{6,4},{1,3},{3,1},{5,7},{7,5},{8,10},{10,8},{12,... | collective-permute-start | bytes 1548296 | tf_op jit(solution)/shard_map/ppermute | solution.py:239
  3.6 16.9 %collective-permute-start.2 = (bf16[63,32,128]{2,1,0:T(8,128)(2,1)S(1)}, bf16[63,32,128]{2,1,0:T(8,128)(2,1)S(1)}, u32[]{:S(2)}, u32[]{:S(2)}) collective-permute-start(bf16[63,32,128]{2,1,0:T(8,128)(2,1)S(1)} %get-tuple-element.42.upper), channel_id=1, source_target_pairs={{0,4},{2,6},{4,0},{6,2},{1,5},{3,7},{5,1},{7,3},{8,12},{10,14},{12... | collective-permute-start | bytes 1548296 | tf_op jit(solution)/shard_map/ppermute | solution.py:239
  6.2 17.4 %collective-permute-start = (bf16[37,32,128]{2,1,0:T(8,128)(2,1)S(1)}, bf16[37,32,128]{2,1,0:T(8,128)(2,1)S(1)}, u32[]{:S(2)}, u32[]{:S(2)}) collective-permute-start(bf16[37,32,128]{2,1,0:T(8,128)(2,1)S(1)} %get-tuple-element.40), channel_id=1, source_target_pairs={{0,1},{1,8},{8,9},{9,16},{16,17},{17,24},{24,25},{25,0},{2,3},{3,1... | collective-permute-start | bytes 909320 | tf_op jit(solution)/shard_map/ppermute | solution.py:236
  7.7 15.9 %collective-permute-start.1 = (bf16[37,32,128]{2,1,0:T(8,128)(2,1)S(1)}, bf16[37,32,128]{2,1,0:T(8,128)(2,1)S(1)}, u32[]{:S(2)}, u32[]{:S(2)}) collective-permute-start(bf16[37,32,128]{2,1,0:T(8,128)(2,1)S(1)} %get-tuple-element.41), channel_id=1, source_target_pairs={{0,25},{1,0},{8,1},{9,8},{16,9},{17,16},{24,17},{25,24},{2,27},{3,... | collective-permute-start | bytes 909320 | tf_op jit(solution)/shard_map/ppermute | solution.py:236
  10.9 9.6 %collective-permute-start.4 = (bf16[3,32,128]{2,1,0:T(8,128)(2,1)S(1)}, bf16[3,32,128]{2,1,0:T(8,128)(2,1)S(1)}, u32[]{:S(2)}, u32[]{:S(2)}) collective-permute-start(bf16[3,32,128]{2,1,0:T(8,128)(2,1)S(1)} %get-tuple-element.45), channel_id=1, source_target_pairs={{0,8},{1,9},{8,16},{9,17},{16,24},{17,25},{24,0},{25,1},{2,10},{3,... | collective-permute-start | bytes 73736 | tf_op jit(solution)/shard_map/ppermute | solution.py:236
  10.9 9.6 %collective-permute-start.5 = (bf16[3,32,128]{2,1,0:T(8,128)(2,1)S(1)}, bf16[3,32,128]{2,1,0:T(8,128)(2,1)S(1)}, u32[]{:S(2)}, u32[]{:S(2)}) collective-permute-start(bf16[3,32,128]{2,1,0:T(8,128)(2,1)S(1)} %get-tuple-element.46), channel_id=1, source_target_pairs={{0,24},{1,25},{8,0},{9,1},{16,8},{17,9},{24,16},{25,17},{2,26},{3,... | collective-permute-start | bytes 73736 | tf_op jit(solution)/shard_map/ppermute | solution.py:236
  20.5 1.5 %collective-permute-start.6 = (bf16[21,32,128]{2,1,0:T(8,128)(2,1)S(1)}, bf16[21,32,128]{2,1,0:T(8,128)(2,1)S(1)}, u32[]{:S(2)}, u32[]{:S(2)}) collective-permute-start(bf16[21,32,128]{2,1,0:T(8,128)(2,1)S(1)} %get-tuple-element.50), channel_id=1, source_target_pairs={{0,2},{2,0},{4,6},{6,4},{1,3},{3,1},{5,7},{7,5},{8,10},{10,8},{12,... | collective-permute-start | bytes 516104 | tf_op jit(solution)/shard_map/ppermute | solution.py:239
  20.6 1.6 %collective-permute-start.7 = (bf16[21,32,128]{2,1,0:T(8,128)(2,1)S(1)}, bf16[21,32,128]{2,1,0:T(8,128)(2,1)S(1)}, u32[]{:S(2)}, u32[]{:S(2)}) collective-permute-start(bf16[21,32,128]{2,1,0:T(8,128)(2,1)S(1)} %get-tuple-element.51), channel_id=1, source_target_pairs={{0,2},{2,0},{4,6},{6,4},{1,3},{3,1},{5,7},{7,5},{8,10},{10,8},{12,... | collective-permute-start | bytes 516104 | tf_op jit(solution)/shard_map/ppermute | solution.py:239
  21.1 1.4 %collective-permute-start.8 = (bf16[21,32,128]{2,1,0:T(8,128)(2,1)S(1)}, bf16[21,32,128]{2,1,0:T(8,128)(2,1)S(1)}, u32[]{:S(2)}, u32[]{:S(2)}) collective-permute-start(bf16[21,32,128]{2,1,0:T(8,128)(2,1)S(1)} %get-tuple-element.52), channel_id=1, source_target_pairs={{0,2},{2,0},{4,6},{6,4},{1,3},{3,1},{5,7},{7,5},{8,10},{10,8},{12,... | collective-permute-start | bytes 516104 | tf_op jit(solution)/shard_map/ppermute | solution.py:239
  21.8 1.8 %copy-start.1 = (s32[64,12]{0,1:T(8,128)S(1)}, s32[64,12]{0,1:T(8,128)}, u32[]{:S(2)}) copy-start(s32[64,12]{0,1:T(8,128)} %param.6) | copy-start | bytes 9220
  25.9 4.7 %copy-start.2 = (s32[64,16]{0,1:T(8,128)S(1)}, s32[64,16]{0,1:T(8,128)}, u32[]{:S(2)}) copy-start(s32[64,16]{0,1:T(8,128)} %param.7) | copy-start | bytes 12292
  25.9 17.6 %collective-permute-start.9 = (bf16[5,12,32,128]{3,2,1,0:T(8,128)(2,1)S(1)}, bf16[5,12,32,128]{3,2,1,0:T(8,128)(2,1)S(1)}, u32[]{:S(2)}, u32[]{:S(2)}) collective-permute-start(bf16[5,12,32,128]{3,2,1,0:T(8,128)(2,1)S(1)} %get-tuple-element.57.low), channel_id=1, source_target_pairs={{0,25},{1,0},{8,1},{9,8},{16,9},{17,16},{24,17},{25,24},{2,27},{3,... | collective-permute-start | bytes 1474568 | tf_op jit(solution)/shard_map/ppermute | solution.py:236
  30.5 13.0 %collective-permute-start.11 = (bf16[2,12,32,128]{3,2,1,0:T(8,128)(2,1)S(1)}, bf16[2,12,32,128]{3,2,1,0:T(8,128)(2,1)S(1)}, u32[]{:S(2)}, u32[]{:S(2)}) collective-permute-start(bf16[2,12,32,128]{3,2,1,0:T(8,128)(2,1)S(1)} %get-tuple-element.60.close), channel_id=1, source_target_pairs={{0,1},{1,8},{8,9},{9,16},{16,17},{17,24},{24,25},{25,0},{2,3},{3,1... | collective-permute-start | bytes 589832 | tf_op jit(solution)/shard_map/ppermute | solution.py:236
  43.5 11.0 %collective-permute-start.10 = (bf16[3,12,32,128]{3,2,1,0:T(8,128)(2,1)S(1)}, bf16[3,12,32,128]{3,2,1,0:T(8,128)(2,1)S(1)}, u32[]{:S(2)}, u32[]{:S(2)}) collective-permute-start(bf16[3,12,32,128]{3,2,1,0:T(8,128)(2,1)S(1)} %get-tuple-element.62.far), channel_id=1, source_target_pairs={{0,1},{1,8},{8,9},{9,16},{16,17},{17,24},{24,25},{25,0},{2,3},{3,1... | collective-permute-start | bytes 884744 | tf_op jit(solution)/shard_map/ppermute | solution.py:236
  45.4 11.3 %collective-permute-start.15 = (bf16[5,4,32,128]{3,2,1,0:T(8,128)(2,1)S(1)}, bf16[5,4,32,128]{3,2,1,0:T(8,128)(2,1)S(1)}, u32[]{:S(2)}, u32[]{:S(2)}) collective-permute-start(bf16[5,4,32,128]{3,2,1,0:T(8,128)(2,1)S(1)} %get-tuple-element.72), channel_id=1, source_target_pairs={{0,2},{2,0},{4,6},{6,4},{1,3},{3,1},{5,7},{7,5},{8,10},{10,8},{12,... | collective-permute-start | bytes 491528 | tf_op jit(solution)/shard_map/ppermute | solution.py:239
  45.5 12.5 %collective-permute-start.16 = (bf16[5,4,32,128]{3,2,1,0:T(8,128)(2,1)S(1)}, bf16[5,4,32,128]{3,2,1,0:T(8,128)(2,1)S(1)}, u32[]{:S(2)}, u32[]{:S(2)}) collective-permute-start(bf16[5,4,32,128]{3,2,1,0:T(8,128)(2,1)S(1)} %get-tuple-element.73), channel_id=1, source_target_pairs={{0,4},{2,6},{4,0},{6,2},{1,5},{3,7},{5,1},{7,3},{8,12},{10,14},{12... | collective-permute-start | bytes 491528 | tf_op jit(solution)/shard_map/ppermute | solution.py:239
  46.1 11.9 %collective-permute-start.17 = (bf16[5,4,32,128]{3,2,1,0:T(8,128)(2,1)S(1)}, bf16[5,4,32,128]{3,2,1,0:T(8,128)(2,1)S(1)}, u32[]{:S(2)}, u32[]{:S(2)}) collective-permute-start(bf16[5,4,32,128]{3,2,1,0:T(8,128)(2,1)S(1)} %get-tuple-element.74), channel_id=1, source_target_pairs={{0,6},{2,4},{4,2},{6,0},{1,7},{3,5},{5,3},{7,1},{8,14},{10,12},{12... | collective-permute-start | bytes 491528 | tf_op jit(solution)/shard_map/ppermute | solution.py:239
  56.0 3.7 %collective-permute-start.12 = (bf16[3,4,32,128]{3,2,1,0:T(8,128)(2,1)S(1)}, bf16[3,4,32,128]{3,2,1,0:T(8,128)(2,1)S(1)}, u32[]{:S(2)}, u32[]{:S(2)}) collective-permute-start(bf16[3,4,32,128]{3,2,1,0:T(8,128)(2,1)S(1)} %get-tuple-element.68), channel_id=1, source_target_pairs={{0,2},{2,0},{4,6},{6,4},{1,3},{3,1},{5,7},{7,5},{8,10},{10,8},{12,... | collective-permute-start | bytes 294920 | tf_op jit(solution)/shard_map/ppermute | solution.py:239
  56.1 5.7 %collective-permute-start.13 = (bf16[3,4,32,128]{3,2,1,0:T(8,128)(2,1)S(1)}, bf16[3,4,32,128]{3,2,1,0:T(8,128)(2,1)S(1)}, u32[]{:S(2)}, u32[]{:S(2)}) collective-permute-start(bf16[3,4,32,128]{3,2,1,0:T(8,128)(2,1)S(1)} %get-tuple-element.69), channel_id=1, source_target_pairs={{0,4},{2,6},{4,0},{6,2},{1,5},{3,7},{5,1},{7,3},{8,12},{10,14},{12... | collective-permute-start | bytes 294920 | tf_op jit(solution)/shard_map/ppermute | solution.py:239
  56.7 6.3 %collective-permute-start.14 = (bf16[3,4,32,128]{3,2,1,0:T(8,128)(2,1)S(1)}, bf16[3,4,32,128]{3,2,1,0:T(8,128)(2,1)S(1)}, u32[]{:S(2)}, u32[]{:S(2)}) collective-permute-start(bf16[3,4,32,128]{3,2,1,0:T(8,128)(2,1)S(1)} %get-tuple-element.70), channel_id=1, source_target_pairs={{0,6},{2,4},{4,2},{6,0},{1,7},{3,5},{5,3},{7,1},{8,14},{10,12},{12... | collective-permute-start | bytes 294920 | tf_op jit(solution)/shard_map/ppermute | solution.py:239

commit v7 on v6

--- a/solution.py
+++ b/solution.py
@@ -30,15 +30,17 @@
 )
 UPPER = [(j, o) for j, o in OWN if o >= RADIUS or j + o < RADIUS]
 LOWER = [(m, j) for m in range(ROWS) for j in range(m + 1, min(ROWS, m + RADIUS + 1))]
-LATE = range(ROWS - RADIUS, ROWS)
-EARLY = range(0, ROWS - RADIUS)
+EARLY = range(0, 2 * RADIUS - ROWS)
+LATE = range(2 * RADIUS - ROWS, ROWS)
 AFTER = range(RADIUS + ROWS, NEAR)
-CLOSE = range(ROWS - RADIUS, RADIUS)
-FAR = range(0, ROWS - RADIUS)
+CLOSE = range(2 * RADIUS - ROWS, RADIUS)
+FAR = range(0, 2 * RADIUS - ROWS)
 RELAY = 21
 
 
 def wrapped(value, total):
+    if total & (total - 1) == 0:
+        return value & (total - 1)
     return jnp.where(value < 0, value + total, jnp.where(value >= total, value - total, value))
 
 
@@ -111,7 +113,7 @@
     return acc.reshape(len(targets), 32, 128).astype(strips.dtype)
 
 
-def low_kernel(meta, kept, h0, h1, h2, h3, left, strips_in, low, strips):
+def low_kernel(meta, kept, h0, h1, h2, h3, left, strips_in, low, far, strips):
     del strips_in
     first = meta[1]
     for halo, entries, shift in zip((h0, h1, h2, h3), LISTS, SHIFTS):
@@ -119,19 +121,15 @@
             row = j - shift * ROWS
             strips[row + 2 * RADIUS, row + o] = halo[e]
     for i in range(RADIUS):
-        low[i] = square_row(kept, strips, left, i, first)
-
-
-def high_kernel(meta, kept, low, strips, left, far, close):
-    first = meta[1]
+        row = square_row(kept, strips, left, i, first)
+        low[i] = row
+        if i >= ROWS - RADIUS:
+            far[i - ROWS + RADIUS] = row
+
+
+def high_kernel(meta, kept, strips, left, close):
     for i in range(RADIUS, ROWS):
-        row = square_row(kept, strips, left, i, first)
-        if i < ROWS - len(CLOSE):
-            far[i - ROWS + RADIUS] = row
-        else:
-            close[i - ROWS + len(CLOSE)] = row
-    for i in range(ROWS - RADIUS, RADIUS):
-        far[i - ROWS + RADIUS] = low[i]
+        close[i - RADIUS] = square_row(kept, strips, left, i, meta[1])
 
 
 def strip_of(table, s, row, first):
@@ -149,12 +147,11 @@
             strips[strip_of(kept, s, first - RADIUS + p, first), p] = rows[k, s]
 
 
-def inner_kernel(meta, kept, cube, low, far, close, left, strips, partial):
+def inner_kernel(meta, kept, cube, low, close, left, strips, partial):
     col, first = meta[0], meta[1]
     strips[...] = jnp.zeros_like(strips)
     insert_rows(strips, kept, low, range(RADIUS, 2 * RADIUS), first)
-    insert_rows(strips, kept, far, range(ROWS, ROWS + len(FAR)), first)
-    insert_rows(strips, kept, close, range(RADIUS + ROWS - len(CLOSE), RADIUS + ROWS), first)
+    insert_rows(strips, kept, close, range(2 * RADIUS, RADIUS + ROWS), first)
     share = cube.shape[0] // 4
 
     @pl.loop(0, ROWS)
@@ -166,7 +163,16 @@
             partial[i, e] = 3.0 * mine - 2.0 * acc[e * 32 : (e + 1) * 32]
 
 
-def outer_kernel(rows, places, arrived):
+def bridge_kernel(meta, kept, cube, left, partial, strips, early):
+    share = cube.shape[0] // 4
+    for n, i in enumerate(EARLY):
+        targets = cube_targets(cube, i, meta[0], meta[1], share)
+        acc = gather_dot(strips, left, targets, i, CLOSE)
+        for e in range(len(targets)):
+            early[n, e] = partial[i, e] - 2.0 * acc[e * 32 : (e + 1) * 32]
+
+
+def outer_kernel(rows, start, places, arrived):
     def kernel(meta, kept, cube, *refs):
         halos, (left, partial, _, o0, o1, o2, o3, strips) = refs[:-8], refs[-8:]
         col, first = meta[0], meta[1]
@@ -177,7 +183,7 @@
             targets = cube_targets(cube, i, col, first, share)
             acc = gather_dot(strips, left, targets, i, [p for p in places if i <= p < i + BAND])
             for e in range(len(targets)):
-                piece = partial[i, e] - 2.0 * acc[e * 32 : (e + 1) * 32]
+                piece = partial[i - start, e] - 2.0 * acc[e * 32 : (e + 1) * 32]
                 (o0, o1, o2, o3)[e // share][n, e % share] = piece.astype(o0.dtype)
 
     return kernel
@@ -261,36 +267,41 @@
         aliases={1 + len(pieces): 0, 2 + len(pieces): 1},
     )
     work = 2 * width * BAND * 128 * 128 * 32
-    low, strips = call(
-        low_kernel, [SMEM] * 2 + [VMEM] * 6, [shape(RADIUS, width, *piece), both[0]],
-        (meta, kept, *halos, left, strips), flops=work * RADIUS, aliases={7: 1},
+    low, far, strips = call(
+        low_kernel, [SMEM] * 2 + [VMEM] * 6,
+        [shape(RADIUS, width, *piece), shape(len(FAR), width, *piece), both[0]],
+        (meta, kept, *halos, left, strips), flops=work * RADIUS, aliases={7: 2},
     )
     after = shifted(low, -1)
-    far, close = call(
-        high_kernel, [SMEM] * 2 + [VMEM] * 3,
-        [shape(len(FAR), width, *piece), shape(len(CLOSE), width, *piece)],
-        (meta, kept, low, strips, left), flops=work * (ROWS - RADIUS),
-    )
+    close = call(
+        high_kernel, [SMEM] * 2 + [VMEM] * 2, [shape(len(CLOSE), width, *piece)],
+        (meta, kept, strips, left), flops=work * (ROWS - RADIUS),
+    )[0]
+    close_in = shifted(close, 1)
+
     tables = (meta, kept, cube)
     strips, partial = call(
-        inner_kernel, [SMEM] * 3 + [VMEM] * 4,
+        inner_kernel, [SMEM] * 3 + [VMEM] * 3,
         [shape(REACH, NEAR, *piece), shape(ROWS, slots, *piece, dtype=jnp.float32)],
-        (*tables, low, far, close, left), flops=2 * slots * ROWS * ROWS * 128 * 128 * 32,
-    )
-    close_in = shifted(close, 1)
+        (*tables, low, close, left), flops=2 * slots * ROWS * ROWS * 128 * 128 * 32,
+    )
     far, after, partial = lax.optimization_barrier((far, after, partial))
     far_in = shifted(far, 1)
 
-    def rest(rows, places, halos, partial, strips):
+    def rest(rows, start, places, halos, partial, strips):
         *own, strips = call(
-            outer_kernel(rows, places, [p for p, _ in halos]), [SMEM] * 3 + [VMEM] * (3 + len(halos)),
+            outer_kernel(rows, start, places, [p for p, _ in halos]), [SMEM] * 3 + [VMEM] * (3 + len(halos)),
             [shape(len(rows), share, *piece)] * 4 + [shape(*strips.shape)],
             (*tables, *(h for _, h in halos), left, partial, strips), aliases={5 + len(halos): 4}, free=True,
         )
         return [own[0], *(across(own[b], b) for b in (1, 2, 3))], strips
 
-    late, strips = rest(LATE, [*CLOSE, *AFTER], ((AFTER, after), (CLOSE, close_in)), partial, strips)
-    early, _ = rest(EARLY, [*FAR, *CLOSE], ((FAR, far_in),), partial, strips)
+    late, strips = rest(LATE, 0, [*CLOSE, *AFTER], ((AFTER, after), (CLOSE, close_in)), partial, strips)
+    partial = call(
+        bridge_kernel, [SMEM] * 3 + [VMEM] * 3, [shape(len(EARLY), slots, *piece, dtype=jnp.float32)],
+        (*tables, left, partial, strips), free=True,
+    )[0]
+    early, _ = rest(EARLY, EARLY[0], FAR, ((FAR, far_in),), partial, strips)
 
     result = shape(ROWS, share, 128, 128, dtype=jnp.float32)
 

time: 64.8 us -> 63.2 us (0.975)
  waiting for transfers between devices: 22.6 us -> 20.6 us
    ppermute x11, waiting for transfers between devices: 3.95 us -> 2.91 us  [across(): return lax.ppermute(x, 'col', [(c, c ^ bits) for c in range(4)])]
    ppermute x7, waiting for transfers between devices: 18.7 us -> 17.7 us  [shifted(): lax.ppermute(x, ('row', 'layer'), [(g, (g + d) % groups) for g in range(g...]
    pallas_call x12 -> x13, Pallas kernels: 20.7 us -> 21.2 us  [call(): pl.pallas_call(kernel, out_shape=outs, in_specs=specs, out_specs=out_spec...]
  transfers between devices with their start and end apart: 18 -> 18, of which waited for: 8 -> 9; matrix products, arithmetic and copies ran while one was open for 0% -> 0% of each run, Pallas kernels for 24% -> 26%
where the time goes in v7:
time: 63.2 us; the launch traced here: 63 us
  Pallas kernels  21.2 us (34%)
  waiting for transfers between devices  20.6 us (33%)
  starting transfers between devices  19.2 us (30%)
  local copies, waits for them, and re-layouts  1.82 us (3%)
    pallas_call x13, Pallas kernels, call(): pl.pallas_call(kernel, out_shape=outs, in_specs=specs, out_specs=out_spec...  21.2 us
    ppermute x7, waiting for transfers between devices, shifted(): lax.ppermute(x, ('row', 'layer'), [(g, (g + d) % groups) for g in range(g...  17.7 us
    ppermute x7, starting transfers between devices, shifted(): lax.ppermute(x, ('row', 'layer'), [(g, (g + d) % groups) for g in range(g...  11.6 us
    ppermute x11, starting transfers between devices, across(): return lax.ppermute(x, 'col', [(c, c ^ bits) for c in range(4)])  7.59 us
    ppermute x11, waiting for transfers between devices, across(): return lax.ppermute(x, 'col', [(c, c ^ bits) for c in range(4)])  2.91 us
    unnamed x8, local copies, waits for them, and re-layouts  1.82 us
  transfers between devices with their start and end apart: 18, of which 9 were waited for; matrix products, arithmetic and copies ran while one was open for 0% of the time, Pallas kernels for 26%

profile of v7, /device:TPU:0, one launch (start us, length us, event | category | flops | bytes accessed | tf_op | source)
XLA Modules:
  0.0 63.0 jit_solution(5747369937522257676)
XLA Ops:
  0.0 0.1 pad_add_fusion.meta
  0.1 0.0 copy-start
  0.1 1.1 %copy-done = bf16[8,11,32,128]{3,2,1,0:T(8,128)(2,1)S(1)} copy-done((bf16[8,11,32,128]{3,2,1,0:T(8,128)(2,1)S(1)}, bf16[8,11,32,128]{3,2,1,0:T(8,128)(2,1)}, u32[]{:S(2)}) %copy-start) | copy-done | bytes 720920
  1.2 0.0 copy-start.3
  1.2 0.7 %copy-done.3 = s32[64,11]{0,1:T(8,128)S(1)} copy-done((s32[64,11]{0,1:T(8,128)S(1)}, s32[64,11]{0,1:T(8,128)}, u32[]{:S(2)}) %copy-start.3) | copy-done | bytes 2840
  1.9 1.1 %shard_map.46 = (bf16[37,32,128]{2,1,0:T(8,128)(2,1)S(1)}, bf16[37,32,128]{2,1,0:T(8,128)(2,1)S(1)}, bf16[3,32,128]{2,1,0:T(8,128)(2,1)S(1)}, bf16[3,32,128]{2,1...) custom-call(s32[2]{0:T(128)S(1)} %pad_add_fusion.meta, ...), custom_call_target="tpu_custom_call" | custom-call | bytes 2681608 | tf_op jit(solution)/shard_map/pallas_call | solution.py:217
  3.0 0.5 collective-permute-start.3
  3.5 2.6 %collective-permute-start.2 = (bf16[63,32,128]{2,1,0:T(8,128)(2,1)S(1)}, bf16[63,32,128]{2,1,0:T(8,128)(2,1)S(1)}, u32[]{:S(2)}, u32[]{:S(2)}) collective-permute-start(bf16[63,32,128]{2,1,0:T(8,128)(2,1)S(1)} %get-tuple-element.41.upper), channel_id=1, source_target_pairs={{0,4},{2,6},{4,0},{6,2},{1,5},{3,7},{5,1},{7,3},{8,12},{10,14},{12... | collective-permute-start | bytes 1548296 | tf_op jit(solution)/shard_map/ppermute | solution.py:245
  6.1 1.5 %collective-permute-start = (bf16[37,32,128]{2,1,0:T(8,128)(2,1)S(1)}, bf16[37,32,128]{2,1,0:T(8,128)(2,1)S(1)}, u32[]{:S(2)}, u32[]{:S(2)}) collective-permute-start(bf16[37,32,128]{2,1,0:T(8,128)(2,1)S(1)} %get-tuple-element.39), channel_id=1, source_target_pairs={{0,1},{1,8},{8,9},{9,16},{16,17},{17,24},{24,25},{25,0},{2,3},{3,1... | collective-permute-start | bytes 909320 | tf_op jit(solution)/shard_map/ppermute | solution.py:242
  7.6 3.2 %collective-permute-start.1 = (bf16[37,32,128]{2,1,0:T(8,128)(2,1)S(1)}, bf16[37,32,128]{2,1,0:T(8,128)(2,1)S(1)}, u32[]{:S(2)}, u32[]{:S(2)}) collective-permute-start(bf16[37,32,128]{2,1,0:T(8,128)(2,1)S(1)} %get-tuple-element.40), channel_id=1, source_target_pairs={{0,25},{1,0},{8,1},{9,8},{16,9},{17,16},{24,17},{25,24},{2,27},{3,... | collective-permute-start | bytes 909320 | tf_op jit(solution)/shard_map/ppermute | solution.py:242
  10.8 0.0 collective-permute-start.4
  10.8 0.0 collective-permute-done.3.u1
  10.8 3.8 %collective-permute-start.5 = (bf16[3,32,128]{2,1,0:T(8,128)(2,1)S(1)}, bf16[3,32,128]{2,1,0:T(8,128)(2,1)S(1)}, u32[]{:S(2)}, u32[]{:S(2)}) collective-permute-start(bf16[3,32,128]{2,1,0:T(8,128)(2,1)S(1)} %get-tuple-element.45), channel_id=1, source_target_pairs={{0,24},{1,25},{8,0},{9,1},{16,8},{17,9},{24,16},{25,17},{2,26},{3,... | collective-permute-start | bytes 73736 | tf_op jit(solution)/shard_map/ppermute | solution.py:242
  14.6 1.8 %shard_map.47 = (bf16[28,18,32,128]{3,2,1,0:T(8,128)(2,1)S(1)}, bf16[8,18,128,128]{3,2,1,0:T(8,128)(2,1)S(1)}) custom-call(s32[2]{0:T(128)S(1)} %pad_add_fusion.meta, bf16[8,12,32,128]{3,2,1,0:T(8,128)(2,1)S(1)} %get-tuple-element.42.band, bf16[63,32,128]{2,1,0:T(8,128)(2,1)S(1)} %get-tuple-element.41.upper, bf16[63,32,128]{2,1,0:T(8,128)(2,1)S(1)} %collective-permute-done.3.u1), custom_call_target="tpu_custom_call" | custom-call | bytes 10665992 | tf_op jit(solution)/shard_map/pallas_call | solution.py:217
  16.4 4.0 %collective-permute-done.4.h2 = bf16[3,32,128]{2,1,0:T(8,128)(2,1)S(1)} collective-permute-done((bf16[3,32,128]{2,1,0:T(8,128)(2,1)S(1)}, bf16[3,32,128]{2,1,0:T(8,128)(2,1)S(1)}, u32[]{:S(2)}, u32[]{:S(2)}) %collective-permute-start.4) | collective-permute-done | bytes 24608 | tf_op jit(solution)/shard_map/ppermute | solution.py:242
  20.4 0.0 collective-permute-done.5.h3
  20.4 0.0 collective-permute-done.2.u2
  20.4 0.1 collective-permute-start.6
  20.5 0.5 collective-permute-start.7
  21.0 0.1 collective-permute-start.8
  21.1 0.6 shard_map.49.refs_4_
  21.7 0.0 copy-start.1
  21.7 0.2 collective-permute-done.6.refs_0_
  21.9 0.2 collective-permute-done.7.refs_1_
  22.2 0.3 collective-permute-done.8.refs_2_
  22.4 1.0 %shard_map.50 = (bf16[28,18,32,128]{3,2,1,0:T(8,128)(2,1)S(1)}, bf16[8,18,128,128]{3,2,1,0:T(8,128)(2,1)S(1)}) custom-call(s32[2]{0:T(128)S(1)} %pad_add_fusion.meta, bf16[21,32,128]{2,1,0:T(8,128)(2,1)S(1)} %collective-permute-done.6.refs_0_, bf16[21,32,128]{2,1,0:T(8,128)(2,1)S(1)} %collective-permute-done.7.refs_1_, ...), custom_call_target="tpu_custom_call", output_to_operand_aliasing={{0}: (4, {}), {1}: (5, {})} | custom-call | bytes 18210824 | tf_op jit(solution)/shard_map/pallas_call | solution.py:217
  23.4 0.0 collective-permute-done.h0
  23.5 0.0 collective-permute-done.1.h1
  23.5 0.0 copy-done.1
  23.5 2.3 %shard_map.51 = (bf16[5,12,32,128]{3,2,1,0:T(8,128)(2,1)S(1)}, bf16[2,12,32,128]{3,2,1,0:T(8,128)(2,1)S(1)}, bf16[28,18,32,128]{3,2,1,0:T(8,128)(2,1)S(1)}) custom-call(s32[2]{0:T(128)S(1)} %pad_add_fusion.meta, s32[12,64]{1,0:T(8,128)S(1)} %bitcast.5, bf16[37,32,128]{2,1,0:T(8,128)(2,1)S(1)} %collective-permute-done.h0, ...), custom_call_target="tpu_custom_call", output_to_operand_aliasing={{2}: (7, {})} | custom-call | flops 692060160 | bytes 14322696 | tf_op jit(solution)/shard_map/pallas_call | solution.py:217
  25.7 0.0 copy-start.2
  25.8 3.0 %collective-permute-start.9 = (bf16[5,12,32,128]{3,2,1,0:T(8,128)(2,1)S(1)}, bf16[5,12,32,128]{3,2,1,0:T(8,128)(2,1)S(1)}, u32[]{:S(2)}, u32[]{:S(2)}) collective-permute-start(bf16[5,12,32,128]{3,2,1,0:T(8,128)(2,1)S(1)} %get-tuple-element.57.low), channel_id=1, source_target_pairs={{0,25},{1,0},{8,1},{9,8},{16,9},{17,16},{24,17},{25,24},{2,27},{3,... | collective-permute-start | bytes 1474568 | tf_op jit(solution)/shard_map/ppermute | solution.py:242
  28.7 1.7 %shard_map.52.close = bf16[3,12,32,128]{3,2,1,0:T(8,128)(2,1)S(1)} custom-call(s32[2]{0:T(128)S(1)} %pad_add_fusion.meta, s32[12,64]{1,0:T(8,128)S(1)} %bitcast.6, bf16[28,18,32,128]{3,2,1,0:T(8,128)(2,1)S(1)} %get-tuple-element.58.strips, bf16[8,18,128,128]{3,2,1,0:T(8,128)(2,1)S(1)} %get-tuple-element.54.left.refs_2_.refs_1_), custom_call_target="tpu_custom_call" | custom-call | flops 415236096 | bytes 9145352 | tf_op jit(solution)/shard_map/pallas_call | solution.py:217
  30.4 0.1 collective-permute-start.11
  30.5 0.0 copy-done.2
  30.5 5.2 %shard_map.53 = (bf16[38,18,32,128]{3,2,1,0:T(8,128)(2,1)S(1)}, f32[8,16,32,128]{3,2,1,0:T(8,128)S(1)}) custom-call(s32[2]{0:T(128)S(1)} %pad_add_fusion.meta, s32[12,64]{1,0:T(8,128)S(1)} %bitcast.7, s32[16,64]{1,0:T(8,128)S(1)} %bitcast.11, bf16[5,12,32,128]{3,2,1,0:T(8,128)(2,1)S(1)} %get-tuple-element.57.low, ...), custom_call_target="tpu_custom_call" | custom-call | flops 1073741824 | bytes 13212680 | tf_op jit(solution)/shard_map/pallas_call | solution.py:217
  35.7 9.8 %collective-permute-done.9.refs_0_ = bf16[5,12,32,128]{3,2,1,0:T(8,128)(2,1)S(1)} collective-permute-done((bf16[5,12,32,128]{3,2,1,0:T(8,128)(2,1)S(1)}, bf16[5,12,32,128]{3,2,1,0:T(8,128)(2,1)S(1)}, u32[]{:S(2)}, u32[]{:S(2)}) %collective-permute-start.9) | collective-permute-done | bytes 491552 | tf_op jit(solution)/shard_map/ppermute | solution.py:242
  45.5 0.0 collective-permute-start.10
  45.5 0.0 collective-permute-done.11.refs_1_
  45.5 1.9 %shard_map.54 = (bf16[6,4,32,128]{3,2,1,0:T(8,128)(2,1)S(1)}, bf16[6,4,32,128]{3,2,1,0:T(8,128)(2,1)S(1)}, bf16[6,4,32,128]{3,2,1,0:T(8,128)(2,1)S(1)}, bf16[6,4...) custom-call(s32[2]{0:T(128)S(1)} %pad_add_fusion.meta, ...), custom_call_target="tpu_custom_call", output_to_operand_aliasing={{4}: (7, {})} | custom-call | tf_op jit(solution)/shard_map/pallas_call | solution.py:217
  47.4 0.1 collective-permute-start.15
  47.5 0.6 collective-permute-start.16
  48.1 1.3 %collective-permute-start.17 = (bf16[6,4,32,128]{3,2,1,0:T(8,128)(2,1)S(1)}, bf16[6,4,32,128]{3,2,1,0:T(8,128)(2,1)S(1)}, u32[]{:S(2)}, u32[]{:S(2)}) collective-permute-start(bf16[6,4,32,128]{3,2,1,0:T(8,128)(2,1)S(1)} %get-tuple-element.72), channel_id=1, source_target_pairs={{0,6},{2,4},{4,2},{6,0},{1,7},{3,5},{5,3},{7,1},{8,14},{10,12},{12... | collective-permute-start | bytes 589832 | tf_op jit(solution)/shard_map/ppermute | solution.py:245
  49.3 1.2 %shard_map.55.refs_2_ = f32[2,16,32,128]{3,2,1,0:T(8,128)S(1)} custom-call(s32[2]{0:T(128)S(1)} %pad_add_fusion.meta, s32[12,64]{1,0:T(8,128)S(1)} %bitcast.9, s32[16,64]{1,0:T(8,128)S(1)} %bitcast.13, bf16[8,18,128,128]{3,2,1,0:T(8,128)(2,1)S(1)} %get-tuple-element.54.left.refs_2_.refs_1_, f32[8,16,32,128]{3,2,1,0:T(8,128)S(1)} %get-tuple-element.61.refs_3_.partial, ...), custom_call_target="tpu_custom_call" | custom-call | tf_op jit(solution)/shard_map/pallas_call | solution.py:217
  50.5 3.9 %collective-permute-done.10.refs_0_ = bf16[2,12,32,128]{3,2,1,0:T(8,128)(2,1)S(1)} collective-permute-done((bf16[2,12,32,128]{3,2,1,0:T(8,128)(2,1)S(1)}, bf16[2,12,32,128]{3,2,1,0:T(8,128)(2,1)S(1)}, u32[]{:S(2)}, u32[]{:S(2)}) %collective-permute-start.10) | collective-permute-done | bytes 196640 | tf_op jit(solution)/shard_map/ppermute | solution.py:242
  54.4 1.1 %shard_map.56 = (bf16[2,4,32,128]{3,2,1,0:T(8,128)(2,1)S(1)}, bf16[2,4,32,128]{3,2,1,0:T(8,128)(2,1)S(1)}, bf16[2,4,32,128]{3,2,1,0:T(8,128)(2,1)S(1)}, bf16[2,4...) custom-call(s32[2]{0:T(128)S(1)} %pad_add_fusion.meta, ...), custom_call_target="tpu_custom_call", output_to_operand_aliasing={{4}: (6, {})} | custom-call | tf_op jit(solution)/shard_map/pallas_call | solution.py:217
  55.6 0.1 collective-permute-start.12
  55.6 0.6 collective-permute-start.13
  56.2 0.0 collective-permute-done.15.refs_1_
  56.2 1.3 %collective-permute-start.14 = (bf16[2,4,32,128]{3,2,1,0:T(8,128)(2,1)S(1)}, bf16[2,4,32,128]{3,2,1,0:T(8,128)(2,1)S(1)}, u32[]{:S(2)}, u32[]{:S(2)}) collective-permute-start(bf16[2,4,32,128]{3,2,1,0:T(8,128)(2,1)S(1)} %get-tuple-element.68), channel_id=1, source_target_pairs={{0,6},{2,4},{4,2},{6,0},{1,7},{3,5},{5,3},{7,1},{8,14},{10,12},{12... | collective-permute-start | bytes 196616 | tf_op jit(solution)/shard_map/ppermute | solution.py:245
  57.5 0.0 collective-permute-done.16.refs_2_
  57.5 1.0 %collective-permute-done.17.refs_3_ = bf16[6,4,32,128]{3,2,1,0:T(8,128)(2,1)S(1)} collective-permute-done((bf16[6,4,32,128]{3,2,1,0:T(8,128)(2,1)S(1)}, bf16[6,4,32,128]{3,2,1,0:T(8,128)(2,1)S(1)}, u32[]{:S(2)}, u32[]{:S(2)}) %collective-permute-start.17) | collective-permute-done | bytes 196640 | tf_op jit(solution)/shard_map/ppermute | solution.py:245
  58.6 1.9 %shard_map.57.refs_4_ = f32[8,4,128,128]{3,2,1,0:T(8,128)} custom-call(s32[2]{0:T(128)S(1)} %pad_add_fusion.meta, bf16[6,4,32,128]{3,2,1,0:T(8,128)(2,1)S(1)} %get-tuple-element.69.refs_0_, bf16[6,4,32,128]{3,2,1,0:T(8,128)(2,1)S(1)} %collective-permute-done.15.refs_1_, bf16[6,4,32,128]{3,2,1,0:T(8,128)(2,1)S(1)} %collective-permute-done.16.refs_2_, ...), custom_call_target="tpu_custom_call" | custom-call | bytes 2883592 | tf_op jit(solution)/shard_map/pallas_call | solution.py:217
  60.4 0.0 collective-permute-done.12.refs_1_
  60.4 0.2 collective-permute-done.13.refs_2_
  60.7 0.9 %collective-permute-done.14.refs_3_ = bf16[2,4,32,128]{3,2,1,0:T(8,128)(2,1)S(1)} collective-permute-done((bf16[2,4,32,128]{3,2,1,0:T(8,128)(2,1)S(1)}, bf16[2,4,32,128]{3,2,1,0:T(8,128)(2,1)S(1)}, u32[]{:S(2)}, u32[]{:S(2)}) %collective-permute-start.14) | collective-permute-done | bytes 65568 | tf_op jit(solution)/shard_map/ppermute | solution.py:245
  61.6 1.5 %shard_map.58 = f32[8,4,128,128]{3,2,1,0:T(8,128)} custom-call(s32[2]{0:T(128)S(1)} %pad_add_fusion.meta, bf16[2,4,32,128]{3,2,1,0:T(8,128)(2,1)S(1)} %get-tuple-element.65.refs_0_, bf16[2,4,32,128]{3,2,1,0:T(8,128)(2,1)S(1)} %collective-permute-done.12.refs_1_, ...), custom_call_target="tpu_custom_call", output_to_operand_aliasing={{}: (5, {})} | custom-call | bytes 4456456 | tf_op jit(solution)/shard_map/pallas_call | solution.py:217
  (1 shorter events, 0.0 us)
Async XLA Ops:
  0.1 1.1 %copy-start = (bf16[8,11,32,128]{3,2,1,0:T(8,128)(2,1)S(1)}, bf16[8,11,32,128]{3,2,1,0:T(8,128)(2,1)}, u32[]{:S(2)}) copy-start(bf16[8,11,32,128]{3,2,1,0:T(8,128)(2,1)} %density.1) | copy-start | bytes 2162692
  1.2 0.7 %copy-start.3 = (s32[64,11]{0,1:T(8,128)S(1)}, s32[64,11]{0,1:T(8,128)}, u32[]{:S(2)}) copy-start(s32[64,11]{0,1:T(8,128)} %param.5) | copy-start | bytes 8452
  3.0 7.8 %collective-permute-start.3 = (bf16[63,32,128]{2,1,0:T(8,128)(2,1)S(1)}, bf16[63,32,128]{2,1,0:T(8,128)(2,1)S(1)}, u32[]{:S(2)}, u32[]{:S(2)}) collective-permute-start(bf16[63,32,128]{2,1,0:T(8,128)(2,1)S(1)} %get-tuple-element.41.upper), channel_id=1, source_target_pairs={{0,2},{2,0},{4,6},{6,4},{1,3},{3,1},{5,7},{7,5},{8,10},{10,8},{12,... | collective-permute-start | bytes 1548296 | tf_op jit(solution)/shard_map/ppermute | solution.py:245
  3.5 16.9 %collective-permute-start.2 = (bf16[63,32,128]{2,1,0:T(8,128)(2,1)S(1)}, bf16[63,32,128]{2,1,0:T(8,128)(2,1)S(1)}, u32[]{:S(2)}, u32[]{:S(2)}) collective-permute-start(bf16[63,32,128]{2,1,0:T(8,128)(2,1)S(1)} %get-tuple-element.41.upper), channel_id=1, source_target_pairs={{0,4},{2,6},{4,0},{6,2},{1,5},{3,7},{5,1},{7,3},{8,12},{10,14},{12... | collective-permute-start | bytes 1548296 | tf_op jit(solution)/shard_map/ppermute | solution.py:245
  6.1 17.4 %collective-permute-start = (bf16[37,32,128]{2,1,0:T(8,128)(2,1)S(1)}, bf16[37,32,128]{2,1,0:T(8,128)(2,1)S(1)}, u32[]{:S(2)}, u32[]{:S(2)}) collective-permute-start(bf16[37,32,128]{2,1,0:T(8,128)(2,1)S(1)} %get-tuple-element.39), channel_id=1, source_target_pairs={{0,1},{1,8},{8,9},{9,16},{16,17},{17,24},{24,25},{25,0},{2,3},{3,1... | collective-permute-start | bytes 909320 | tf_op jit(solution)/shard_map/ppermute | solution.py:242
  7.6 15.9 %collective-permute-start.1 = (bf16[37,32,128]{2,1,0:T(8,128)(2,1)S(1)}, bf16[37,32,128]{2,1,0:T(8,128)(2,1)S(1)}, u32[]{:S(2)}, u32[]{:S(2)}) collective-permute-start(bf16[37,32,128]{2,1,0:T(8,128)(2,1)S(1)} %get-tuple-element.40), channel_id=1, source_target_pairs={{0,25},{1,0},{8,1},{9,8},{16,9},{17,16},{24,17},{25,24},{2,27},{3,... | collective-permute-start | bytes 909320 | tf_op jit(solution)/shard_map/ppermute | solution.py:242
  10.8 9.6 %collective-permute-start.4 = (bf16[3,32,128]{2,1,0:T(8,128)(2,1)S(1)}, bf16[3,32,128]{2,1,0:T(8,128)(2,1)S(1)}, u32[]{:S(2)}, u32[]{:S(2)}) collective-permute-start(bf16[3,32,128]{2,1,0:T(8,128)(2,1)S(1)} %get-tuple-element.44), channel_id=1, source_target_pairs={{0,8},{1,9},{8,16},{9,17},{16,24},{17,25},{24,0},{25,1},{2,10},{3,... | collective-permute-start | bytes 73736 | tf_op jit(solution)/shard_map/ppermute | solution.py:242
  10.8 9.6 %collective-permute-start.5 = (bf16[3,32,128]{2,1,0:T(8,128)(2,1)S(1)}, bf16[3,32,128]{2,1,0:T(8,128)(2,1)S(1)}, u32[]{:S(2)}, u32[]{:S(2)}) collective-permute-start(bf16[3,32,128]{2,1,0:T(8,128)(2,1)S(1)} %get-tuple-element.45), channel_id=1, source_target_pairs={{0,24},{1,25},{8,0},{9,1},{16,8},{17,9},{24,16},{25,17},{2,26},{3,... | collective-permute-start | bytes 73736 | tf_op jit(solution)/shard_map/ppermute | solution.py:242
  20.4 1.5 %collective-permute-start.6 = (bf16[21,32,128]{2,1,0:T(8,128)(2,1)S(1)}, bf16[21,32,128]{2,1,0:T(8,128)(2,1)S(1)}, u32[]{:S(2)}, u32[]{:S(2)}) collective-permute-start(bf16[21,32,128]{2,1,0:T(8,128)(2,1)S(1)} %get-tuple-element.49), channel_id=1, source_target_pairs={{0,2},{2,0},{4,6},{6,4},{1,3},{3,1},{5,7},{7,5},{8,10},{10,8},{12,... | collective-permute-start | bytes 516104 | tf_op jit(solution)/shard_map/ppermute | solution.py:245
  20.5 1.6 %collective-permute-start.7 = (bf16[21,32,128]{2,1,0:T(8,128)(2,1)S(1)}, bf16[21,32,128]{2,1,0:T(8,128)(2,1)S(1)}, u32[]{:S(2)}, u32[]{:S(2)}) collective-permute-start(bf16[21,32,128]{2,1,0:T(8,128)(2,1)S(1)} %get-tuple-element.50), channel_id=1, source_target_pairs={{0,2},{2,0},{4,6},{6,4},{1,3},{3,1},{5,7},{7,5},{8,10},{10,8},{12,... | collective-permute-start | bytes 516104 | tf_op jit(solution)/shard_map/ppermute | solution.py:245
  21.0 1.4 %collective-permute-start.8 = (bf16[21,32,128]{2,1,0:T(8,128)(2,1)S(1)}, bf16[21,32,128]{2,1,0:T(8,128)(2,1)S(1)}, u32[]{:S(2)}, u32[]{:S(2)}) collective-permute-start(bf16[21,32,128]{2,1,0:T(8,128)(2,1)S(1)} %get-tuple-element.51), channel_id=1, source_target_pairs={{0,2},{2,0},{4,6},{6,4},{1,3},{3,1},{5,7},{7,5},{8,10},{10,8},{12,... | collective-permute-start | bytes 516104 | tf_op jit(solution)/shard_map/ppermute | solution.py:245
  21.7 1.8 %copy-start.1 = (s32[64,12]{0,1:T(8,128)S(1)}, s32[64,12]{0,1:T(8,128)}, u32[]{:S(2)}) copy-start(s32[64,12]{0,1:T(8,128)} %param.6) | copy-start | bytes 9220
  25.7 4.7 %copy-start.2 = (s32[64,16]{0,1:T(8,128)S(1)}, s32[64,16]{0,1:T(8,128)}, u32[]{:S(2)}) copy-start(s32[64,16]{0,1:T(8,128)} %param.7) | copy-start | bytes 12292
  25.8 19.7 %collective-permute-start.9 = (bf16[5,12,32,128]{3,2,1,0:T(8,128)(2,1)S(1)}, bf16[5,12,32,128]{3,2,1,0:T(8,128)(2,1)S(1)}, u32[]{:S(2)}, u32[]{:S(2)}) collective-permute-start(bf16[5,12,32,128]{3,2,1,0:T(8,128)(2,1)S(1)} %get-tuple-element.57.low), channel_id=1, source_target_pairs={{0,25},{1,0},{8,1},{9,8},{16,9},{17,16},{24,17},{25,24},{2,27},{3,... | collective-permute-start | bytes 1474568 | tf_op jit(solution)/shard_map/ppermute | solution.py:242
  30.4 15.1 %collective-permute-start.11 = (bf16[3,12,32,128]{3,2,1,0:T(8,128)(2,1)S(1)}, bf16[3,12,32,128]{3,2,1,0:T(8,128)(2,1)S(1)}, u32[]{:S(2)}, u32[]{:S(2)}) collective-permute-start(bf16[3,12,32,128]{3,2,1,0:T(8,128)(2,1)S(1)} %shard_map.52.close), channel_id=1, source_target_pairs={{0,1},{1,8},{8,9},{9,16},{16,17},{17,24},{24,25},{25,0},{2,3},{3,1... | collective-permute-start | bytes 884744 | tf_op jit(solution)/shard_map/ppermute | solution.py:242
  45.5 8.9 %collective-permute-start.10 = (bf16[2,12,32,128]{3,2,1,0:T(8,128)(2,1)S(1)}, bf16[2,12,32,128]{3,2,1,0:T(8,128)(2,1)S(1)}, u32[]{:S(2)}, u32[]{:S(2)}) collective-permute-start(bf16[2,12,32,128]{3,2,1,0:T(8,128)(2,1)S(1)} %get-tuple-element.60), channel_id=1, source_target_pairs={{0,1},{1,8},{8,9},{9,16},{16,17},{17,24},{24,25},{25,0},{2,3},{3,1... | collective-permute-start | bytes 589832 | tf_op jit(solution)/shard_map/ppermute | solution.py:242
  47.4 8.8 %collective-permute-start.15 = (bf16[6,4,32,128]{3,2,1,0:T(8,128)(2,1)S(1)}, bf16[6,4,32,128]{3,2,1,0:T(8,128)(2,1)S(1)}, u32[]{:S(2)}, u32[]{:S(2)}) collective-permute-start(bf16[6,4,32,128]{3,2,1,0:T(8,128)(2,1)S(1)} %get-tuple-element.70), channel_id=1, source_target_pairs={{0,2},{2,0},{4,6},{6,4},{1,3},{3,1},{5,7},{7,5},{8,10},{10,8},{12,... | collective-permute-start | bytes 589832 | tf_op jit(solution)/shard_map/ppermute | solution.py:245
  47.5 10.0 %collective-permute-start.16 = (bf16[6,4,32,128]{3,2,1,0:T(8,128)(2,1)S(1)}, bf16[6,4,32,128]{3,2,1,0:T(8,128)(2,1)S(1)}, u32[]{:S(2)}, u32[]{:S(2)}) collective-permute-start(bf16[6,4,32,128]{3,2,1,0:T(8,128)(2,1)S(1)} %get-tuple-element.71), channel_id=1, source_target_pairs={{0,4},{2,6},{4,0},{6,2},{1,5},{3,7},{5,1},{7,3},{8,12},{10,14},{12... | collective-permute-start | bytes 589832 | tf_op jit(solution)/shard_map/ppermute | solution.py:245
  48.1 10.5 %collective-permute-start.17 = (bf16[6,4,32,128]{3,2,1,0:T(8,128)(2,1)S(1)}, bf16[6,4,32,128]{3,2,1,0:T(8,128)(2,1)S(1)}, u32[]{:S(2)}, u32[]{:S(2)}) collective-permute-start(bf16[6,4,32,128]{3,2,1,0:T(8,128)(2,1)S(1)} %get-tuple-element.72), channel_id=1, source_target_pairs={{0,6},{2,4},{4,2},{6,0},{1,7},{3,5},{5,3},{7,1},{8,14},{10,12},{12... | collective-permute-start | bytes 589832 | tf_op jit(solution)/shard_map/ppermute | solution.py:245
  55.6 4.9 %collective-permute-start.12 = (bf16[2,4,32,128]{3,2,1,0:T(8,128)(2,1)S(1)}, bf16[2,4,32,128]{3,2,1,0:T(8,128)(2,1)S(1)}, u32[]{:S(2)}, u32[]{:S(2)}) collective-permute-start(bf16[2,4,32,128]{3,2,1,0:T(8,128)(2,1)S(1)} %get-tuple-element.66), channel_id=1, source_target_pairs={{0,2},{2,0},{4,6},{6,4},{1,3},{3,1},{5,7},{7,5},{8,10},{10,8},{12,... | collective-permute-start | bytes 196616 | tf_op jit(solution)/shard_map/ppermute | solution.py:245
  55.6 5.0 %collective-permute-start.13 = (bf16[2,4,32,128]{3,2,1,0:T(8,128)(2,1)S(1)}, bf16[2,4,32,128]{3,2,1,0:T(8,128)(2,1)S(1)}, u32[]{:S(2)}, u32[]{:S(2)}) collective-permute-start(bf16[2,4,32,128]{3,2,1,0:T(8,128)(2,1)S(1)} %get-tuple-element.67), channel_id=1, source_target_pairs={{0,4},{2,6},{4,0},{6,2},{1,5},{3,7},{5,1},{7,3},{8,12},{10,14},{12... | collective-permute-start | bytes 196616 | tf_op jit(solution)/shard_map/ppermute | solution.py:245
  56.2 5.3 %collective-permute-start.14 = (bf16[2,4,32,128]{3,2,1,0:T(8,128)(2,1)S(1)}, bf16[2,4,32,128]{3,2,1,0:T(8,128)(2,1)S(1)}, u32[]{:S(2)}, u32[]{:S(2)}) collective-permute-start(bf16[2,4,32,128]{3,2,1,0:T(8,128)(2,1)S(1)} %get-tuple-element.68), channel_id=1, source_target_pairs={{0,6},{2,4},{4,2},{6,0},{1,7},{3,5},{5,3},{7,1},{8,14},{10,12},{12... | collective-permute-start | bytes 196616 | tf_op jit(solution)/shard_map/ppermute | solution.py:245

commit v8 on v7

--- a/solution.py
+++ b/solution.py
@@ -38,14 +38,19 @@
 RELAY = 21
 
 
+def own_place():
+    group = lax.axis_index("row") * lax.axis_size("layer") + lax.axis_index("layer")
+    return lax.axis_index("col"), group * ROWS
+
+
 def wrapped(value, total):
     if total & (total - 1) == 0:
         return value & (total - 1)
     return jnp.where(value < 0, value + total, jnp.where(value >= total, value - total, value))
 
 
-def reorder_kernel(meta, pattern, density, h0, h1, h2, h3, upper, band):
-    first, total = meta[1], pattern.shape[1]
+def reorder_kernel(pattern, density, h0, h1, h2, h3, upper, band):
+    first, total = own_place()[1], pattern.shape[1]
     band[...] = jnp.zeros_like(band)
     for i in range(ROWS):
         for s in range(density.shape[1]):
@@ -63,13 +68,14 @@
         left[i, i + o, pl.ds(start, 32), :] = piece[e]
 
 
-def prepare_kernel(meta, band, upper, u1, strips, left):
+def prepare_kernel(band, upper, u1, strips, left):
     strips[...] = jnp.zeros_like(strips)
     left[...] = jnp.zeros_like(left)
     for i in range(ROWS):
         strips[i + 2 * RADIUS, i : i + BAND] = band[i, :BAND]
-    place(left, upper, UPPER, meta[0], 0)
-    place(left, u1, UPPER, meta[0], 1)
+    col = own_place()[0]
+    place(left, upper, UPPER, col, 0)
+    place(left, u1, UPPER, col, 1)
 
 
 def relay_kernel(u2, *pieces):
@@ -77,14 +83,14 @@
         piece[...] = u2[n * RELAY : n * RELAY + piece.shape[0]]
 
 
-def place_kernel(meta, u2, left_in, left):
+def place_kernel(u2, left_in, left):
     del left_in
-    place(left, u2, UPPER, meta[0], 2)
-
-
-def complete_kernel(meta, *refs):
+    place(left, u2, UPPER, own_place()[0], 2)
+
+
+def complete_kernel(*refs):
     pieces, (strips, left) = refs[:-4], refs[-2:]
-    col = meta[0]
+    col = own_place()[0]
     for n, piece in enumerate(pieces):
         place(left, piece, UPPER[n * RELAY : n * RELAY + piece.shape[0]], col, 3)
     shape = (32, 128)
@@ -113,9 +119,9 @@
     return acc.reshape(len(targets), 32, 128).astype(strips.dtype)
 
 
-def low_kernel(meta, kept, h0, h1, h2, h3, left, strips_in, low, far, strips):
+def low_kernel(kept, h0, h1, h2, h3, left, strips_in, low, far, strips):
     del strips_in
-    first = meta[1]
+    first = own_place()[1]
     for halo, entries, shift in zip((h0, h1, h2, h3), LISTS, SHIFTS):
         for e, (j, o) in enumerate(entries):
             row = j - shift * ROWS
@@ -127,9 +133,9 @@
             far[i - ROWS + RADIUS] = row
 
 
-def high_kernel(meta, kept, strips, left, close):
+def high_kernel(kept, strips, left, close):
     for i in range(RADIUS, ROWS):
-        close[i - RADIUS] = square_row(kept, strips, left, i, meta[1])
+        close[i - RADIUS] = square_row(kept, strips, left, i, own_place()[1])
 
 
 def strip_of(table, s, row, first):
@@ -147,8 +153,8 @@
             strips[strip_of(kept, s, first - RADIUS + p, first), p] = rows[k, s]
 
 
-def inner_kernel(meta, kept, cube, low, close, left, strips, partial):
-    col, first = meta[0], meta[1]
+def inner_kernel(kept, cube, low, close, left, strips, partial):
+    col, first = own_place()
     strips[...] = jnp.zeros_like(strips)
     insert_rows(strips, kept, low, range(RADIUS, 2 * RADIUS), first)
     insert_rows(strips, kept, close, range(2 * RADIUS, RADIUS + ROWS), first)
@@ -163,19 +169,19 @@
             partial[i, e] = 3.0 * mine - 2.0 * acc[e * 32 : (e + 1) * 32]
 
 
-def bridge_kernel(meta, kept, cube, left, partial, strips, early):
+def bridge_kernel(kept, cube, left, partial, strips, early):
     share = cube.shape[0] // 4
     for n, i in enumerate(EARLY):
-        targets = cube_targets(cube, i, meta[0], meta[1], share)
+        targets = cube_targets(cube, i, *own_place(), share)
         acc = gather_dot(strips, left, targets, i, CLOSE)
         for e in range(len(targets)):
             early[n, e] = partial[i, e] - 2.0 * acc[e * 32 : (e + 1) * 32]
 
 
 def outer_kernel(rows, start, places, arrived):
-    def kernel(meta, kept, cube, *refs):
+    def kernel(kept, cube, *refs):
         halos, (left, partial, _, o0, o1, o2, o3, strips) = refs[:-8], refs[-8:]
-        col, first = meta[0], meta[1]
+        col, first = own_place()
         for halo, span in zip(halos, arrived):
             insert_rows(strips, kept, halo, span, first)
         share = cube.shape[0] // 4
@@ -190,8 +196,8 @@
 
 
 def final_kernel(rows):
-    def kernel(meta, *refs):
-        col = meta[0]
+    def kernel(*refs):
+        col = own_place()[0]
         out, whole, turned, sems = refs[-4:]
         for b, p in enumerate(refs[:4]):
             whole[:, :, pl.ds(pl.multiple_of((col ^ b) * 32, 32), 32), :] = p[...]
@@ -231,9 +237,6 @@
     groups = lax.axis_size("row") * layers
     assert density.shape[0] == ROWS and lax.axis_size("col") == 4
     piece = density.shape[2:]
-    col = lax.axis_index("col")
-    first = (lax.axis_index("row") * layers + lax.axis_index("layer")) * ROWS
-    meta = jnp.stack([col, first]).astype(jnp.int32)
     pattern, kept, cube = pattern.T, square_filter.T, cube_filter.T
     width, slots = kept.shape[0], cube.shape[0]
     share = slots // 4
@@ -245,43 +248,43 @@
         return lax.ppermute(x, "col", [(c, c ^ bits) for c in range(4)])
 
     *halos, upper, band = call(
-        reorder_kernel, [SMEM, SMEM, VMEM],
+        reorder_kernel, [SMEM, VMEM],
         [*(shape(len(e), *piece) for e in (*LISTS, UPPER)), shape(ROWS, BAND + 1, *piece)],
-        (meta, pattern, density),
+        (pattern, density),
     )
     u2 = across(upper, 2)
     u1 = across(upper, 1)
     halos = [shifted(p, d) for p, d in zip(halos, SHIFTS)]
     strips, left = call(
-        prepare_kernel, [SMEM] + [VMEM] * 3,
-        [shape(STRIPS, NEAR, *piece), shape(ROWS, NEAR, 128, 128)], (meta, band, upper, u1),
+        prepare_kernel, [VMEM] * 3,
+        [shape(STRIPS, NEAR, *piece), shape(ROWS, NEAR, 128, 128)], (band, upper, u1),
     )
     u2, left, halos[2:] = lax.optimization_barrier((u2, left, halos[2:]))
     sizes = [min(RELAY, len(UPPER) - e) for e in range(0, len(UPPER), RELAY)]
     pieces = call(relay_kernel, [VMEM], [shape(n, *piece) for n in sizes], (u2,))
     pieces = [across(p, 1) for p in pieces]
-    left = call(place_kernel, [SMEM] + [VMEM] * 2, [shape(*left.shape)], (meta, u2, left), aliases={2: 0})[0]
+    left = call(place_kernel, [VMEM] * 2, [shape(*left.shape)], (u2, left), aliases={1: 0})[0]
     both = [shape(*strips.shape), shape(*left.shape)]
     strips, left = call(
-        complete_kernel, [SMEM] + [VMEM] * (len(pieces) + 2), both, (meta, *pieces, strips, left),
-        aliases={1 + len(pieces): 0, 2 + len(pieces): 1},
+        complete_kernel, [VMEM] * (len(pieces) + 2), both, (*pieces, strips, left),
+        aliases={len(pieces): 0, 1 + len(pieces): 1},
     )
     work = 2 * width * BAND * 128 * 128 * 32
     low, far, strips = call(
-        low_kernel, [SMEM] * 2 + [VMEM] * 6,
+        low_kernel, [SMEM] + [VMEM] * 6,
         [shape(RADIUS, width, *piece), shape(len(FAR), width, *piece), both[0]],
-        (meta, kept, *halos, left, strips), flops=work * RADIUS, aliases={7: 2},
+        (kept, *halos, left, strips), flops=work * RADIUS, aliases={6: 2},
     )
     after = shifted(low, -1)
     close = call(
-        high_kernel, [SMEM] * 2 + [VMEM] * 2, [shape(len(CLOSE), width, *piece)],
-        (meta, kept, strips, left), flops=work * (ROWS - RADIUS),
+        high_kernel, [SMEM] + [VMEM] * 2, [shape(len(CLOSE), width, *piece)],
+        (kept, strips, left), flops=work * (ROWS - RADIUS),
     )[0]
     close_in = shifted(close, 1)
 
-    tables = (meta, kept, cube)
+    tables = (kept, cube)
     strips, partial = call(
-        inner_kernel, [SMEM] * 3 + [VMEM] * 3,
+        inner_kernel, [SMEM] * 2 + [VMEM] * 3,
         [shape(REACH, NEAR, *piece), shape(ROWS, slots, *piece, dtype=jnp.float32)],
         (*tables, low, close, left), flops=2 * slots * ROWS * ROWS * 128 * 128 * 32,
     )
@@ -290,15 +293,15 @@
 
     def rest(rows, start, places, halos, partial, strips):
         *own, strips = call(
-            outer_kernel(rows, start, places, [p for p, _ in halos]), [SMEM] * 3 + [VMEM] * (3 + len(halos)),
+            outer_kernel(rows, start, places, [p for p, _ in halos]), [SMEM] * 2 + [VMEM] * (3 + len(halos)),
             [shape(len(rows), share, *piece)] * 4 + [shape(*strips.shape)],
-            (*tables, *(h for _, h in halos), left, partial, strips), aliases={5 + len(halos): 4}, free=True,
+            (*tables, *(h for _, h in halos), left, partial, strips), aliases={4 + len(halos): 4}, free=True,
         )
         return [own[0], *(across(own[b], b) for b in (1, 2, 3))], strips
 
     late, strips = rest(LATE, 0, [*CLOSE, *AFTER], ((AFTER, after), (CLOSE, close_in)), partial, strips)
     partial = call(
-        bridge_kernel, [SMEM] * 3 + [VMEM] * 3, [shape(len(EARLY), slots, *piece, dtype=jnp.float32)],
+        bridge_kernel, [SMEM] * 2 + [VMEM] * 3, [shape(len(EARLY), slots, *piece, dtype=jnp.float32)],
         (*tables, left, partial, strips), free=True,
     )[0]
     early, _ = rest(EARLY, EARLY[0], FAR, ((FAR, far_in),), partial, strips)
@@ -311,12 +314,12 @@
                 pltpu.SemaphoreType.DMA((len(rows),))]
 
     out = call(
-        final_kernel(LATE), [SMEM] + [VMEM] * 4, [result], (meta, *late),
+        final_kernel(LATE), [VMEM] * 4, [result], late,
         scratch(LATE), out_specs=[ANY],
     )[0]
     return call(
-        final_kernel(EARLY), [SMEM] + [VMEM] * 4 + [ANY], [result], (meta, *early, out),
-        scratch(EARLY), out_specs=[ANY], aliases={5: 0},
+        final_kernel(EARLY), [VMEM] * 4 + [ANY], [result], (*early, out),
+        scratch(EARLY), out_specs=[ANY], aliases={4: 0},
     )[0]
 
 

time: 63.2 us -> 62 us (0.981)
  Pallas kernels: 21.2 us -> 18.5 us
  waiting for transfers between devices: 20.6 us -> 21.7 us
    pallas_call x13, Pallas kernels: 21.2 us -> 18.5 us  [call(): pl.pallas_call(kernel, out_shape=outs, in_specs=specs, out_specs=out_spec...]
    ppermute x11, waiting for transfers between devices: 2.91 us -> 4.02 us  [across(): return lax.ppermute(x, 'col', [(c, c ^ bits) for c in range(4)])]
  transfers between devices with their start and end apart: 18 -> 18, of which waited for: 9 -> 10; matrix products, arithmetic and copies ran while one was open for 0% -> 0% of each run, Pallas kernels for 26% -> 23%
where the time goes in v8:
time: 62 us; the launch traced here: 61.8 us
  waiting for transfers between devices  21.7 us (35%)
  starting transfers between devices  19.6 us (32%)
  Pallas kernels  18.5 us (30%)
  local copies, waits for them, and re-layouts  1.82 us (3%)
    pallas_call x13, Pallas kernels, call(): pl.pallas_call(kernel, out_shape=outs, in_specs=specs, out_specs=out_spec...  18.5 us
    ppermute x7, waiting for transfers between devices, shifted(): lax.ppermute(x, ('row', 'layer'), [(g, (g + d) % groups) for g in range(g...  17.7 us
    ppermute x7, starting transfers between devices, shifted(): lax.ppermute(x, ('row', 'layer'), [(g, (g + d) % groups) for g in range(g...  12 us
    ppermute x11, starting transfers between devices, across(): return lax.ppermute(x, 'col', [(c, c ^ bits) for c in range(4)])  7.59 us
    ppermute x11, waiting for transfers between devices, across(): return lax.ppermute(x, 'col', [(c, c ^ bits) for c in range(4)])  4.02 us
    unnamed x8, local copies, waits for them, and re-layouts  1.82 us
  transfers between devices with their start and end apart: 18, of which 10 were waited for; matrix products, arithmetic and copies ran while one was open for 0% of the time, Pallas kernels for 23%

profile of v8, /device:TPU:0, one launch (start us, length us, event | category | flops | bytes accessed | tf_op | source)
XLA Modules:
  0.0 61.8 jit_solution(6052920469249473022)
XLA Ops:
  0.0 0.0 copy-start
  0.0 1.1 %copy-done = bf16[8,11,32,128]{3,2,1,0:T(8,128)(2,1)S(1)} copy-done((bf16[8,11,32,128]{3,2,1,0:T(8,128)(2,1)S(1)}, bf16[8,11,32,128]{3,2,1,0:T(8,128)(2,1)}, u32[]{:S(2)}) %copy-start) | copy-done | bytes 720920
  1.1 0.0 copy-start.3
  1.1 0.7 %copy-done.3 = s32[64,11]{0,1:T(8,128)S(1)} copy-done((s32[64,11]{0,1:T(8,128)S(1)}, s32[64,11]{0,1:T(8,128)}, u32[]{:S(2)}) %copy-start.3) | copy-done | bytes 2840
  1.8 1.1 %shard_map.46 = (bf16[37,32,128]{2,1,0:T(8,128)(2,1)S(1)}, bf16[37,32,128]{2,1,0:T(8,128)(2,1)S(1)}, bf16[3,32,128]{2,1,0:T(8,128)(2,1)S(1)}, bf16[3,32,128]{2,1...) custom-call(s32[11,64]{1,0:T(8,128)S(1)} %bitcast.13, ...), custom_call_target="tpu_custom_call" | custom-call | bytes 2681600 | tf_op jit(solution)/shard_map/pallas_call | solution.py:223
  2.9 0.5 collective-permute-start.3
  3.4 2.6 %collective-permute-start.2 = (bf16[63,32,128]{2,1,0:T(8,128)(2,1)S(1)}, bf16[63,32,128]{2,1,0:T(8,128)(2,1)S(1)}, u32[]{:S(2)}, u32[]{:S(2)}) collective-permute-start(bf16[63,32,128]{2,1,0:T(8,128)(2,1)S(1)} %get-tuple-element.41.upper), channel_id=1, source_target_pairs={{0,4},{2,6},{4,0},{6,2},{1,5},{3,7},{5,1},{7,3},{8,12},{10,14},{12... | collective-permute-start | bytes 1548296 | tf_op jit(solution)/shard_map/ppermute | solution.py:248
  6.0 1.5 %collective-permute-start = (bf16[37,32,128]{2,1,0:T(8,128)(2,1)S(1)}, bf16[37,32,128]{2,1,0:T(8,128)(2,1)S(1)}, u32[]{:S(2)}, u32[]{:S(2)}) collective-permute-start(bf16[37,32,128]{2,1,0:T(8,128)(2,1)S(1)} %get-tuple-element.39), channel_id=1, source_target_pairs={{0,1},{1,8},{8,9},{9,16},{16,17},{17,24},{24,25},{25,0},{2,3},{3,1... | collective-permute-start | bytes 909320 | tf_op jit(solution)/shard_map/ppermute | solution.py:245
  7.5 3.2 %collective-permute-start.1 = (bf16[37,32,128]{2,1,0:T(8,128)(2,1)S(1)}, bf16[37,32,128]{2,1,0:T(8,128)(2,1)S(1)}, u32[]{:S(2)}, u32[]{:S(2)}) collective-permute-start(bf16[37,32,128]{2,1,0:T(8,128)(2,1)S(1)} %get-tuple-element.40), channel_id=1, source_target_pairs={{0,25},{1,0},{8,1},{9,8},{16,9},{17,16},{24,17},{25,24},{2,27},{3,... | collective-permute-start | bytes 909320 | tf_op jit(solution)/shard_map/ppermute | solution.py:245
  10.7 0.0 collective-permute-start.4
  10.7 0.0 collective-permute-done.3.u1
  10.7 3.8 %collective-permute-start.5 = (bf16[3,32,128]{2,1,0:T(8,128)(2,1)S(1)}, bf16[3,32,128]{2,1,0:T(8,128)(2,1)S(1)}, u32[]{:S(2)}, u32[]{:S(2)}) collective-permute-start(bf16[3,32,128]{2,1,0:T(8,128)(2,1)S(1)} %get-tuple-element.45), channel_id=1, source_target_pairs={{0,24},{1,25},{8,0},{9,1},{16,8},{17,9},{24,16},{25,17},{2,26},{3,... | collective-permute-start | bytes 73736 | tf_op jit(solution)/shard_map/ppermute | solution.py:245
  14.6 1.3 %shard_map.47 = (bf16[28,18,32,128]{3,2,1,0:T(8,128)(2,1)S(1)}, bf16[8,18,128,128]{3,2,1,0:T(8,128)(2,1)S(1)}) custom-call(bf16[8,12,32,128]{3,2,1,0:T(8,128)(2,1)S(1)} %get-tuple-element.42.band, bf16[63,32,128]{2,1,0:T(8,128)(2,1)S(1)} %get-tuple-element.41.upper, bf16[63,32,128]{2,1,0:T(8,128)(2,1)S(1)} %collective-permute-done.3.u1), custom_call_target="tpu_custom_call" | custom-call | bytes 10665984 | tf_op jit(solution)/shard_map/pallas_call | solution.py:223
  15.8 4.5 %collective-permute-done.4.h2 = bf16[3,32,128]{2,1,0:T(8,128)(2,1)S(1)} collective-permute-done((bf16[3,32,128]{2,1,0:T(8,128)(2,1)S(1)}, bf16[3,32,128]{2,1,0:T(8,128)(2,1)S(1)}, u32[]{:S(2)}, u32[]{:S(2)}) %collective-permute-start.4) | collective-permute-done | bytes 24608 | tf_op jit(solution)/shard_map/ppermute | solution.py:245
  20.3 0.0 collective-permute-done.5.h3
  20.3 0.0 collective-permute-done.2.u2
  20.4 0.1 collective-permute-start.6
  20.4 0.5 collective-permute-start.7
  20.9 0.1 collective-permute-start.8
  21.1 0.0 copy-start.1
  21.1 0.8 %collective-permute-done.6.refs_0_ = bf16[21,32,128]{2,1,0:T(8,128)(2,1)S(1)} collective-permute-done((bf16[21,32,128]{2,1,0:T(8,128)(2,1)S(1)}, bf16[21,32,128]{2,1,0:T(8,128)(2,1)S(1)}, u32[]{:S(2)}, u32[]{:S(2)}) %collective-permute-start.6) | collective-permute-done | bytes 172064 | tf_op jit(solution)/shard_map/ppermute | solution.py:248
  21.8 0.2 collective-permute-done.7.refs_1_
  22.1 0.3 collective-permute-done.8.refs_2_
  22.3 0.5 shard_map.50
  22.8 0.0 collective-permute-done.h0
  22.9 0.1 collective-permute-done.1.h1
  23.0 0.0 copy-done.1
  23.0 2.3 %shard_map.51 = (bf16[5,12,32,128]{3,2,1,0:T(8,128)(2,1)S(1)}, bf16[2,12,32,128]{3,2,1,0:T(8,128)(2,1)S(1)}, bf16[28,18,32,128]{3,2,1,0:T(8,128)(2,1)S(1)}) custom-call(s32[12,64]{1,0:T(8,128)S(1)} %bitcast.3, bf16[37,32,128]{2,1,0:T(8,128)(2,1)S(1)} %collective-permute-done.h0, ...), custom_call_target="tpu_custom_call", output_to_operand_aliasing={{2}: (6, {})} | custom-call | flops 692060160 | bytes 14322688 | tf_op jit(solution)/shard_map/pallas_call | solution.py:223
  25.3 0.0 copy-start.2
  25.3 3.4 %collective-permute-start.9 = (bf16[5,12,32,128]{3,2,1,0:T(8,128)(2,1)S(1)}, bf16[5,12,32,128]{3,2,1,0:T(8,128)(2,1)S(1)}, u32[]{:S(2)}, u32[]{:S(2)}) collective-permute-start(bf16[5,12,32,128]{3,2,1,0:T(8,128)(2,1)S(1)} %get-tuple-element.57.low), channel_id=1, source_target_pairs={{0,25},{1,0},{8,1},{9,8},{16,9},{17,16},{24,17},{25,24},{2,27},{3,... | collective-permute-start | bytes 1474568 | tf_op jit(solution)/shard_map/ppermute | solution.py:245
  28.6 1.7 %shard_map.52.close = bf16[3,12,32,128]{3,2,1,0:T(8,128)(2,1)S(1)} custom-call(s32[12,64]{1,0:T(8,128)S(1)} %bitcast.4, bf16[28,18,32,128]{3,2,1,0:T(8,128)(2,1)S(1)} %get-tuple-element.58.strips, bf16[8,18,128,128]{3,2,1,0:T(8,128)(2,1)S(1)} %get-tuple-element.54.left.refs_2_.refs_1_), custom_call_target="tpu_custom_call" | custom-call | flops 415236096 | bytes 9145344 | tf_op jit(solution)/shard_map/pallas_call | solution.py:223
  30.3 0.1 collective-permute-start.11
  30.4 0.0 copy-done.2
  30.4 5.2 %shard_map.53 = (bf16[38,18,32,128]{3,2,1,0:T(8,128)(2,1)S(1)}, f32[8,16,32,128]{3,2,1,0:T(8,128)S(1)}) custom-call(s32[12,64]{1,0:T(8,128)S(1)} %bitcast.5, s32[16,64]{1,0:T(8,128)S(1)} %bitcast.9, bf16[5,12,32,128]{3,2,1,0:T(8,128)(2,1)S(1)} %get-tuple-element.57.low, bf16[3,12,32,128]{3,2,1,0:T(8,128)(2,1)S(1)} %shard_map.52.close, ...), custom_call_target="tpu_custom_call" | custom-call | flops 1073741824 | bytes 13212672 | tf_op jit(solution)/shard_map/pallas_call | solution.py:223
  35.6 9.3 %collective-permute-done.9.refs_0_ = bf16[5,12,32,128]{3,2,1,0:T(8,128)(2,1)S(1)} collective-permute-done((bf16[5,12,32,128]{3,2,1,0:T(8,128)(2,1)S(1)}, bf16[5,12,32,128]{3,2,1,0:T(8,128)(2,1)S(1)}, u32[]{:S(2)}, u32[]{:S(2)}) %collective-permute-start.9) | collective-permute-done | bytes 491552 | tf_op jit(solution)/shard_map/ppermute | solution.py:245
  44.9 0.0 collective-permute-start.10
  44.9 0.0 collective-permute-done.11.refs_1_
  44.9 1.9 %shard_map.54 = (bf16[6,4,32,128]{3,2,1,0:T(8,128)(2,1)S(1)}, bf16[6,4,32,128]{3,2,1,0:T(8,128)(2,1)S(1)}, bf16[6,4,32,128]{3,2,1,0:T(8,128)(2,1)S(1)}, bf16[6,4...) custom-call(s32[12,64]{1,0:T(8,128)S(1)} %bitcast.6, ...), custom_call_target="tpu_custom_call", output_to_operand_aliasing={{4}: (6, {})} | custom-call | tf_op jit(solution)/shard_map/pallas_call | solution.py:223
  46.8 0.1 collective-permute-start.15
  46.9 0.6 collective-permute-start.16
  47.5 1.3 %collective-permute-start.17 = (bf16[6,4,32,128]{3,2,1,0:T(8,128)(2,1)S(1)}, bf16[6,4,32,128]{3,2,1,0:T(8,128)(2,1)S(1)}, u32[]{:S(2)}, u32[]{:S(2)}) collective-permute-start(bf16[6,4,32,128]{3,2,1,0:T(8,128)(2,1)S(1)} %get-tuple-element.72), channel_id=1, source_target_pairs={{0,6},{2,4},{4,2},{6,0},{1,7},{3,5},{5,3},{7,1},{8,14},{10,12},{12... | collective-permute-start | bytes 589832 | tf_op jit(solution)/shard_map/ppermute | solution.py:248
  48.7 1.2 %shard_map.55.refs_2_ = f32[2,16,32,128]{3,2,1,0:T(8,128)S(1)} custom-call(s32[12,64]{1,0:T(8,128)S(1)} %bitcast.7, s32[16,64]{1,0:T(8,128)S(1)} %bitcast.11, bf16[8,18,128,128]{3,2,1,0:T(8,128)(2,1)S(1)} %get-tuple-element.54.left.refs_2_.refs_1_, f32[8,16,32,128]{3,2,1,0:T(8,128)S(1)} %get-tuple-element.61.refs_3_.partial, ...), custom_call_target="tpu_custom_call" | custom-call | tf_op jit(solution)/shard_map/pallas_call | solution.py:223
  49.9 3.8 %collective-permute-done.10.refs_0_ = bf16[2,12,32,128]{3,2,1,0:T(8,128)(2,1)S(1)} collective-permute-done((bf16[2,12,32,128]{3,2,1,0:T(8,128)(2,1)S(1)}, bf16[2,12,32,128]{3,2,1,0:T(8,128)(2,1)S(1)}, u32[]{:S(2)}, u32[]{:S(2)}) %collective-permute-start.10) | collective-permute-done | bytes 196640 | tf_op jit(solution)/shard_map/ppermute | solution.py:245
  53.7 1.1 %shard_map.56 = (bf16[2,4,32,128]{3,2,1,0:T(8,128)(2,1)S(1)}, bf16[2,4,32,128]{3,2,1,0:T(8,128)(2,1)S(1)}, bf16[2,4,32,128]{3,2,1,0:T(8,128)(2,1)S(1)}, bf16[2,4...) custom-call(s32[12,64]{1,0:T(8,128)S(1)} %bitcast.8, ...), custom_call_target="tpu_custom_call", output_to_operand_aliasing={{4}: (5, {})} | custom-call | tf_op jit(solution)/shard_map/pallas_call | solution.py:223
  54.8 0.1 collective-permute-start.12
  54.9 0.6 collective-permute-start.13
  55.5 0.0 collective-permute-done.15.refs_1_
  55.5 1.3 %collective-permute-start.14 = (bf16[2,4,32,128]{3,2,1,0:T(8,128)(2,1)S(1)}, bf16[2,4,32,128]{3,2,1,0:T(8,128)(2,1)S(1)}, u32[]{:S(2)}, u32[]{:S(2)}) collective-permute-start(bf16[2,4,32,128]{3,2,1,0:T(8,128)(2,1)S(1)} %get-tuple-element.68), channel_id=1, source_target_pairs={{0,6},{2,4},{4,2},{6,0},{1,7},{3,5},{5,3},{7,1},{8,14},{10,12},{12... | collective-permute-start | bytes 196616 | tf_op jit(solution)/shard_map/ppermute | solution.py:248
  56.8 0.0 collective-permute-done.16.refs_2_
  56.8 1.2 %collective-permute-done.17.refs_3_ = bf16[6,4,32,128]{3,2,1,0:T(8,128)(2,1)S(1)} collective-permute-done((bf16[6,4,32,128]{3,2,1,0:T(8,128)(2,1)S(1)}, bf16[6,4,32,128]{3,2,1,0:T(8,128)(2,1)S(1)}, u32[]{:S(2)}, u32[]{:S(2)}) %collective-permute-start.17) | collective-permute-done | bytes 196640 | tf_op jit(solution)/shard_map/ppermute | solution.py:248
  58.0 1.3 %shard_map.57.refs_4_ = f32[8,4,128,128]{3,2,1,0:T(8,128)} custom-call(bf16[6,4,32,128]{3,2,1,0:T(8,128)(2,1)S(1)} %get-tuple-element.69.refs_0_, bf16[6,4,32,128]{3,2,1,0:T(8,128)(2,1)S(1)} %collective-permute-done.15.refs_1_, bf16[6,4,32,128]{3,2,1,0:T(8,128)(2,1)S(1)} %collective-permute-done.16.refs_2_, ...), custom_call_target="tpu_custom_call" | custom-call | bytes 2883584 | tf_op jit(solution)/shard_map/pallas_call | solution.py:223
  59.3 0.0 collective-permute-done.12.refs_1_
  59.3 0.8 %collective-permute-done.13.refs_2_ = bf16[2,4,32,128]{3,2,1,0:T(8,128)(2,1)S(1)} collective-permute-done((bf16[2,4,32,128]{3,2,1,0:T(8,128)(2,1)S(1)}, bf16[2,4,32,128]{3,2,1,0:T(8,128)(2,1)S(1)}, u32[]{:S(2)}, u32[]{:S(2)}) %collective-permute-start.13) | collective-permute-done | bytes 65568 | tf_op jit(solution)/shard_map/ppermute | solution.py:248
  60.1 0.7 %collective-permute-done.14.refs_3_ = bf16[2,4,32,128]{3,2,1,0:T(8,128)(2,1)S(1)} collective-permute-done((bf16[2,4,32,128]{3,2,1,0:T(8,128)(2,1)S(1)}, bf16[2,4,32,128]{3,2,1,0:T(8,128)(2,1)S(1)}, u32[]{:S(2)}, u32[]{:S(2)}) %collective-permute-start.14) | collective-permute-done | bytes 65568 | tf_op jit(solution)/shard_map/ppermute | solution.py:248
  60.9 0.9 %shard_map.58 = f32[8,4,128,128]{3,2,1,0:T(8,128)} custom-call(bf16[2,4,32,128]{3,2,1,0:T(8,128)(2,1)S(1)} %get-tuple-element.65.refs_0_, bf16[2,4,32,128]{3,2,1,0:T(8,128)(2,1)S(1)} %collective-permute-done.12.refs_1_, bf16[2,4,32,128]{3,2,1,0:T(8,128)(2,1)S(1)} %collective-permute-done.13.refs_2_, ...), custom_call_target="tpu_custom_call", output_to_operand_aliasing={{}: (4, {})} | custom-call | bytes 4456448 | tf_op jit(solution)/shard_map/pallas_call | solution.py:223
  (2 shorter events, 0.1 us)
Async XLA Ops:
  0.0 1.1 %copy-start = (bf16[8,11,32,128]{3,2,1,0:T(8,128)(2,1)S(1)}, bf16[8,11,32,128]{3,2,1,0:T(8,128)(2,1)}, u32[]{:S(2)}) copy-start(bf16[8,11,32,128]{3,2,1,0:T(8,128)(2,1)} %density.1) | copy-start | bytes 2162692
  1.1 0.7 %copy-start.3 = (s32[64,11]{0,1:T(8,128)S(1)}, s32[64,11]{0,1:T(8,128)}, u32[]{:S(2)}) copy-start(s32[64,11]{0,1:T(8,128)} %param.5) | copy-start | bytes 8452
  2.9 7.8 %collective-permute-start.3 = (bf16[63,32,128]{2,1,0:T(8,128)(2,1)S(1)}, bf16[63,32,128]{2,1,0:T(8,128)(2,1)S(1)}, u32[]{:S(2)}, u32[]{:S(2)}) collective-permute-start(bf16[63,32,128]{2,1,0:T(8,128)(2,1)S(1)} %get-tuple-element.41.upper), channel_id=1, source_target_pairs={{0,2},{2,0},{4,6},{6,4},{1,3},{3,1},{5,7},{7,5},{8,10},{10,8},{12,... | collective-permute-start | bytes 1548296 | tf_op jit(solution)/shard_map/ppermute | solution.py:248
  3.4 16.9 %collective-permute-start.2 = (bf16[63,32,128]{2,1,0:T(8,128)(2,1)S(1)}, bf16[63,32,128]{2,1,0:T(8,128)(2,1)S(1)}, u32[]{:S(2)}, u32[]{:S(2)}) collective-permute-start(bf16[63,32,128]{2,1,0:T(8,128)(2,1)S(1)} %get-tuple-element.41.upper), channel_id=1, source_target_pairs={{0,4},{2,6},{4,0},{6,2},{1,5},{3,7},{5,1},{7,3},{8,12},{10,14},{12... | collective-permute-start | bytes 1548296 | tf_op jit(solution)/shard_map/ppermute | solution.py:248
  6.0 16.8 %collective-permute-start = (bf16[37,32,128]{2,1,0:T(8,128)(2,1)S(1)}, bf16[37,32,128]{2,1,0:T(8,128)(2,1)S(1)}, u32[]{:S(2)}, u32[]{:S(2)}) collective-permute-start(bf16[37,32,128]{2,1,0:T(8,128)(2,1)S(1)} %get-tuple-element.39), channel_id=1, source_target_pairs={{0,1},{1,8},{8,9},{9,16},{16,17},{17,24},{24,25},{25,0},{2,3},{3,1... | collective-permute-start | bytes 909320 | tf_op jit(solution)/shard_map/ppermute | solution.py:245
  7.5 15.5 %collective-permute-start.1 = (bf16[37,32,128]{2,1,0:T(8,128)(2,1)S(1)}, bf16[37,32,128]{2,1,0:T(8,128)(2,1)S(1)}, u32[]{:S(2)}, u32[]{:S(2)}) collective-permute-start(bf16[37,32,128]{2,1,0:T(8,128)(2,1)S(1)} %get-tuple-element.40), channel_id=1, source_target_pairs={{0,25},{1,0},{8,1},{9,8},{16,9},{17,16},{24,17},{25,24},{2,27},{3,... | collective-permute-start | bytes 909320 | tf_op jit(solution)/shard_map/ppermute | solution.py:245
  10.7 9.6 %collective-permute-start.4 = (bf16[3,32,128]{2,1,0:T(8,128)(2,1)S(1)}, bf16[3,32,128]{2,1,0:T(8,128)(2,1)S(1)}, u32[]{:S(2)}, u32[]{:S(2)}) collective-permute-start(bf16[3,32,128]{2,1,0:T(8,128)(2,1)S(1)} %get-tuple-element.44), channel_id=1, source_target_pairs={{0,8},{1,9},{8,16},{9,17},{16,24},{17,25},{24,0},{25,1},{2,10},{3,... | collective-permute-start | bytes 73736 | tf_op jit(solution)/shard_map/ppermute | solution.py:245
  10.7 9.6 %collective-permute-start.5 = (bf16[3,32,128]{2,1,0:T(8,128)(2,1)S(1)}, bf16[3,32,128]{2,1,0:T(8,128)(2,1)S(1)}, u32[]{:S(2)}, u32[]{:S(2)}) collective-permute-start(bf16[3,32,128]{2,1,0:T(8,128)(2,1)S(1)} %get-tuple-element.45), channel_id=1, source_target_pairs={{0,24},{1,25},{8,0},{9,1},{16,8},{17,9},{24,16},{25,17},{2,26},{3,... | collective-permute-start | bytes 73736 | tf_op jit(solution)/shard_map/ppermute | solution.py:245
  20.4 1.5 %collective-permute-start.6 = (bf16[21,32,128]{2,1,0:T(8,128)(2,1)S(1)}, bf16[21,32,128]{2,1,0:T(8,128)(2,1)S(1)}, u32[]{:S(2)}, u32[]{:S(2)}) collective-permute-start(bf16[21,32,128]{2,1,0:T(8,128)(2,1)S(1)} %get-tuple-element.49), channel_id=1, source_target_pairs={{0,2},{2,0},{4,6},{6,4},{1,3},{3,1},{5,7},{7,5},{8,10},{10,8},{12,... | collective-permute-start | bytes 516104 | tf_op jit(solution)/shard_map/ppermute | solution.py:248
  20.4 1.6 %collective-permute-start.7 = (bf16[21,32,128]{2,1,0:T(8,128)(2,1)S(1)}, bf16[21,32,128]{2,1,0:T(8,128)(2,1)S(1)}, u32[]{:S(2)}, u32[]{:S(2)}) collective-permute-start(bf16[21,32,128]{2,1,0:T(8,128)(2,1)S(1)} %get-tuple-element.50), channel_id=1, source_target_pairs={{0,2},{2,0},{4,6},{6,4},{1,3},{3,1},{5,7},{7,5},{8,10},{10,8},{12,... | collective-permute-start | bytes 516104 | tf_op jit(solution)/shard_map/ppermute | solution.py:248
  20.9 1.4 %collective-permute-start.8 = (bf16[21,32,128]{2,1,0:T(8,128)(2,1)S(1)}, bf16[21,32,128]{2,1,0:T(8,128)(2,1)S(1)}, u32[]{:S(2)}, u32[]{:S(2)}) collective-permute-start(bf16[21,32,128]{2,1,0:T(8,128)(2,1)S(1)} %get-tuple-element.51), channel_id=1, source_target_pairs={{0,2},{2,0},{4,6},{6,4},{1,3},{3,1},{5,7},{7,5},{8,10},{10,8},{12,... | collective-permute-start | bytes 516104 | tf_op jit(solution)/shard_map/ppermute | solution.py:248
  21.1 1.9 %copy-start.1 = (s32[64,12]{0,1:T(8,128)S(1)}, s32[64,12]{0,1:T(8,128)}, u32[]{:S(2)}) copy-start(s32[64,12]{0,1:T(8,128)} %param.6) | copy-start | bytes 9220
  25.3 5.1 %copy-start.2 = (s32[64,16]{0,1:T(8,128)S(1)}, s32[64,16]{0,1:T(8,128)}, u32[]{:S(2)}) copy-start(s32[64,16]{0,1:T(8,128)} %param.7) | copy-start | bytes 12292
  25.3 19.6 %collective-permute-start.9 = (bf16[5,12,32,128]{3,2,1,0:T(8,128)(2,1)S(1)}, bf16[5,12,32,128]{3,2,1,0:T(8,128)(2,1)S(1)}, u32[]{:S(2)}, u32[]{:S(2)}) collective-permute-start(bf16[5,12,32,128]{3,2,1,0:T(8,128)(2,1)S(1)} %get-tuple-element.57.low), channel_id=1, source_target_pairs={{0,25},{1,0},{8,1},{9,8},{16,9},{17,16},{24,17},{25,24},{2,27},{3,... | collective-permute-start | bytes 1474568 | tf_op jit(solution)/shard_map/ppermute | solution.py:245
  30.3 14.6 %collective-permute-start.11 = (bf16[3,12,32,128]{3,2,1,0:T(8,128)(2,1)S(1)}, bf16[3,12,32,128]{3,2,1,0:T(8,128)(2,1)S(1)}, u32[]{:S(2)}, u32[]{:S(2)}) collective-permute-start(bf16[3,12,32,128]{3,2,1,0:T(8,128)(2,1)S(1)} %shard_map.52.close), channel_id=1, source_target_pairs={{0,1},{1,8},{8,9},{9,16},{16,17},{17,24},{24,25},{25,0},{2,3},{3,1... | collective-permute-start | bytes 884744 | tf_op jit(solution)/shard_map/ppermute | solution.py:245
  44.9 8.8 %collective-permute-start.10 = (bf16[2,12,32,128]{3,2,1,0:T(8,128)(2,1)S(1)}, bf16[2,12,32,128]{3,2,1,0:T(8,128)(2,1)S(1)}, u32[]{:S(2)}, u32[]{:S(2)}) collective-permute-start(bf16[2,12,32,128]{3,2,1,0:T(8,128)(2,1)S(1)} %get-tuple-element.60), channel_id=1, source_target_pairs={{0,1},{1,8},{8,9},{9,16},{16,17},{17,24},{24,25},{25,0},{2,3},{3,1... | collective-permute-start | bytes 589832 | tf_op jit(solution)/shard_map/ppermute | solution.py:245
  46.8 8.7 %collective-permute-start.15 = (bf16[6,4,32,128]{3,2,1,0:T(8,128)(2,1)S(1)}, bf16[6,4,32,128]{3,2,1,0:T(8,128)(2,1)S(1)}, u32[]{:S(2)}, u32[]{:S(2)}) collective-permute-start(bf16[6,4,32,128]{3,2,1,0:T(8,128)(2,1)S(1)} %get-tuple-element.70), channel_id=1, source_target_pairs={{0,2},{2,0},{4,6},{6,4},{1,3},{3,1},{5,7},{7,5},{8,10},{10,8},{12,... | collective-permute-start | bytes 589832 | tf_op jit(solution)/shard_map/ppermute | solution.py:248
  46.9 9.9 %collective-permute-start.16 = (bf16[6,4,32,128]{3,2,1,0:T(8,128)(2,1)S(1)}, bf16[6,4,32,128]{3,2,1,0:T(8,128)(2,1)S(1)}, u32[]{:S(2)}, u32[]{:S(2)}) collective-permute-start(bf16[6,4,32,128]{3,2,1,0:T(8,128)(2,1)S(1)} %get-tuple-element.71), channel_id=1, source_target_pairs={{0,4},{2,6},{4,0},{6,2},{1,5},{3,7},{5,1},{7,3},{8,12},{10,14},{12... | collective-permute-start | bytes 589832 | tf_op jit(solution)/shard_map/ppermute | solution.py:248
  47.5 10.5 %collective-permute-start.17 = (bf16[6,4,32,128]{3,2,1,0:T(8,128)(2,1)S(1)}, bf16[6,4,32,128]{3,2,1,0:T(8,128)(2,1)S(1)}, u32[]{:S(2)}, u32[]{:S(2)}) collective-permute-start(bf16[6,4,32,128]{3,2,1,0:T(8,128)(2,1)S(1)} %get-tuple-element.72), channel_id=1, source_target_pairs={{0,6},{2,4},{4,2},{6,0},{1,7},{3,5},{5,3},{7,1},{8,14},{10,12},{12... | collective-permute-start | bytes 589832 | tf_op jit(solution)/shard_map/ppermute | solution.py:248
  54.8 4.5 %collective-permute-start.12 = (bf16[2,4,32,128]{3,2,1,0:T(8,128)(2,1)S(1)}, bf16[2,4,32,128]{3,2,1,0:T(8,128)(2,1)S(1)}, u32[]{:S(2)}, u32[]{:S(2)}) collective-permute-start(bf16[2,4,32,128]{3,2,1,0:T(8,128)(2,1)S(1)} %get-tuple-element.66), channel_id=1, source_target_pairs={{0,2},{2,0},{4,6},{6,4},{1,3},{3,1},{5,7},{7,5},{8,10},{10,8},{12,... | collective-permute-start | bytes 196616 | tf_op jit(solution)/shard_map/ppermute | solution.py:248
  54.9 5.2 %collective-permute-start.13 = (bf16[2,4,32,128]{3,2,1,0:T(8,128)(2,1)S(1)}, bf16[2,4,32,128]{3,2,1,0:T(8,128)(2,1)S(1)}, u32[]{:S(2)}, u32[]{:S(2)}) collective-permute-start(bf16[2,4,32,128]{3,2,1,0:T(8,128)(2,1)S(1)} %get-tuple-element.67), channel_id=1, source_target_pairs={{0,4},{2,6},{4,0},{6,2},{1,5},{3,7},{5,1},{7,3},{8,12},{10,14},{12... | collective-permute-start | bytes 196616 | tf_op jit(solution)/shard_map/ppermute | solution.py:248
  55.5 5.4 %collective-permute-start.14 = (bf16[2,4,32,128]{3,2,1,0:T(8,128)(2,1)S(1)}, bf16[2,4,32,128]{3,2,1,0:T(8,128)(2,1)S(1)}, u32[]{:S(2)}, u32[]{:S(2)}) collective-permute-start(bf16[2,4,32,128]{3,2,1,0:T(8,128)(2,1)S(1)} %get-tuple-element.68), channel_id=1, source_target_pairs={{0,6},{2,4},{4,2},{6,0},{1,7},{3,5},{5,3},{7,1},{8,14},{10,12},{12... | collective-permute-start | bytes 196616 | tf_op jit(solution)/shard_map/ppermute | solution.py:248

commit v9 on v8

--- a/solution.py
+++ b/solution.py
@@ -119,15 +119,18 @@
     return acc.reshape(len(targets), 32, 128).astype(strips.dtype)
 
 
-def low_kernel(kept, h0, h1, h2, h3, left, strips_in, low, far, strips):
+def low_kernel(kept, h0, h1, h2, h3, left, strips_in, low, far, strips, table, sem):
     del strips_in
+    copy = pltpu.make_async_copy(kept, table, sem)
+    copy.start()
     first = own_place()[1]
     for halo, entries, shift in zip((h0, h1, h2, h3), LISTS, SHIFTS):
         for e, (j, o) in enumerate(entries):
             row = j - shift * ROWS
             strips[row + 2 * RADIUS, row + o] = halo[e]
+    copy.wait()
     for i in range(RADIUS):
-        row = square_row(kept, strips, left, i, first)
+        row = square_row(table, strips, left, i, first)
         low[i] = row
         if i >= ROWS - RADIUS:
             far[i - ROWS + RADIUS] = row
@@ -180,13 +183,19 @@
 
 def outer_kernel(rows, start, places, arrived):
     def kernel(kept, cube, *refs):
-        halos, (left, partial, _, o0, o1, o2, o3, strips) = refs[:-8], refs[-8:]
+        halos, (left, partial, _, o0, o1, o2, o3, strips, near, wanted, sems) = refs[:-11], refs[-11:]
+        first_copy = pltpu.make_async_copy(kept, near, sems.at[0])
+        second_copy = pltpu.make_async_copy(cube, wanted, sems.at[1])
+        first_copy.start()
+        second_copy.start()
         col, first = own_place()
+        first_copy.wait()
         for halo, span in zip(halos, arrived):
-            insert_rows(strips, kept, halo, span, first)
+            insert_rows(strips, near, halo, span, first)
+        second_copy.wait()
         share = cube.shape[0] // 4
         for n, i in enumerate(rows):
-            targets = cube_targets(cube, i, col, first, share)
+            targets = cube_targets(wanted, i, col, first, share)
             acc = gather_dot(strips, left, targets, i, [p for p in places if i <= p < i + BAND])
             for e in range(len(targets)):
                 piece = partial[i - start, e] - 2.0 * acc[e * 32 : (e + 1) * 32]
@@ -271,9 +280,10 @@
     )
     work = 2 * width * BAND * 128 * 128 * 32
     low, far, strips = call(
-        low_kernel, [SMEM] + [VMEM] * 6,
+        low_kernel, [ANY] + [VMEM] * 6,
         [shape(RADIUS, width, *piece), shape(len(FAR), width, *piece), both[0]],
-        (kept, *halos, left, strips), flops=work * RADIUS, aliases={6: 2},
+        (kept, *halos, left, strips),
+        [pltpu.SMEM(kept.shape, kept.dtype), pltpu.SemaphoreType.DMA], flops=work * RADIUS, aliases={6: 2},
     )
     after = shifted(low, -1)
     close = call(
@@ -293,9 +303,11 @@
 
     def rest(rows, start, places, halos, partial, strips):
         *own, strips = call(
-            outer_kernel(rows, start, places, [p for p, _ in halos]), [SMEM] * 2 + [VMEM] * (3 + len(halos)),
+            outer_kernel(rows, start, places, [p for p, _ in halos]), [ANY] * 2 + [VMEM] * (3 + len(halos)),
             [shape(len(rows), share, *piece)] * 4 + [shape(*strips.shape)],
-            (*tables, *(h for _, h in halos), left, partial, strips), aliases={4 + len(halos): 4}, free=True,
+            (*tables, *(h for _, h in halos), left, partial, strips),
+            [pltpu.SMEM(kept.shape, kept.dtype), pltpu.SMEM(cube.shape, cube.dtype), pltpu.SemaphoreType.DMA((2,))],
+            aliases={4 + len(halos): 4}, free=True,
         )
         return [own[0], *(across(own[b], b) for b in (1, 2, 3))], strips
 

time: 62 us -> 61.9 us (level)
  no operation moved by 1% of the time
where the time goes in v9:
time: 61.9 us; the launch traced here: 61.7 us
  waiting for transfers between devices  21.8 us (35%)
  starting transfers between devices  19.6 us (32%)
  Pallas kernels  18.3 us (30%)
  local copies, waits for them, and re-layouts  1.82 us (3%)
    pallas_call x13, Pallas kernels, call(): pl.pallas_call(kernel, out_shape=outs, in_specs=specs, out_specs=out_spec...  18.3 us
    ppermute x7, waiting for transfers between devices, shifted(): lax.ppermute(x, ('row', 'layer'), [(g, (g + d) % groups) for g in range(g...  17.8 us
    ppermute x7, starting transfers between devices, shifted(): lax.ppermute(x, ('row', 'layer'), [(g, (g + d) % groups) for g in range(g...  12 us
    ppermute x11, starting transfers between devices, across(): return lax.ppermute(x, 'col', [(c, c ^ bits) for c in range(4)])  7.59 us
    ppermute x11, waiting for transfers between devices, across(): return lax.ppermute(x, 'col', [(c, c ^ bits) for c in range(4)])  4.03 us
    unnamed x8, local copies, waits for them, and re-layouts  1.82 us
  transfers between devices with their start and end apart: 18, of which 10 were waited for; matrix products, arithmetic and copies ran while one was open for 0% of the time, Pallas kernels for 23%

profile of v9, /device:TPU:0, one launch (start us, length us, event | category | flops | bytes accessed | tf_op | source)
XLA Modules:
  0.0 61.7 jit_solution(17493062304945619537)
XLA Ops:
  0.0 0.0 copy-start
  0.0 1.1 %copy-done = bf16[8,11,32,128]{3,2,1,0:T(8,128)(2,1)S(1)} copy-done((bf16[8,11,32,128]{3,2,1,0:T(8,128)(2,1)S(1)}, bf16[8,11,32,128]{3,2,1,0:T(8,128)(2,1)}, u32[]{:S(2)}) %copy-start) | copy-done | bytes 720920
  1.1 0.0 copy-start.3
  1.1 0.7 %copy-done.3 = s32[64,11]{0,1:T(8,128)S(1)} copy-done((s32[64,11]{0,1:T(8,128)S(1)}, s32[64,11]{0,1:T(8,128)}, u32[]{:S(2)}) %copy-start.3) | copy-done | bytes 2840
  1.8 1.1 %shard_map.46 = (bf16[37,32,128]{2,1,0:T(8,128)(2,1)S(1)}, bf16[37,32,128]{2,1,0:T(8,128)(2,1)S(1)}, bf16[3,32,128]{2,1,0:T(8,128)(2,1)S(1)}, bf16[3,32,128]{2,1...) custom-call(s32[11,64]{1,0:T(8,128)S(1)} %bitcast.13, ...), custom_call_target="tpu_custom_call" | custom-call | bytes 2681600 | tf_op jit(solution)/shard_map/pallas_call | solution.py:232
  2.9 0.5 collective-permute-start.3
  3.4 2.6 %collective-permute-start.2 = (bf16[63,32,128]{2,1,0:T(8,128)(2,1)S(1)}, bf16[63,32,128]{2,1,0:T(8,128)(2,1)S(1)}, u32[]{:S(2)}, u32[]{:S(2)}) collective-permute-start(bf16[63,32,128]{2,1,0:T(8,128)(2,1)S(1)} %get-tuple-element.41.upper), channel_id=1, source_target_pairs={{0,4},{2,6},{4,0},{6,2},{1,5},{3,7},{5,1},{7,3},{8,12},{10,14},{12... | collective-permute-start | bytes 1548296 | tf_op jit(solution)/shard_map/ppermute | solution.py:257
  6.0 1.5 %collective-permute-start = (bf16[37,32,128]{2,1,0:T(8,128)(2,1)S(1)}, bf16[37,32,128]{2,1,0:T(8,128)(2,1)S(1)}, u32[]{:S(2)}, u32[]{:S(2)}) collective-permute-start(bf16[37,32,128]{2,1,0:T(8,128)(2,1)S(1)} %get-tuple-element.39), channel_id=1, source_target_pairs={{0,1},{1,8},{8,9},{9,16},{16,17},{17,24},{24,25},{25,0},{2,3},{3,1... | collective-permute-start | bytes 909320 | tf_op jit(solution)/shard_map/ppermute | solution.py:254
  7.5 3.2 %collective-permute-start.1 = (bf16[37,32,128]{2,1,0:T(8,128)(2,1)S(1)}, bf16[37,32,128]{2,1,0:T(8,128)(2,1)S(1)}, u32[]{:S(2)}, u32[]{:S(2)}) collective-permute-start(bf16[37,32,128]{2,1,0:T(8,128)(2,1)S(1)} %get-tuple-element.40), channel_id=1, source_target_pairs={{0,25},{1,0},{8,1},{9,8},{16,9},{17,16},{24,17},{25,24},{2,27},{3,... | collective-permute-start | bytes 909320 | tf_op jit(solution)/shard_map/ppermute | solution.py:254
  10.7 0.0 collective-permute-start.4
  10.7 0.0 collective-permute-done.3.u1
  10.7 3.8 %collective-permute-start.5 = (bf16[3,32,128]{2,1,0:T(8,128)(2,1)S(1)}, bf16[3,32,128]{2,1,0:T(8,128)(2,1)S(1)}, u32[]{:S(2)}, u32[]{:S(2)}) collective-permute-start(bf16[3,32,128]{2,1,0:T(8,128)(2,1)S(1)} %get-tuple-element.45), channel_id=1, source_target_pairs={{0,24},{1,25},{8,0},{9,1},{16,8},{17,9},{24,16},{25,17},{2,26},{3,... | collective-permute-start | bytes 73736 | tf_op jit(solution)/shard_map/ppermute | solution.py:254
  14.6 1.3 %shard_map.47 = (bf16[28,18,32,128]{3,2,1,0:T(8,128)(2,1)S(1)}, bf16[8,18,128,128]{3,2,1,0:T(8,128)(2,1)S(1)}) custom-call(bf16[8,12,32,128]{3,2,1,0:T(8,128)(2,1)S(1)} %get-tuple-element.42.band, bf16[63,32,128]{2,1,0:T(8,128)(2,1)S(1)} %get-tuple-element.41.upper, bf16[63,32,128]{2,1,0:T(8,128)(2,1)S(1)} %collective-permute-done.3.u1), custom_call_target="tpu_custom_call" | custom-call | bytes 10665984 | tf_op jit(solution)/shard_map/pallas_call | solution.py:232
  15.8 4.5 %collective-permute-done.4.h2 = bf16[3,32,128]{2,1,0:T(8,128)(2,1)S(1)} collective-permute-done((bf16[3,32,128]{2,1,0:T(8,128)(2,1)S(1)}, bf16[3,32,128]{2,1,0:T(8,128)(2,1)S(1)}, u32[]{:S(2)}, u32[]{:S(2)}) %collective-permute-start.4) | collective-permute-done | bytes 24608 | tf_op jit(solution)/shard_map/ppermute | solution.py:254
  20.3 0.0 collective-permute-done.5.h3
  20.3 0.0 collective-permute-done.2.u2
  20.4 0.1 collective-permute-start.6
  20.4 0.5 collective-permute-start.7
  20.9 0.1 collective-permute-start.8
  21.1 0.0 copy-start.1
  21.1 0.8 %collective-permute-done.6.refs_0_ = bf16[21,32,128]{2,1,0:T(8,128)(2,1)S(1)} collective-permute-done((bf16[21,32,128]{2,1,0:T(8,128)(2,1)S(1)}, bf16[21,32,128]{2,1,0:T(8,128)(2,1)S(1)}, u32[]{:S(2)}, u32[]{:S(2)}) %collective-permute-start.6) | collective-permute-done | bytes 172064 | tf_op jit(solution)/shard_map/ppermute | solution.py:257
  21.8 0.2 collective-permute-done.7.refs_1_
  22.1 0.3 collective-permute-done.8.refs_2_
  22.3 0.5 shard_map.50
  22.8 0.0 collective-permute-done.h0
  22.9 0.1 collective-permute-done.1.h1
  23.0 0.0 copy-done.1
  23.0 2.2 %shard_map.51 = (bf16[5,12,32,128]{3,2,1,0:T(8,128)(2,1)S(1)}, bf16[2,12,32,128]{3,2,1,0:T(8,128)(2,1)S(1)}, bf16[28,18,32,128]{3,2,1,0:T(8,128)(2,1)S(1)}) custom-call(s32[12,64]{1,0:T(8,128)S(1)} %bitcast.3, bf16[37,32,128]{2,1,0:T(8,128)(2,1)S(1)} %collective-permute-done.h0, ...), custom_call_target="tpu_custom_call", output_to_operand_aliasing={{2}: (6, {})} | custom-call | flops 692060160 | bytes 14322688 | tf_op jit(solution)/shard_map/pallas_call | solution.py:232
  25.2 0.0 copy-start.2
  25.2 3.4 %collective-permute-start.9 = (bf16[5,12,32,128]{3,2,1,0:T(8,128)(2,1)S(1)}, bf16[5,12,32,128]{3,2,1,0:T(8,128)(2,1)S(1)}, u32[]{:S(2)}, u32[]{:S(2)}) collective-permute-start(bf16[5,12,32,128]{3,2,1,0:T(8,128)(2,1)S(1)} %get-tuple-element.57.low), channel_id=1, source_target_pairs={{0,25},{1,0},{8,1},{9,8},{16,9},{17,16},{24,17},{25,24},{2,27},{3,... | collective-permute-start | bytes 1474568 | tf_op jit(solution)/shard_map/ppermute | solution.py:254
  28.6 1.7 %shard_map.52.close = bf16[3,12,32,128]{3,2,1,0:T(8,128)(2,1)S(1)} custom-call(s32[12,64]{1,0:T(8,128)S(1)} %bitcast.4, bf16[28,18,32,128]{3,2,1,0:T(8,128)(2,1)S(1)} %get-tuple-element.58.strips, bf16[8,18,128,128]{3,2,1,0:T(8,128)(2,1)S(1)} %get-tuple-element.54.left.refs_2_.refs_1_), custom_call_target="tpu_custom_call" | custom-call | flops 415236096 | bytes 9145344 | tf_op jit(solution)/shard_map/pallas_call | solution.py:232
  30.3 0.1 collective-permute-start.11
  30.4 0.0 copy-done.2
  30.4 5.2 %shard_map.53 = (bf16[38,18,32,128]{3,2,1,0:T(8,128)(2,1)S(1)}, f32[8,16,32,128]{3,2,1,0:T(8,128)S(1)}) custom-call(s32[12,64]{1,0:T(8,128)S(1)} %bitcast.5, s32[16,64]{1,0:T(8,128)S(1)} %bitcast.9, bf16[5,12,32,128]{3,2,1,0:T(8,128)(2,1)S(1)} %get-tuple-element.57.low, bf16[3,12,32,128]{3,2,1,0:T(8,128)(2,1)S(1)} %shard_map.52.close, ...), custom_call_target="tpu_custom_call" | custom-call | flops 1073741824 | bytes 13212672 | tf_op jit(solution)/shard_map/pallas_call | solution.py:232
  35.6 9.3 %collective-permute-done.9.refs_0_ = bf16[5,12,32,128]{3,2,1,0:T(8,128)(2,1)S(1)} collective-permute-done((bf16[5,12,32,128]{3,2,1,0:T(8,128)(2,1)S(1)}, bf16[5,12,32,128]{3,2,1,0:T(8,128)(2,1)S(1)}, u32[]{:S(2)}, u32[]{:S(2)}) %collective-permute-start.9) | collective-permute-done | bytes 491552 | tf_op jit(solution)/shard_map/ppermute | solution.py:254
  44.9 0.0 collective-permute-start.10
  44.9 0.0 collective-permute-done.11.refs_1_
  44.9 1.8 %shard_map.54 = (bf16[6,4,32,128]{3,2,1,0:T(8,128)(2,1)S(1)}, bf16[6,4,32,128]{3,2,1,0:T(8,128)(2,1)S(1)}, bf16[6,4,32,128]{3,2,1,0:T(8,128)(2,1)S(1)}, bf16[6,4...) custom-call(s32[12,64]{1,0:T(8,128)S(1)} %bitcast.6, ...), custom_call_target="tpu_custom_call", output_to_operand_aliasing={{4}: (6, {})} | custom-call | tf_op jit(solution)/shard_map/pallas_call | solution.py:232
  46.6 0.1 collective-permute-start.15
  46.7 0.6 collective-permute-start.16
  47.3 1.3 %collective-permute-start.17 = (bf16[6,4,32,128]{3,2,1,0:T(8,128)(2,1)S(1)}, bf16[6,4,32,128]{3,2,1,0:T(8,128)(2,1)S(1)}, u32[]{:S(2)}, u32[]{:S(2)}) collective-permute-start(bf16[6,4,32,128]{3,2,1,0:T(8,128)(2,1)S(1)} %get-tuple-element.72), channel_id=1, source_target_pairs={{0,6},{2,4},{4,2},{6,0},{1,7},{3,5},{5,3},{7,1},{8,14},{10,12},{12... | collective-permute-start | bytes 589832 | tf_op jit(solution)/shard_map/ppermute | solution.py:257
  48.6 1.2 %shard_map.55.refs_2_ = f32[2,16,32,128]{3,2,1,0:T(8,128)S(1)} custom-call(s32[12,64]{1,0:T(8,128)S(1)} %bitcast.7, s32[16,64]{1,0:T(8,128)S(1)} %bitcast.11, bf16[8,18,128,128]{3,2,1,0:T(8,128)(2,1)S(1)} %get-tuple-element.54.left.refs_2_.refs_1_, f32[8,16,32,128]{3,2,1,0:T(8,128)S(1)} %get-tuple-element.61.refs_3_.partial, ...), custom_call_target="tpu_custom_call" | custom-call | tf_op jit(solution)/shard_map/pallas_call | solution.py:232
  49.7 3.9 %collective-permute-done.10.refs_0_ = bf16[2,12,32,128]{3,2,1,0:T(8,128)(2,1)S(1)} collective-permute-done((bf16[2,12,32,128]{3,2,1,0:T(8,128)(2,1)S(1)}, bf16[2,12,32,128]{3,2,1,0:T(8,128)(2,1)S(1)}, u32[]{:S(2)}, u32[]{:S(2)}) %collective-permute-start.10) | collective-permute-done | bytes 196640 | tf_op jit(solution)/shard_map/ppermute | solution.py:254
  53.6 1.1 %shard_map.56 = (bf16[2,4,32,128]{3,2,1,0:T(8,128)(2,1)S(1)}, bf16[2,4,32,128]{3,2,1,0:T(8,128)(2,1)S(1)}, bf16[2,4,32,128]{3,2,1,0:T(8,128)(2,1)S(1)}, bf16[2,4...) custom-call(s32[12,64]{1,0:T(8,128)S(1)} %bitcast.8, ...), custom_call_target="tpu_custom_call", output_to_operand_aliasing={{4}: (5, {})} | custom-call | tf_op jit(solution)/shard_map/pallas_call | solution.py:232
  54.7 0.1 collective-permute-start.12
  54.8 0.6 collective-permute-start.13
  55.4 0.0 collective-permute-done.15.refs_1_
  55.4 1.3 %collective-permute-start.14 = (bf16[2,4,32,128]{3,2,1,0:T(8,128)(2,1)S(1)}, bf16[2,4,32,128]{3,2,1,0:T(8,128)(2,1)S(1)}, u32[]{:S(2)}, u32[]{:S(2)}) collective-permute-start(bf16[2,4,32,128]{3,2,1,0:T(8,128)(2,1)S(1)} %get-tuple-element.68), channel_id=1, source_target_pairs={{0,6},{2,4},{4,2},{6,0},{1,7},{3,5},{5,3},{7,1},{8,14},{10,12},{12... | collective-permute-start | bytes 196616 | tf_op jit(solution)/shard_map/ppermute | solution.py:257
  56.7 0.0 collective-permute-done.16.refs_2_
  56.7 1.1 %collective-permute-done.17.refs_3_ = bf16[6,4,32,128]{3,2,1,0:T(8,128)(2,1)S(1)} collective-permute-done((bf16[6,4,32,128]{3,2,1,0:T(8,128)(2,1)S(1)}, bf16[6,4,32,128]{3,2,1,0:T(8,128)(2,1)S(1)}, u32[]{:S(2)}, u32[]{:S(2)}) %collective-permute-start.17) | collective-permute-done | bytes 196640 | tf_op jit(solution)/shard_map/ppermute | solution.py:257
  57.8 1.3 %shard_map.57.refs_4_ = f32[8,4,128,128]{3,2,1,0:T(8,128)} custom-call(bf16[6,4,32,128]{3,2,1,0:T(8,128)(2,1)S(1)} %get-tuple-element.69.refs_0_, bf16[6,4,32,128]{3,2,1,0:T(8,128)(2,1)S(1)} %collective-permute-done.15.refs_1_, bf16[6,4,32,128]{3,2,1,0:T(8,128)(2,1)S(1)} %collective-permute-done.16.refs_2_, ...), custom_call_target="tpu_custom_call" | custom-call | bytes 2883584 | tf_op jit(solution)/shard_map/pallas_call | solution.py:232
  59.1 0.0 collective-permute-done.12.refs_1_
  59.1 0.8 %collective-permute-done.13.refs_2_ = bf16[2,4,32,128]{3,2,1,0:T(8,128)(2,1)S(1)} collective-permute-done((bf16[2,4,32,128]{3,2,1,0:T(8,128)(2,1)S(1)}, bf16[2,4,32,128]{3,2,1,0:T(8,128)(2,1)S(1)}, u32[]{:S(2)}, u32[]{:S(2)}) %collective-permute-start.13) | collective-permute-done | bytes 65568 | tf_op jit(solution)/shard_map/ppermute | solution.py:257
  59.9 0.8 %collective-permute-done.14.refs_3_ = bf16[2,4,32,128]{3,2,1,0:T(8,128)(2,1)S(1)} collective-permute-done((bf16[2,4,32,128]{3,2,1,0:T(8,128)(2,1)S(1)}, bf16[2,4,32,128]{3,2,1,0:T(8,128)(2,1)S(1)}, u32[]{:S(2)}, u32[]{:S(2)}) %collective-permute-start.14) | collective-permute-done | bytes 65568 | tf_op jit(solution)/shard_map/ppermute | solution.py:257
  60.8 0.9 %shard_map.58 = f32[8,4,128,128]{3,2,1,0:T(8,128)} custom-call(bf16[2,4,32,128]{3,2,1,0:T(8,128)(2,1)S(1)} %get-tuple-element.65.refs_0_, bf16[2,4,32,128]{3,2,1,0:T(8,128)(2,1)S(1)} %collective-permute-done.12.refs_1_, bf16[2,4,32,128]{3,2,1,0:T(8,128)(2,1)S(1)} %collective-permute-done.13.refs_2_, ...), custom_call_target="tpu_custom_call", output_to_operand_aliasing={{}: (4, {})} | custom-call | bytes 4456448 | tf_op jit(solution)/shard_map/pallas_call | solution.py:232
  (2 shorter events, 0.1 us)
Async XLA Ops:
  0.0 1.1 %copy-start = (bf16[8,11,32,128]{3,2,1,0:T(8,128)(2,1)S(1)}, bf16[8,11,32,128]{3,2,1,0:T(8,128)(2,1)}, u32[]{:S(2)}) copy-start(bf16[8,11,32,128]{3,2,1,0:T(8,128)(2,1)} %density.1) | copy-start | bytes 2162692
  1.1 0.7 %copy-start.3 = (s32[64,11]{0,1:T(8,128)S(1)}, s32[64,11]{0,1:T(8,128)}, u32[]{:S(2)}) copy-start(s32[64,11]{0,1:T(8,128)} %param.5) | copy-start | bytes 8452
  2.9 7.8 %collective-permute-start.3 = (bf16[63,32,128]{2,1,0:T(8,128)(2,1)S(1)}, bf16[63,32,128]{2,1,0:T(8,128)(2,1)S(1)}, u32[]{:S(2)}, u32[]{:S(2)}) collective-permute-start(bf16[63,32,128]{2,1,0:T(8,128)(2,1)S(1)} %get-tuple-element.41.upper), channel_id=1, source_target_pairs={{0,2},{2,0},{4,6},{6,4},{1,3},{3,1},{5,7},{7,5},{8,10},{10,8},{12,... | collective-permute-start | bytes 1548296 | tf_op jit(solution)/shard_map/ppermute | solution.py:257
  3.4 16.9 %collective-permute-start.2 = (bf16[63,32,128]{2,1,0:T(8,128)(2,1)S(1)}, bf16[63,32,128]{2,1,0:T(8,128)(2,1)S(1)}, u32[]{:S(2)}, u32[]{:S(2)}) collective-permute-start(bf16[63,32,128]{2,1,0:T(8,128)(2,1)S(1)} %get-tuple-element.41.upper), channel_id=1, source_target_pairs={{0,4},{2,6},{4,0},{6,2},{1,5},{3,7},{5,1},{7,3},{8,12},{10,14},{12... | collective-permute-start | bytes 1548296 | tf_op jit(solution)/shard_map/ppermute | solution.py:257
  6.0 16.8 %collective-permute-start = (bf16[37,32,128]{2,1,0:T(8,128)(2,1)S(1)}, bf16[37,32,128]{2,1,0:T(8,128)(2,1)S(1)}, u32[]{:S(2)}, u32[]{:S(2)}) collective-permute-start(bf16[37,32,128]{2,1,0:T(8,128)(2,1)S(1)} %get-tuple-element.39), channel_id=1, source_target_pairs={{0,1},{1,8},{8,9},{9,16},{16,17},{17,24},{24,25},{25,0},{2,3},{3,1... | collective-permute-start | bytes 909320 | tf_op jit(solution)/shard_map/ppermute | solution.py:254
  7.5 15.5 %collective-permute-start.1 = (bf16[37,32,128]{2,1,0:T(8,128)(2,1)S(1)}, bf16[37,32,128]{2,1,0:T(8,128)(2,1)S(1)}, u32[]{:S(2)}, u32[]{:S(2)}) collective-permute-start(bf16[37,32,128]{2,1,0:T(8,128)(2,1)S(1)} %get-tuple-element.40), channel_id=1, source_target_pairs={{0,25},{1,0},{8,1},{9,8},{16,9},{17,16},{24,17},{25,24},{2,27},{3,... | collective-permute-start | bytes 909320 | tf_op jit(solution)/shard_map/ppermute | solution.py:254
  10.7 9.6 %collective-permute-start.4 = (bf16[3,32,128]{2,1,0:T(8,128)(2,1)S(1)}, bf16[3,32,128]{2,1,0:T(8,128)(2,1)S(1)}, u32[]{:S(2)}, u32[]{:S(2)}) collective-permute-start(bf16[3,32,128]{2,1,0:T(8,128)(2,1)S(1)} %get-tuple-element.44), channel_id=1, source_target_pairs={{0,8},{1,9},{8,16},{9,17},{16,24},{17,25},{24,0},{25,1},{2,10},{3,... | collective-permute-start | bytes 73736 | tf_op jit(solution)/shard_map/ppermute | solution.py:254
  10.7 9.6 %collective-permute-start.5 = (bf16[3,32,128]{2,1,0:T(8,128)(2,1)S(1)}, bf16[3,32,128]{2,1,0:T(8,128)(2,1)S(1)}, u32[]{:S(2)}, u32[]{:S(2)}) collective-permute-start(bf16[3,32,128]{2,1,0:T(8,128)(2,1)S(1)} %get-tuple-element.45), channel_id=1, source_target_pairs={{0,24},{1,25},{8,0},{9,1},{16,8},{17,9},{24,16},{25,17},{2,26},{3,... | collective-permute-start | bytes 73736 | tf_op jit(solution)/shard_map/ppermute | solution.py:254
  20.4 1.5 %collective-permute-start.6 = (bf16[21,32,128]{2,1,0:T(8,128)(2,1)S(1)}, bf16[21,32,128]{2,1,0:T(8,128)(2,1)S(1)}, u32[]{:S(2)}, u32[]{:S(2)}) collective-permute-start(bf16[21,32,128]{2,1,0:T(8,128)(2,1)S(1)} %get-tuple-element.49), channel_id=1, source_target_pairs={{0,2},{2,0},{4,6},{6,4},{1,3},{3,1},{5,7},{7,5},{8,10},{10,8},{12,... | collective-permute-start | bytes 516104 | tf_op jit(solution)/shard_map/ppermute | solution.py:257
  20.4 1.6 %collective-permute-start.7 = (bf16[21,32,128]{2,1,0:T(8,128)(2,1)S(1)}, bf16[21,32,128]{2,1,0:T(8,128)(2,1)S(1)}, u32[]{:S(2)}, u32[]{:S(2)}) collective-permute-start(bf16[21,32,128]{2,1,0:T(8,128)(2,1)S(1)} %get-tuple-element.50), channel_id=1, source_target_pairs={{0,2},{2,0},{4,6},{6,4},{1,3},{3,1},{5,7},{7,5},{8,10},{10,8},{12,... | collective-permute-start | bytes 516104 | tf_op jit(solution)/shard_map/ppermute | solution.py:257
  20.9 1.4 %collective-permute-start.8 = (bf16[21,32,128]{2,1,0:T(8,128)(2,1)S(1)}, bf16[21,32,128]{2,1,0:T(8,128)(2,1)S(1)}, u32[]{:S(2)}, u32[]{:S(2)}) collective-permute-start(bf16[21,32,128]{2,1,0:T(8,128)(2,1)S(1)} %get-tuple-element.51), channel_id=1, source_target_pairs={{0,2},{2,0},{4,6},{6,4},{1,3},{3,1},{5,7},{7,5},{8,10},{10,8},{12,... | collective-permute-start | bytes 516104 | tf_op jit(solution)/shard_map/ppermute | solution.py:257
  21.1 1.9 %copy-start.1 = (s32[64,12]{0,1:T(8,128)S(1)}, s32[64,12]{0,1:T(8,128)}, u32[]{:S(2)}) copy-start(s32[64,12]{0,1:T(8,128)} %param.6) | copy-start | bytes 9220
  25.2 5.1 %copy-start.2 = (s32[64,16]{0,1:T(8,128)S(1)}, s32[64,16]{0,1:T(8,128)}, u32[]{:S(2)}) copy-start(s32[64,16]{0,1:T(8,128)} %param.7) | copy-start | bytes 12292
  25.2 19.6 %collective-permute-start.9 = (bf16[5,12,32,128]{3,2,1,0:T(8,128)(2,1)S(1)}, bf16[5,12,32,128]{3,2,1,0:T(8,128)(2,1)S(1)}, u32[]{:S(2)}, u32[]{:S(2)}) collective-permute-start(bf16[5,12,32,128]{3,2,1,0:T(8,128)(2,1)S(1)} %get-tuple-element.57.low), channel_id=1, source_target_pairs={{0,25},{1,0},{8,1},{9,8},{16,9},{17,16},{24,17},{25,24},{2,27},{3,... | collective-permute-start | bytes 1474568 | tf_op jit(solution)/shard_map/ppermute | solution.py:254
  30.3 14.6 %collective-permute-start.11 = (bf16[3,12,32,128]{3,2,1,0:T(8,128)(2,1)S(1)}, bf16[3,12,32,128]{3,2,1,0:T(8,128)(2,1)S(1)}, u32[]{:S(2)}, u32[]{:S(2)}) collective-permute-start(bf16[3,12,32,128]{3,2,1,0:T(8,128)(2,1)S(1)} %shard_map.52.close), channel_id=1, source_target_pairs={{0,1},{1,8},{8,9},{9,16},{16,17},{17,24},{24,25},{25,0},{2,3},{3,1... | collective-permute-start | bytes 884744 | tf_op jit(solution)/shard_map/ppermute | solution.py:254
  44.9 8.8 %collective-permute-start.10 = (bf16[2,12,32,128]{3,2,1,0:T(8,128)(2,1)S(1)}, bf16[2,12,32,128]{3,2,1,0:T(8,128)(2,1)S(1)}, u32[]{:S(2)}, u32[]{:S(2)}) collective-permute-start(bf16[2,12,32,128]{3,2,1,0:T(8,128)(2,1)S(1)} %get-tuple-element.60), channel_id=1, source_target_pairs={{0,1},{1,8},{8,9},{9,16},{16,17},{17,24},{24,25},{25,0},{2,3},{3,1... | collective-permute-start | bytes 589832 | tf_op jit(solution)/shard_map/ppermute | solution.py:254
  46.6 8.8 %collective-permute-start.15 = (bf16[6,4,32,128]{3,2,1,0:T(8,128)(2,1)S(1)}, bf16[6,4,32,128]{3,2,1,0:T(8,128)(2,1)S(1)}, u32[]{:S(2)}, u32[]{:S(2)}) collective-permute-start(bf16[6,4,32,128]{3,2,1,0:T(8,128)(2,1)S(1)} %get-tuple-element.70), channel_id=1, source_target_pairs={{0,2},{2,0},{4,6},{6,4},{1,3},{3,1},{5,7},{7,5},{8,10},{10,8},{12,... | collective-permute-start | bytes 589832 | tf_op jit(solution)/shard_map/ppermute | solution.py:257
  46.7 9.9 %collective-permute-start.16 = (bf16[6,4,32,128]{3,2,1,0:T(8,128)(2,1)S(1)}, bf16[6,4,32,128]{3,2,1,0:T(8,128)(2,1)S(1)}, u32[]{:S(2)}, u32[]{:S(2)}) collective-permute-start(bf16[6,4,32,128]{3,2,1,0:T(8,128)(2,1)S(1)} %get-tuple-element.71), channel_id=1, source_target_pairs={{0,4},{2,6},{4,0},{6,2},{1,5},{3,7},{5,1},{7,3},{8,12},{10,14},{12... | collective-permute-start | bytes 589832 | tf_op jit(solution)/shard_map/ppermute | solution.py:257
  47.3 10.5 %collective-permute-start.17 = (bf16[6,4,32,128]{3,2,1,0:T(8,128)(2,1)S(1)}, bf16[6,4,32,128]{3,2,1,0:T(8,128)(2,1)S(1)}, u32[]{:S(2)}, u32[]{:S(2)}) collective-permute-start(bf16[6,4,32,128]{3,2,1,0:T(8,128)(2,1)S(1)} %get-tuple-element.72), channel_id=1, source_target_pairs={{0,6},{2,4},{4,2},{6,0},{1,7},{3,5},{5,3},{7,1},{8,14},{10,12},{12... | collective-permute-start | bytes 589832 | tf_op jit(solution)/shard_map/ppermute | solution.py:257
  54.7 4.4 %collective-permute-start.12 = (bf16[2,4,32,128]{3,2,1,0:T(8,128)(2,1)S(1)}, bf16[2,4,32,128]{3,2,1,0:T(8,128)(2,1)S(1)}, u32[]{:S(2)}, u32[]{:S(2)}) collective-permute-start(bf16[2,4,32,128]{3,2,1,0:T(8,128)(2,1)S(1)} %get-tuple-element.66), channel_id=1, source_target_pairs={{0,2},{2,0},{4,6},{6,4},{1,3},{3,1},{5,7},{7,5},{8,10},{10,8},{12,... | collective-permute-start | bytes 196616 | tf_op jit(solution)/shard_map/ppermute | solution.py:257
  54.8 5.1 %collective-permute-start.13 = (bf16[2,4,32,128]{3,2,1,0:T(8,128)(2,1)S(1)}, bf16[2,4,32,128]{3,2,1,0:T(8,128)(2,1)S(1)}, u32[]{:S(2)}, u32[]{:S(2)}) collective-permute-start(bf16[2,4,32,128]{3,2,1,0:T(8,128)(2,1)S(1)} %get-tuple-element.67), channel_id=1, source_target_pairs={{0,4},{2,6},{4,0},{6,2},{1,5},{3,7},{5,1},{7,3},{8,12},{10,14},{12... | collective-permute-start | bytes 196616 | tf_op jit(solution)/shard_map/ppermute | solution.py:257
  55.4 5.4 %collective-permute-start.14 = (bf16[2,4,32,128]{3,2,1,0:T(8,128)(2,1)S(1)}, bf16[2,4,32,128]{3,2,1,0:T(8,128)(2,1)S(1)}, u32[]{:S(2)}, u32[]{:S(2)}) collective-permute-start(bf16[2,4,32,128]{3,2,1,0:T(8,128)(2,1)S(1)} %get-tuple-element.68), channel_id=1, source_target_pairs={{0,6},{2,4},{4,2},{6,0},{1,7},{3,5},{5,3},{7,1},{8,14},{10,12},{12... | collective-permute-start | bytes 196616 | tf_op jit(solution)/shard_map/ppermute | solution.py:257

commit v10 on v9

--- a/solution.py
+++ b/solution.py
@@ -49,14 +49,20 @@
     return jnp.where(value < 0, value + total, jnp.where(value >= total, value - total, value))
 
 
-def reorder_kernel(pattern, density, h0, h1, h2, h3, upper, band):
+def reorder_kernel(pattern, density, h0, h1, h2, h3, upper, band, blocks, table, sems):
     first, total = own_place()[1], pattern.shape[1]
+    copies = [pltpu.make_async_copy(density.at[i], blocks.at[i], sems.at[i]) for i in range(ROWS)]
+    listing = pltpu.make_async_copy(pattern, table, sems.at[ROWS])
+    for copy in (listing, *copies):
+        copy.start()
     band[...] = jnp.zeros_like(band)
+    listing.wait()
     for i in range(ROWS):
-        for s in range(density.shape[1]):
-            listed = pattern[s, first + i]
+        copies[i].wait()
+        for s in range(blocks.shape[1]):
+            listed = table[s, first + i]
             o = wrapped(listed - (first + i) + RADIUS, total)
-            band[i, jnp.where(listed >= 0, o, BAND)] = density[i, s]
+            band[i, jnp.where(listed >= 0, o, BAND)] = blocks[i, s]
     for out, entries in zip((h0, h1, h2, h3, upper), (*LISTS, UPPER)):
         for e, (j, o) in enumerate(entries):
             out[e] = band[j, o]
@@ -257,9 +263,11 @@
         return lax.ppermute(x, "col", [(c, c ^ bits) for c in range(4)])
 
     *halos, upper, band = call(
-        reorder_kernel, [SMEM, VMEM],
+        reorder_kernel, [ANY, ANY],
         [*(shape(len(e), *piece) for e in (*LISTS, UPPER)), shape(ROWS, BAND + 1, *piece)],
         (pattern, density),
+        [pltpu.VMEM(density.shape, density.dtype), pltpu.SMEM(pattern.shape, pattern.dtype),
+         pltpu.SemaphoreType.DMA((ROWS + 1,))], limit=60,
     )
     u2 = across(upper, 2)
     u1 = across(upper, 1)

time: 61.9 us -> 61.8 us (level)
  waiting for transfers between devices: 21.8 us -> 19.9 us
  Pallas kernels: 18.3 us -> 19.7 us
    ppermute x7, waiting for transfers between devices: 17.8 us -> 15.9 us  [shifted(): lax.ppermute(x, ('row', 'layer'), [(g, (g + d) % groups) for g in range(g...]
    pallas_call x13, Pallas kernels: 18.3 us -> 19.7 us  [call(): pl.pallas_call(kernel, out_shape=outs, in_specs=specs, out_specs=out_spec...]
where the time goes in v10:
time: 61.8 us; the launch traced here: 61.5 us
  waiting for transfers between devices  19.9 us (32%)
  Pallas kernels  19.7 us (32%)
  starting transfers between devices  19.6 us (32%)
  local copies, waits for them, and re-layouts  2.18 us (4%)
    pallas_call x13, Pallas kernels, call(): pl.pallas_call(kernel, out_shape=outs, in_specs=specs, out_specs=out_spec...  19.7 us
    ppermute x7, waiting for transfers between devices, shifted(): lax.ppermute(x, ('row', 'layer'), [(g, (g + d) % groups) for g in range(g...  15.9 us
    ppermute x7, starting transfers between devices, shifted(): lax.ppermute(x, ('row', 'layer'), [(g, (g + d) % groups) for g in range(g...  12 us
    ppermute x11, starting transfers between devices, across(): return lax.ppermute(x, 'col', [(c, c ^ bits) for c in range(4)])  7.59 us
    ppermute x11, waiting for transfers between devices, across(): return lax.ppermute(x, 'col', [(c, c ^ bits) for c in range(4)])  4.02 us
    unnamed x8, local copies, waits for them, and re-layouts  2.18 us
  transfers between devices with their start and end apart: 18, of which 10 were waited for; matrix products, arithmetic and copies ran while one was open for 0% of the time, Pallas kernels for 23%

profile of v10, /device:TPU:0, one launch (start us, length us, event | category | flops | bytes accessed | tf_op | source)
XLA Modules:
  0.0 61.5 jit_solution(16864223556659548865)
XLA Ops:
  0.0 2.5 %shard_map.46 = (bf16[37,32,128]{2,1,0:T(8,128)(2,1)}, bf16[37,32,128]{2,1,0:T(8,128)(2,1)}, bf16[3,32,128]{2,1,0:T(8,128)(2,1)}, bf16[3,32,128]{2,1,0:T(8,128)(...) custom-call(s32[11,64]{1,0:T(8,128)} %bitcast.13, bf16[8,11,32,128]{3,2,1,0:T(8,128)(2,1)} %density.1), custom_call_target="tpu_custom_call" | custom-call | bytes 2681600 | tf_op jit(solution)/shard_map/pallas_call | solution.py:238
  2.5 0.5 collective-permute-start.3
  3.1 2.6 %collective-permute-start.2 = (bf16[63,32,128]{2,1,0:T(8,128)(2,1)}, bf16[63,32,128]{2,1,0:T(8,128)(2,1)S(1)}, u32[]{:S(2)}, u32[]{:S(2)}) collective-permute-start(bf16[63,32,128]{2,1,0:T(8,128)(2,1)} %get-tuple-element.41.upper), channel_id=1, source_target_pairs={{0,4},{2,6},{4,0},{6,2},{1,5},{3,7},{5,1},{7,3},{8,12},{10,14},{12... | collective-permute-start | bytes 1548296 | tf_op jit(solution)/shard_map/ppermute | solution.py:263
  5.6 1.5 %collective-permute-start = (bf16[37,32,128]{2,1,0:T(8,128)(2,1)}, bf16[37,32,128]{2,1,0:T(8,128)(2,1)S(1)}, u32[]{:S(2)}, u32[]{:S(2)}) collective-permute-start(bf16[37,32,128]{2,1,0:T(8,128)(2,1)} %get-tuple-element.39), channel_id=1, source_target_pairs={{0,1},{1,8},{8,9},{9,16},{16,17},{17,24},{24,25},{25,0},{2,3},{3,1... | collective-permute-start | bytes 909320 | tf_op jit(solution)/shard_map/ppermute | solution.py:260
  7.2 3.2 %collective-permute-start.1 = (bf16[37,32,128]{2,1,0:T(8,128)(2,1)}, bf16[37,32,128]{2,1,0:T(8,128)(2,1)S(1)}, u32[]{:S(2)}, u32[]{:S(2)}) collective-permute-start(bf16[37,32,128]{2,1,0:T(8,128)(2,1)} %get-tuple-element.40), channel_id=1, source_target_pairs={{0,25},{1,0},{8,1},{9,8},{16,9},{17,16},{24,17},{25,24},{2,27},{3,... | collective-permute-start | bytes 909320 | tf_op jit(solution)/shard_map/ppermute | solution.py:260
  10.4 0.0 collective-permute-start.4
  10.4 0.0 collective-permute-done.3.u1
  10.4 3.8 %collective-permute-start.5 = (bf16[3,32,128]{2,1,0:T(8,128)(2,1)}, bf16[3,32,128]{2,1,0:T(8,128)(2,1)S(1)}, u32[]{:S(2)}, u32[]{:S(2)}) collective-permute-start(bf16[3,32,128]{2,1,0:T(8,128)(2,1)} %get-tuple-element.45), channel_id=1, source_target_pairs={{0,24},{1,25},{8,0},{9,1},{16,8},{17,9},{24,16},{25,17},{2,26},{3,... | collective-permute-start | bytes 73736 | tf_op jit(solution)/shard_map/ppermute | solution.py:260
  14.2 0.0 copy-start
  14.2 1.1 %copy-done = bf16[8,12,32,128]{3,2,1,0:T(8,128)(2,1)S(1)} copy-done((bf16[8,12,32,128]{3,2,1,0:T(8,128)(2,1)S(1)}, bf16[8,12,32,128]{3,2,1,0:T(8,128)(2,1)}, u32[]{:S(2)}) %copy-start) | copy-done | bytes 786456
  15.3 0.0 copy-start.1
  15.3 1.0 %copy-done.1 = bf16[63,32,128]{2,1,0:T(8,128)(2,1)S(1)} copy-done((bf16[63,32,128]{2,1,0:T(8,128)(2,1)S(1)}, bf16[63,32,128]{2,1,0:T(8,128)(2,1)}, u32[]{:S(2)}) %copy-start.1) | copy-done | bytes 516120
  16.4 1.3 %shard_map.47 = (bf16[28,18,32,128]{3,2,1,0:T(8,128)(2,1)S(1)}, bf16[8,18,128,128]{3,2,1,0:T(8,128)(2,1)S(1)}) custom-call(bf16[8,12,32,128]{3,2,1,0:T(8,128)(2,1)S(1)} %copy-done, bf16[63,32,128]{2,1,0:T(8,128)(2,1)S(1)} %copy-done.1, bf16[63,32,128]{2,1,0:T(8,128)(2,1)S(1)} %collective-permute-done.3.u1), custom_call_target="tpu_custom_call" | custom-call | bytes 10665984 | tf_op jit(solution)/shard_map/pallas_call | solution.py:238
  17.6 2.5 %collective-permute-done.4.h2 = bf16[3,32,128]{2,1,0:T(8,128)(2,1)S(1)} collective-permute-done((bf16[3,32,128]{2,1,0:T(8,128)(2,1)}, bf16[3,32,128]{2,1,0:T(8,128)(2,1)S(1)}, u32[]{:S(2)}, u32[]{:S(2)}) %collective-permute-start.4) | collective-permute-done | bytes 24608 | tf_op jit(solution)/shard_map/ppermute | solution.py:260
  20.2 0.0 collective-permute-done.5.h3
  20.2 0.0 collective-permute-done.2.u2
  20.2 0.1 collective-permute-start.6
  20.3 0.5 collective-permute-start.7
  20.8 0.1 collective-permute-start.8
  20.9 0.0 copy-start.2
  20.9 0.8 %collective-permute-done.6.refs_0_ = bf16[21,32,128]{2,1,0:T(8,128)(2,1)S(1)} collective-permute-done((bf16[21,32,128]{2,1,0:T(8,128)(2,1)S(1)}, bf16[21,32,128]{2,1,0:T(8,128)(2,1)S(1)}, u32[]{:S(2)}, u32[]{:S(2)}) %collective-permute-start.6) | collective-permute-done | bytes 172064 | tf_op jit(solution)/shard_map/ppermute | solution.py:263
  21.7 0.2 collective-permute-done.7.refs_1_
  21.9 0.3 collective-permute-done.8.refs_2_
  22.2 0.5 shard_map.50
  22.7 0.0 collective-permute-done.h0
  22.7 0.1 collective-permute-done.1.h1
  22.8 0.0 copy-done.2
  22.8 2.2 %shard_map.51 = (bf16[5,12,32,128]{3,2,1,0:T(8,128)(2,1)S(1)}, bf16[2,12,32,128]{3,2,1,0:T(8,128)(2,1)S(1)}, bf16[28,18,32,128]{3,2,1,0:T(8,128)(2,1)S(1)}) custom-call(s32[12,64]{1,0:T(8,128)S(1)} %bitcast.3, bf16[37,32,128]{2,1,0:T(8,128)(2,1)S(1)} %collective-permute-done.h0, ...), custom_call_target="tpu_custom_call", output_to_operand_aliasing={{2}: (6, {})} | custom-call | flops 692060160 | bytes 14322688 | tf_op jit(solution)/shard_map/pallas_call | solution.py:238
  25.1 0.0 copy-start.3
  25.1 3.4 %collective-permute-start.9 = (bf16[5,12,32,128]{3,2,1,0:T(8,128)(2,1)S(1)}, bf16[5,12,32,128]{3,2,1,0:T(8,128)(2,1)S(1)}, u32[]{:S(2)}, u32[]{:S(2)}) collective-permute-start(bf16[5,12,32,128]{3,2,1,0:T(8,128)(2,1)S(1)} %get-tuple-element.57.low), channel_id=1, source_target_pairs={{0,25},{1,0},{8,1},{9,8},{16,9},{17,16},{24,17},{25,24},{2,27},{3,... | collective-permute-start | bytes 1474568 | tf_op jit(solution)/shard_map/ppermute | solution.py:260
  28.4 1.7 %shard_map.52.close = bf16[3,12,32,128]{3,2,1,0:T(8,128)(2,1)S(1)} custom-call(s32[12,64]{1,0:T(8,128)S(1)} %bitcast.4, bf16[28,18,32,128]{3,2,1,0:T(8,128)(2,1)S(1)} %get-tuple-element.58.strips, bf16[8,18,128,128]{3,2,1,0:T(8,128)(2,1)S(1)} %get-tuple-element.54.left.refs_2_.refs_1_), custom_call_target="tpu_custom_call" | custom-call | flops 415236096 | bytes 9145344 | tf_op jit(solution)/shard_map/pallas_call | solution.py:238
  30.1 0.1 collective-permute-start.11
  30.2 0.0 copy-done.3
  30.2 5.2 %shard_map.53 = (bf16[38,18,32,128]{3,2,1,0:T(8,128)(2,1)S(1)}, f32[8,16,32,128]{3,2,1,0:T(8,128)S(1)}) custom-call(s32[12,64]{1,0:T(8,128)S(1)} %bitcast.5, s32[16,64]{1,0:T(8,128)S(1)} %bitcast.9, bf16[5,12,32,128]{3,2,1,0:T(8,128)(2,1)S(1)} %get-tuple-element.57.low, bf16[3,12,32,128]{3,2,1,0:T(8,128)(2,1)S(1)} %shard_map.52.close, ...), custom_call_target="tpu_custom_call" | custom-call | flops 1073741824 | bytes 13212672 | tf_op jit(solution)/shard_map/pallas_call | solution.py:238
  35.4 9.3 %collective-permute-done.9.refs_0_ = bf16[5,12,32,128]{3,2,1,0:T(8,128)(2,1)S(1)} collective-permute-done((bf16[5,12,32,128]{3,2,1,0:T(8,128)(2,1)S(1)}, bf16[5,12,32,128]{3,2,1,0:T(8,128)(2,1)S(1)}, u32[]{:S(2)}, u32[]{:S(2)}) %collective-permute-start.9) | collective-permute-done | bytes 491552 | tf_op jit(solution)/shard_map/ppermute | solution.py:260
  44.7 0.0 collective-permute-start.10
  44.7 0.0 collective-permute-done.11.refs_1_
  44.7 1.8 %shard_map.54 = (bf16[6,4,32,128]{3,2,1,0:T(8,128)(2,1)S(1)}, bf16[6,4,32,128]{3,2,1,0:T(8,128)(2,1)S(1)}, bf16[6,4,32,128]{3,2,1,0:T(8,128)(2,1)S(1)}, bf16[6,4...) custom-call(s32[12,64]{1,0:T(8,128)S(1)} %bitcast.6, ...), custom_call_target="tpu_custom_call", output_to_operand_aliasing={{4}: (6, {})} | custom-call | tf_op jit(solution)/shard_map/pallas_call | solution.py:238
  46.5 0.1 collective-permute-start.15
  46.5 0.6 collective-permute-start.16
  47.2 1.3 %collective-permute-start.17 = (bf16[6,4,32,128]{3,2,1,0:T(8,128)(2,1)S(1)}, bf16[6,4,32,128]{3,2,1,0:T(8,128)(2,1)S(1)}, u32[]{:S(2)}, u32[]{:S(2)}) collective-permute-start(bf16[6,4,32,128]{3,2,1,0:T(8,128)(2,1)S(1)} %get-tuple-element.72), channel_id=1, source_target_pairs={{0,6},{2,4},{4,2},{6,0},{1,7},{3,5},{5,3},{7,1},{8,14},{10,12},{12... | collective-permute-start | bytes 589832 | tf_op jit(solution)/shard_map/ppermute | solution.py:263
  48.4 1.2 %shard_map.55.refs_2_ = f32[2,16,32,128]{3,2,1,0:T(8,128)S(1)} custom-call(s32[12,64]{1,0:T(8,128)S(1)} %bitcast.7, s32[16,64]{1,0:T(8,128)S(1)} %bitcast.11, bf16[8,18,128,128]{3,2,1,0:T(8,128)(2,1)S(1)} %get-tuple-element.54.left.refs_2_.refs_1_, f32[8,16,32,128]{3,2,1,0:T(8,128)S(1)} %get-tuple-element.61.refs_3_.partial, ...), custom_call_target="tpu_custom_call" | custom-call | tf_op jit(solution)/shard_map/pallas_call | solution.py:238
  49.6 3.9 %collective-permute-done.10.refs_0_ = bf16[2,12,32,128]{3,2,1,0:T(8,128)(2,1)S(1)} collective-permute-done((bf16[2,12,32,128]{3,2,1,0:T(8,128)(2,1)S(1)}, bf16[2,12,32,128]{3,2,1,0:T(8,128)(2,1)S(1)}, u32[]{:S(2)}, u32[]{:S(2)}) %collective-permute-start.10) | collective-permute-done | bytes 196640 | tf_op jit(solution)/shard_map/ppermute | solution.py:260
  53.5 1.1 %shard_map.56 = (bf16[2,4,32,128]{3,2,1,0:T(8,128)(2,1)S(1)}, bf16[2,4,32,128]{3,2,1,0:T(8,128)(2,1)S(1)}, bf16[2,4,32,128]{3,2,1,0:T(8,128)(2,1)S(1)}, bf16[2,4...) custom-call(s32[12,64]{1,0:T(8,128)S(1)} %bitcast.8, ...), custom_call_target="tpu_custom_call", output_to_operand_aliasing={{4}: (5, {})} | custom-call | tf_op jit(solution)/shard_map/pallas_call | solution.py:238
  54.5 0.1 collective-permute-start.12
  54.6 0.6 collective-permute-start.13
  55.2 0.0 collective-permute-done.15.refs_1_
  55.2 1.3 %collective-permute-start.14 = (bf16[2,4,32,128]{3,2,1,0:T(8,128)(2,1)S(1)}, bf16[2,4,32,128]{3,2,1,0:T(8,128)(2,1)S(1)}, u32[]{:S(2)}, u32[]{:S(2)}) collective-permute-start(bf16[2,4,32,128]{3,2,1,0:T(8,128)(2,1)S(1)} %get-tuple-element.68), channel_id=1, source_target_pairs={{0,6},{2,4},{4,2},{6,0},{1,7},{3,5},{5,3},{7,1},{8,14},{10,12},{12... | collective-permute-start | bytes 196616 | tf_op jit(solution)/shard_map/ppermute | solution.py:263
  56.5 0.0 collective-permute-done.16.refs_2_
  56.5 1.1 %collective-permute-done.17.refs_3_ = bf16[6,4,32,128]{3,2,1,0:T(8,128)(2,1)S(1)} collective-permute-done((bf16[6,4,32,128]{3,2,1,0:T(8,128)(2,1)S(1)}, bf16[6,4,32,128]{3,2,1,0:T(8,128)(2,1)S(1)}, u32[]{:S(2)}, u32[]{:S(2)}) %collective-permute-start.17) | collective-permute-done | bytes 196640 | tf_op jit(solution)/shard_map/ppermute | solution.py:263
  57.6 1.3 %shard_map.57.refs_4_ = f32[8,4,128,128]{3,2,1,0:T(8,128)} custom-call(bf16[6,4,32,128]{3,2,1,0:T(8,128)(2,1)S(1)} %get-tuple-element.69.refs_0_, bf16[6,4,32,128]{3,2,1,0:T(8,128)(2,1)S(1)} %collective-permute-done.15.refs_1_, bf16[6,4,32,128]{3,2,1,0:T(8,128)(2,1)S(1)} %collective-permute-done.16.refs_2_, ...), custom_call_target="tpu_custom_call" | custom-call | bytes 2883584 | tf_op jit(solution)/shard_map/pallas_call | solution.py:238
  59.0 0.0 collective-permute-done.12.refs_1_
  59.0 0.8 %collective-permute-done.13.refs_2_ = bf16[2,4,32,128]{3,2,1,0:T(8,128)(2,1)S(1)} collective-permute-done((bf16[2,4,32,128]{3,2,1,0:T(8,128)(2,1)S(1)}, bf16[2,4,32,128]{3,2,1,0:T(8,128)(2,1)S(1)}, u32[]{:S(2)}, u32[]{:S(2)}) %collective-permute-start.13) | collective-permute-done | bytes 65568 | tf_op jit(solution)/shard_map/ppermute | solution.py:263
  59.8 0.8 %collective-permute-done.14.refs_3_ = bf16[2,4,32,128]{3,2,1,0:T(8,128)(2,1)S(1)} collective-permute-done((bf16[2,4,32,128]{3,2,1,0:T(8,128)(2,1)S(1)}, bf16[2,4,32,128]{3,2,1,0:T(8,128)(2,1)S(1)}, u32[]{:S(2)}, u32[]{:S(2)}) %collective-permute-start.14) | collective-permute-done | bytes 65568 | tf_op jit(solution)/shard_map/ppermute | solution.py:263
  60.6 0.9 %shard_map.58 = f32[8,4,128,128]{3,2,1,0:T(8,128)} custom-call(bf16[2,4,32,128]{3,2,1,0:T(8,128)(2,1)S(1)} %get-tuple-element.65.refs_0_, bf16[2,4,32,128]{3,2,1,0:T(8,128)(2,1)S(1)} %collective-permute-done.12.refs_1_, bf16[2,4,32,128]{3,2,1,0:T(8,128)(2,1)S(1)} %collective-permute-done.13.refs_2_, ...), custom_call_target="tpu_custom_call", output_to_operand_aliasing={{}: (4, {})} | custom-call | bytes 4456448 | tf_op jit(solution)/shard_map/pallas_call | solution.py:238
  (2 shorter events, 0.1 us)
Async XLA Ops:
  2.5 7.8 %collective-permute-start.3 = (bf16[63,32,128]{2,1,0:T(8,128)(2,1)}, bf16[63,32,128]{2,1,0:T(8,128)(2,1)S(1)}, u32[]{:S(2)}, u32[]{:S(2)}) collective-permute-start(bf16[63,32,128]{2,1,0:T(8,128)(2,1)} %get-tuple-element.41.upper), channel_id=1, source_target_pairs={{0,2},{2,0},{4,6},{6,4},{1,3},{3,1},{5,7},{7,5},{8,10},{10,8},{12,... | collective-permute-start | bytes 1548296 | tf_op jit(solution)/shard_map/ppermute | solution.py:263
  3.1 17.1 %collective-permute-start.2 = (bf16[63,32,128]{2,1,0:T(8,128)(2,1)}, bf16[63,32,128]{2,1,0:T(8,128)(2,1)S(1)}, u32[]{:S(2)}, u32[]{:S(2)}) collective-permute-start(bf16[63,32,128]{2,1,0:T(8,128)(2,1)} %get-tuple-element.41.upper), channel_id=1, source_target_pairs={{0,4},{2,6},{4,0},{6,2},{1,5},{3,7},{5,1},{7,3},{8,12},{10,14},{12... | collective-permute-start | bytes 1548296 | tf_op jit(solution)/shard_map/ppermute | solution.py:263
  5.6 17.1 %collective-permute-start = (bf16[37,32,128]{2,1,0:T(8,128)(2,1)}, bf16[37,32,128]{2,1,0:T(8,128)(2,1)S(1)}, u32[]{:S(2)}, u32[]{:S(2)}) collective-permute-start(bf16[37,32,128]{2,1,0:T(8,128)(2,1)} %get-tuple-element.39), channel_id=1, source_target_pairs={{0,1},{1,8},{8,9},{9,16},{16,17},{17,24},{24,25},{25,0},{2,3},{3,1... | collective-permute-start | bytes 909320 | tf_op jit(solution)/shard_map/ppermute | solution.py:260
  7.2 15.7 %collective-permute-start.1 = (bf16[37,32,128]{2,1,0:T(8,128)(2,1)}, bf16[37,32,128]{2,1,0:T(8,128)(2,1)S(1)}, u32[]{:S(2)}, u32[]{:S(2)}) collective-permute-start(bf16[37,32,128]{2,1,0:T(8,128)(2,1)} %get-tuple-element.40), channel_id=1, source_target_pairs={{0,25},{1,0},{8,1},{9,8},{16,9},{17,16},{24,17},{25,24},{2,27},{3,... | collective-permute-start | bytes 909320 | tf_op jit(solution)/shard_map/ppermute | solution.py:260
  10.4 9.8 %collective-permute-start.4 = (bf16[3,32,128]{2,1,0:T(8,128)(2,1)}, bf16[3,32,128]{2,1,0:T(8,128)(2,1)S(1)}, u32[]{:S(2)}, u32[]{:S(2)}) collective-permute-start(bf16[3,32,128]{2,1,0:T(8,128)(2,1)} %get-tuple-element.44), channel_id=1, source_target_pairs={{0,8},{1,9},{8,16},{9,17},{16,24},{17,25},{24,0},{25,1},{2,10},{3,... | collective-permute-start | bytes 73736 | tf_op jit(solution)/shard_map/ppermute | solution.py:260
  10.4 9.8 %collective-permute-start.5 = (bf16[3,32,128]{2,1,0:T(8,128)(2,1)}, bf16[3,32,128]{2,1,0:T(8,128)(2,1)S(1)}, u32[]{:S(2)}, u32[]{:S(2)}) collective-permute-start(bf16[3,32,128]{2,1,0:T(8,128)(2,1)} %get-tuple-element.45), channel_id=1, source_target_pairs={{0,24},{1,25},{8,0},{9,1},{16,8},{17,9},{24,16},{25,17},{2,26},{3,... | collective-permute-start | bytes 73736 | tf_op jit(solution)/shard_map/ppermute | solution.py:260
  14.2 1.1 %copy-start = (bf16[8,12,32,128]{3,2,1,0:T(8,128)(2,1)S(1)}, bf16[8,12,32,128]{3,2,1,0:T(8,128)(2,1)}, u32[]{:S(2)}) copy-start(bf16[8,12,32,128]{3,2,1,0:T(8,128)(2,1)} %get-tuple-element.42.band) | copy-start | bytes 2359300
  15.3 1.0 %copy-start.1 = (bf16[63,32,128]{2,1,0:T(8,128)(2,1)S(1)}, bf16[63,32,128]{2,1,0:T(8,128)(2,1)}, u32[]{:S(2)}) copy-start(bf16[63,32,128]{2,1,0:T(8,128)(2,1)} %get-tuple-element.41.upper) | copy-start | bytes 1548292
  20.2 1.5 %collective-permute-start.6 = (bf16[21,32,128]{2,1,0:T(8,128)(2,1)S(1)}, bf16[21,32,128]{2,1,0:T(8,128)(2,1)S(1)}, u32[]{:S(2)}, u32[]{:S(2)}) collective-permute-start(bf16[21,32,128]{2,1,0:T(8,128)(2,1)S(1)} %get-tuple-element.49), channel_id=1, source_target_pairs={{0,2},{2,0},{4,6},{6,4},{1,3},{3,1},{5,7},{7,5},{8,10},{10,8},{12,... | collective-permute-start | bytes 516104 | tf_op jit(solution)/shard_map/ppermute | solution.py:263
  20.3 1.6 %collective-permute-start.7 = (bf16[21,32,128]{2,1,0:T(8,128)(2,1)S(1)}, bf16[21,32,128]{2,1,0:T(8,128)(2,1)S(1)}, u32[]{:S(2)}, u32[]{:S(2)}) collective-permute-start(bf16[21,32,128]{2,1,0:T(8,128)(2,1)S(1)} %get-tuple-element.50), channel_id=1, source_target_pairs={{0,2},{2,0},{4,6},{6,4},{1,3},{3,1},{5,7},{7,5},{8,10},{10,8},{12,... | collective-permute-start | bytes 516104 | tf_op jit(solution)/shard_map/ppermute | solution.py:263
  20.8 1.4 %collective-permute-start.8 = (bf16[21,32,128]{2,1,0:T(8,128)(2,1)S(1)}, bf16[21,32,128]{2,1,0:T(8,128)(2,1)S(1)}, u32[]{:S(2)}, u32[]{:S(2)}) collective-permute-start(bf16[21,32,128]{2,1,0:T(8,128)(2,1)S(1)} %get-tuple-element.51), channel_id=1, source_target_pairs={{0,2},{2,0},{4,6},{6,4},{1,3},{3,1},{5,7},{7,5},{8,10},{10,8},{12,... | collective-permute-start | bytes 516104 | tf_op jit(solution)/shard_map/ppermute | solution.py:263
  20.9 1.9 %copy-start.2 = (s32[64,12]{0,1:T(8,128)S(1)}, s32[64,12]{0,1:T(8,128)}, u32[]{:S(2)}) copy-start(s32[64,12]{0,1:T(8,128)} %param.6) | copy-start | bytes 9220
  25.1 5.1 %copy-start.3 = (s32[64,16]{0,1:T(8,128)S(1)}, s32[64,16]{0,1:T(8,128)}, u32[]{:S(2)}) copy-start(s32[64,16]{0,1:T(8,128)} %param.7) | copy-start | bytes 12292
  25.1 19.6 %collective-permute-start.9 = (bf16[5,12,32,128]{3,2,1,0:T(8,128)(2,1)S(1)}, bf16[5,12,32,128]{3,2,1,0:T(8,128)(2,1)S(1)}, u32[]{:S(2)}, u32[]{:S(2)}) collective-permute-start(bf16[5,12,32,128]{3,2,1,0:T(8,128)(2,1)S(1)} %get-tuple-element.57.low), channel_id=1, source_target_pairs={{0,25},{1,0},{8,1},{9,8},{16,9},{17,16},{24,17},{25,24},{2,27},{3,... | collective-permute-start | bytes 1474568 | tf_op jit(solution)/shard_map/ppermute | solution.py:260
  30.1 14.6 %collective-permute-start.11 = (bf16[3,12,32,128]{3,2,1,0:T(8,128)(2,1)S(1)}, bf16[3,12,32,128]{3,2,1,0:T(8,128)(2,1)S(1)}, u32[]{:S(2)}, u32[]{:S(2)}) collective-permute-start(bf16[3,12,32,128]{3,2,1,0:T(8,128)(2,1)S(1)} %shard_map.52.close), channel_id=1, source_target_pairs={{0,1},{1,8},{8,9},{9,16},{16,17},{17,24},{24,25},{25,0},{2,3},{3,1... | collective-permute-start | bytes 884744 | tf_op jit(solution)/shard_map/ppermute | solution.py:260
  44.7 8.8 %collective-permute-start.10 = (bf16[2,12,32,128]{3,2,1,0:T(8,128)(2,1)S(1)}, bf16[2,12,32,128]{3,2,1,0:T(8,128)(2,1)S(1)}, u32[]{:S(2)}, u32[]{:S(2)}) collective-permute-start(bf16[2,12,32,128]{3,2,1,0:T(8,128)(2,1)S(1)} %get-tuple-element.60), channel_id=1, source_target_pairs={{0,1},{1,8},{8,9},{9,16},{16,17},{17,24},{24,25},{25,0},{2,3},{3,1... | collective-permute-start | bytes 589832 | tf_op jit(solution)/shard_map/ppermute | solution.py:260
  46.5 8.8 %collective-permute-start.15 = (bf16[6,4,32,128]{3,2,1,0:T(8,128)(2,1)S(1)}, bf16[6,4,32,128]{3,2,1,0:T(8,128)(2,1)S(1)}, u32[]{:S(2)}, u32[]{:S(2)}) collective-permute-start(bf16[6,4,32,128]{3,2,1,0:T(8,128)(2,1)S(1)} %get-tuple-element.70), channel_id=1, source_target_pairs={{0,2},{2,0},{4,6},{6,4},{1,3},{3,1},{5,7},{7,5},{8,10},{10,8},{12,... | collective-permute-start | bytes 589832 | tf_op jit(solution)/shard_map/ppermute | solution.py:263
  46.5 9.9 %collective-permute-start.16 = (bf16[6,4,32,128]{3,2,1,0:T(8,128)(2,1)S(1)}, bf16[6,4,32,128]{3,2,1,0:T(8,128)(2,1)S(1)}, u32[]{:S(2)}, u32[]{:S(2)}) collective-permute-start(bf16[6,4,32,128]{3,2,1,0:T(8,128)(2,1)S(1)} %get-tuple-element.71), channel_id=1, source_target_pairs={{0,4},{2,6},{4,0},{6,2},{1,5},{3,7},{5,1},{7,3},{8,12},{10,14},{12... | collective-permute-start | bytes 589832 | tf_op jit(solution)/shard_map/ppermute | solution.py:263
  47.2 10.5 %collective-permute-start.17 = (bf16[6,4,32,128]{3,2,1,0:T(8,128)(2,1)S(1)}, bf16[6,4,32,128]{3,2,1,0:T(8,128)(2,1)S(1)}, u32[]{:S(2)}, u32[]{:S(2)}) collective-permute-start(bf16[6,4,32,128]{3,2,1,0:T(8,128)(2,1)S(1)} %get-tuple-element.72), channel_id=1, source_target_pairs={{0,6},{2,4},{4,2},{6,0},{1,7},{3,5},{5,3},{7,1},{8,14},{10,12},{12... | collective-permute-start | bytes 589832 | tf_op jit(solution)/shard_map/ppermute | solution.py:263
  54.5 4.4 %collective-permute-start.12 = (bf16[2,4,32,128]{3,2,1,0:T(8,128)(2,1)S(1)}, bf16[2,4,32,128]{3,2,1,0:T(8,128)(2,1)S(1)}, u32[]{:S(2)}, u32[]{:S(2)}) collective-permute-start(bf16[2,4,32,128]{3,2,1,0:T(8,128)(2,1)S(1)} %get-tuple-element.66), channel_id=1, source_target_pairs={{0,2},{2,0},{4,6},{6,4},{1,3},{3,1},{5,7},{7,5},{8,10},{10,8},{12,... | collective-permute-start | bytes 196616 | tf_op jit(solution)/shard_map/ppermute | solution.py:263
  54.6 5.1 %collective-permute-start.13 = (bf16[2,4,32,128]{3,2,1,0:T(8,128)(2,1)S(1)}, bf16[2,4,32,128]{3,2,1,0:T(8,128)(2,1)S(1)}, u32[]{:S(2)}, u32[]{:S(2)}) collective-permute-start(bf16[2,4,32,128]{3,2,1,0:T(8,128)(2,1)S(1)} %get-tuple-element.67), channel_id=1, source_target_pairs={{0,4},{2,6},{4,0},{6,2},{1,5},{3,7},{5,1},{7,3},{8,12},{10,14},{12... | collective-permute-start | bytes 196616 | tf_op jit(solution)/shard_map/ppermute | solution.py:263
  55.2 5.4 %collective-permute-start.14 = (bf16[2,4,32,128]{3,2,1,0:T(8,128)(2,1)S(1)}, bf16[2,4,32,128]{3,2,1,0:T(8,128)(2,1)S(1)}, u32[]{:S(2)}, u32[]{:S(2)}) collective-permute-start(bf16[2,4,32,128]{3,2,1,0:T(8,128)(2,1)S(1)} %get-tuple-element.68), channel_id=1, source_target_pairs={{0,6},{2,4},{4,2},{6,0},{1,7},{3,5},{5,3},{7,1},{8,14},{10,12},{12... | collective-permute-start | bytes 196616 | tf_op jit(solution)/shard_map/ppermute | solution.py:263
